TPU v7x, 32 devices: a whole 2x2x4 slice. The times are simulated.
32 devices in a mesh: seq: 8 (over y, x, core), tp: 4 (over z).
Axes of the slice: x: 2, y: 2, z: 4, core: 2. Of those that a mesh axis runs over, the one named last changes fastest.
Arguments:
- block_in: bfloat16 [8, 1024, 2048], P(None, 'seq'), may hold values from -6 to 6
- segment_ids: int32 [8, 1024], replicated, may hold values from 0 to 7, as said below
- first_gain: bfloat16 [2048], replicated, may hold values from 0.25 to 1.75
- first_bias: bfloat16 [2048], replicated, may hold values from -3 to 3
- w_query: bfloat16 [2048, 2048], P(None, 'tp'), may hold values from -0.125 to 0.125
- w_key: bfloat16 [2048, 2048], P(None, 'tp'), may hold values from -0.125 to 0.125
- w_value: bfloat16 [2048, 2048], P(None, 'tp'), may hold values from -0.125 to 0.125
- head_gain: bfloat16 [2048], P('tp'), may hold values from 0.25 to 1.75
- head_bias: bfloat16 [2048], P('tp'), may hold values from -3 to 3
- w_out: bfloat16 [2048, 2048], P(None, 'tp'), may hold values from -0.125 to 0.125
- second_gain: bfloat16 [2048], replicated, may hold values from 0.25 to 1.75
- second_bias: bfloat16 [2048], replicated, may hold values from -3 to 3
- w_up: bfloat16 [2048, 8192], P(None, 'tp'), may hold values from -0.125 to 0.125
- hidden_gain: bfloat16 [8192], P('tp'), may hold values from 0.25 to 1.75
- hidden_bias: bfloat16 [8192], P('tp'), may hold values from -3 to 3
- w_down: bfloat16 [2048, 8192], P(None, 'tp'), may hold values from -0.088388348 to 0.088388348
- out_cotangent: bfloat16 [8, 1024, 2048], P(None, 'seq'), may hold values from -6 to 6
Outputs:
- block_out: bfloat16 [8, 1024, 2048], P(None, 'seq')
- input_grad: bfloat16 [8, 1024, 2048], P(None, 'seq')
- first_gain_grad: float32 [2048], P('seq')
- first_bias_grad: float32 [2048], P('seq')
- w_query_grad: float32 [2048, 2048], P('seq', 'tp')
- w_key_grad: float32 [2048, 2048], P('seq', 'tp')
- w_value_grad: float32 [2048, 2048], P('seq', 'tp')
- head_gain_grad: float32 [2048], P('tp')
- head_bias_grad: float32 [2048], P('tp')
- w_out_grad: float32 [2048, 2048], P('seq', 'tp')
- second_gain_grad: float32 [2048], P('seq')
- second_bias_grad: float32 [2048], P('seq')
- w_up_grad: float32 [2048, 8192], P('seq', 'tp')
- hidden_gain_grad: float32 [8192], P('tp')
- hidden_bias_grad: float32 [8192], P('tp')
- w_down_grad: float32 [2048, 8192], P('seq', 'tp')
Inputs may be any that keep to these rules, and one draw needn't show every extreme that they name: `segment_ids`: in each row the ids start at 0, never fall and rise by at most one from one place to the next; a row holds 1 to 8 documents; in every draw one row, drawn from the seed, is a single document and another holds exactly 8.
All inputs are finite; a program needn't handle non-finite values.
Results may differ from a plain program's by a relative error of at most 0.02.
Values may be sent and summed in bfloat16 or wider, within the bound.
A program may use at most 320 MiB of HBM per device.

v0:
```python
import jax
import jax.numpy as jnp
from jax import lax
from jax.sharding import PartitionSpec as P

HEAD = 64
FF = 8192


EPSILON = 1e-05
MASKED = -1e30


def norm_parts(values):
    center = jnp.mean(values, axis=-1, keepdims=True)
    spread = jnp.mean(jnp.square(values - center), axis=-1, keepdims=True)
    inverse = lax.rsqrt(spread + EPSILON)
    return ((values - center) * inverse, inverse)


def norm_back(grad_normed, gain_vec, normed, inverse):
    scaled = grad_normed * gain_vec
    return inverse * (
        scaled
        - jnp.mean(scaled, axis=-1, keepdims=True)
        - normed * jnp.mean(scaled * normed, axis=-1, keepdims=True)
    )


def split_normed(values, stat_sums, feature_count):
    center = stat_sums[0][..., None] / feature_count
    inverse = lax.rsqrt(stat_sums[1][..., None] / feature_count - center * center + EPSILON)
    return ((values - center) * inverse, inverse)


def split_back(scaled, normed, inverse, stat_sums, feature_count):
    return inverse * (
        scaled
        - stat_sums[0][..., None] / feature_count
        - normed * stat_sums[1][..., None] / feature_count
    )


def rotation_tables(positions, head_size):
    half_size = head_size // 2
    index_pairs = jnp.arange(half_size, dtype=jnp.float32)
    theta_rate = jnp.exp(-2.0 * index_pairs / head_size * jnp.log(10000.0))
    zeta_base = (2.0 * index_pairs + 0.4 * head_size) / (1.4 * head_size)
    place_float = positions.astype(jnp.float32)[..., None]
    angles = place_float * theta_rate
    growth = jnp.exp(jnp.log(zeta_base) * place_float / 512.0)
    return (jnp.cos(angles), jnp.sin(angles), growth)


def rotate(values, cos_table, sin_table, factor):
    half_size = values.shape[-1] // 2
    first_half = values[..., :half_size]
    second_half = values[..., half_size:]
    cos_heads = cos_table[..., None, :]
    sin_heads = sin_table[..., None, :]
    factor_heads = factor[..., None, :]
    return jnp.concatenate(
        [
            (first_half * cos_heads - second_half * sin_heads) * factor_heads,
            (second_half * cos_heads + first_half * sin_heads) * factor_heads,
        ],
        axis=-1,
    )


def rotate_back(grad_rot, cos_table, sin_table, factor):
    half_size = grad_rot.shape[-1] // 2
    first_half = grad_rot[..., :half_size]
    second_half = grad_rot[..., half_size:]
    cos_heads = cos_table[..., None, :]
    sin_heads = sin_table[..., None, :]
    factor_heads = factor[..., None, :]
    return jnp.concatenate(
        [
            factor_heads * (first_half * cos_heads + second_half * sin_heads),
            factor_heads * (second_half * cos_heads - first_half * sin_heads),
        ],
        axis=-1,
    )


def row_scores(query_row, key_row, mask_row):
    scores = jnp.einsum(
        "qhd,khd->hqk", query_row, key_row, preferred_element_type=jnp.float32
    ) * HEAD ** (-0.5)
    return jnp.where(mask_row[None], scores, MASKED)


def attend_row(operands):
    query_row, key_row, value_row, mask_row = operands
    scores = row_scores(query_row, key_row, mask_row)
    top_score = jnp.max(scores, axis=-1, keepdims=True)
    expo = jnp.exp(scores - top_score)
    row_total = jnp.sum(expo, axis=-1, keepdims=True)
    prob_low = (expo / row_total).astype(jnp.bfloat16)
    mixed_out = jnp.einsum("hqk,khd->qhd", prob_low, value_row, preferred_element_type=jnp.float32)
    return (mixed_out, (top_score + jnp.log(row_total))[..., 0])


def score_grads(query_row, key_row, value_row, grad_row, lse_row, mask_row):
    prob_rows = jnp.exp(row_scores(query_row, key_row, mask_row) - lse_row[..., None])
    grad_probs = jnp.einsum("qhd,khd->hqk", grad_row, value_row, preferred_element_type=jnp.float32)
    delta_row = jnp.sum(prob_rows * grad_probs, axis=-1)
    grad_scores = (prob_rows * (grad_probs - delta_row[..., None])).astype(jnp.bfloat16)
    grad_query = jnp.einsum(
        "hqk,khd->qhd", grad_scores, key_row, preferred_element_type=jnp.float32
    ) * HEAD ** (-0.5)
    return (prob_rows, grad_scores, delta_row, grad_query)


def full_row(operands):
    query_row, key_row, value_row, grad_row, lse_row, mask_row = operands
    prob_rows, grad_scores, delta_row, grad_query = score_grads(
        query_row, key_row, value_row, grad_row, lse_row, mask_row
    )
    grad_key = jnp.einsum(
        "hqk,qhd->khd", grad_scores, query_row, preferred_element_type=jnp.float32
    ) * HEAD ** (-0.5)
    grad_value = jnp.einsum(
        "hqk,qhd->khd", prob_rows.astype(jnp.bfloat16), grad_row, preferred_element_type=jnp.float32
    )
    return (grad_query, jnp.stack([grad_key, grad_value], axis=1))


def exact_gelu(values):
    return jax.nn.gelu(values, approximate=False)


def body(
    block_in,
    segment_ids,
    first_gain,
    first_bias,
    w_query,
    w_key,
    w_value,
    head_gain,
    head_bias,
    w_out,
    second_gain,
    second_bias,
    w_up,
    hidden_gain,
    hidden_bias,
    w_down,
    out_cotangent,
):
    seq_index = lax.axis_index("seq")
    seq_count = lax.axis_size("seq")
    row_count, span_len, model_width = block_in.shape
    row_len = span_len * seq_count
    head_width = w_query.shape[1]
    local_heads = head_width // HEAD
    first_token = seq_index * span_len
    local_index = first_token + jnp.arange(span_len, dtype=jnp.int32)
    key_index = jnp.arange(row_len, dtype=jnp.int32)
    local_segments = lax.dynamic_slice_in_dim(segment_ids, first_token, span_len, 1)
    earlier = jnp.sum(
        (segment_ids[:, None, :] < local_segments[:, :, None]).astype(jnp.int32), axis=-1
    )
    positions = local_index[None, :] - earlier
    visible = (key_index[None, None, :] <= local_index[None, :, None]) & (
        segment_ids[:, None, :] == local_segments[:, :, None]
    )
    cos_table, sin_table, growth = rotation_tables(positions, HEAD)
    first_gain_f = first_gain.astype(jnp.float32)
    second_gain_f = second_gain.astype(jnp.float32)
    head_gain_f = head_gain.astype(jnp.float32)
    hidden_gain_f = hidden_gain.astype(jnp.float32)
    block_float = block_in.astype(jnp.float32)
    normed_one, inverse_one = norm_parts(block_float)
    first_act = (normed_one * first_gain_f + first_bias.astype(jnp.float32)).astype(jnp.bfloat16)
    head_shape = (row_count, span_len, local_heads, HEAD)
    query_pre = jnp.dot(first_act, w_query, preferred_element_type=jnp.float32).reshape(head_shape)
    key_pre = jnp.dot(first_act, w_key, preferred_element_type=jnp.float32).reshape(head_shape)
    value_pre = jnp.dot(first_act, w_value, preferred_element_type=jnp.float32).reshape(head_shape)
    query_rot = rotate(query_pre, cos_table, sin_table, growth).astype(jnp.bfloat16)
    key_rot = rotate(key_pre, cos_table, sin_table, 1.0 / growth).astype(jnp.bfloat16)
    value_low = value_pre.astype(jnp.bfloat16)
    key_all, value_all = (
        lax.all_gather(key_rot, "seq", axis=1, tiled=True),
        lax.all_gather(value_low, "seq", axis=1, tiled=True),
    )
    mixed_out, lse_rows = lax.map(attend_row, (query_rot, key_all, value_all, visible))
    mixed_flat = mixed_out.reshape(row_count, span_len, head_width)
    head_sums = lax.psum(
        (jnp.sum(mixed_flat, axis=-1), jnp.sum(mixed_flat * mixed_flat, axis=-1)), "tp"
    )
    head_normed, head_inverse = split_normed(mixed_flat, head_sums, model_width)
    head_act = (head_normed * head_gain_f + head_bias.astype(jnp.float32)).astype(jnp.bfloat16)
    out_part = jnp.einsum("rci,oi->rco", head_act, w_out, preferred_element_type=jnp.float32)
    middle = block_float + lax.psum(out_part, "tp")
    normed_two, inverse_two = norm_parts(middle)
    second_act = (normed_two * second_gain_f + second_bias.astype(jnp.float32)).astype(jnp.bfloat16)
    up_pre = jnp.dot(second_act, w_up, preferred_element_type=jnp.float32)
    gelu_out, gelu_pullback = jax.vjp(exact_gelu, up_pre)
    hidden_sums = lax.psum(
        (jnp.sum(gelu_out, axis=-1), jnp.sum(gelu_out * gelu_out, axis=-1)), "tp"
    )
    hidden_normed, hidden_inverse = split_normed(gelu_out, hidden_sums, FF)
    hidden_act = (hidden_normed * hidden_gain_f + hidden_bias.astype(jnp.float32)).astype(
        jnp.bfloat16
    )
    down_part = jnp.einsum("rci,oi->rco", hidden_act, w_down, preferred_element_type=jnp.float32)
    block_out = (
        middle + lax.psum(down_part.astype(jnp.bfloat16), "tp").astype(jnp.float32)
    ).astype(jnp.bfloat16)
    grad_top = out_cotangent.astype(jnp.float32)
    grad_hidden_act = jnp.einsum(
        "rco,oi->rci", out_cotangent, w_down, preferred_element_type=jnp.float32
    )
    w_down_grad = jnp.einsum(
        "rco,rci->oi", out_cotangent, hidden_act, preferred_element_type=jnp.float32
    )
    hidden_gain_grad = jnp.sum(grad_hidden_act * hidden_normed, axis=(0, 1))
    hidden_bias_grad = jnp.sum(grad_hidden_act, axis=(0, 1))
    hidden_scaled = grad_hidden_act * hidden_gain_f
    hidden_back = lax.psum(
        (jnp.sum(hidden_scaled, axis=-1), jnp.sum(hidden_scaled * hidden_normed, axis=-1)), "tp"
    )
    grad_gelu = split_back(hidden_scaled, hidden_normed, hidden_inverse, hidden_back, FF)
    grad_up = gelu_pullback(grad_gelu)[0].astype(jnp.bfloat16)
    w_up_grad = jnp.einsum("rci,rcj->ij", second_act, grad_up, preferred_element_type=jnp.float32)
    grad_second = lax.psum(
        jnp.einsum("rcj,ij->rci", grad_up, w_up, preferred_element_type=jnp.float32), "tp"
    )
    second_gain_grad = jnp.sum(grad_second * normed_two, axis=(0, 1))
    second_bias_grad = jnp.sum(grad_second, axis=(0, 1))
    grad_middle = grad_top + norm_back(grad_second, second_gain_f, normed_two, inverse_two)
    grad_middle_low = grad_middle.astype(jnp.bfloat16)
    w_out_grad = jnp.einsum(
        "rco,rci->oi", grad_middle_low, head_act, preferred_element_type=jnp.float32
    )
    grad_head_act = jnp.einsum(
        "rco,oi->rci", grad_middle_low, w_out, preferred_element_type=jnp.float32
    )
    head_gain_grad = jnp.sum(grad_head_act * head_normed, axis=(0, 1))
    head_bias_grad = jnp.sum(grad_head_act, axis=(0, 1))
    head_scaled = grad_head_act * head_gain_f
    head_back = lax.psum(
        (jnp.sum(head_scaled, axis=-1), jnp.sum(head_scaled * head_normed, axis=-1)), "tp"
    )
    grad_mixed = (
        split_back(head_scaled, head_normed, head_inverse, head_back, model_width)
        .astype(jnp.bfloat16)
        .reshape(head_shape)
    )
    grad_query_rot, key_terms = lax.map(
        full_row, (query_rot, key_all, value_all, grad_mixed, lse_rows, visible)
    )
    own_terms = lax.psum_scatter(
        jnp.transpose(key_terms, (1, 0, 2, 3, 4)).reshape(
            span_len * lax.axis_size("seq"), row_count, 2 * head_width
        ),
        "seq",
        scatter_dimension=0,
        tiled=True,
    )
    own_terms = jnp.transpose(
        own_terms.reshape(span_len, row_count, 2, local_heads, HEAD), (1, 0, 2, 3, 4)
    )
    grad_key_rot = own_terms[:, :, 0]
    grad_value = own_terms[:, :, 1]
    flat_shape = (row_count, span_len, head_width)
    grad_query = (
        rotate_back(grad_query_rot, cos_table, sin_table, growth)
        .astype(jnp.bfloat16)
        .reshape(flat_shape)
    )
    grad_key = (
        rotate_back(grad_key_rot, cos_table, sin_table, 1.0 / growth)
        .astype(jnp.bfloat16)
        .reshape(flat_shape)
    )
    grad_value_low = grad_value.astype(jnp.bfloat16).reshape(flat_shape)
    w_query_grad = jnp.einsum(
        "rci,rcj->ij", first_act, grad_query, preferred_element_type=jnp.float32
    )
    w_key_grad = jnp.einsum("rci,rcj->ij", first_act, grad_key, preferred_element_type=jnp.float32)
    w_value_grad = jnp.einsum(
        "rci,rcj->ij", first_act, grad_value_low, preferred_element_type=jnp.float32
    )
    first_terms = jnp.einsum("rcj,ij->rci", grad_query, w_query, preferred_element_type=jnp.float32)
    first_terms = first_terms + jnp.einsum(
        "rcj,ij->rci", grad_key, w_key, preferred_element_type=jnp.float32
    )
    first_terms = first_terms + jnp.einsum(
        "rcj,ij->rci", grad_value_low, w_value, preferred_element_type=jnp.float32
    )
    grad_first = lax.psum(first_terms.astype(jnp.bfloat16), "tp").astype(jnp.float32)
    first_gain_grad = jnp.sum(grad_first * normed_one, axis=(0, 1))
    first_bias_grad = jnp.sum(grad_first, axis=(0, 1))
    input_grad = (
        grad_middle + norm_back(grad_first, first_gain_f, normed_one, inverse_one)
    ).astype(jnp.bfloat16)
    summed = (
        lax.psum_scatter(
            w_query_grad.astype(jnp.bfloat16), "seq", scatter_dimension=0, tiled=True
        ).astype(jnp.float32),
        lax.psum_scatter(
            w_key_grad.astype(jnp.bfloat16), "seq", scatter_dimension=0, tiled=True
        ).astype(jnp.float32),
        lax.psum_scatter(
            w_value_grad.astype(jnp.bfloat16), "seq", scatter_dimension=0, tiled=True
        ).astype(jnp.float32),
        lax.psum_scatter(
            w_out_grad.astype(jnp.bfloat16), "seq", scatter_dimension=0, tiled=True
        ).astype(jnp.float32),
        lax.psum_scatter(
            w_up_grad.astype(jnp.bfloat16), "seq", scatter_dimension=0, tiled=True
        ).astype(jnp.float32),
        lax.psum_scatter(
            w_down_grad.astype(jnp.bfloat16), "seq", scatter_dimension=0, tiled=True
        ).astype(jnp.float32),
        lax.psum_scatter(
            first_gain_grad.astype(jnp.bfloat16), "seq", scatter_dimension=0, tiled=True
        ).astype(jnp.float32),
        lax.psum_scatter(
            first_bias_grad.astype(jnp.bfloat16), "seq", scatter_dimension=0, tiled=True
        ).astype(jnp.float32),
        lax.psum_scatter(
            second_gain_grad.astype(jnp.bfloat16), "seq", scatter_dimension=0, tiled=True
        ).astype(jnp.float32),
        lax.psum_scatter(
            second_bias_grad.astype(jnp.bfloat16), "seq", scatter_dimension=0, tiled=True
        ).astype(jnp.float32),
    )
    norm_summed = lax.psum(
        (head_gain_grad, head_bias_grad, hidden_gain_grad, hidden_bias_grad), "seq"
    )
    return (
        block_out,
        input_grad,
        summed[6],
        summed[7],
        summed[0],
        summed[1],
        summed[2],
        norm_summed[0],
        norm_summed[1],
        summed[3],
        summed[8],
        summed[9],
        summed[4],
        norm_summed[2],
        norm_summed[3],
        summed[5],
    )


def solution(mesh):
    return jax.shard_map(
        body,
        mesh=mesh,
        in_specs=(
            P(None, "seq", None),
            P(),
            P(),
            P(),
            P(None, "tp"),
            P(None, "tp"),
            P(None, "tp"),
            P("tp"),
            P("tp"),
            P(None, "tp"),
            P(),
            P(),
            P(None, "tp"),
            P("tp"),
            P("tp"),
            P(None, "tp"),
            P(None, "seq", None),
        ),
        out_specs=(
            P(None, "seq", None),
            P(None, "seq", None),
            P("seq"),
            P("seq"),
            P("seq", "tp"),
            P("seq", "tp"),
            P("seq", "tp"),
            P("tp"),
            P("tp"),
            P("seq", "tp"),
            P("seq"),
            P("seq"),
            P("seq", "tp"),
            P("tp"),
            P("tp"),
            P("seq", "tp"),
        ),
        check_vma=False,
    )
```

profile of v0, /device:TPU:0, one launch (start us, length us, event | category | flops | bytes accessed | tf_op | source)
XLA Modules:
  0.0 1956.2 jit_solution(18332769329700954295)
XLA Ops:
  34.1 42.5 %all-gather.3.cloned.1.call-done = bf16[8,1024,8,64]{1,3,2,0:T(8,128)(2,1)} async-done(((bf16[8,128,8,64]{1,3,2,0:T(8,128)(2,1)}), bf16[8,1024,8,64]{1,3,2,0:T(8,128)(2,1)}) %all-gather.3.cloned.1.call-update) | async-done | bytes 8388624 | tf_op jit(solution)/shard_map/all_gather | solution.py:187
  76.6 58.4 %all-gather.5.cloned.1.call-done = bf16[8,1024,8,64]{1,3,2,0:T(8,128)(2,1)} async-done(((bf16[8,128,8,64]{1,3,2,0:T(8,128)(2,1)}), bf16[8,1024,8,64]{1,3,2,0:T(8,128)(2,1)}) %all-gather.5.cloned.1.call-update) | async-done | bytes 8388624 | tf_op jit(solution)/shard_map/all_gather | solution.py:186
  136.6 60.1 %while.24 = (s32[]{:T(128)}, f32[8,128,8,64]{1,3,2,0:T(8,128)}, f32[8,8,128]{2,1,0:T(8,128)S(1)}, bf16[8,1024,8,64]{1,3,2,0:T(8,128)(2,1)}, pred[8,128,1024]{2,1...) while((s32[]{:T(128)}, f32[8,128,8,64]{1,3,2,0:T(8,128)}, ...), condition=%wide.region_6.7_spmd, body=%wide.region_3.6_spmd.sunk | while | flops 281017344 | bytes 15763557 | solution.py:189
  201.4 11.8 all-reduce.8
  221.1 287.7 %all-reduce.15.cloned.1.call-done = f32[8,128,2048]{2,1,0:T(8,128)} async-done(((f32[8,128,2048]{2,1,0:T(8,128)}), f32[8,128,2048]{2,1,0:T(8,128)}) %all-reduce.15.cloned.1.call-update) | async-done | bytes 8388624 | tf_op jit(solution)/shard_map/psum | solution.py:197
  515.2 18.4 fusion.104
  533.7 23.2 %fusion.115 = (f32[8,128]{1,0:T(8,128)S(1)}, f32[8,128]{1,0:T(8,128)S(1)}, f32[8,128,2048]{2,1,0:T(8,128)}, f32[8,128,2048]{2,1,0:T(8,128)}) fusion(f32[8,128,2048]{2,1,0:T(8,128)} %get-tuple-element.265, u8[128,2048]{1,0:T(8,128)(4,1)S(1)} %get-tuple-element.176, u8[128,2048]{1,0:T(8,128)(4,1)S(1)} %get-tuple-element.177, ...), kind=kLoop, calls=%fused_computation.210 | loop fusion | flops 155187200 | bytes 25960448 | tf_op jit(solution)/shard_map/reduce_sum | solution.py:203
  566.7 17.2 multiply_reduce_fusion.1
  593.3 13.7 add_convert_fusion.1
  609.0 13.2 fusion.73
  622.6 289.6 %all-reduce.17.cloned.1.call-done = f32[8,128,2048]{2,1,0:T(8,128)} async-done(((f32[8,128,2048]{2,1,0:T(8,128)}), f32[8,128,2048]{2,1,0:T(8,128)}) %all-reduce.17.cloned.1.call-update) | async-done | bytes 8388624 | tf_op jit(solution)/shard_map/psum | solution.py:229
  949.5 120.6 %while.25 = (s32[]{:T(128)}, f32[8,128,8,64]{1,3,2,0:T(8,128)}, f32[8,1024,2,8,64]{1,4,3,2,0:T(8,128)}, bf16[8,1024,8,64]{1,3,2,0:T(8,128)(2,1)}, pred[8,128,102...) while((s32[]{:T(128)}, f32[8,128,8,64]{1,3,2,0:T(8,128)}, ...), condition=%wide.region_32.33_spmd, body=%wide.region_30.32_spmd.sunk | while | flops 688454656 | bytes 48659584 | solution.py:253
  1079.7 17.1 fusion.82
  1097.5 17.1 bitcast_convert_fusion.1
  1114.8 159.3 %reduce-scatter.8.cloned.1.call-done = f32[128,8,1024]{0,2,1:T(8,128)} async-done(((f32[1024,8,1024]{0,2,1:T(8,128)}), f32[128,8,1024]{0,2,1:T(8,128)}) %reduce-scatter.8.cloned.1.call-update) | async-done | bytes 4194320 | tf_op jit(solution)/shard_map/reduce_scatter | solution.py:256
  1302.6 15.4 fusion.83
  1331.0 24.2 %all-reduce.4 = (f32[512]{0:T(512)}, f32[512]{0:T(512)}, f32[2048]{0:T(1024)}, f32[2048]{0:T(1024)}) all-reduce(f32[512]{0:T(512)S(1)} %copy-done.54, f32[512]{0:T(512)S(1)} %copy-done.55, f32[2048]{0:T(1024)S(1)} %copy-done.46, f32[2048]{0:T(1024)S(1)} %copy-done.47), channel_id=1, replica_groups=mesh['seq'=8,'tp'=4] {'seq'}, use_global_device_ids=true, to_apply=%region_45.46 | all-reduce | flops 5120 | bytes 40960 | tf_op jit(solution)/shard_map/psum | solution.py:333
  1356.9 37.3 %reduce-scatter.20.cloned.1.call-done = bf16[256,2048]{0,1:T(8,128)(2,1)} async-done(((bf16[2048,2048]{0,1:T(8,128)(2,1)}), bf16[256,2048]{0,1:T(8,128)(2,1)}) %reduce-scatter.20.cloned.1.call-update) | async-done | bytes 1048592 | tf_op jit(solution)/shard_map/reduce_scatter | solution.py:317
  1396.8 72.6 %reduce-scatter.18.cloned.1.call-done = bf16[256,2048]{1,0:T(8,128)(2,1)} async-done(((bf16[2048,2048]{1,0:T(8,128)(2,1)}), bf16[256,2048]{1,0:T(8,128)(2,1)}) %reduce-scatter.18.cloned.1.call-update) | async-done | bytes 1048592 | tf_op jit(solution)/shard_map/reduce_scatter | solution.py:314
  1472.2 41.8 %reduce-scatter.10.cloned.1.call-done = bf16[256,512]{1,0:T(8,128)(2,1)} async-done(((bf16[2048,512]{1,0:T(8,128)(2,1)}), bf16[256,512]{1,0:T(8,128)(2,1)}) %reduce-scatter.10.cloned.1.call-update) | async-done | bytes 262160 | tf_op jit(solution)/shard_map/reduce_scatter | solution.py:302
  1515.8 43.0 %reduce-scatter.12.cloned.1.call-done = bf16[256,512]{1,0:T(8,128)(2,1)} async-done(((bf16[2048,512]{1,0:T(8,128)(2,1)}), bf16[256,512]{1,0:T(8,128)(2,1)}) %reduce-scatter.12.cloned.1.call-update) | async-done | bytes 262160 | tf_op jit(solution)/shard_map/reduce_scatter | solution.py:305
  1560.5 42.7 %reduce-scatter.14.cloned.1.call-done = bf16[256,512]{1,0:T(8,128)(2,1)} async-done(((bf16[2048,512]{1,0:T(8,128)(2,1)}), bf16[256,512]{1,0:T(8,128)(2,1)}) %reduce-scatter.14.cloned.1.call-update) | async-done | bytes 262160 | tf_op jit(solution)/shard_map/reduce_scatter | solution.py:308
  1605.0 293.0 %all-reduce.19.cloned.1.call-done = (bf16[8,128,2048]{2,1,0:T(8,128)(2,1)}, bf16[8,128,2048]{2,1,0:T(8,128)(2,1)}) async-done(((bf16[8,128,2048]{2,1,0:T(8,128)(2,1)}, bf16[8,128,2048]{2,1,0:T(8,128)(2,1)}), (bf16[8,128,2048]{2,1,0:T(8,128)(2,1)}, bf16[8,128,2048]{2,1,0:T(8,128)(2,1)})) %all-reduce.19.cloned.1.call-update) | async-done | bytes 8388624 | tf_op jit(solution)/shard_map/psum | solution.py:211
  1913.3 24.0 %all-reduce.9 = (bf16[2048]{0:T(1024)(128)(2,1)S(1)}, bf16[2048]{0:T(1024)(128)(2,1)S(1)}, bf16[2048]{0:T(1024)(128)(2,1)S(1)}, bf16[2048]{0:T(1024)(128)(2,1)S(1)}) all-reduce(bf16[2048]{0:T(1024)(128)(2,1)S(1)} %get-tuple-element.169, bf16[2048]{0:T(1024)(128)(2,1)S(1)} %reduce_sum.264, ...), channel_id=3, replica_groups=mesh['seq'=8,'tp'=4] {'seq'}, use_global_device_ids=true, to_apply=%region_38.39.clone | all-reduce | flops 8192 | bytes 32768
  (347 shorter events, 376.1 us)
Async XLA Ops:
  7.2 206.0 %copy-start = (bf16[2048,512]{1,0:T(8,128)(2,1)S(1)}, bf16[2048,512]{1,0:T(8,128)(2,1)}, u32[]{:S(2)}) copy-start(bf16[2048,512]{1,0:T(8,128)(2,1)} %param.30) | copy-start | bytes 6291460
  7.2 69.4 %all-gather.3.cloned.1.call-start = ((), (), s32[]{:S(2)}) async-start(), calls=%async_computation.7 | async-start | bytes 9437184 | tf_op jit(solution)/shard_map/all_gather | solution.py:187
  17.8 117.2 %all-gather.5.cloned.1.call-start = ((), (), s32[]{:S(2)}) async-start(), calls=%async_computation.8 | async-start | bytes 9437184 | tf_op jit(solution)/shard_map/all_gather | solution.py:186
  30.5 478.2 %all-reduce.15.cloned.1.call-start = ((), (), s32[]{:S(2)}) async-start(), calls=%async_computation.9 | async-start | bytes 16777216 | tf_op jit(solution)/shard_map/psum | solution.py:197
  30.8 182.4 %copy-start.56 = (f32[512]{0:T(512)}, f32[512]{0:T(512)S(1)}, u32[]{:S(2)}) copy-start(f32[512]{0:T(512)S(1)} %convert_element_type.181) | copy-start | bytes 6148
  220.5 691.7 %all-reduce.17.cloned.1.call-start = ((), (), s32[]{:S(2)}) async-start(), calls=%async_computation.10 | async-start | bytes 16777216 | tf_op jit(solution)/shard_map/psum | solution.py:229
  221.0 858.6 %copy-start.31 = (f32[2048]{0:T(1024)}, f32[2048]{0:T(1024)S(1)}, u32[]{:S(2)}) copy-start(f32[2048]{0:T(1024)S(1)} %convert_element_type.186) | copy-start | bytes 24580
  221.0 294.2 %copy-start.42 = (f32[2048]{0:T(1024)}, f32[2048]{0:T(1024)S(1)}, u32[]{:S(2)}) copy-start(f32[2048]{0:T(1024)S(1)} %convert_element_type.184) | copy-start | bytes 24580
  514.2 19.5 copy-start.2
  566.7 513.0 %copy-start.33 = (f32[8,128]{1,0:T(8,128)}, f32[8,128]{1,0:T(8,128)S(1)}, u32[]{:S(2)}) copy-start(f32[8,128]{1,0:T(8,128)S(1)} %get-tuple-element.259) | copy-start | bytes 12292
  566.7 513.0 %copy-start.35 = (f32[8,128]{1,0:T(8,128)}, f32[8,128]{1,0:T(8,128)S(1)}, u32[]{:S(2)}) copy-start(f32[8,128]{1,0:T(8,128)S(1)} %get-tuple-element.260) | copy-start | bytes 12292
  622.3 651.8 %reduce-scatter.8.cloned.1.call-start = ((), (), s32[]{:S(2)}) async-start(), calls=%async_computation.11 | async-start | bytes 37748736 | tf_op jit(solution)/shard_map/reduce_scatter | solution.py:256
  1070.1 285.0 %reduce-scatter.16.cloned.1.call-start = ((), (), s32[]{:S(2)}) async-start(), calls=%async_computation.15 | async-start | bytes 2359296 | tf_op jit(solution)/shard_map/reduce_scatter | solution.py:311
  1079.6 314.6 %reduce-scatter.20.cloned.1.call-start = ((), (), s32[]{:S(2)}) async-start(), calls=%async_computation.17 | async-start | bytes 9437184 | tf_op jit(solution)/shard_map/reduce_scatter | solution.py:317
  1079.7 17.1 copy-start.44
  1096.9 372.5 %reduce-scatter.18.cloned.1.call-start = ((), (), s32[]{:S(2)}) async-start(), calls=%async_computation.16 | async-start | bytes 9437184 | tf_op jit(solution)/shard_map/reduce_scatter | solution.py:314
  1114.7 164.5 %copy-start.16 = (f32[8,128,32]{1,2,0:T(8,128)S(1)}, f32[8,128,32]{1,2,0:T(8,128)}, u32[]{:S(2)}) copy-start(f32[8,128,32]{1,2,0:T(8,128)} %copy-done.15) | copy-start | bytes 393220
  1114.7 164.5 %copy-start.18 = (f32[8,128,32]{1,2,0:T(8,128)S(1)}, f32[8,128,32]{1,2,0:T(8,128)}, u32[]{:S(2)}) copy-start(f32[8,128,32]{1,2,0:T(8,128)} %copy-done.17) | copy-start | bytes 393220
  1114.7 164.5 %copy-start.20 = (f32[8,128,32]{1,2,0:T(8,128)S(1)}, f32[8,128,32]{1,2,0:T(8,128)}, u32[]{:S(2)}) copy-start(f32[8,128,32]{1,2,0:T(8,128)} %copy-done.19) | copy-start | bytes 393220
  1114.7 399.2 %reduce-scatter.10.cloned.1.call-start = ((), (), s32[]{:S(2)}) async-start(), calls=%async_computation.12 | async-start | bytes 2359296 | tf_op jit(solution)/shard_map/reduce_scatter | solution.py:302
  1286.5 272.2 %reduce-scatter.12.cloned.1.call-start = ((), (), s32[]{:S(2)}) async-start(), calls=%async_computation.13 | async-start | bytes 2359296 | tf_op jit(solution)/shard_map/reduce_scatter | solution.py:305
  1293.9 309.3 %reduce-scatter.14.cloned.1.call-start = ((), (), s32[]{:S(2)}) async-start(), calls=%async_computation.14 | async-start | bytes 2359296 | tf_op jit(solution)/shard_map/reduce_scatter | solution.py:308
  1302.3 15.8 copy-start.23
  1302.3 595.8 %all-reduce.19.cloned.1.call-start = ((), (), s32[]{:S(2)}) async-start(), calls=%async_computation.18 | async-start | bytes 16777216 | tf_op jit(solution)/shard_map/psum | solution.py:211
  (52 other events, 322.1 us)
Sparse Core Ops, SparseCore 0:
  17.9 58.6 all-gather.2
  79.0 55.9 all-gather.4
  220.6 288.0 all-reduce.14
  622.4 289.7 all-reduce.16
  1070.2 203.7 reduce-scatter.7
  1278.1 41.2 reduce-scatter.15
  1322.9 71.2 reduce-scatter.19
  1398.1 71.2 reduce-scatter.17
  1472.7 41.2 reduce-scatter.9
  1517.4 41.2 reduce-scatter.11
  1562.0 41.1 reduce-scatter.13
  1606.4 291.5 all-reduce.18
where the time goes:
time: 1970 us; the launch traced here: 1960 us
  waiting for transfers between devices  1370 us (70%)
  matrix products  285 us (14%)
  other arithmetic  154 us (8%)
  blocking collectives  88.8 us (5%)
  local copies, waits for them, and re-layouts  41 us (2%)
    psum x1, waiting for transfers between devices, body(): lax.psum(down_part.astype(jnp.bfloat16), 'tp').astype(jnp.float32)  293 us
    psum x1, waiting for transfers between devices, body(): lax.psum(jnp.einsum('rcj,ij->rci', grad_up, w_up, preferred_element_type=...  290 us
    psum x1, waiting for transfers between devices, body(): middle = block_float + lax.psum(out_part, 'tp')  288 us
    reduce_scatter x1, waiting for transfers between devices, body(): lax.psum_scatter(jnp.transpose(key_terms, (1, 0, 2, 3, 4)).reshape(span_l...  159 us
    reduce_scatter x1, waiting for transfers between devices, body(): lax.psum_scatter(w_up_grad.astype(jnp.bfloat16), 'seq', scatter_dimension...  72.6 us
    all_gather x1, waiting for transfers between devices, body(): lax.all_gather(key_rot, 'seq', axis=1, tiled=True)  58.4 us
    reduce_scatter x1, waiting for transfers between devices, body(): lax.psum_scatter(w_key_grad.astype(jnp.bfloat16), 'seq', scatter_dimensio...  43 us
    reduce_scatter x1, waiting for transfers between devices, body(): lax.psum_scatter(w_value_grad.astype(jnp.bfloat16), 'seq', scatter_dimens...  42.7 us
  transfers between devices with their start and end apart: 12, of which 11 were waited for; matrix products, arithmetic and copies ran while one was open for 6% of the time, Pallas kernels for 0%

commit v1 on v0

v1 whole, which is shorter than its diff:
```python
import functools
import math

import jax
import jax.numpy as jnp
from jax import lax
from jax.experimental import pallas as pl
from jax.experimental.pallas import tpu as pltpu
from jax.sharding import PartitionSpec as P

HEAD = 64
LANES = 128
BLOCK = 256
EPSILON = 1e-05
MASKED = -1e30
MESH = pl.DeviceIdType.MESH
F32 = jnp.float32
BF16 = jnp.bfloat16
VMEM_LIMIT = 58 * 1024 * 1024


def dot(left, right, left_dim, right_dim):
    return lax.dot_general(
        left, right, (((left_dim,), (right_dim,)), ((), ())), preferred_element_type=F32
    )


def seq_barrier(count):
    me = lax.axis_index("seq")
    barrier = pltpu.get_barrier_semaphore()
    for k in range(1, count):
        pl.semaphore_signal(
            barrier, inc=1, device_id={"seq": lax.rem(me + k, count)}, device_id_type=MESH
        )
    pl.semaphore_wait(barrier, count - 1)


def rows_out_kernel(count, groups, num, *refs):
    sources, targets = refs[:num], refs[num : 2 * num]
    send_sem, recv_sem, own_sem = refs[2 * num :]
    me = lax.axis_index("seq")
    span = sources[0].shape[1]
    width = targets[0].shape[1]
    seq_barrier(count)

    def piece(source, device):
        lane = pl.multiple_of(lax.rem(device, groups) * width, LANES)
        return source.at[device // groups, :, pl.ds(lane, width)]

    def place(target):
        return target.at[pl.ds(pl.multiple_of(me * span, LANES), span), :]

    copies = []
    for k in range(1, count):
        device = lax.rem(me + k, count)
        for i in range(num):
            copy = pltpu.make_async_remote_copy(
                src_ref=piece(sources[i], device),
                dst_ref=place(targets[i]),
                send_sem=send_sem.at[i, k],
                recv_sem=recv_sem.at[i, k],
                device_id={"seq": device},
                device_id_type=MESH,
            )
            copy.start()
            copies.append(copy)
    for i in range(num):
        copy = pltpu.make_async_copy(piece(sources[i], me), place(targets[i]), own_sem.at[i])
        copy.start()
        copies.append(copy)
    for copy in copies:
        copy.wait()


def rows_back_kernel(count, groups, num, *refs):
    sources, targets = refs[:num], refs[num : 2 * num]
    send_sem, recv_sem, own_sem = refs[2 * num :]
    me = lax.axis_index("seq")
    span = targets[0].shape[1]
    width = sources[0].shape[1]
    seq_barrier(count)

    def piece(source, device):
        return source.at[pl.ds(pl.multiple_of(device * span, LANES), span), :]

    def place(target):
        lane = pl.multiple_of(lax.rem(me, groups) * width, LANES)
        return target.at[me // groups, :, pl.ds(lane, width)]

    copies = []
    for k in range(1, count):
        device = lax.rem(me + k, count)
        for i in range(num):
            copy = pltpu.make_async_remote_copy(
                src_ref=piece(sources[i], device),
                dst_ref=place(targets[i]),
                send_sem=send_sem.at[i, k],
                recv_sem=recv_sem.at[i, k],
                device_id={"seq": device},
                device_id_type=MESH,
            )
            copy.start()
            copies.append(copy)
    for i in range(num):
        copy = pltpu.make_async_copy(piece(sources[i], me), place(targets[i]), own_sem.at[i])
        copy.start()
        copies.append(copy)
    for copy in copies:
        copy.wait()


def exchange(kernel, count, groups, arrays, shape, collective_id):
    num = len(arrays)
    outs = pl.pallas_call(
        functools.partial(kernel, count, groups, num),
        out_shape=[jax.ShapeDtypeStruct(shape, BF16)] * num,
        in_specs=[pl.BlockSpec(memory_space=pl.ANY)] * num,
        out_specs=[pl.BlockSpec(memory_space=pl.ANY)] * num,
        scratch_shapes=[
            pltpu.SemaphoreType.DMA((num, count)),
            pltpu.SemaphoreType.DMA((num, count)),
            pltpu.SemaphoreType.DMA((num,)),
        ],
        compiler_params=pltpu.CompilerParams(collective_id=collective_id, has_side_effects=True),
    )(*arrays)
    return outs


def swap_halves(values):
    lane = lax.broadcasted_iota(jnp.int32, values.shape, 1)
    return jnp.where(
        lane % HEAD < HEAD // 2,
        pltpu.roll(values, LANES - HEAD // 2, 1),
        pltpu.roll(values, HEAD // 2, 1),
    )


def head_masks(values):
    lane = lax.broadcasted_iota(jnp.int32, values.shape, 1)
    zero = jnp.zeros_like(values)
    return jnp.where(lane < HEAD, values, zero), jnp.where(lane < HEAD, zero, values)


def attend_kernel(length, q_ref, k_ref, v_ref, tab_ref, segc_ref, segr_ref, o_ref, lse_ref, bias, qs, ks):
    blocks = length // BLOCK

    @pl.when(pl.program_id(0) == 0)
    def _():
        for qb in range(blocks):
            rows = slice(qb * BLOCK, (qb + 1) * BLOCK)
            keys = (qb + 1) * BLOCK
            same = segc_ref[rows, :] == segr_ref[:, :keys]
            row = lax.broadcasted_iota(jnp.int32, (BLOCK, keys), 0) + qb * BLOCK
            col = lax.broadcasted_iota(jnp.int32, (BLOCK, keys), 1)
            bias[rows, :keys] = jnp.where(same & (col <= row), 0.0, MASKED)

    for qb in range(blocks):
        rows = slice(qb * BLOCK, (qb + 1) * BLOCK)
        q = q_ref[rows, :].astype(F32)
        q = (q * tab_ref[0, rows, :] + swap_halves(q) * tab_ref[1, rows, :]) * (HEAD**-0.5)
        q0, q1 = head_masks(q)
        qs[0, rows, :] = q0.astype(BF16)
        qs[1, rows, :] = q1.astype(BF16)
        k = k_ref[rows, :].astype(F32)
        k = k * tab_ref[2, rows, :] + swap_halves(k) * tab_ref[3, rows, :]
        ks[rows, :] = k.astype(BF16)
    for qb in range(blocks):
        rows = slice(qb * BLOCK, (qb + 1) * BLOCK)
        keys = (qb + 1) * BLOCK
        outs = []
        logs = []
        for h in range(2):
            scores = dot(qs[h, rows, :], ks[:keys, :], 1, 1) + bias[rows, :keys]
            top = jnp.max(scores, axis=1, keepdims=True)
            expo = jnp.exp(scores - top)
            total = jnp.sum(expo, axis=1, keepdims=True)
            outs.append(dot(expo.astype(BF16), v_ref[:keys, :], 1, 0) / total)
            logs.append(jnp.broadcast_to(top + jnp.log(total), (BLOCK, LANES)))
        lane = lax.broadcasted_iota(jnp.int32, (BLOCK, LANES), 1)
        o_ref[rows, :] = jnp.where(lane < HEAD, outs[0], outs[1]).astype(BF16)
        logs_t = jnp.transpose(jnp.where(lane < HEAD, logs[0], logs[1]))
        lse_ref[0, 0:1, rows] = logs_t[0:1]
        lse_ref[0, 1:2, rows] = logs_t[HEAD : HEAD + 1]


def attend(q, k, v, tables, seg_col, seg_row):
    length, width = q.shape
    pairs = width // LANES
    lane_block = pl.BlockSpec((length, LANES), lambda p: (0, p))
    return pl.pallas_call(
        functools.partial(attend_kernel, length),
        grid=(pairs,),
        out_shape=[
            jax.ShapeDtypeStruct((length, width), BF16),
            jax.ShapeDtypeStruct((pairs, 8, length), F32),
        ],
        in_specs=[
            lane_block,
            lane_block,
            lane_block,
            pl.BlockSpec((4, length, LANES), lambda p: (0, 0, 0)),
            pl.BlockSpec((length, 1), lambda p: (0, 0)),
            pl.BlockSpec((1, length), lambda p: (0, 0)),
        ],
        out_specs=[lane_block, pl.BlockSpec((1, 8, length), lambda p: (p, 0, 0))],
        scratch_shapes=[
            pltpu.VMEM((length, length), F32),
            pltpu.VMEM((2, length, LANES), BF16),
            pltpu.VMEM((length, LANES), BF16),
        ],
        compiler_params=pltpu.CompilerParams(vmem_limit_bytes=VMEM_LIMIT),
    )(q, k, v, tables, seg_col, seg_row)


def attend_back_kernel(
    length, q_ref, k_ref, v_ref, do_ref, o_ref, lse_ref, tab_ref, segc_ref, segr_ref,
    dq_ref, dk_ref, dv_ref, bias, qs, ks, kms, dos, delta, dq, dk, dv,
):
    blocks = length // BLOCK

    @pl.when(pl.program_id(0) == 0)
    def _():
        for kb in range(blocks):
            rows = slice(kb * BLOCK, (kb + 1) * BLOCK)
            first = kb * BLOCK
            shape = (BLOCK, length - first)
            same = segc_ref[rows, :] == segr_ref[:, first:]
            key = lax.broadcasted_iota(jnp.int32, shape, 0)
            query = lax.broadcasted_iota(jnp.int32, shape, 1)
            bias[rows, first:] = jnp.where(same & (key <= query), 0.0, MASKED)

    for qb in range(blocks):
        rows = slice(qb * BLOCK, (qb + 1) * BLOCK)
        q = q_ref[rows, :].astype(F32)
        q = (q * tab_ref[0, rows, :] + swap_halves(q) * tab_ref[1, rows, :]) * (HEAD**-0.5)
        q0, q1 = head_masks(q)
        qs[0, rows, :] = q0.astype(BF16)
        qs[1, rows, :] = q1.astype(BF16)
        k = k_ref[rows, :].astype(F32)
        k = k * tab_ref[2, rows, :] + swap_halves(k) * tab_ref[3, rows, :]
        ks[rows, :] = k.astype(BF16)
        k0, k1 = head_masks(k)
        kms[0, rows, :] = k0.astype(BF16)
        kms[1, rows, :] = k1.astype(BF16)
        grad = do_ref[rows, :].astype(F32)
        d0, d1 = head_masks(grad)
        dos[0, rows, :] = d0.astype(BF16)
        dos[1, rows, :] = d1.astype(BF16)
        prod = jnp.transpose(grad * o_ref[rows, :].astype(F32))
        delta[0:1, rows] = jnp.sum(prod[:HEAD], axis=0, keepdims=True)
        delta[1:2, rows] = jnp.sum(prod[HEAD:], axis=0, keepdims=True)
    dq[...] = jnp.zeros_like(dq)
    dk[...] = jnp.zeros_like(dk)
    dv[...] = jnp.zeros_like(dv)
    for qb in range(blocks):
        cols = slice(qb * BLOCK, (qb + 1) * BLOCK)
        for kb in range(qb + 1):
            rows = slice(kb * BLOCK, (kb + 1) * BLOCK)
            for h in range(2):
                scores = dot(ks[rows, :], qs[h, cols, :], 1, 1) + bias[rows, cols]
                probs = jnp.exp(scores - lse_ref[0, h : h + 1, cols])
                grads = dot(v_ref[rows, :], dos[h, cols, :], 1, 1)
                dscores = (probs * (grads - delta[h : h + 1, cols])).astype(BF16)
                dv[rows, :] += dot(probs.astype(BF16), dos[h, cols, :], 1, 0)
                dk[rows, :] += dot(dscores, qs[h, cols, :], 1, 0)
                dq[cols, :] += dot(dscores, kms[h, rows, :], 0, 0)
    for qb in range(blocks):
        rows = slice(qb * BLOCK, (qb + 1) * BLOCK)
        grad = dq[rows, :] * (HEAD**-0.5)
        dq_ref[rows, :] = (
            grad * tab_ref[0, rows, :] - swap_halves(grad) * tab_ref[1, rows, :]
        ).astype(BF16)
        grad = dk[rows, :]
        dk_ref[rows, :] = (
            grad * tab_ref[2, rows, :] - swap_halves(grad) * tab_ref[3, rows, :]
        ).astype(BF16)
        dv_ref[rows, :] = dv[rows, :].astype(BF16)


def attend_back(q, k, v, do, o, lse, tables, seg_col, seg_row):
    length, width = q.shape
    pairs = width // LANES
    lane_block = pl.BlockSpec((length, LANES), lambda p: (0, p))
    return pl.pallas_call(
        functools.partial(attend_back_kernel, length),
        grid=(pairs,),
        out_shape=[jax.ShapeDtypeStruct((length, width), BF16)] * 3,
        in_specs=[lane_block] * 5
        + [
            pl.BlockSpec((1, 8, length), lambda p: (p, 0, 0)),
            pl.BlockSpec((4, length, LANES), lambda p: (0, 0, 0)),
            pl.BlockSpec((length, 1), lambda p: (0, 0)),
            pl.BlockSpec((1, length), lambda p: (0, 0)),
        ],
        out_specs=[lane_block] * 3,
        scratch_shapes=[
            pltpu.VMEM((length, length), F32),
            pltpu.VMEM((2, length, LANES), BF16),
            pltpu.VMEM((length, LANES), BF16),
            pltpu.VMEM((2, length, LANES), BF16),
            pltpu.VMEM((2, length, LANES), BF16),
            pltpu.VMEM((8, length), F32),
            pltpu.VMEM((length, LANES), F32),
            pltpu.VMEM((length, LANES), F32),
            pltpu.VMEM((length, LANES), F32),
        ],
        compiler_params=pltpu.CompilerParams(vmem_limit_bytes=VMEM_LIMIT),
    )(q, k, v, do, o, lse, tables, seg_col, seg_row)


def norm_parts(values):
    center = jnp.mean(values, axis=-1, keepdims=True)
    shifted = values - center
    inverse = lax.rsqrt(jnp.mean(shifted * shifted, axis=-1, keepdims=True) + EPSILON)
    return shifted * inverse, inverse


def fold(values):
    rows, width = values.shape
    return jnp.sum(values.reshape(rows // 8, 8, width), axis=0)


def finish_middle(total, here, own, ins, outs):
    x_ref, gain_ref, bias_ref = ins
    middle = x_ref[here, :].astype(F32) + total
    outs[0][own, :] = middle
    normed, _ = norm_parts(middle)
    return normed * gain_ref[...] + bias_ref[...]


def finish_out(total, here, own, ins, outs):
    return ins[0][own, :] + total


def finish_back(total, here, own, ins, outs):
    base_ref, values_ref, gain_ref = ins[:3]
    flip = len(outs) == 1
    base = base_ref[own if flip else here, :].astype(F32)
    values = values_ref[here if flip else own, :].astype(F32)
    normed, inverse = norm_parts(values)
    scaled = total * gain_ref[...]
    grad = base + inverse * (
        scaled
        - jnp.mean(scaled, axis=-1, keepdims=True)
        - normed * jnp.mean(scaled * normed, axis=-1, keepdims=True)
    )
    outs[0][0] += fold(total * normed)
    outs[0][1] += fold(total)
    if not flip:
        outs[1][own, :] = grad
    return grad


def line_kernel(finish, count, chunks, num_in, num_out, clear, *refs):
    part_ref, ins = refs[0], refs[1 : 1 + num_in]
    out_ref, outs = refs[1 + num_in], refs[2 + num_in : 2 + num_in + num_out]
    in_a, in_b, send_a, send_b = refs[2 + num_in + num_out : 6 + num_in + num_out]
    (rsa_s, rsa_r, rsb_s, rsb_r, aga_s, aga_r, agb_s, agb_r) = refs[6 + num_in + num_out :]
    z = lax.axis_index("tp")
    half = part_ref.shape[0] // 2
    size = half // chunks
    lag = 2 * (count - 1)
    first, last = z == 0, z == count - 1
    up = jnp.minimum(z + 1, count - 1)
    down = jnp.maximum(z - 1, 0)

    barrier = pltpu.get_barrier_semaphore()

    @pl.when(jnp.logical_not(last))
    def _():
        pl.semaphore_signal(barrier, inc=1, device_id={"tp": up}, device_id_type=MESH)

    @pl.when(jnp.logical_not(first))
    def _():
        pl.semaphore_signal(barrier, inc=1, device_id={"tp": down}, device_id_type=MESH)

    @pl.when(first | last)
    def _():
        pl.semaphore_wait(barrier, 1)

    @pl.when(jnp.logical_not(first | last))
    def _():
        pl.semaphore_wait(barrier, 2)

    if clear:
        outs[0][...] = jnp.zeros_like(outs[0])

    def own_rows(c):
        return pl.ds(pl.multiple_of(c * size, size), size)

    def a_rows(c):
        return own_rows(c)

    def b_rows(c):
        return pl.ds(pl.multiple_of(half + c * size, size), size)

    def hop(source, target, send, recv, c, device):
        return pltpu.make_async_remote_copy(
            src_ref=source,
            dst_ref=target,
            send_sem=send.at[c],
            recv_sem=recv.at[c],
            device_id={"tp": device},
            device_id_type=MESH,
        )

    def gather_a(c):
        rows = out_ref.at[a_rows(c), :]
        return hop(rows, rows, aga_s, aga_r, c, up)

    def gather_b(c):
        rows = out_ref.at[b_rows(c), :]
        return hop(rows, rows, agb_s, agb_r, c, down)

    def reduce_a(c, source):
        return hop(source, in_a.at[own_rows(c), :], rsa_s, rsa_r, c, down)

    def reduce_b(c, source):
        return hop(source, in_b.at[own_rows(c), :], rsb_s, rsb_r, c, up)

    def reduce_step(c, rows, landed, staged, move, gather, starts, ends):
        here = rows(c)
        own = own_rows(c)

        @pl.when(starts)
        def _():
            move(c, part_ref.at[here, :]).start()

        @pl.when(jnp.logical_not(starts))
        def _():
            move(c, part_ref.at[here, :]).wait_recv()

        @pl.when(jnp.logical_not(starts | ends))
        def _():
            staged[own, :] = (
                landed[own, :].astype(F32) + part_ref[here, :].astype(F32)
            ).astype(BF16)
            move(c, staged.at[own, :]).start()

        @pl.when(ends)
        def _():
            total = landed[own, :].astype(F32) + part_ref[here, :].astype(F32)
            out_ref[here, :] = finish(total, here, own, ins, outs).astype(BF16)
            gather(c).start()

    def gather_step(c, gather, starts, ends):
        @pl.when(jnp.logical_not(starts))
        def _():
            gather(c).wait_recv()

        @pl.when(jnp.logical_not(starts | ends))
        def _():
            gather(c).start()

    def step(t, carry):
        @pl.when(t < chunks)
        def _():
            reduce_step(t, a_rows, in_a, send_a, reduce_a, gather_a, last, first)
            reduce_step(t, b_rows, in_b, send_b, reduce_b, gather_b, first, last)

        @pl.when(t >= lag)
        def _():
            gather_step(t - lag, gather_a, first, last)
            gather_step(t - lag, gather_b, last, first)

        return carry

    lax.fori_loop(0, chunks + lag, step, 0)

    def drain(c, carry):
        @pl.when(jnp.logical_not(first))
        def _():
            reduce_a(c, send_a.at[own_rows(c), :]).wait_send()
            gather_b(c).wait_send()

        @pl.when(jnp.logical_not(last))
        def _():
            reduce_b(c, send_b.at[own_rows(c), :]).wait_send()
            gather_a(c).wait_send()

        return carry

    lax.fori_loop(0, chunks, drain, 0)


def line_sum(finish, count, part, ins, out_shapes, clear, collective_id):
    tokens, width = part.shape
    half = tokens // 2
    chunks = 16
    whole = pl.BlockSpec(memory_space=pltpu.VMEM)
    return pl.pallas_call(
        functools.partial(
            line_kernel, finish, count, chunks, len(ins), len(out_shapes), clear
        ),
        out_shape=[jax.ShapeDtypeStruct((tokens, width), BF16)] + out_shapes,
        in_specs=[whole] * (1 + len(ins)),
        out_specs=[whole] * (1 + len(out_shapes)),
        scratch_shapes=[pltpu.VMEM((half, width), BF16)] * 4
        + [pltpu.SemaphoreType.DMA((chunks,))] * 8,
        compiler_params=pltpu.CompilerParams(
            collective_id=collective_id, has_side_effects=True, vmem_limit_bytes=VMEM_LIMIT
        ),
    )(part, *ins)


def matmul(left, right, left_dim, right_dim, kind=F32):
    return dot(left, right, left_dim, right_dim).astype(kind)


def rotation_tables(positions):
    half_size = HEAD // 2
    index_pairs = jnp.arange(half_size, dtype=F32)
    theta_rate = jnp.exp(-2.0 * index_pairs / HEAD * jnp.log(10000.0))
    zeta_base = (2.0 * index_pairs + 0.4 * HEAD) / (1.4 * HEAD)
    place_float = positions.astype(F32)[..., None]
    angles = place_float * theta_rate
    power = jnp.log(zeta_base) * place_float / 512.0
    cos_part, sin_part = jnp.cos(angles), jnp.sin(angles)
    grow, shrink = jnp.exp(power), jnp.exp(-power)
    cos_full = jnp.concatenate([cos_part] * 4, axis=-1)
    sin_full = jnp.concatenate([-sin_part, sin_part] * 2, axis=-1)
    grow = jnp.concatenate([grow] * 4, axis=-1)
    shrink = jnp.concatenate([shrink] * 4, axis=-1)
    return jnp.stack([cos_full * grow, sin_full * grow, cos_full * shrink, sin_full * shrink])


def body(
    seq_count,
    tp_count,
    block_in,
    segment_ids,
    first_gain,
    first_bias,
    w_query,
    w_key,
    w_value,
    head_gain,
    head_bias,
    w_out,
    second_gain,
    second_bias,
    w_up,
    hidden_gain,
    hidden_bias,
    w_down,
    out_cotangent,
):
    seq_index = lax.axis_index("seq")
    row_count, span, model_width = block_in.shape
    length = span * seq_count
    tokens = row_count * span
    head_width = w_query.shape[1]
    hidden_width = w_up.shape[1] * tp_count
    groups = seq_count // row_count
    width = head_width // groups

    first_gain_f = first_gain.astype(F32)[None]
    first_bias_f = first_bias.astype(F32)[None]
    second_gain_f = second_gain.astype(F32)[None]
    second_bias_f = second_bias.astype(F32)[None]
    head_gain_f = head_gain.astype(F32)[None]
    head_bias_f = head_bias.astype(F32)[None]
    hidden_gain_f = hidden_gain.astype(F32)[None]
    hidden_bias_f = hidden_bias.astype(F32)[None]

    seg_row = lax.dynamic_slice_in_dim(segment_ids, seq_index // groups, 1, 0)
    seg_col = seg_row.reshape(length, 1)
    earlier = jnp.sum((seg_row < seg_col).astype(jnp.int32), axis=-1)
    tables = rotation_tables(jnp.arange(length, dtype=jnp.int32) - earlier)

    block = block_in.reshape(tokens, model_width)
    cotangent = out_cotangent.reshape(tokens, model_width)

    normed_one, _ = norm_parts(block.astype(F32))
    first_act = (normed_one * first_gain_f + first_bias_f).astype(BF16)
    shape3 = (row_count, span, head_width)
    query = matmul(first_act, w_query, 1, 0, BF16).reshape(shape3)
    key = matmul(first_act, w_key, 1, 0, BF16).reshape(shape3)
    value = matmul(first_act, w_value, 1, 0, BF16).reshape(shape3)
    q_row, k_row, v_row = exchange(
        rows_out_kernel, seq_count, groups, (query, key, value), (length, width), 1
    )
    o_row, lse = attend(q_row, k_row, v_row, tables, seg_col, seg_row)
    (mixed,) = exchange(rows_back_kernel, seq_count, groups, (o_row,), shape3, 2)
    mixed = mixed.reshape(tokens, head_width).astype(F32)
    head_sums = lax.psum(jnp.stack([jnp.sum(mixed, axis=-1), jnp.sum(mixed * mixed, axis=-1)]), "tp")
    head_center = head_sums[0][:, None] / model_width
    head_inverse = lax.rsqrt(
        head_sums[1][:, None] / model_width - head_center * head_center + EPSILON
    )
    head_normed = (mixed - head_center) * head_inverse
    head_act = (head_normed * head_gain_f + head_bias_f).astype(BF16)
    out_part = matmul(head_act, w_out, 1, 1, BF16)
    own_shape = jax.ShapeDtypeStruct((tokens // 2, model_width), F32)
    sums_shape = jax.ShapeDtypeStruct((2, 8, model_width), F32)
    second_act, middle_own = line_sum(
        finish_middle, tp_count, out_part, (block, second_gain_f, second_bias_f), [own_shape], False, 3
    )

    up_pre = matmul(second_act, w_up, 1, 0)
    grad_hidden_act = matmul(cotangent, w_down, 1, 0)
    cdf = 0.5 * lax.erfc(up_pre * (-(0.5**0.5)))
    gelu_out = up_pre * cdf
    hidden_scaled = grad_hidden_act * hidden_gain_f
    stats = lax.psum(
        jnp.stack(
            [
                jnp.sum(gelu_out, axis=-1),
                jnp.sum(gelu_out * gelu_out, axis=-1),
                jnp.sum(hidden_scaled, axis=-1),
                jnp.sum(hidden_scaled * gelu_out, axis=-1),
            ]
        ),
        "tp",
    )
    stats = stats[:, :, None] / hidden_width
    hidden_center = stats[0]
    hidden_inverse = lax.rsqrt(stats[1] - hidden_center * hidden_center + EPSILON)
    hidden_normed = (gelu_out - hidden_center) * hidden_inverse
    hidden_act = (hidden_normed * hidden_gain_f + hidden_bias_f).astype(BF16)
    hidden_gain_grad = jnp.sum(grad_hidden_act * hidden_normed, axis=0)
    hidden_bias_grad = jnp.sum(grad_hidden_act, axis=0)
    hidden_cross = hidden_inverse * (stats[3] - hidden_center * stats[2])
    grad_gelu = hidden_inverse * (hidden_scaled - stats[2] - hidden_normed * hidden_cross)
    pdf = jnp.exp(-0.5 * up_pre * up_pre) * (1.0 / math.sqrt(2.0 * math.pi))
    grad_up = (grad_gelu * (cdf + up_pre * pdf)).astype(BF16)

    second_part = matmul(grad_up, w_up, 1, 1, BF16)
    grad_middle_low, second_sums, grad_middle_own = line_sum(
        finish_back,
        tp_count,
        second_part,
        (cotangent, middle_own, second_gain_f),
        [sums_shape, own_shape],
        True,
        4,
    )
    down_part = matmul(hidden_act, w_down, 1, 1, BF16)
    (block_out,) = line_sum(finish_out, tp_count, down_part, (middle_own,), [], False, 5)

    def scatter(grad):
        return lax.psum_scatter(grad, "seq", scatter_dimension=0, tiled=True).astype(F32)

    w_down_grad = scatter(matmul(cotangent, hidden_act, 0, 0, BF16))
    w_up_grad = scatter(matmul(second_act, grad_up, 0, 0, BF16))
    w_out_grad = scatter(matmul(grad_middle_low, head_act, 0, 0, BF16))

    grad_head_act = matmul(grad_middle_low, w_out, 1, 0)
    head_gain_grad = jnp.sum(grad_head_act * head_normed, axis=0)
    head_bias_grad = jnp.sum(grad_head_act, axis=0)
    head_scaled = grad_head_act * head_gain_f
    head_back = lax.psum(
        jnp.stack([jnp.sum(head_scaled, axis=-1), jnp.sum(head_scaled * head_normed, axis=-1)]), "tp"
    )
    head_back = head_back[:, :, None] / model_width
    grad_mixed = head_inverse * (head_scaled - head_back[0] - head_normed * head_back[1])
    (do_row,) = exchange(
        rows_out_kernel,
        seq_count,
        groups,
        (grad_mixed.astype(BF16).reshape(shape3),),
        (length, width),
        6,
    )
    grads_row = attend_back(q_row, k_row, v_row, do_row, o_row, lse, tables, seg_col, seg_row)
    grads = exchange(rows_back_kernel, seq_count, groups, grads_row, shape3, 7)
    grad_query, grad_key, grad_value = (g.reshape(tokens, head_width) for g in grads)
    first_part = (
        dot(grad_query, w_query, 1, 1) + dot(grad_key, w_key, 1, 1) + dot(grad_value, w_value, 1, 1)
    ).astype(BF16)
    w_query_grad = scatter(matmul(first_act, grad_query, 0, 0, BF16))
    w_key_grad = scatter(matmul(first_act, grad_key, 0, 0, BF16))
    w_value_grad = scatter(matmul(first_act, grad_value, 0, 0, BF16))
    input_grad, first_sums = line_sum(
        finish_back, tp_count, first_part, (grad_middle_own, block, first_gain_f), [sums_shape], True, 8
    )

    norm_sums = lax.psum(
        jnp.concatenate([jnp.sum(second_sums, axis=1), jnp.sum(first_sums, axis=1)]), ("seq", "tp")
    )
    own_width = model_width // seq_count
    norm_own = lax.dynamic_slice_in_dim(norm_sums, seq_index * own_width, own_width, 1)
    split_sums = lax.psum((head_gain_grad, head_bias_grad, hidden_gain_grad, hidden_bias_grad), "seq")
    return (
        block_out.reshape(block_in.shape),
        input_grad.reshape(block_in.shape),
        norm_own[2],
        norm_own[3],
        w_query_grad,
        w_key_grad,
        w_value_grad,
        split_sums[0],
        split_sums[1],
        w_out_grad,
        norm_own[0],
        norm_own[1],
        w_up_grad,
        split_sums[2],
        split_sums[3],
        w_down_grad,
    )


def solution(mesh):
    return jax.shard_map(
        functools.partial(body, mesh.shape["seq"], mesh.shape["tp"]),
        mesh=mesh,
        in_specs=(
            P(None, "seq", None),
            P(),
            P(),
            P(),
            P(None, "tp"),
            P(None, "tp"),
            P(None, "tp"),
            P("tp"),
            P("tp"),
            P(None, "tp"),
            P(),
            P(),
            P(None, "tp"),
            P("tp"),
            P("tp"),
            P(None, "tp"),
            P(None, "seq", None),
        ),
        out_specs=(
            P(None, "seq", None),
            P(None, "seq", None),
            P("seq"),
            P("seq"),
            P("seq", "tp"),
            P("seq", "tp"),
            P("seq", "tp"),
            P("tp"),
            P("tp"),
            P("seq", "tp"),
            P("seq"),
            P("seq"),
            P("seq", "tp"),
            P("tp"),
            P("tp"),
            P("seq", "tp"),
        ),
        check_vma=False,
    )
```

time: 1970 us -> 2560 us (1.30)
  Pallas kernels: 0 us -> 2210 us
  waiting for transfers between devices: 1370 us -> 0.11 us
  matrix products: 285 us -> 162 us
  other arithmetic: 154 us -> 52.6 us
    pallas_call x0 -> x10, Pallas kernels: none -> 2210 us  [the longest x4 2060 us: line_sum(): pl.pallas_call(functools.partial(line_kernel, finish, count, chunks, len(...]
    psum x3 -> x0, waiting for transfers between devices: 870 us -> none  [the longest x1 293 us: body(): lax.psum(down_part.astype(jnp.bfloat16), 'tp').astype(jnp.float32)]
    reduce_scatter x7 -> x6, waiting for transfers between devices: 397 us -> 0.01 us  [scatter(): lax.psum_scatter(grad, 'seq', scatter_dimension=0, tiled=True).astype(F32)]
    dot_general x74 -> x18, matrix products: 285 us -> 162 us  [dot(): lax.dot_general(left, right, (((left_dim,), (right_dim,)), ((), ())), pre...]
    all_gather x2 -> x0, waiting for transfers between devices: 101 us -> none  [the longest x1 58.4 us: body(): lax.all_gather(key_rot, 'seq', axis=1, tiled=True)]
    convert_element_type x30 -> x15, other arithmetic: 56.2 us -> 20.1 us  [the longest x5 10 us: scatter(): lax.psum_scatter(grad, 'seq', scatter_dimension=0, tiled=True).astype(F32)]
    reduce_sum x16 -> x6, other arithmetic: 54 us -> 19.6 us  [the longest x1 13.1 us: body(): hidden_bias_grad = jnp.sum(grad_hidden_act, axis=0)]
    psum x4, blocking collectives: 40.6 us -> 73.9 us  [the longest x1 37.3 us: body(): lax.psum(jnp.concatenate([jnp.sum(second_sums, axis=1), jnp.sum(first_sum...]
  transfers between devices with their start and end apart: 12 -> 6, of which waited for: 11 -> 0; matrix products, arithmetic and copies ran while one was open for 6% -> 4% of each run, Pallas kernels for 0% -> 43%
where the time goes in v1:
time: 2560 us; the launch traced here: 2550 us
  Pallas kernels  2210 us (86%)
  matrix products  162 us (6%)
  blocking collectives  96.9 us (4%)
  other arithmetic  52.6 us (2%)
    pallas_call x4, Pallas kernels, line_sum(): pl.pallas_call(functools.partial(line_kernel, finish, count, chunks, len(...  2060 us
    dot_general x18, matrix products, dot(): lax.dot_general(left, right, (((left_dim,), (right_dim,)), ((), ())), pre...  162 us
    pallas_call x4, Pallas kernels, exchange(): pl.pallas_call(functools.partial(kernel, count, groups, num), out_shape=[...  109 us
  transfers between devices with their start and end apart: 6, of which 0 were waited for; matrix products, arithmetic and copies ran while one was open for 4% of the time, Pallas kernels for 43%

profile of v1, /device:TPU:0, one launch (start us, length us, event | category | flops | bytes accessed | tf_op | source)
XLA Modules:
  0.0 2554.4 jit_solution(9143213666455469023)
XLA Ops:
  39.3 39.0 %shard_map.288 = (bf16[1024,512]{1,0:T(8,128)(2,1)}, bf16[1024,512]{1,0:T(8,128)(2,1)}, bf16[1024,512]{1,0:T(8,128)(2,1)}) custom-call(bf16[8,128,512]{2,1,0:T(8,128)(2,1)} %bitcast.114, bf16[8,128,512]{2,1,0:T(8,128)(2,1)} %bitcast.113, bf16[8,128,512]{2,1,0:T(8,128)(2,1)} %bitcast.112), custom_call_target="tpu_custom_call" | custom-call | tf_op jit(solution)/shard_map/pallas_call | solution.py:114
  80.9 17.9 shard_map.289
  98.9 15.0 shard_map.290
  115.5 12.2 psum.56
  136.1 514.6 %shard_map.291 = (bf16[1024,2048]{1,0:T(8,128)(2,1)}, f32[512,2048]{1,0:T(8,128)}) custom-call(bf16[1024,2048]{1,0:T(8,128)(2,1)} %convolution_convert_fusion.3.refs_0_, bf16[1024,2048]{1,0:T(8,128)(2,1)} %bitcast.103, f32[1,2048]{1,0:T(1,128)} %bitcast.117, f32[1,2048]{1,0:T(1,128)} %bitcast.129), custom_call_target="tpu_custom_call" | custom-call | tf_op jit(solution)/shard_map/pallas_call | solution.py:491
  650.6 12.6 fusion.39
  663.3 32.7 %multiply_reduce_fusion.3 = (f32[1024]{0:T(1024)S(1)}, f32[1024]{0:T(1024)S(1)}, f32[1024]{0:T(1024)S(1)}, f32[1024]{0:T(1024)S(1)}, f32[1024,2048]{1,0:T(8,128)...) fusion(f32[2048]{0:T(1024)S(1)} %convert_element_type.147, f32[1024,2048]{1,0:T(8,128)S(1)} %fusion.39, ...), kind=kOutput, calls=%fused_computation.40 | convolution fusion | flops 8736731136 | bytes 46161920 | tf_op jit(solution)/shard_map/dot_general | solution.py:23
  696.0 15.8 psum.57
  711.8 13.1 fusion.34
  724.9 14.1 convolution_convert_fusion.1.refs_0_
  739.0 515.4 %shard_map.293 = (bf16[1024,2048]{1,0:T(8,128)(2,1)}, f32[2,8,2048]{2,1,0:T(8,128)}, f32[512,2048]{1,0:T(8,128)}) custom-call(bf16[1024,2048]{1,0:T(8,128)(2,1)} %convolution_convert_fusion.1.refs_0_, bf16[1024,2048]{1,0:T(8,128)(2,1)} %bitcast.108, f32[512,2048]{1,0:T(8,128)} %get-tuple-element.39.refs_1_.refs_2_, f32[1,2048]{1,0:T(1,128)} %bitcast.118), custom_call_target="tpu_custom_call" | custom-call | tf_op jit(solution)/shard_map/pallas_call | solution.py:491
  1266.8 8.5 psum.58
  1278.7 16.6 shard_map.294.do_ref
  1295.3 30.0 %shard_map.295 = (bf16[1024,512]{1,0:T(8,128)(2,1)}, bf16[1024,512]{1,0:T(8,128)(2,1)}, bf16[1024,512]{1,0:T(8,128)(2,1)}) custom-call(bf16[1024,512]{1,0:T(8,128)(2,1)} %get-tuple-element.34.q_ref, bf16[1024,512]{1,0:T(8,128)(2,1)} %get-tuple-element.35.k_ref, bf16[1024,512]{1,0:T(8,128)(2,1)} %get-tuple-element.36.v_ref, ...), custom_call_target="tpu_custom_call" | custom-call | tf_op jit(solution)/shard_map/pallas_call | solution.py:284
  1325.3 38.1 %shard_map.296 = (bf16[8,128,512]{2,1,0:T(8,128)(2,1)}, bf16[8,128,512]{2,1,0:T(8,128)(2,1)}, bf16[8,128,512]{2,1,0:T(8,128)(2,1)}) custom-call(bf16[1024,512]{1,0:T(8,128)(2,1)} %get-tuple-element.42.refs_0_, bf16[1024,512]{1,0:T(8,128)(2,1)} %get-tuple-element.43.refs_1_, bf16[1024,512]{1,0:T(8,128)(2,1)} %get-tuple-element.44.refs_2_), custom_call_target="tpu_custom_call" | custom-call | tf_op jit(solution)/shard_map/pallas_call | solution.py:114
  1363.4 6.7 bitcast_convert_fusion.2
  1370.4 6.8 bitcast_convert_fusion.1
  1383.8 14.1 convolution_convert_fusion
  1398.6 15.4 convert_bitcast_fusion
  1414.1 15.2 convolution_convert_fusion.2.refs_0_
  1429.2 515.0 %shard_map.292 = bf16[1024,2048]{1,0:T(8,128)(2,1)} custom-call(bf16[1024,2048]{1,0:T(8,128)(2,1)} %convolution_convert_fusion.2.refs_0_, f32[512,2048]{1,0:T(8,128)} %get-tuple-element.39.refs_1_.refs_2_), custom_call_target="tpu_custom_call" | custom-call | tf_op jit(solution)/shard_map/pallas_call | solution.py:491
  1955.4 510.4 %shard_map.297 = (bf16[1024,2048]{1,0:T(8,128)(2,1)}, f32[2,8,2048]{2,1,0:T(8,128)}) custom-call(bf16[1024,2048]{1,0:T(8,128)(2,1)} %add_convert_fusion.refs_0_, f32[512,2048]{1,0:T(8,128)} %get-tuple-element.48.refs_1_, bf16[1024,2048]{1,0:T(8,128)(2,1)} %bitcast.104, f32[1,2048]{1,0:T(1,128)} %bitcast.116), custom_call_target="tpu_custom_call" | custom-call | tf_op jit(solution)/shard_map/pallas_call | solution.py:491
  2466.8 22.9 all-reduce
  2489.8 37.3 %psum.59 = f32[4,2048]{1,0:T(4,128)S(1)} all-reduce(f32[4,2048]{1,0:T(4,128)S(1)} %pad_maximum_fusion.5), channel_id=1, replica_groups=mesh['seq'=8,'tp'=4] {'seq','tp'}, use_global_device_ids=true, to_apply=%region_16.17 | all-reduce | flops 8192 | bytes 65536 | tf_op jit(solution)/shard_map/psum | solution.py:678
  (150 shorter events, 100.0 us)
Async XLA Ops:
  7.2 124.4 %copy-start = (bf16[2048,512]{1,0:T(8,128)(2,1)S(1)}, bf16[2048,512]{1,0:T(8,128)(2,1)}, u32[]{:S(2)}) copy-start(bf16[2048,512]{1,0:T(8,128)(2,1)} %param.26) | copy-start | bytes 6291460
  7.2 10.6 copy-start.24
  7.2 10.6 copy-start.26
  7.2 10.6 copy-start.27
  7.2 11.2 copy-start.28
  7.2 2520.5 %reduce-scatter.13.cloned.1.call-start = ((), (), s32[]{:S(2)}) async-start(), calls=%async_computation.9 | async-start | bytes 2359296 | tf_op jit(solution)/shard_map/reduce_scatter | solution.py:642
  8.2 15.6 copy-start.11
  9.7 118.2 %copy-start.20 = (f32[512]{0:T(512)}, f32[512]{0:T(512)S(1)}, u32[]{:S(2)}) copy-start(f32[512]{0:T(512)S(1)} %convert_element_type.143) | copy-start | bytes 6148
  650.6 12.6 copy-start.5
  663.2 32.7 %copy-start.2 = (f32[1024,2048]{1,0:T(8,128)}, f32[1024,2048]{1,0:T(8,128)S(1)}, u32[]{:S(2)}) copy-start(f32[1024,2048]{1,0:T(8,128)S(1)} %fusion.39) | copy-start | bytes 25165828
  724.9 14.1 copy-start.3
  739.0 515.4 %copy-start.9 = (bf16[1024,512]{1,0:T(8,128)(2,1)S(1)}, bf16[1024,512]{1,0:T(8,128)(2,1)}, u32[]{:S(2)}) copy-start(bf16[1024,512]{1,0:T(8,128)(2,1)} %copy-done.8) | copy-start | bytes 3145732
  1260.5 1269.1 %reduce-scatter.7.cloned.1.call-start = ((), (), s32[]{:S(2)}) async-start(), calls=%async_computation.6 | async-start | bytes 2359296 | tf_op jit(solution)/shard_map/reduce_scatter | solution.py:642
  1275.4 88.0 %copy-start.13 = (f32[2048]{0:T(1024)S(1)}, f32[2048]{0:T(1024)}, u32[]{:S(2)}) copy-start(f32[2048]{0:T(1024)} %copy-done.12) | copy-start | bytes 24580
  1275.4 88.0 %copy-start.19 = (f32[2048]{0:T(1024)S(1)}, f32[2048]{0:T(1024)}, u32[]{:S(2)}) copy-start(f32[2048]{0:T(1024)} %copy-done.18) | copy-start | bytes 24580
  1275.4 88.0 %copy-start.23 = (f32[8,128]{1,0:T(8,128)S(1)}, f32[8,128]{1,0:T(8,128)}, u32[]{:S(2)}) copy-start(f32[8,128]{1,0:T(8,128)} %copy-done.22) | copy-start | bytes 12292
  1275.4 88.0 %copy-start.30 = (f32[8,128]{1,0:T(8,128)S(1)}, f32[8,128]{1,0:T(8,128)}, u32[]{:S(2)}) copy-start(f32[8,128]{1,0:T(8,128)} %get-tuple-element.142) | copy-start | bytes 12292
  1370.1 1161.2 %reduce-scatter.9.cloned.1.call-start = ((), (), s32[]{:S(2)}) async-start(), calls=%async_computation.7 | async-start | bytes 2359296 | tf_op jit(solution)/shard_map/reduce_scatter | solution.py:642
  1377.2 1156.0 %reduce-scatter.11.cloned.1.call-start = ((), (), s32[]{:S(2)}) async-start(), calls=%async_computation.8 | async-start | bytes 2359296 | tf_op jit(solution)/shard_map/reduce_scatter | solution.py:642
  1383.8 1151.2 %reduce-scatter.15.cloned.1.call-start = ((), (), s32[]{:S(2)}) async-start(), calls=%async_computation.10 | async-start | bytes 9437184 | tf_op jit(solution)/shard_map/reduce_scatter | solution.py:642
  1397.9 1139.8 %reduce-scatter.17.cloned.1.call-start = ((), (), s32[]{:S(2)}) async-start(), calls=%async_computation.11 | async-start | bytes 9437184 | tf_op jit(solution)/shard_map/reduce_scatter | solution.py:642
  1429.2 515.1 %copy-start.32 = (bf16[2048,512]{1,0:T(8,128)(2,1)S(1)}, bf16[2048,512]{1,0:T(8,128)(2,1)}, u32[]{:S(2)}) copy-start(bf16[2048,512]{1,0:T(8,128)(2,1)} %param.22) | copy-start | bytes 6291460
  1429.2 515.1 %copy-start.36 = (bf16[8,128,512]{2,1,0:T(8,128)(2,1)S(1)}, bf16[8,128,512]{2,1,0:T(8,128)(2,1)}, u32[]{:S(2)}) copy-start(bf16[8,128,512]{2,1,0:T(8,128)(2,1)} %get-tuple-element.46) | copy-start | bytes 3145732
  1955.4 510.4 %copy-start.10 = (f32[2,8,2048]{2,1,0:T(8,128)S(1)}, f32[2,8,2048]{2,1,0:T(8,128)}, u32[]{:S(2)}) copy-start(f32[2,8,2048]{2,1,0:T(8,128)} %get-tuple-element.50) | copy-start | bytes 393220
  (19 other events, 87.7 us)
Sparse Core Ops, SparseCore 0:
  1260.6 47.9 reduce-scatter.12
  1370.3 42.5 reduce-scatter.6
  1416.8 41.1 reduce-scatter.8
  1461.5 41.2 reduce-scatter.10
  1506.0 71.2 reduce-scatter.14
  1581.1 71.2 reduce-scatter.16

commit v2 on v1

--- a/solution.py
+++ b/solution.py
@@ -16,7 +16,13 @@
 MESH = pl.DeviceIdType.MESH
 F32 = jnp.float32
 BF16 = jnp.bfloat16
+CHUNKS = 16
+SLACK = 2
 VMEM_LIMIT = 58 * 1024 * 1024
+
+
+def cost(micros):
+    return pl.CostEstimate(flops=int(micros * 1.1e9), bytes_accessed=0, transcendentals=0)
 
 
 def dot(left, right, left_dim, right_dim):
@@ -122,6 +128,7 @@
             pltpu.SemaphoreType.DMA((num,)),
         ],
         compiler_params=pltpu.CompilerParams(collective_id=collective_id, has_side_effects=True),
+        cost_estimate=cost(4 + 12 * num),
     )(*arrays)
     return outs
 
@@ -209,6 +216,7 @@
             pltpu.VMEM((length, LANES), BF16),
         ],
         compiler_params=pltpu.CompilerParams(vmem_limit_bytes=VMEM_LIMIT),
+        cost_estimate=cost(17),
     )(q, k, v, tables, seg_col, seg_row)
 
 
@@ -305,6 +313,7 @@
             pltpu.VMEM((length, LANES), F32),
         ],
         compiler_params=pltpu.CompilerParams(vmem_limit_bytes=VMEM_LIMIT),
+        cost_estimate=cost(30),
     )(q, k, v, do, o, lse, tables, seg_col, seg_row)
 
 
@@ -326,10 +335,6 @@
     outs[0][own, :] = middle
     normed, _ = norm_parts(middle)
     return normed * gain_ref[...] + bias_ref[...]
-
-
-def finish_out(total, here, own, ins, outs):
-    return ins[0][own, :] + total
 
 
 def finish_back(total, here, own, ins, outs):
@@ -351,15 +356,16 @@
     return grad
 
 
-def line_kernel(finish, count, chunks, num_in, num_out, clear, *refs):
+def line_kernel(finish, count, chunks, slack, num_in, num_out, clear, *refs):
     part_ref, ins = refs[0], refs[1 : 1 + num_in]
     out_ref, outs = refs[1 + num_in], refs[2 + num_in : 2 + num_in + num_out]
-    in_a, in_b, send_a, send_b = refs[2 + num_in + num_out : 6 + num_in + num_out]
-    (rsa_s, rsa_r, rsb_s, rsb_r, aga_s, aga_r, agb_s, agb_r) = refs[6 + num_in + num_out :]
+    in_a, in_b = refs[2 + num_in + num_out : 4 + num_in + num_out]
+    (rsa_s, rsa_r, rsb_s, rsb_r, aga_s, aga_r, agb_s, agb_r) = refs[4 + num_in + num_out :]
     z = lax.axis_index("tp")
     half = part_ref.shape[0] // 2
     size = half // chunks
-    lag = 2 * (count - 1)
+    ahead = slack * (count - 1)
+    from_first, from_last = slack * z, slack * (count - 1 - z)
     first, last = z == 0, z == count - 1
     up = jnp.minimum(z + 1, count - 1)
     down = jnp.maximum(z - 1, 0)
@@ -418,7 +424,7 @@
     def reduce_b(c, source):
         return hop(source, in_b.at[own_rows(c), :], rsb_s, rsb_r, c, up)
 
-    def reduce_step(c, rows, landed, staged, move, gather, starts, ends):
+    def reduce_step(c, rows, landed, move, gather, starts, ends):
         here = rows(c)
         own = own_rows(c)
 
@@ -432,10 +438,10 @@
 
         @pl.when(jnp.logical_not(starts | ends))
         def _():
-            staged[own, :] = (
+            landed[own, :] = (
                 landed[own, :].astype(F32) + part_ref[here, :].astype(F32)
             ).astype(BF16)
-            move(c, staged.at[own, :]).start()
+            move(c, landed.at[own, :]).start()
 
         @pl.when(ends)
         def _():
@@ -452,30 +458,33 @@
         def _():
             gather(c).start()
 
+    def when_chunk(c, work):
+        pl.when((c >= 0) & (c < chunks))(lambda: work(c))
+
     def step(t, carry):
-        @pl.when(t < chunks)
-        def _():
-            reduce_step(t, a_rows, in_a, send_a, reduce_a, gather_a, last, first)
-            reduce_step(t, b_rows, in_b, send_b, reduce_b, gather_b, first, last)
-
-        @pl.when(t >= lag)
-        def _():
-            gather_step(t - lag, gather_a, first, last)
-            gather_step(t - lag, gather_b, last, first)
-
+        when_chunk(
+            t - from_last,
+            lambda c: reduce_step(c, a_rows, in_a, reduce_a, gather_a, last, first),
+        )
+        when_chunk(
+            t - from_first,
+            lambda c: reduce_step(c, b_rows, in_b, reduce_b, gather_b, first, last),
+        )
+        when_chunk(t - ahead - from_first, lambda c: gather_step(c, gather_a, first, last))
+        when_chunk(t - ahead - from_last, lambda c: gather_step(c, gather_b, last, first))
         return carry
 
-    lax.fori_loop(0, chunks + lag, step, 0)
+    lax.fori_loop(0, chunks + 2 * ahead, step, 0)
 
     def drain(c, carry):
         @pl.when(jnp.logical_not(first))
         def _():
-            reduce_a(c, send_a.at[own_rows(c), :]).wait_send()
+            reduce_a(c, in_a.at[own_rows(c), :]).wait_send()
             gather_b(c).wait_send()
 
         @pl.when(jnp.logical_not(last))
         def _():
-            reduce_b(c, send_b.at[own_rows(c), :]).wait_send()
+            reduce_b(c, in_b.at[own_rows(c), :]).wait_send()
             gather_a(c).wait_send()
 
         return carry
@@ -486,21 +495,132 @@
 def line_sum(finish, count, part, ins, out_shapes, clear, collective_id):
     tokens, width = part.shape
     half = tokens // 2
-    chunks = 16
+    chunks = CHUNKS
     whole = pl.BlockSpec(memory_space=pltpu.VMEM)
     return pl.pallas_call(
         functools.partial(
-            line_kernel, finish, count, chunks, len(ins), len(out_shapes), clear
+            line_kernel, finish, count, CHUNKS, SLACK, len(ins), len(out_shapes), clear
         ),
         out_shape=[jax.ShapeDtypeStruct((tokens, width), BF16)] + out_shapes,
         in_specs=[whole] * (1 + len(ins)),
         out_specs=[whole] * (1 + len(out_shapes)),
-        scratch_shapes=[pltpu.VMEM((half, width), BF16)] * 4
+        scratch_shapes=[pltpu.VMEM((half, width), BF16)] * 2
         + [pltpu.SemaphoreType.DMA((chunks,))] * 8,
         compiler_params=pltpu.CompilerParams(
             collective_id=collective_id, has_side_effects=True, vmem_limit_bytes=VMEM_LIMIT
         ),
+        cost_estimate=cost(120),
     )(part, *ins)
+
+
+def axis_barrier(counts):
+    barrier = pltpu.get_barrier_semaphore()
+    for axis, count in counts:
+        me = lax.axis_index(axis)
+        for k in range(1, count):
+            pl.semaphore_signal(
+                barrier, inc=1, device_id={axis: lax.rem(me + k, count)}, device_id_type=MESH
+            )
+    pl.semaphore_wait(barrier, sum(count - 1 for _, count in counts))
+
+
+def share(axis, count, pick, landed, send_sem, recv_sem):
+    me = lax.axis_index(axis)
+    copies = []
+    for k in range(1, count):
+        device = lax.rem(me + k, count)
+        copy = pltpu.make_async_remote_copy(
+            src_ref=pick(device),
+            dst_ref=landed.at[me],
+            send_sem=send_sem.at[k],
+            recv_sem=recv_sem.at[k],
+            device_id={axis: device},
+            device_id_type=MESH,
+        )
+        copy.start()
+        copies.append(copy)
+    return copies
+
+
+def total_of(landed, count):
+    total = landed[0]
+    for k in range(1, count):
+        total = total + landed[k]
+    return total
+
+
+def tp_sum_kernel(count, x_ref, out_ref, landed, send_sem, recv_sem):
+    axis_barrier([("tp", count)])
+    copies = share("tp", count, lambda d: x_ref, landed, send_sem, recv_sem)
+    landed[lax.axis_index("tp")] = x_ref[...]
+    for copy in copies:
+        copy.wait()
+    out_ref[...] = total_of(landed, count)
+
+
+def tp_sum(values, count, collective_id):
+    whole = pl.BlockSpec(memory_space=pltpu.VMEM)
+    return pl.pallas_call(
+        functools.partial(tp_sum_kernel, count),
+        out_shape=jax.ShapeDtypeStruct(values.shape, F32),
+        in_specs=[whole],
+        out_specs=whole,
+        scratch_shapes=[
+            pltpu.VMEM((count,) + values.shape, F32),
+            pltpu.SemaphoreType.DMA((count,)),
+            pltpu.SemaphoreType.DMA((count,)),
+        ],
+        compiler_params=pltpu.CompilerParams(collective_id=collective_id, has_side_effects=True),
+        cost_estimate=cost(5),
+    )(values)
+
+
+def norm_sum_kernel(
+    seq_count, tp_count, full_ref, split_ref, own_ref, sum_ref,
+    tp_landed, summed, own_landed, split_landed, sem_a, sem_b, sem_c, sem_d, sem_e, sem_f,
+):
+    me = lax.axis_index("seq")
+    axis_barrier([("seq", seq_count), ("tp", tp_count)])
+    tp_copies = share("tp", tp_count, lambda d: full_ref, tp_landed, sem_a, sem_b)
+    split_copies = share("seq", seq_count, lambda d: split_ref, split_landed, sem_c, sem_d)
+    tp_landed[lax.axis_index("tp")] = full_ref[...]
+    split_landed[me] = split_ref[...]
+    for copy in tp_copies:
+        copy.wait()
+    summed[...] = total_of(tp_landed, tp_count)
+    own_copies = share("seq", seq_count, lambda d: summed.at[d], own_landed, sem_e, sem_f)
+    own_landed[me] = summed[me]
+    for copy in split_copies:
+        copy.wait()
+    sum_ref[...] = total_of(split_landed, seq_count)
+    for copy in own_copies:
+        copy.wait()
+    own_ref[...] = total_of(own_landed, seq_count)
+
+
+def norm_sum(full, split, seq_count, tp_count, collective_id):
+    whole = pl.BlockSpec(memory_space=pltpu.VMEM)
+    piece = full.shape[1:]
+    return pl.pallas_call(
+        functools.partial(norm_sum_kernel, seq_count, tp_count),
+        out_shape=[
+            jax.ShapeDtypeStruct(piece, F32),
+            jax.ShapeDtypeStruct(split.shape, F32),
+        ],
+        in_specs=[whole] * 2,
+        out_specs=[whole] * 2,
+        scratch_shapes=[
+            pltpu.VMEM((tp_count,) + full.shape, F32),
+            pltpu.VMEM(full.shape, F32),
+            pltpu.VMEM((seq_count,) + piece, F32),
+            pltpu.VMEM((seq_count,) + split.shape, F32),
+            pltpu.SemaphoreType.DMA((tp_count,)),
+            pltpu.SemaphoreType.DMA((tp_count,)),
+        ]
+        + [pltpu.SemaphoreType.DMA((seq_count,))] * 4,
+        compiler_params=pltpu.CompilerParams(collective_id=collective_id, has_side_effects=True),
+        cost_estimate=cost(10),
+    )(full, split)
 
 
 def matmul(left, right, left_dim, right_dim, kind=F32):
@@ -583,7 +703,9 @@
     o_row, lse = attend(q_row, k_row, v_row, tables, seg_col, seg_row)
     (mixed,) = exchange(rows_back_kernel, seq_count, groups, (o_row,), shape3, 2)
     mixed = mixed.reshape(tokens, head_width).astype(F32)
-    head_sums = lax.psum(jnp.stack([jnp.sum(mixed, axis=-1), jnp.sum(mixed * mixed, axis=-1)]), "tp")
+    head_sums = tp_sum(
+        jnp.stack([jnp.sum(mixed, axis=-1), jnp.sum(mixed * mixed, axis=-1)]), tp_count, 9
+    )
     head_center = head_sums[0][:, None] / model_width
     head_inverse = lax.rsqrt(
         head_sums[1][:, None] / model_width - head_center * head_center + EPSILON
@@ -602,7 +724,7 @@
     cdf = 0.5 * lax.erfc(up_pre * (-(0.5**0.5)))
     gelu_out = up_pre * cdf
     hidden_scaled = grad_hidden_act * hidden_gain_f
-    stats = lax.psum(
+    stats = tp_sum(
         jnp.stack(
             [
                 jnp.sum(gelu_out, axis=-1),
@@ -611,7 +733,8 @@
                 jnp.sum(hidden_scaled * gelu_out, axis=-1),
             ]
         ),
-        "tp",
+        tp_count,
+        10,
     )
     stats = stats[:, :, None] / hidden_width
     hidden_center = stats[0]
@@ -625,7 +748,12 @@
     pdf = jnp.exp(-0.5 * up_pre * up_pre) * (1.0 / math.sqrt(2.0 * math.pi))
     grad_up = (grad_gelu * (cdf + up_pre * pdf)).astype(BF16)
 
+    w_down_terms = matmul(cotangent, hidden_act, 0, 0, BF16)
+    w_up_terms = matmul(second_act, grad_up, 0, 0, BF16)
     second_part = matmul(grad_up, w_up, 1, 1, BF16)
+    second_part, w_down_terms, w_up_terms = lax.optimization_barrier(
+        (second_part, w_down_terms, w_up_terms)
+    )
     grad_middle_low, second_sums, grad_middle_own = line_sum(
         finish_back,
         tp_count,
@@ -635,30 +763,40 @@
         True,
         4,
     )
-    down_part = matmul(hidden_act, w_down, 1, 1, BF16)
-    (block_out,) = line_sum(finish_out, tp_count, down_part, (middle_own,), [], False, 5)
+    hidden_late, _ = lax.optimization_barrier((hidden_act, grad_middle_low))
+    down_part = matmul(hidden_late, w_down, 1, 1)
+    tp_index = lax.axis_index("tp")
+    half = tokens // 2
+    owner = jnp.where(tp_index == 0, 0, jnp.where(tp_index == tp_count - 1, 1, 2))
+    mine = (jnp.arange(2, dtype=jnp.int32) == owner)[:, None, None]
+    down_part = down_part.reshape(2, half, model_width) + jnp.where(mine, middle_own[None], 0.0)
+    block_out = lax.psum(down_part.astype(BF16), "tp")
 
     def scatter(grad):
-        return lax.psum_scatter(grad, "seq", scatter_dimension=0, tiled=True).astype(F32)
-
-    w_down_grad = scatter(matmul(cotangent, hidden_act, 0, 0, BF16))
-    w_up_grad = scatter(matmul(second_act, grad_up, 0, 0, BF16))
-    w_out_grad = scatter(matmul(grad_middle_low, head_act, 0, 0, BF16))
+        return lax.psum_scatter(grad, "seq", scatter_dimension=0, tiled=True)
+
+    w_down_grad = scatter(w_down_terms)
+    w_up_grad = scatter(w_up_terms)
 
     grad_head_act = matmul(grad_middle_low, w_out, 1, 0)
     head_gain_grad = jnp.sum(grad_head_act * head_normed, axis=0)
     head_bias_grad = jnp.sum(grad_head_act, axis=0)
     head_scaled = grad_head_act * head_gain_f
-    head_back = lax.psum(
-        jnp.stack([jnp.sum(head_scaled, axis=-1), jnp.sum(head_scaled * head_normed, axis=-1)]), "tp"
+    head_back = tp_sum(
+        jnp.stack([jnp.sum(head_scaled, axis=-1), jnp.sum(head_scaled * head_normed, axis=-1)]),
+        tp_count,
+        11,
     )
     head_back = head_back[:, :, None] / model_width
     grad_mixed = head_inverse * (head_scaled - head_back[0] - head_normed * head_back[1])
+    grad_mixed, w_down_grad, w_up_grad = lax.optimization_barrier(
+        (grad_mixed.astype(BF16), w_down_grad, w_up_grad)
+    )
     (do_row,) = exchange(
         rows_out_kernel,
         seq_count,
         groups,
-        (grad_mixed.astype(BF16).reshape(shape3),),
+        (grad_mixed.reshape(shape3),),
         (length, width),
         6,
     )
@@ -668,19 +806,42 @@
     first_part = (
         dot(grad_query, w_query, 1, 1) + dot(grad_key, w_key, 1, 1) + dot(grad_value, w_value, 1, 1)
     ).astype(BF16)
-    w_query_grad = scatter(matmul(first_act, grad_query, 0, 0, BF16))
-    w_key_grad = scatter(matmul(first_act, grad_key, 0, 0, BF16))
-    w_value_grad = scatter(matmul(first_act, grad_value, 0, 0, BF16))
+    first_part, block_out = lax.optimization_barrier((first_part, block_out))
+    head_grads = scatter(
+        jnp.concatenate(
+            [
+                matmul(first_act, grad_query, 0, 0, BF16),
+                matmul(first_act, grad_key, 0, 0, BF16),
+                matmul(first_act, grad_value, 0, 0, BF16),
+                matmul(grad_middle_low, head_act, 0, 0, BF16),
+            ],
+            axis=1,
+        )
+    )
+    w_query_grad, w_key_grad, w_value_grad, w_out_grad = jnp.split(
+        head_grads.astype(F32), 4, axis=1
+    )
     input_grad, first_sums = line_sum(
         finish_back, tp_count, first_part, (grad_middle_own, block, first_gain_f), [sums_shape], True, 8
     )
 
-    norm_sums = lax.psum(
-        jnp.concatenate([jnp.sum(second_sums, axis=1), jnp.sum(first_sums, axis=1)]), ("seq", "tp")
-    )
     own_width = model_width // seq_count
-    norm_own = lax.dynamic_slice_in_dim(norm_sums, seq_index * own_width, own_width, 1)
-    split_sums = lax.psum((head_gain_grad, head_bias_grad, hidden_gain_grad, hidden_bias_grad), "seq")
+    full = jnp.concatenate([jnp.sum(second_sums, axis=1), jnp.sum(first_sums, axis=1)])
+    full = full.reshape(4, seq_count, own_width).transpose(1, 0, 2)
+    full = full.reshape(seq_count, 4 * own_width // LANES, LANES)
+    split = jnp.concatenate([hidden_gain_grad, hidden_bias_grad, head_gain_grad, head_bias_grad])
+    norm_own, split = norm_sum(
+        full, split.reshape(split.shape[0] // LANES, LANES), seq_count, tp_count, 12
+    )
+    norm_own = norm_own.reshape(4, own_width)
+    split = split.reshape(-1)
+    hidden_size = hidden_gain.shape[0]
+    split_sums = (
+        split[2 * hidden_size : 2 * hidden_size + head_width],
+        split[2 * hidden_size + head_width :],
+        split[:hidden_size],
+        split[hidden_size : 2 * hidden_size],
+    )
     return (
         block_out.reshape(block_in.shape),
         input_grad.reshape(block_in.shape),
@@ -694,10 +855,10 @@
         w_out_grad,
         norm_own[0],
         norm_own[1],
-        w_up_grad,
+        w_up_grad.astype(F32),
         split_sums[2],
         split_sums[3],
-        w_down_grad,
+        w_down_grad.astype(F32),
     )
 
 

time: 2560 us -> 811 us (0.32)
  Pallas kernels: 2210 us -> 536 us
  blocking collectives: 96.9 us -> 0 us
    pallas_call x4 -> x7, Pallas kernels: 2060 us -> 379 us  [the longest x3 345 us: line_sum(): pl.pallas_call(functools.partial(line_kernel, finish, count, CHUNKS, SLAC...]
    psum x5 -> x0, blocking collectives: 96.9 us -> none  [the longest x1 37.3 us: body(): lax.psum(jnp.concatenate([jnp.sum(second_sums, axis=1), jnp.sum(first_sum...]
  transfers between devices with their start and end apart: 6 -> 4, of which waited for: 0 -> 1; matrix products, arithmetic and copies ran while one was open for 4% -> 11% of each run, Pallas kernels for 43% -> 41%
where the time goes in v2:
time: 811 us; the launch traced here: 807 us
  Pallas kernels  536 us (66%)
  matrix products  154 us (19%)
  other arithmetic  64.9 us (8%)
  local copies, waits for them, and re-layouts  29.2 us (4%)
  between operations  16.1 us (2%)
    pallas_call x3, Pallas kernels, line_sum(): pl.pallas_call(functools.partial(line_kernel, finish, count, CHUNKS, SLAC...  345 us
    dot_general x18, matrix products, dot(): lax.dot_general(left, right, (((left_dim,), (right_dim,)), ((), ())), pre...  154 us
    pallas_call x4, Pallas kernels, exchange(): pl.pallas_call(functools.partial(kernel, count, groups, num), out_shape=[...  110 us
    pallas_call x1, Pallas kernels, attend_back(): pl.pallas_call(functools.partial(attend_back_kernel, length), grid=(pairs...  30 us
    pallas_call x3, Pallas kernels, tp_sum(): pl.pallas_call(functools.partial(tp_sum_kernel, count), out_shape=jax.Sha...  22.5 us
    unnamed x107, local copies, waits for them, and re-layouts  19.4 us
    pallas_call x1, Pallas kernels, attend(): pl.pallas_call(functools.partial(attend_kernel, length), grid=(pairs,), o...  17.6 us
    reduce_sum x1, other arithmetic, body(): hidden_gain_grad = jnp.sum(grad_hidden_act * hidden_normed, axis=0)  16.4 us
  transfers between devices with their start and end apart: 4, of which 1 were waited for; matrix products, arithmetic and copies ran while one was open for 11% of the time, Pallas kernels for 41%

profile of v2, /device:TPU:0, one launch (start us, length us, event | category | flops | bytes accessed | tf_op | source)
XLA Modules:
  0.0 807.3 jit_solution(12635853089341774810)
XLA Ops:
  41.2 39.0 %shard_map.288 = (bf16[1024,512]{1,0:T(8,128)(2,1)}, bf16[1024,512]{1,0:T(8,128)(2,1)}, bf16[1024,512]{1,0:T(8,128)(2,1)}) custom-call(bf16[8,128,512]{2,1,0:T(8,128)(2,1)} %bitcast.162, bf16[8,128,512]{2,1,0:T(8,128)(2,1)} %bitcast.161, bf16[8,128,512]{2,1,0:T(8,128)(2,1)} %bitcast.160), custom_call_target="tpu_custom_call" | custom-call | flops 44000002048 | tf_op jit(solution)/shard_map/pallas_call | solution.py:120
  82.8 17.6 %shard_map.289 = (bf16[1024,512]{1,0:T(8,128)(2,1)}, f32[4,8,1024]{2,1,0:T(8,128)}) custom-call(bf16[1024,512]{1,0:T(8,128)(2,1)} %get-tuple-element.45.q_ref, bf16[1024,512]{1,0:T(8,128)(2,1)} %get-tuple-element.46.k_ref, bf16[1024,512]{1,0:T(8,128)(2,1)} %get-tuple-element.47.v_ref, f32[4,1024,128]{2,1,0:T(8,128)} %pad_maximum_fusion.1.tab_ref, ...), custom_call_target="tpu_custom_call" | custom-call | flops 18699999232 | tf_op jit(solution)/shard_map/pallas_call | solution.py:197
  100.5 15.0 %shard_map.290 = bf16[8,128,512]{2,1,0:T(8,128)(2,1)} custom-call(bf16[1024,512]{1,0:T(8,128)(2,1)} %get-tuple-element.48.refs_0_.o_ref), custom_call_target="tpu_custom_call" | custom-call | flops 17600000000 | tf_op jit(solution)/shard_map/pallas_call | solution.py:120
  117.7 7.5 shard_map.291
  133.1 116.1 %shard_map.292 = (bf16[1024,2048]{1,0:T(8,128)(2,1)}, f32[512,2048]{1,0:T(8,128)}) custom-call(bf16[1024,2048]{1,0:T(8,128)(2,1)} %convolution_convert_fusion.2.refs_0_, bf16[1024,2048]{1,0:T(8,128)(2,1)} %bitcast.123, f32[1,2048]{1,0:T(1,128)} %bitcast.148, f32[1,2048]{1,0:T(1,128)} %bitcast.150), custom_call_target="tpu_custom_call" | custom-call | flops 131999997952 | tf_op jit(solution)/shard_map/pallas_call | solution.py:500
  249.2 12.6 %fusion.38 = f32[1024,2048]{1,0:T(8,128)S(1)} fusion(bf16[1024,2048]{1,0:T(8,128)(2,1)} %get-tuple-element.49, bf16[2048,2048]{1,0:T(8,128)(2,1)} %param.29), kind=kOutput, calls=%fused_computation.112 | convolution fusion | flops 8589934592 | bytes 20971520 | tf_op jit(solution)/shard_map/dot_general | solution.py:29
  261.9 30.8 %multiply_reduce_fusion.3 = (f32[1024]{0:T(1024)S(1)}, f32[1024]{0:T(1024)S(1)}, f32[1024]{0:T(1024)S(1)}, f32[1024]{0:T(1024)S(1)}, f32[1024,2048]{1,0:T(8,128)...) fusion(f32[2048]{0:T(1024)S(1)} %copy-done.27, f32[1024,2048]{1,0:T(8,128)S(1)} %fusion.38, ...), kind=kOutput, calls=%fused_computation.42 | convolution fusion | flops 8736731136 | bytes 46161920 | tf_op jit(solution)/shard_map/dot_general | solution.py:29
  293.3 7.0 shard_map.293
  301.1 16.4 %multiply_reduce_fusion = (f32[2048]{0:T(1024)}, f32[2048]{0:T(1024)}, bf16[1024,2048]{1,0:T(8,128)(2,1)S(1)}, bf16[1024,2048]{1,0:T(8,128)(2,1)}) fusion(f32[1024,2048]{1,0:T(8,128)} %get-tuple-element.176, f32[1024,2048]{1,0:T(8,128)} %get-tuple-element.134, f32[1024]{0:T(1024)S(1)} %bitcast.138, f32[1024]{0:T(1024)S(1)} %get-tuple-element.156, ...), kind=kLoop, calls=%fused_computation.19 | loop fusion | flops 41938944 | bytes 41992192 | tf_op jit(solution)/shard_map/reduce_sum | solution.py:744
  319.4 11.8 %convolution_convert_fusion = bf16[2048,2048]{1,0:T(8,128)(2,1)} fusion(bf16[1024,2048]{1,0:T(8,128)(2,1)S(1)} %copy-done.49, bf16[1024,2048]{1,0:T(8,128)(2,1)S(1)} %get-tuple-element.136), kind=kOutput, calls=%fused_computation.41 | convolution fusion | flops 8594128896 | bytes 16777216 | tf_op jit(solution)/shard_map/dot_general | solution.py:29
  331.3 14.0 %convolution_convert_fusion.1.refs_0_ = bf16[1024,2048]{1,0:T(8,128)(2,1)} fusion(bf16[1024,2048]{1,0:T(8,128)(2,1)} %copy-done.8, bf16[2048,2048]{1,0:T(8,128)(2,1)} %param.29), kind=kOutput, calls=%fused_computation.47 | convolution fusion | flops 8592031744 | bytes 16777216 | tf_op jit(solution)/shard_map/dot_general | solution.py:29
  345.3 11.3 %convert_bitcast_fusion = bf16[2048,2048]{0,1:T(8,128)(2,1)} fusion(bf16[1024,2048]{1,0:T(8,128)(2,1)S(1)} %copy-done.7, bf16[1024,2048]{1,0:T(8,128)(2,1)S(1)} %bitcast.159), kind=kOutput, calls=%fused_computation.22 | convolution fusion | flops 8594128896 | bytes 16777216 | tf_op jit(solution)/shard_map/dot_general | solution.py:29
  357.5 113.6 %shard_map.294 = (bf16[1024,2048]{1,0:T(8,128)(2,1)}, f32[2,8,2048]{2,1,0:T(8,128)}, f32[512,2048]{1,0:T(8,128)}) custom-call(bf16[1024,2048]{1,0:T(8,128)(2,1)} %convolution_convert_fusion.1.refs_0_, bf16[1024,2048]{1,0:T(8,128)(2,1)} %bitcast.157, f32[512,2048]{1,0:T(8,128)} %get-tuple-element.51.refs_2_, f32[1,2048]{1,0:T(1,128)} %bitcast.149), custom_call_target="tpu_custom_call" | custom-call | flops 131999997952 | tf_op jit(solution)/shard_map/pallas_call | solution.py:500
  471.1 15.0 %fusion.41 = f32[1024,2048]{1,0:T(8,128)} fusion(bf16[1024,2048]{1,0:T(8,128)(2,1)} %get-tuple-element.63, bf16[2048,2048]{1,0:T(8,128)(2,1)} %param.32), kind=kOutput, calls=%fused_computation.115 | convolution fusion | flops 8589934592 | bytes 20971520 | tf_op jit(solution)/shard_map/dot_general | solution.py:29
  486.1 7.6 add_convert_fusion
  494.0 6.4 convolution_convert_fusion.3
  505.1 8.0 shard_map.295
  518.0 17.8 %shard_map.296.do_ref = bf16[1024,512]{1,0:T(8,128)(2,1)} custom-call(bf16[8,128,512]{2,1,0:T(8,128)(2,1)} %bitcast.129), custom_call_target="tpu_custom_call" | custom-call | flops 17600000000 | tf_op jit(solution)/shard_map/pallas_call | solution.py:120
  535.8 30.0 %shard_map.297 = (bf16[1024,512]{1,0:T(8,128)(2,1)}, bf16[1024,512]{1,0:T(8,128)(2,1)}, bf16[1024,512]{1,0:T(8,128)(2,1)}) custom-call(bf16[1024,512]{1,0:T(8,128)(2,1)} %get-tuple-element.45.q_ref, bf16[1024,512]{1,0:T(8,128)(2,1)} %get-tuple-element.46.k_ref, bf16[1024,512]{1,0:T(8,128)(2,1)} %get-tuple-element.47.v_ref, ...), custom_call_target="tpu_custom_call" | custom-call | flops 32999999488 | tf_op jit(solution)/shard_map/pallas_call | solution.py:292
  565.8 38.2 %shard_map.298 = (bf16[8,128,512]{2,1,0:T(8,128)(2,1)}, bf16[8,128,512]{2,1,0:T(8,128)(2,1)}, bf16[8,128,512]{2,1,0:T(8,128)(2,1)}) custom-call(bf16[1024,512]{1,0:T(8,128)(2,1)} %get-tuple-element.57.refs_0_, bf16[1024,512]{1,0:T(8,128)(2,1)} %get-tuple-element.58.refs_1_, bf16[1024,512]{1,0:T(8,128)(2,1)} %get-tuple-element.59.refs_2_), custom_call_target="tpu_custom_call" | custom-call | flops 44000002048 | tf_op jit(solution)/shard_map/pallas_call | solution.py:120
  609.0 7.7 fusion.40
  635.4 11.4 %add_convert_fusion.1.refs_0_ = bf16[1024,2048]{1,0:T(8,128)(2,1)} fusion(f32[1024,2048]{1,0:T(8,128)} %fusion.39, f32[1024,2048]{1,0:T(8,128)} %fusion.40, bf16[1024,512]{1,0:T(8,128)(2,1)S(1)} %bitcast.128, bf16[2048,512]{1,0:T(8,128)(2,1)} %param.23), kind=kOutput, calls=%fused_computation.21 | convolution fusion | flops 2153775104 | bytes 24117248 | tf_op jit(solution)/shard_map/dot_general | solution.py:29
  652.6 114.7 %shard_map.299 = (bf16[1024,2048]{1,0:T(8,128)(2,1)}, f32[2,8,2048]{2,1,0:T(8,128)}) custom-call(bf16[1024,2048]{1,0:T(8,128)(2,1)} %add_convert_fusion.1.refs_0_, f32[512,2048]{1,0:T(8,128)} %get-tuple-element.66.refs_1_, bf16[1024,2048]{1,0:T(8,128)(2,1)} %bitcast.124, f32[1,2048]{1,0:T(1,128)} %bitcast.140), custom_call_target="tpu_custom_call" | custom-call | flops 131999997952 | tf_op jit(solution)/shard_map/pallas_call | solution.py:500
  769.0 11.6 %shard_map.300 = (f32[8,128]{1,0:T(8,128)}, f32[40,128]{1,0:T(8,128)}) custom-call(f32[8,8,128]{2,1,0:T(8,128)} %reshape.1249.full_ref, f32[40,128]{1,0:T(8,128)} %maximum_bitcast_fusion.split_ref), custom_call_target="tpu_custom_call" | custom-call | flops 11000000512 | tf_op jit(solution)/shard_map/pallas_call | solution.py:604
  (176 shorter events, 109.9 us)
Async XLA Ops:
  8.0 120.6 %copy-start = (bf16[2048,512]{1,0:T(8,128)(2,1)S(1)}, bf16[2048,512]{1,0:T(8,128)(2,1)}, u32[]{:S(2)}) copy-start(bf16[2048,512]{1,0:T(8,128)(2,1)} %param.26) | copy-start | bytes 6291460
  8.1 10.6 %copy-start.35 = (bf16[2048]{0:T(1024)(128)(2,1)S(1)}, bf16[2048]{0:T(1024)(128)(2,1)}, u32[]{:S(2)}) copy-start(bf16[2048]{0:T(1024)(128)(2,1)} %param.30) | copy-start | bytes 12292
  8.1 11.2 %copy-start.36 = (bf16[2048]{0:T(1024)(128)(2,1)S(1)}, bf16[2048]{0:T(1024)(128)(2,1)}, u32[]{:S(2)}) copy-start(bf16[2048]{0:T(1024)(128)(2,1)} %param.27) | copy-start | bytes 12292
  8.1 11.8 %copy-start.37 = (bf16[2048]{0:T(1024)(128)(2,1)S(1)}, bf16[2048]{0:T(1024)(128)(2,1)}, u32[]{:S(2)}) copy-start(bf16[2048]{0:T(1024)(128)(2,1)} %param.28) | copy-start | bytes 12292
  8.1 12.4 %copy-start.38 = (bf16[2048]{0:T(1024)(128)(2,1)S(1)}, bf16[2048]{0:T(1024)(128)(2,1)}, u32[]{:S(2)}) copy-start(bf16[2048]{0:T(1024)(128)(2,1)} %param.31) | copy-start | bytes 12292
  8.1 509.9 %reduce-scatter.4.cloned.1.call-start = ((), (), s32[]{:S(2)}) async-start(), calls=%async_computation.3 | async-start | bytes 9437184 | tf_op jit(solution)/shard_map/reduce_scatter | solution.py:776
  9.1 16.7 %copy-start.18 = (s32[1,1024]{1,0:T(1,128)}, s32[1,1024]{1,0:T(1,128)S(1)}, u32[]{:S(2)}) copy-start(s32[1,1024]{1,0:T(1,128)S(1)} %constant_dynamic-slice_fusion.segr_ref) | copy-start | bytes 12292
  10.5 115.6 %copy-start.29 = (f32[512]{0:T(512)}, f32[512]{0:T(512)S(1)}, u32[]{:S(2)}) copy-start(f32[512]{0:T(512)S(1)} %convert_element_type.134) | copy-start | bytes 6148
  14.6 14.5 %copy-start.31 = (f32[8,128]{1,0:T(8,128)}, f32[8,128]{1,0:T(8,128)S(1)}, u32[]{:S(2)}) copy-start(f32[8,128]{1,0:T(8,128)S(1)} %get-tuple-element.175) | copy-start | bytes 12292
  249.2 12.7 %copy-start.27 = (f32[2048]{0:T(1024)S(1)}, f32[2048]{0:T(1024)}, u32[]{:S(2)}) copy-start(f32[2048]{0:T(1024)} %convert_element_type.138) | copy-start | bytes 24580
  249.2 12.7 %copy-start.40 = (bf16[2048,2048]{1,0:T(8,128)(2,1)S(1)}, bf16[2048,2048]{1,0:T(8,128)(2,1)}, u32[]{:S(2)}) copy-start(bf16[2048,2048]{1,0:T(8,128)(2,1)} %param.32) | copy-start | bytes 25165828
  249.2 12.7 %copy-start.41 = (bf16[8,128,2048]{2,1,0:T(8,128)(2,1)S(1)}, bf16[8,128,2048]{2,1,0:T(8,128)(2,1)}, u32[]{:S(2)}) copy-start(bf16[8,128,2048]{2,1,0:T(8,128)(2,1)} %param.33) | copy-start | bytes 12582916
  261.9 30.8 %copy-start.4 = (f32[1024,2048]{1,0:T(8,128)}, f32[1024,2048]{1,0:T(8,128)S(1)}, u32[]{:S(2)}) copy-start(f32[1024,2048]{1,0:T(8,128)S(1)} %fusion.38) | copy-start | bytes 25165828
  301.1 18.4 %copy-start.49 = (bf16[1024,2048]{1,0:T(8,128)(2,1)S(1)}, bf16[1024,2048]{1,0:T(8,128)(2,1)}, u32[]{:S(2)}) copy-start(bf16[1024,2048]{1,0:T(8,128)(2,1)} %get-tuple-element.49) | copy-start | bytes 12582916
  331.3 14.0 %copy-start.7 = (bf16[1024,2048]{1,0:T(8,128)(2,1)S(1)}, bf16[1024,2048]{1,0:T(8,128)(2,1)}, u32[]{:S(2)}) copy-start(bf16[1024,2048]{1,0:T(8,128)(2,1)} %get-tuple-element.63) | copy-start | bytes 12582916
  331.3 14.0 %copy-start.42 = (bf16[8,128,2048]{2,1,0:T(8,128)(2,1)S(1)}, bf16[8,128,2048]{2,1,0:T(8,128)(2,1)}, u32[]{:S(2)}) copy-start(bf16[8,128,2048]{2,1,0:T(8,128)(2,1)} %param.33) | copy-start | bytes 12582916
  356.6 161.3 %reduce-scatter.6.cloned.1.call-start = ((), (), s32[]{:S(2)}) async-start(), calls=%async_computation.4 | async-start | bytes 9437184 | tf_op jit(solution)/shard_map/reduce_scatter | solution.py:776
  357.4 295.2 %all-reduce.2.cloned.1.call-start = ((), (), s32[]{:S(2)}) async-start(), calls=%async_computation.5 | async-start | bytes 8388608 | tf_op jit(solution)/shard_map/psum | solution.py:773
  471.1 15.0 %copy-start.5 = (f32[512,2048]{1,0:T(8,128)S(1)}, f32[512,2048]{1,0:T(8,128)}, u32[]{:S(2)}) copy-start(f32[512,2048]{1,0:T(8,128)} %get-tuple-element.51.refs_2_) | copy-start | bytes 12582916
  493.8 290.9 %reduce-scatter.8.cloned.1.call-start = ((), (), s32[]{:S(2)}) async-start(), calls=%async_computation.6 | async-start | bytes 9437184 | tf_op jit(solution)/shard_map/reduce_scatter | solution.py:776
  505.1 12.3 %copy-start.25 = (f32[2048]{0:T(1024)S(1)}, f32[2048]{0:T(1024)}, u32[]{:S(2)}) copy-start(f32[2048]{0:T(1024)} %get-tuple-element.126) | copy-start | bytes 24580
  505.1 12.3 %copy-start.26 = (f32[2048]{0:T(1024)S(1)}, f32[2048]{0:T(1024)}, u32[]{:S(2)}) copy-start(f32[2048]{0:T(1024)} %get-tuple-element.127) | copy-start | bytes 24580
  565.8 41.0 %copy-start.11 = (bf16[256,2048]{0,1:T(8,128)(2,1)S(1)}, bf16[256,2048]{0,1:T(8,128)(2,1)}, u32[]{:S(2)}) copy-start(bf16[256,2048]{0,1:T(8,128)(2,1)} %reduce-scatter.4.cloned.1.call-done) | copy-start | bytes 3145732
  652.6 115.7 %copy-start.15 = (f32[2,2048]{1,0:T(2,128)S(1)}, f32[2,2048]{1,0:T(2,128)}, u32[]{:S(2)}) copy-start(f32[2,2048]{1,0:T(2,128)} %reduce_sum.164) | copy-start | bytes 49156
  (30 other events, 174.0 us)
Sparse Core Ops, SparseCore 0:
  356.8 72.2 reduce-scatter.3
  432.5 71.2 reduce-scatter.5
  635.5 71.6 reduce-scatter.7
Sparse Core Ops, SparseCore 1:
  493.9 158.7 all-reduce.1

commit v3 on v2

--- a/solution.py
+++ b/solution.py
@@ -18,7 +18,10 @@
 BF16 = jnp.bfloat16
 CHUNKS = 16
 SLACK = 2
-VMEM_LIMIT = 58 * 1024 * 1024
+GROUP = 4
+ROWS = 256
+TILE = 512
+VMEM_LIMIT = 60 * 1024 * 1024
 
 
 def cost(micros):
@@ -329,46 +332,75 @@
     return jnp.sum(values.reshape(rows // 8, 8, width), axis=0)
 
 
-def finish_middle(total, here, own, ins, outs):
-    x_ref, gain_ref, bias_ref = ins
-    middle = x_ref[here, :].astype(F32) + total
+def finish_middle(total, here, own, held, vecs, outs):
+    middle = held["block"][here, :].astype(F32) + total
     outs[0][own, :] = middle
     normed, _ = norm_parts(middle)
-    return normed * gain_ref[...] + bias_ref[...]
-
-
-def finish_back(total, here, own, ins, outs):
-    base_ref, values_ref, gain_ref = ins[:3]
-    flip = len(outs) == 1
-    base = base_ref[own if flip else here, :].astype(F32)
-    values = values_ref[here if flip else own, :].astype(F32)
+    return normed * vecs[0][...] + vecs[1][...]
+
+
+def norm_back(base, values, total, vecs, sums):
     normed, inverse = norm_parts(values)
-    scaled = total * gain_ref[...]
+    scaled = total * vecs[0][...]
     grad = base + inverse * (
         scaled
         - jnp.mean(scaled, axis=-1, keepdims=True)
         - normed * jnp.mean(scaled * normed, axis=-1, keepdims=True)
     )
-    outs[0][0] += fold(total * normed)
-    outs[0][1] += fold(total)
-    if not flip:
-        outs[1][own, :] = grad
+    sums[0] += fold(total * normed)
+    sums[1] += fold(total)
     return grad
 
 
-def line_kernel(finish, count, chunks, slack, num_in, num_out, clear, *refs):
-    part_ref, ins = refs[0], refs[1 : 1 + num_in]
-    out_ref, outs = refs[1 + num_in], refs[2 + num_in : 2 + num_in + num_out]
-    in_a, in_b = refs[2 + num_in + num_out : 4 + num_in + num_out]
-    (rsa_s, rsa_r, rsb_s, rsb_r, aga_s, aga_r, agb_s, agb_r) = refs[4 + num_in + num_out :]
+def finish_second(total, here, own, held, vecs, outs):
+    base = held["cotangent"][here, :].astype(F32)
+    grad = norm_back(base, held["middle"][own, :], total, vecs, outs[0])
+    outs[1][own, :] = grad
+    return grad
+
+
+def finish_first(total, here, own, held, vecs, outs):
+    values = held["block"][here, :].astype(F32)
+    return norm_back(held["middle_grad"][own, :], values, total, vecs, outs[0])
+
+
+def line_kernel(plan, count, chunks, slack, *refs):
+    finish, clear = plan["finish"], plan["clear"]
+    names, parts, tasks = plan["names"], plan["parts"], plan["tasks"]
+    num_vec, num_own, num_task = plan["vecs"], plan["owns"], len(tasks)
+    refs = list(refs)
+
+    def take(number):
+        taken = refs[:number]
+        del refs[:number]
+        return taken
+
+    sources = take(len(names))
+    vecs = take(num_vec)
+    (out_ref,) = take(1)
+    outs = take(num_own)
+    task_outs = take(num_task)
+    held = dict(zip(names, take(len(names))))
+    in_a, in_b, part, turned, stage = take(5)
+    load_sem, stage_sem = take(2)
+    (rsa_s, rsa_r, rsb_s, rsb_r, aga_s, aga_r, agb_s, agb_r) = refs
     z = lax.axis_index("tp")
-    half = part_ref.shape[0] // 2
+    tokens, width = out_ref.shape
+    half = tokens // 2
     size = half // chunks
     ahead = slack * (count - 1)
+    steps = chunks + 2 * ahead
     from_first, from_last = slack * z, slack * (count - 1 - z)
     first, last = z == 0, z == count - 1
     up = jnp.minimum(z + 1, count - 1)
     down = jnp.maximum(z - 1, 0)
+
+    loads = {
+        name: pltpu.make_async_copy(source, held[name], load_sem.at[i])
+        for i, (name, source) in enumerate(zip(names, sources))
+    }
+    for name in names:
+        loads[name].start()
 
     barrier = pltpu.get_barrier_semaphore()
 
@@ -418,35 +450,41 @@
         rows = out_ref.at[b_rows(c), :]
         return hop(rows, rows, agb_s, agb_r, c, down)
 
-    def reduce_a(c, source):
-        return hop(source, in_a.at[own_rows(c), :], rsa_s, rsa_r, c, down)
-
-    def reduce_b(c, source):
-        return hop(source, in_b.at[own_rows(c), :], rsb_s, rsb_r, c, up)
-
-    def reduce_step(c, rows, landed, move, gather, starts, ends):
+    def reduce_a(c):
+        rows = in_a.at[own_rows(c), :]
+        return hop(rows, rows, rsa_s, rsa_r, c, down)
+
+    def reduce_b(c):
+        rows = in_b.at[own_rows(c), :]
+        return hop(rows, rows, rsb_s, rsb_r, c, up)
+
+    def block_start(t, offset):
+        return jnp.clip((t - lax.rem(t, GROUP) - offset) * size, 0, half - GROUP * size)
+
+    def reduce_step(t, c, offset, place, rows, landed, move, gather, starts, ends):
         here = rows(c)
         own = own_rows(c)
+        row = place * GROUP * size + c * size - block_start(t, offset)
+        term_rows = pl.ds(pl.multiple_of(row, size), size)
 
         @pl.when(starts)
         def _():
-            move(c, part_ref.at[here, :]).start()
+            landed[own, :] = part[term_rows, :].astype(BF16)
+            move(c).start()
 
         @pl.when(jnp.logical_not(starts))
         def _():
-            move(c, part_ref.at[here, :]).wait_recv()
+            move(c).wait_recv()
 
         @pl.when(jnp.logical_not(starts | ends))
         def _():
-            landed[own, :] = (
-                landed[own, :].astype(F32) + part_ref[here, :].astype(F32)
-            ).astype(BF16)
-            move(c, landed.at[own, :]).start()
+            landed[own, :] = (landed[own, :].astype(F32) + part[term_rows, :]).astype(BF16)
+            move(c).start()
 
         @pl.when(ends)
         def _():
-            total = landed[own, :].astype(F32) + part_ref[here, :].astype(F32)
-            out_ref[here, :] = finish(total, here, own, ins, outs).astype(BF16)
+            total = landed[own, :].astype(F32) + part[term_rows, :]
+            out_ref[here, :] = finish(total, here, own, held, vecs, outs).astype(BF16)
             gather(c).start()
 
     def gather_step(c, gather, starts, ends):
@@ -461,30 +499,115 @@
     def when_chunk(c, work):
         pl.when((c >= 0) & (c < chunks))(lambda: work(c))
 
+    def make_parts(t):
+        top = pl.ds(pl.multiple_of(block_start(t, from_last), size), GROUP * size)
+        low = pl.ds(pl.multiple_of(half + block_start(t, from_first), size), GROUP * size)
+
+        def columns(n, carry):
+            cols = pl.ds(pl.multiple_of(n * TILE, TILE), TILE)
+            total = 0.0
+            for left, right in parts:
+                rows = jnp.concatenate([held[left][top, :], held[left][low, :]], axis=0)
+                total = total + dot(rows, held[right][cols, :], 1, 1)
+            part[:, cols] = total
+            return carry
+
+        lax.fori_loop(0, width // TILE, columns, 0)
+
+    def run_task(index, tile, slot):
+        kind, left, right = tasks[index]
+        target = task_outs[index]
+        wide = target.shape[1]
+        rows = pl.ds(pl.multiple_of(tile * ROWS, ROWS), ROWS)
+        if kind == "weight":
+            depth = tokens
+            turned[:, :depth] = jnp.transpose(held[left][:, rows])
+
+        def columns(n, carry):
+            cols = pl.ds(pl.multiple_of(n * TILE, TILE), TILE)
+            if kind == "weight":
+                value = dot(turned[:, :depth], held[right][:, cols], 1, 0)
+            elif kind == "rows":
+                value = dot(held[left][rows, :], held[right][:, cols], 1, 0)
+            else:
+                value = dot(held[left][rows, :], held[right][cols, :], 1, 1)
+                top = tile * ROWS < half
+                mine = (first & top) | (last & jnp.logical_not(top))
+                own = pl.multiple_of(lax.rem(tile * ROWS, half), ROWS)
+                base = held["middle"][pl.ds(own, ROWS), cols]
+                value = value + jnp.where(mine, base, 0.0)
+            stage[slot, :, cols] = value.astype(BF16)
+            return carry
+
+        lax.fori_loop(0, wide // TILE, columns, 0)
+        stage_copy(index, tile, slot).start()
+
+    def stage_copy(index, tile, slot):
+        target = task_outs[index]
+        rows = pl.ds(pl.multiple_of(tile * ROWS, ROWS), ROWS)
+        return pltpu.make_async_copy(
+            stage.at[slot, :, : target.shape[1]], target.at[rows, :], stage_sem.at[slot]
+        )
+
+    starts_at = [0]
+    for index in range(num_task):
+        starts_at.append(starts_at[-1] + task_outs[index].shape[0] // ROWS)
+    task_total = starts_at[-1]
+    per_group = GROUP - 1
+
     def step(t, carry):
+        pl.when(lax.rem(t, GROUP) == 0)(lambda: make_parts(t))
         when_chunk(
             t - from_last,
-            lambda c: reduce_step(c, a_rows, in_a, reduce_a, gather_a, last, first),
+            lambda c: reduce_step(t, c, from_last, 0, a_rows, in_a, reduce_a, gather_a, last, first),
         )
         when_chunk(
             t - from_first,
-            lambda c: reduce_step(c, b_rows, in_b, reduce_b, gather_b, first, last),
+            lambda c: reduce_step(t, c, from_first, 1, b_rows, in_b, reduce_b, gather_b, first, last),
         )
         when_chunk(t - ahead - from_first, lambda c: gather_step(c, gather_a, first, last))
         when_chunk(t - ahead - from_last, lambda c: gather_step(c, gather_b, last, first))
+        if num_task:
+            turn = (t // GROUP) * per_group + lax.rem(t, GROUP) - 1
+            free = lax.rem(t, GROUP) != 0
+            slot = lax.rem(turn + per_group + 1, 2)
+
+            @pl.when(t == 1)
+            def _():
+                for name in plan["late"]:
+                    loads[name].wait()
+
+            for index in range(num_task):
+                low, high = starts_at[index] + 2, min(starts_at[index + 1] + 2, task_total)
+                pl.when(free & (turn >= low) & (turn < high))(
+                    lambda index=index, low=low: stage_copy(index, turn - low, slot).wait()
+                )
+            for index in range(num_task):
+                low, high = starts_at[index], starts_at[index + 1]
+                pl.when(free & (turn >= low) & (turn < high))(
+                    lambda index=index, low=low: run_task(index, turn - low, slot)
+                )
         return carry
 
-    lax.fori_loop(0, chunks + 2 * ahead, step, 0)
+    for name in names:
+        if name not in plan["late"]:
+            loads[name].wait()
+    lax.fori_loop(0, steps, step, 0)
+    if num_task:
+        assert task_total >= 2 and (steps // GROUP) * per_group >= task_total
+        for turn in (task_total - 2, task_total - 1):
+            index = max(i for i in range(num_task) if starts_at[i] <= turn)
+            stage_copy(index, turn - starts_at[index], turn % 2).wait()
 
     def drain(c, carry):
         @pl.when(jnp.logical_not(first))
         def _():
-            reduce_a(c, in_a.at[own_rows(c), :]).wait_send()
+            reduce_a(c).wait_send()
             gather_b(c).wait_send()
 
         @pl.when(jnp.logical_not(last))
         def _():
-            reduce_b(c, in_b.at[own_rows(c), :]).wait_send()
+            reduce_b(c).wait_send()
             gather_a(c).wait_send()
 
         return carry
@@ -492,25 +615,47 @@
     lax.fori_loop(0, chunks, drain, 0)
 
 
-def line_sum(finish, count, part, ins, out_shapes, clear, collective_id):
-    tokens, width = part.shape
+def line_sum(finish, count, held, vecs, parts, late, tasks, own_shapes, clear, collective_id):
+    names = list(held)
+    tokens = held[parts[0][0]].shape[0]
+    width = held[parts[0][1]].shape[0]
     half = tokens // 2
-    chunks = CHUNKS
+    plan = dict(
+        finish=finish,
+        clear=clear,
+        names=names,
+        parts=parts,
+        late=late,
+        tasks=[task[:3] for task in tasks],
+        vecs=len(vecs),
+        owns=len(own_shapes),
+    )
     whole = pl.BlockSpec(memory_space=pltpu.VMEM)
+    any_space = pl.BlockSpec(memory_space=pl.ANY)
+    depth = tokens if any(task[0] == "weight" for task in tasks) else LANES
+    stage_width = max([task[3][1] for task in tasks] + [LANES])
     return pl.pallas_call(
-        functools.partial(
-            line_kernel, finish, count, CHUNKS, SLACK, len(ins), len(out_shapes), clear
-        ),
-        out_shape=[jax.ShapeDtypeStruct((tokens, width), BF16)] + out_shapes,
-        in_specs=[whole] * (1 + len(ins)),
-        out_specs=[whole] * (1 + len(out_shapes)),
-        scratch_shapes=[pltpu.VMEM((half, width), BF16)] * 2
-        + [pltpu.SemaphoreType.DMA((chunks,))] * 8,
+        functools.partial(line_kernel, plan, count, CHUNKS, SLACK),
+        out_shape=[jax.ShapeDtypeStruct((tokens, width), BF16)]
+        + own_shapes
+        + [jax.ShapeDtypeStruct(task[3], BF16) for task in tasks],
+        in_specs=[any_space] * len(names) + [whole] * len(vecs),
+        out_specs=[whole] * (1 + len(own_shapes)) + [any_space] * len(tasks),
+        scratch_shapes=[pltpu.VMEM(array.shape, array.dtype) for array in held.values()]
+        + [pltpu.VMEM((half, width), BF16)] * 2
+        + [
+            pltpu.VMEM((2 * GROUP * half // CHUNKS, width), F32),
+            pltpu.VMEM((ROWS, depth), BF16),
+            pltpu.VMEM((2, ROWS if tasks else 16, stage_width), BF16),
+            pltpu.SemaphoreType.DMA((len(names),)),
+            pltpu.SemaphoreType.DMA((2,)),
+        ]
+        + [pltpu.SemaphoreType.DMA((CHUNKS,))] * 8,
         compiler_params=pltpu.CompilerParams(
             collective_id=collective_id, has_side_effects=True, vmem_limit_bytes=VMEM_LIMIT
         ),
-        cost_estimate=cost(120),
-    )(part, *ins)
+        cost_estimate=cost(110),
+    )(*held.values(), *vecs)
 
 
 def axis_barrier(counts):
@@ -712,15 +857,24 @@
     )
     head_normed = (mixed - head_center) * head_inverse
     head_act = (head_normed * head_gain_f + head_bias_f).astype(BF16)
-    out_part = matmul(head_act, w_out, 1, 1, BF16)
     own_shape = jax.ShapeDtypeStruct((tokens // 2, model_width), F32)
     sums_shape = jax.ShapeDtypeStruct((2, 8, model_width), F32)
-    second_act, middle_own = line_sum(
-        finish_middle, tp_count, out_part, (block, second_gain_f, second_bias_f), [own_shape], False, 3
-    )
+    hidden_size = hidden_gain.shape[0]
+    second_act, middle_own, grad_hidden_act = line_sum(
+        finish_middle,
+        tp_count,
+        dict(head_act=head_act, w_out=w_out, block=block, cotangent=cotangent, w_down=w_down),
+        (second_gain_f, second_bias_f),
+        [("head_act", "w_out")],
+        ("cotangent", "w_down"),
+        [("rows", "cotangent", "w_down", (tokens, hidden_size))],
+        [own_shape],
+        False,
+        3,
+    )
+    grad_hidden_act = grad_hidden_act.astype(F32)
 
     up_pre = matmul(second_act, w_up, 1, 0)
-    grad_hidden_act = matmul(cotangent, w_down, 1, 0)
     cdf = 0.5 * lax.erfc(up_pre * (-(0.5**0.5)))
     gelu_out = up_pre * cdf
     hidden_scaled = grad_hidden_act * hidden_gain_f
@@ -748,29 +902,32 @@
     pdf = jnp.exp(-0.5 * up_pre * up_pre) * (1.0 / math.sqrt(2.0 * math.pi))
     grad_up = (grad_gelu * (cdf + up_pre * pdf)).astype(BF16)
 
-    w_down_terms = matmul(cotangent, hidden_act, 0, 0, BF16)
-    w_up_terms = matmul(second_act, grad_up, 0, 0, BF16)
-    second_part = matmul(grad_up, w_up, 1, 1, BF16)
-    second_part, w_down_terms, w_up_terms = lax.optimization_barrier(
-        (second_part, w_down_terms, w_up_terms)
-    )
-    grad_middle_low, second_sums, grad_middle_own = line_sum(
-        finish_back,
+    weight_shape = (model_width, hidden_size)
+    grad_middle_low, second_sums, grad_middle_own, down_part, w_down_terms, w_up_terms = line_sum(
+        finish_second,
         tp_count,
-        second_part,
-        (cotangent, middle_own, second_gain_f),
+        dict(
+            grad_up=grad_up,
+            w_up=w_up,
+            cotangent=cotangent,
+            middle=middle_own,
+            hidden_act=hidden_act,
+            w_down=w_down,
+            second_act=second_act,
+        ),
+        (second_gain_f,),
+        [("grad_up", "w_up")],
+        ("hidden_act", "w_down", "second_act"),
+        [
+            ("down", "hidden_act", "w_down", (tokens, model_width)),
+            ("weight", "cotangent", "hidden_act", weight_shape),
+            ("weight", "second_act", "grad_up", weight_shape),
+        ],
         [sums_shape, own_shape],
         True,
         4,
     )
-    hidden_late, _ = lax.optimization_barrier((hidden_act, grad_middle_low))
-    down_part = matmul(hidden_late, w_down, 1, 1)
-    tp_index = lax.axis_index("tp")
-    half = tokens // 2
-    owner = jnp.where(tp_index == 0, 0, jnp.where(tp_index == tp_count - 1, 1, 2))
-    mine = (jnp.arange(2, dtype=jnp.int32) == owner)[:, None, None]
-    down_part = down_part.reshape(2, half, model_width) + jnp.where(mine, middle_own[None], 0.0)
-    block_out = lax.psum(down_part.astype(BF16), "tp")
+    block_out = lax.psum(down_part, "tp")
 
     def scatter(grad):
         return lax.psum_scatter(grad, "seq", scatter_dimension=0, tiled=True)
@@ -789,25 +946,18 @@
     )
     head_back = head_back[:, :, None] / model_width
     grad_mixed = head_inverse * (head_scaled - head_back[0] - head_normed * head_back[1])
-    grad_mixed, w_down_grad, w_up_grad = lax.optimization_barrier(
-        (grad_mixed.astype(BF16), w_down_grad, w_up_grad)
-    )
     (do_row,) = exchange(
         rows_out_kernel,
         seq_count,
         groups,
-        (grad_mixed.reshape(shape3),),
+        (grad_mixed.astype(BF16).reshape(shape3),),
         (length, width),
         6,
     )
     grads_row = attend_back(q_row, k_row, v_row, do_row, o_row, lse, tables, seg_col, seg_row)
     grads = exchange(rows_back_kernel, seq_count, groups, grads_row, shape3, 7)
     grad_query, grad_key, grad_value = (g.reshape(tokens, head_width) for g in grads)
-    first_part = (
-        dot(grad_query, w_query, 1, 1) + dot(grad_key, w_key, 1, 1) + dot(grad_value, w_value, 1, 1)
-    ).astype(BF16)
-    first_part, block_out = lax.optimization_barrier((first_part, block_out))
-    head_grads = scatter(
+    head_terms = (
         jnp.concatenate(
             [
                 matmul(first_act, grad_query, 0, 0, BF16),
@@ -818,11 +968,33 @@
             axis=1,
         )
     )
+    grad_query, head_terms, w_down_grad, block_out = lax.optimization_barrier(
+        (grad_query, head_terms, w_down_grad, block_out)
+    )
+    head_grads = scatter(head_terms)
     w_query_grad, w_key_grad, w_value_grad, w_out_grad = jnp.split(
         head_grads.astype(F32), 4, axis=1
     )
     input_grad, first_sums = line_sum(
-        finish_back, tp_count, first_part, (grad_middle_own, block, first_gain_f), [sums_shape], True, 8
+        finish_first,
+        tp_count,
+        dict(
+            grad_query=grad_query,
+            w_query=w_query,
+            grad_key=grad_key,
+            w_key=w_key,
+            grad_value=grad_value,
+            w_value=w_value,
+            block=block,
+            middle_grad=grad_middle_own,
+        ),
+        (first_gain_f,),
+        [("grad_query", "w_query"), ("grad_key", "w_key"), ("grad_value", "w_value")],
+        (),
+        [],
+        [sums_shape],
+        True,
+        8,
     )
 
     own_width = model_width // seq_count
@@ -835,7 +1007,6 @@
     )
     norm_own = norm_own.reshape(4, own_width)
     split = split.reshape(-1)
-    hidden_size = hidden_gain.shape[0]
     split_sums = (
         split[2 * hidden_size : 2 * hidden_size + head_width],
         split[2 * hidden_size + head_width :],

time: 811 us -> 755 us (0.931)
  matrix products: 154 us -> 69.4 us
  Pallas kernels: 536 us -> 575 us
  local copies, waits for them, and re-layouts: 29.2 us -> 18.9 us
  other arithmetic: 64.9 us -> 56 us
  waiting for transfers between devices: 6.56 us -> 15.2 us
    dot_general x18 -> x9, matrix products: 154 us -> 69.4 us  [dot(): lax.dot_general(left, right, (((left_dim,), (right_dim,)), ((), ())), pre...]
    pallas_call x3, Pallas kernels: 345 us -> 367 us  [line_sum(): pl.pallas_call(functools.partial(line_kernel, plan, count, CHUNKS, SLACK)...]
    pallas_call x4, Pallas kernels: 110 us -> 126 us  [exchange(): pl.pallas_call(functools.partial(kernel, count, groups, num), out_shape=[...]
    psum x1, waiting for transfers between devices: 5.8 us -> 14.2 us  [body(): block_out = lax.psum(down_part, 'tp')]
    unnamed x107 -> x78, local copies, waits for them, and re-layouts: 19.4 us -> 11.8 us
  transfers between devices with their start and end apart: 4 -> 4, of which waited for: 1 -> 1; matrix products, arithmetic and copies ran while one was open for 11% -> 5% of each run, Pallas kernels for 41% -> 32%
where the time goes in v3:
time: 755 us; the launch traced here: 752 us
  Pallas kernels  575 us (76%)
  matrix products  69.4 us (9%)
  other arithmetic  56 us (7%)
  local copies, waits for them, and re-layouts  18.9 us (3%)
  between operations  16.6 us (2%)
  waiting for transfers between devices  15.2 us (2%)
    pallas_call x3, Pallas kernels, line_sum(): pl.pallas_call(functools.partial(line_kernel, plan, count, CHUNKS, SLACK)...  367 us
    pallas_call x4, Pallas kernels, exchange(): pl.pallas_call(functools.partial(kernel, count, groups, num), out_shape=[...  126 us
    dot_general x9, matrix products, dot(): lax.dot_general(left, right, (((left_dim,), (right_dim,)), ((), ())), pre...  69.4 us
    pallas_call x1, Pallas kernels, attend_back(): pl.pallas_call(functools.partial(attend_back_kernel, length), grid=(pairs...  30.2 us
    pallas_call x3, Pallas kernels, tp_sum(): pl.pallas_call(functools.partial(tp_sum_kernel, count), out_shape=jax.Sha...  22.7 us
    pallas_call x1, Pallas kernels, attend(): pl.pallas_call(functools.partial(attend_kernel, length), grid=(pairs,), o...  17.8 us
    reduce_sum x1, other arithmetic, body(): hidden_gain_grad = jnp.sum(grad_hidden_act * hidden_normed, axis=0)  15.9 us
  transfers between devices with their start and end apart: 4, of which 1 were waited for; matrix products, arithmetic and copies ran while one was open for 5% of the time, Pallas kernels for 32%

profile of v3, /device:TPU:0, one launch (start us, length us, event | category | flops | bytes accessed | tf_op | source)
XLA Modules:
  0.0 751.5 jit_solution(6876083241262720233)
XLA Ops:
  13.6 3.4 fusion.5
  21.1 3.5 add_convert_fusion.1
  24.6 5.0 convolution_convert_fusion.1
  40.9 39.0 %shard_map.288 = (bf16[1024,512]{1,0:T(8,128)(2,1)}, bf16[1024,512]{1,0:T(8,128)(2,1)}, bf16[1024,512]{1,0:T(8,128)(2,1)}) custom-call(bf16[8,128,512]{2,1,0:T(8,128)(2,1)} %bitcast.141, bf16[8,128,512]{2,1,0:T(8,128)(2,1)} %bitcast.140, bf16[8,128,512]{2,1,0:T(8,128)(2,1)} %bitcast.139), custom_call_target="tpu_custom_call" | custom-call | flops 44000002048 | tf_op jit(solution)/shard_map/pallas_call | solution.py:123
  81.4 17.8 %shard_map.289 = (bf16[1024,512]{1,0:T(8,128)(2,1)}, f32[4,8,1024]{2,1,0:T(8,128)}) custom-call(bf16[1024,512]{1,0:T(8,128)(2,1)} %get-tuple-element.44.q_ref, bf16[1024,512]{1,0:T(8,128)(2,1)} %get-tuple-element.45.k_ref, bf16[1024,512]{1,0:T(8,128)(2,1)} %get-tuple-element.46.v_ref, f32[4,1024,128]{2,1,0:T(8,128)} %pad_maximum_fusion.1.tab_ref, ...), custom_call_target="tpu_custom_call" | custom-call | flops 18699999232 | tf_op jit(solution)/shard_map/pallas_call | solution.py:200
  99.1 15.0 %shard_map.290 = bf16[8,128,512]{2,1,0:T(8,128)(2,1)} custom-call(bf16[1024,512]{1,0:T(8,128)(2,1)} %get-tuple-element.47.refs_0_.o_ref), custom_call_target="tpu_custom_call" | custom-call | flops 17600000000 | tf_op jit(solution)/shard_map/pallas_call | solution.py:123
  116.4 7.5 shard_map.291
  126.2 118.1 %shard_map.292 = (bf16[1024,2048]{1,0:T(8,128)(2,1)}, f32[512,2048]{1,0:T(8,128)}, bf16[1024,2048]{1,0:T(8,128)(2,1)}) custom-call(bf16[1024,512]{1,0:T(8,128)(2,1)} %add_convert_fusion.2.refs_0_, bf16[2048,512]{1,0:T(8,128)(2,1)} %refs_1_.3, bf16[1024,2048]{1,0:T(8,128)(2,1)} %bitcast.102, bf16[1024,2048]{1,0:T(8,128)(2,1)} %bitcast.134, ...), custom_call_target="tpu_custom_call" | custom-call | flops 121000001536 | tf_op jit(solution)/shard_map/pallas_call | solution.py:637
  244.3 35.1 %fusion.41 = (f32[1024]{0:T(1024)S(1)}, f32[1024]{0:T(1024)S(1)}, f32[1024]{0:T(1024)S(1)}, f32[1024]{0:T(1024)S(1)}, f32[2048]{0:T(1024)}, /*index=5*/f32[1024,...) fusion(f32[2048]{0:T(1024)S(1)} %copy-done.18, bf16[1024,2048]{1,0:T(8,128)(2,1)} %get-tuple-element.49, ...), kind=kOutput, calls=%fused_computation.109 | convolution fusion | flops 8740923392 | bytes 41975808 | tf_op jit(solution)/shard_map/dot_general | solution.py:32
  280.0 7.5 shard_map.293
  288.2 15.9 %fusion.16 = (f32[2048]{0:T(1024)S(1)}, bf16[1024,2048]{1,0:T(8,128)(2,1)}, bf16[1024,2048]{1,0:T(8,128)(2,1)}) fusion(bf16[1024,2048]{1,0:T(8,128)(2,1)} %get-tuple-element.49, f32[1024,2048]{1,0:T(8,128)} %get-tuple-element.131, f32[1024]{0:T(1024)S(1)} %bitcast.115, f32[1024]{0:T(1024)S(1)} %get-tuple-element.154, f32[1024,2048]{1,0:T(8,128)} %get-tuple-element.132, ...), kind=kLoop, calls=%fused_computation.23 | loop fusion | flops 41940992 | bytes 37789696 | tf_op jit(solution)/shard_map/reduce_sum | solution.py:898
  304.1 128.5 %shard_map.294 = (bf16[1024,2048]{1,0:T(8,128)(2,1)}, f32[2,8,2048]{2,1,0:T(8,128)}, f32[512,2048]{1,0:T(8,128)}, bf16[1024,2048]{1,0:T(8,128)(2,1)}, bf16[2048,...) custom-call(bf16[1024,2048]{1,0:T(8,128)(2,1)} %get-tuple-element.134.refs_0_, bf16[2048,2048]{1,0:T(8,128)(2,1)} %refs_1_.4, ...), custom_call_target="tpu_custom_call" | custom-call | flops 121000001536 | tf_op jit(solution)/shard_map/pallas_call | solution.py:637
  433.9 5.6 multiply_reduce_fusion.1
  440.1 7.8 %shard_map.295 = f32[2,1024]{1,0:T(2,128)} custom-call(f32[2,1024]{1,0:T(2,128)} %pad_maximum_fusion.9.x_ref), custom_call_target="tpu_custom_call" | custom-call | flops 5500000256 | tf_op jit(solution)/shard_map/pallas_call | solution.py:708
  451.6 5.4 convolution_convert_fusion
  457.0 26.6 %shard_map.296.do_ref = bf16[1024,512]{1,0:T(8,128)(2,1)} custom-call(bf16[8,128,512]{2,1,0:T(8,128)(2,1)} %bitcast.106), custom_call_target="tpu_custom_call" | custom-call | flops 17600000000 | tf_op jit(solution)/shard_map/pallas_call | solution.py:123
  483.6 30.2 %shard_map.297 = (bf16[1024,512]{1,0:T(8,128)(2,1)}, bf16[1024,512]{1,0:T(8,128)(2,1)}, bf16[1024,512]{1,0:T(8,128)(2,1)}) custom-call(bf16[1024,512]{1,0:T(8,128)(2,1)} %get-tuple-element.44.q_ref, bf16[1024,512]{1,0:T(8,128)(2,1)} %get-tuple-element.45.k_ref, bf16[1024,512]{1,0:T(8,128)(2,1)} %get-tuple-element.46.v_ref, ...), custom_call_target="tpu_custom_call" | custom-call | flops 32999999488 | tf_op jit(solution)/shard_map/pallas_call | solution.py:295
  513.8 45.1 %shard_map.298 = (bf16[8,128,512]{2,1,0:T(8,128)(2,1)}, bf16[8,128,512]{2,1,0:T(8,128)(2,1)}, bf16[8,128,512]{2,1,0:T(8,128)(2,1)}) custom-call(bf16[1024,512]{1,0:T(8,128)(2,1)} %get-tuple-element.53.refs_0_, bf16[1024,512]{1,0:T(8,128)(2,1)} %get-tuple-element.54.refs_1_, bf16[1024,512]{1,0:T(8,128)(2,1)} %get-tuple-element.55.refs_2_), custom_call_target="tpu_custom_call" | custom-call | flops 44000002048 | tf_op jit(solution)/shard_map/pallas_call | solution.py:123
  559.0 5.8 bitcast_convert_fusion.2
  570.6 4.1 pad_maximum_fusion
  574.7 14.2 %all-reduce.2.cloned.1.call-done = bf16[1024,2048]{1,0:T(8,128)(2,1)} async-done(((bf16[1024,2048]{1,0:T(8,128)(2,1)}), bf16[1024,2048]{1,0:T(8,128)(2,1)}) %all-reduce.2.cloned.1.call-update) | async-done | bytes 4194320 | tf_op jit(solution)/shard_map/psum | solution.py:930
  589.0 120.8 %shard_map.299 = (bf16[1024,2048]{1,0:T(8,128)(2,1)}, f32[2,8,2048]{2,1,0:T(8,128)}) custom-call(bf16[1024,512]{1,0:T(8,128)(2,1)} %bitcast.136, bf16[2048,512]{1,0:T(8,128)(2,1)} %refs_1_.5, bf16[1024,512]{1,0:T(8,128)(2,1)} %bitcast.137, bf16[2048,512]{1,0:T(8,128)(2,1)} %refs_3_.1, bf16[1024,512]{1,0:T(8,128)(2,1)} %bitcast.138, ...), custom_call_target="tpu_custom_call" | custom-call | flops 121000001536 | tf_op jit(solution)/shard_map/pallas_call | solution.py:637
  715.8 11.5 %shard_map.300 = (f32[8,128]{1,0:T(8,128)}, f32[40,128]{1,0:T(8,128)}) custom-call(f32[8,8,128]{2,1,0:T(8,128)} %reshape.1240.full_ref, f32[40,128]{1,0:T(8,128)} %maximum_bitcast_fusion.split_ref), custom_call_target="tpu_custom_call" | custom-call | flops 11000000512 | tf_op jit(solution)/shard_map/pallas_call | solution.py:749
  736.7 4.9 copy.64
  (137 shorter events, 56.7 us)
Async XLA Ops:
  8.0 9.6 %copy-start.25 = (bf16[2048]{0:T(1024)(128)(2,1)S(1)}, bf16[2048]{0:T(1024)(128)(2,1)}, u32[]{:S(2)}) copy-start(bf16[2048]{0:T(1024)(128)(2,1)} %param.19) | copy-start | bytes 12292
  8.0 9.6 %copy-start.26 = (bf16[2048]{0:T(1024)(128)(2,1)S(1)}, bf16[2048]{0:T(1024)(128)(2,1)}, u32[]{:S(2)}) copy-start(bf16[2048]{0:T(1024)(128)(2,1)} %param.20) | copy-start | bytes 12292
  8.1 9.6 %copy-start.27 = (bf16[2048]{0:T(1024)(128)(2,1)S(1)}, bf16[2048]{0:T(1024)(128)(2,1)}, u32[]{:S(2)}) copy-start(bf16[2048]{0:T(1024)(128)(2,1)} %param.30) | copy-start | bytes 12292
  8.1 10.2 %copy-start.28 = (bf16[2048]{0:T(1024)(128)(2,1)S(1)}, bf16[2048]{0:T(1024)(128)(2,1)}, u32[]{:S(2)}) copy-start(bf16[2048]{0:T(1024)(128)(2,1)} %param.27) | copy-start | bytes 12292
  8.1 10.8 %copy-start.29 = (bf16[2048]{0:T(1024)(128)(2,1)S(1)}, bf16[2048]{0:T(1024)(128)(2,1)}, u32[]{:S(2)}) copy-start(bf16[2048]{0:T(1024)(128)(2,1)} %param.28) | copy-start | bytes 12292
  8.1 11.4 %copy-start.30 = (bf16[2048]{0:T(1024)(128)(2,1)S(1)}, bf16[2048]{0:T(1024)(128)(2,1)}, u32[]{:S(2)}) copy-start(bf16[2048]{0:T(1024)(128)(2,1)} %param.31) | copy-start | bytes 12292
  8.1 580.8 %all-reduce.2.cloned.1.call-start = ((), (), s32[]{:S(2)}) async-start(), calls=%async_computation.4 | async-start | bytes 8388608 | tf_op jit(solution)/shard_map/psum | solution.py:930
  8.8 15.8 %copy-start.11 = (s32[1,1024]{1,0:T(1,128)}, s32[1,1024]{1,0:T(1,128)S(1)}, u32[]{:S(2)}) copy-start(s32[1,1024]{1,0:T(1,128)S(1)} %constant_dynamic-slice_fusion.segr_ref) | copy-start | bytes 12292
  9.5 115.2 %copy-start.20 = (f32[512]{0:T(512)}, f32[512]{0:T(512)S(1)}, u32[]{:S(2)}) copy-start(f32[512]{0:T(512)S(1)} %convert_element_type.116) | copy-start | bytes 6148
  17.6 12.0 %copy-start.14 = (f32[2048]{0:T(1024)}, f32[2048]{0:T(1024)S(1)}, u32[]{:S(2)}) copy-start(f32[2048]{0:T(1024)S(1)} %convert_element_type.105) | copy-start | bytes 24580
  17.6 12.0 %copy-start.16 = (f32[2048]{0:T(1024)}, f32[2048]{0:T(1024)S(1)}, u32[]{:S(2)}) copy-start(f32[2048]{0:T(1024)S(1)} %convert_element_type.106) | copy-start | bytes 24580
  124.7 119.5 %copy-start.9 = (f32[1,1024]{1,0:T(1,128)}, f32[1,1024]{1,0:T(1,128)S(1)}, u32[]{:S(2)}) copy-start(f32[1,1024]{1,0:T(1,128)S(1)} %get-tuple-element.157) | copy-start | bytes 12292
  124.7 119.5 %copy-start.12 = (f32[1024]{0:T(1024)}, f32[1024]{0:T(1024)S(1)}, u32[]{:S(2)}) copy-start(f32[1024]{0:T(1024)S(1)} %add_rsqrt_fusion.1) | copy-start | bytes 12292
  126.2 118.1 %copy-start.18 = (f32[2048]{0:T(1024)S(1)}, f32[2048]{0:T(1024)}, u32[]{:S(2)}) copy-start(f32[2048]{0:T(1024)} %convert_element_type.120) | copy-start | bytes 24580
  432.6 156.3 %reduce-scatter.4.cloned.1.call-start = ((), (), s32[]{:S(2)}) async-start(), calls=%async_computation.3 | async-start | bytes 9437184 | tf_op jit(solution)/shard_map/reduce_scatter | solution.py:933
  433.2 279.8 %reduce-scatter.8.cloned.1.call-start = ((), (), s32[]{:S(2)}) async-start(), calls=%async_computation.6 | async-start | bytes 9437184 | tf_op jit(solution)/shard_map/reduce_scatter | solution.py:933
  433.8 297.6 %reduce-scatter.6.cloned.1.call-start = ((), (), s32[]{:S(2)}) async-start(), calls=%async_computation.5 | async-start | bytes 9437184 | tf_op jit(solution)/shard_map/reduce_scatter | solution.py:933
  440.1 10.8 %copy-start.24 = (f32[2048]{0:T(1024)S(1)}, f32[2048]{0:T(1024)}, u32[]{:S(2)}) copy-start(f32[2048]{0:T(1024)} %get-tuple-element.124) | copy-start | bytes 24580
  513.8 45.1 %copy-start.15 = (f32[2048]{0:T(1024)S(1)}, f32[2048]{0:T(1024)}, u32[]{:S(2)}) copy-start(f32[2048]{0:T(1024)} %copy-done.14) | copy-start | bytes 24580
  513.8 45.1 %copy-start.17 = (f32[2048]{0:T(1024)S(1)}, f32[2048]{0:T(1024)}, u32[]{:S(2)}) copy-start(f32[2048]{0:T(1024)} %copy-done.16) | copy-start | bytes 24580
  513.8 45.1 %copy-start.23 = (f32[8,128]{1,0:T(8,128)S(1)}, f32[8,128]{1,0:T(8,128)}, u32[]{:S(2)}) copy-start(f32[8,128]{1,0:T(8,128)} %copy-done.22) | copy-start | bytes 12292
  513.8 45.1 %copy-start.31 = (f32[8,128]{1,0:T(8,128)S(1)}, f32[8,128]{1,0:T(8,128)}, u32[]{:S(2)}) copy-start(f32[8,128]{1,0:T(8,128)} %get-tuple-element.167) | copy-start | bytes 12292
  588.9 121.8 %copy-start.8 = (f32[2,2048]{1,0:T(2,128)S(1)}, f32[2,2048]{1,0:T(2,128)}, u32[]{:S(2)}) copy-start(f32[2,2048]{1,0:T(2,128)} %reduce_sum.164) | copy-start | bytes 49156
  589.0 122.5 %copy-start.6 = (bf16[256,2048]{1,0:T(8,128)(2,1)S(1)}, bf16[256,2048]{1,0:T(8,128)(2,1)}, u32[]{:S(2)}) copy-start(bf16[256,2048]{1,0:T(8,128)(2,1)} %reduce-scatter.4.cloned.1.call-done) | copy-start | bytes 3145732
  (16 other events, 68.9 us)
Sparse Core Ops, SparseCore 0:
  432.7 156.1 all-reduce.1
Sparse Core Ops, SparseCore 1:
  436.9 79.4 reduce-scatter.3
  519.7 75.0 reduce-scatter.7
  598.5 71.1 reduce-scatter.5

commit v4 on v3

--- a/solution.py
+++ b/solution.py
@@ -34,106 +34,32 @@
     )
 
 
-def seq_barrier(count):
+def seq_signal(count):
     me = lax.axis_index("seq")
     barrier = pltpu.get_barrier_semaphore()
     for k in range(1, count):
         pl.semaphore_signal(
             barrier, inc=1, device_id={"seq": lax.rem(me + k, count)}, device_id_type=MESH
         )
-    pl.semaphore_wait(barrier, count - 1)
-
-
-def rows_out_kernel(count, groups, num, *refs):
-    sources, targets = refs[:num], refs[num : 2 * num]
-    send_sem, recv_sem, own_sem = refs[2 * num :]
-    me = lax.axis_index("seq")
-    span = sources[0].shape[1]
-    width = targets[0].shape[1]
-    seq_barrier(count)
-
-    def piece(source, device):
-        lane = pl.multiple_of(lax.rem(device, groups) * width, LANES)
-        return source.at[device // groups, :, pl.ds(lane, width)]
-
-    def place(target):
-        return target.at[pl.ds(pl.multiple_of(me * span, LANES), span), :]
-
-    copies = []
-    for k in range(1, count):
-        device = lax.rem(me + k, count)
-        for i in range(num):
-            copy = pltpu.make_async_remote_copy(
-                src_ref=piece(sources[i], device),
-                dst_ref=place(targets[i]),
-                send_sem=send_sem.at[i, k],
-                recv_sem=recv_sem.at[i, k],
-                device_id={"seq": device},
-                device_id_type=MESH,
-            )
-            copy.start()
-            copies.append(copy)
-    for i in range(num):
-        copy = pltpu.make_async_copy(piece(sources[i], me), place(targets[i]), own_sem.at[i])
-        copy.start()
-        copies.append(copy)
-    for copy in copies:
-        copy.wait()
-
-
-def rows_back_kernel(count, groups, num, *refs):
-    sources, targets = refs[:num], refs[num : 2 * num]
-    send_sem, recv_sem, own_sem = refs[2 * num :]
-    me = lax.axis_index("seq")
-    span = targets[0].shape[1]
-    width = sources[0].shape[1]
-    seq_barrier(count)
-
-    def piece(source, device):
-        return source.at[pl.ds(pl.multiple_of(device * span, LANES), span), :]
-
-    def place(target):
-        lane = pl.multiple_of(lax.rem(me, groups) * width, LANES)
-        return target.at[me // groups, :, pl.ds(lane, width)]
-
-    copies = []
-    for k in range(1, count):
-        device = lax.rem(me + k, count)
-        for i in range(num):
-            copy = pltpu.make_async_remote_copy(
-                src_ref=piece(sources[i], device),
-                dst_ref=place(targets[i]),
-                send_sem=send_sem.at[i, k],
-                recv_sem=recv_sem.at[i, k],
-                device_id={"seq": device},
-                device_id_type=MESH,
-            )
-            copy.start()
-            copies.append(copy)
-    for i in range(num):
-        copy = pltpu.make_async_copy(piece(sources[i], me), place(targets[i]), own_sem.at[i])
-        copy.start()
-        copies.append(copy)
-    for copy in copies:
-        copy.wait()
-
-
-def exchange(kernel, count, groups, arrays, shape, collective_id):
-    num = len(arrays)
-    outs = pl.pallas_call(
-        functools.partial(kernel, count, groups, num),
-        out_shape=[jax.ShapeDtypeStruct(shape, BF16)] * num,
-        in_specs=[pl.BlockSpec(memory_space=pl.ANY)] * num,
-        out_specs=[pl.BlockSpec(memory_space=pl.ANY)] * num,
-        scratch_shapes=[
-            pltpu.SemaphoreType.DMA((num, count)),
-            pltpu.SemaphoreType.DMA((num, count)),
-            pltpu.SemaphoreType.DMA((num,)),
-        ],
-        compiler_params=pltpu.CompilerParams(collective_id=collective_id, has_side_effects=True),
-        cost_estimate=cost(4 + 12 * num),
-    )(*arrays)
-    return outs
+
+
+def seq_wait(count):
+    pl.semaphore_wait(pltpu.get_barrier_semaphore(), count - 1)
+
+
+def send(source, target, send_sem, recv_sem, device):
+    return pltpu.make_async_remote_copy(
+        src_ref=source,
+        dst_ref=target,
+        send_sem=send_sem,
+        recv_sem=recv_sem,
+        device_id={"seq": device},
+        device_id_type=MESH,
+    )
+
+
+def spans(index, span):
+    return pl.ds(pl.multiple_of(index * span, LANES), span)
 
 
 def swap_halves(values):
@@ -151,160 +77,312 @@
     return jnp.where(lane < HEAD, values, zero), jnp.where(lane < HEAD, zero, values)
 
 
-def attend_kernel(length, q_ref, k_ref, v_ref, tab_ref, segc_ref, segr_ref, o_ref, lse_ref, bias, qs, ks):
+def block_rows(index):
+    return slice(index * BLOCK, (index + 1) * BLOCK)
+
+
+def rotated(values, tables, first, rows):
+    values = values.astype(F32)
+    return values * tables[first, rows, :] + swap_halves(values) * tables[first + 1, rows, :]
+
+
+def rotated_back(values, tables, first, rows):
+    return values * tables[first, rows, :] - swap_halves(values) * tables[first + 1, rows, :]
+
+
+def norm_parts(values):
+    center = jnp.mean(values, axis=-1, keepdims=True)
+    shifted = values - center
+    inverse = lax.rsqrt(jnp.mean(shifted * shifted, axis=-1, keepdims=True) + EPSILON)
+    return shifted * inverse, inverse
+
+
+def front_kernel(
+    count, groups, x_ref, wq_ref, wk_ref, wv_ref, gain_ref, bias_ref, tab_ref, segc_ref, segr_ref,
+    act_ref, qkv_ref, o_ref, lse_ref, mixed_ref,
+    weights, staged, bias, qs, ks, load_sem, send_sem, recv_sem, back_send_sem, back_recv_sem,
+):
+    me = lax.axis_index("seq")
+    pairs, length = qkv_ref.shape[:2]
+    tokens = x_ref.shape[0]
+    span = length // count
     blocks = length // BLOCK
-
-    @pl.when(pl.program_id(0) == 0)
-    def _():
+    mine, row = lax.rem(me, groups), me // groups
+    seq_signal(count)
+    loads = []
+    for j in range(pairs * groups):
+        for i, source in enumerate((wq_ref, wk_ref, wv_ref)):
+            copy = pltpu.make_async_copy(
+                source.at[:, j * LANES : (j + 1) * LANES],
+                weights.at[j, :, i * LANES : (i + 1) * LANES],
+                load_sem.at[3 * j + i],
+            )
+            copy.start()
+            loads.append(copy)
+
+    def norm_step(r, carry):
+        rows = pl.ds(pl.multiple_of(r * LANES, LANES), LANES)
+        normed, _ = norm_parts(x_ref[rows, :].astype(F32))
+        act_ref[rows, :] = (normed * gain_ref[...] + bias_ref[...]).astype(BF16)
+        return carry
+
+    lax.fori_loop(0, tokens // LANES, norm_step, 0)
+    for copy in loads:
+        copy.wait()
+
+    def there(p, k):
+        device = lax.rem(me + k, count)
+        return send(
+            staged.at[lax.rem(device, groups) * pairs + p, spans(device // groups, span), :],
+            qkv_ref.at[p, spans(me, span), :],
+            send_sem.at[p, k],
+            recv_sem.at[p, k],
+            device,
+        )
+
+    def back(p, k):
+        device = lax.rem(me + k, count)
+        return send(
+            o_ref.at[p, spans(device, span), :],
+            mixed_ref.at[spans(row, span), spans(mine * pairs + p, LANES)],
+            back_send_sem.at[p, k],
+            back_recv_sem.at[p, k],
+            device,
+        )
+
+    def project(p, carry):
+        for group in range(groups):
+
+            def rows_step(r, inner):
+                rows = pl.ds(pl.multiple_of(r * BLOCK, BLOCK), BLOCK)
+                j = group * pairs + p
+                staged[j, rows, :] = dot(act_ref[rows, :], weights[j], 1, 0).astype(BF16)
+                return inner
+
+            lax.fori_loop(0, tokens // BLOCK, rows_step, 0)
+
+        @pl.when(p == 0)
+        def _():
+            seq_wait(count)
+
+        for k in range(1, count):
+            there(p, k).start()
+        qkv_ref[p, spans(me, span), :] = staged[mine * pairs + p, spans(row, span), :]
+        return carry
+
+    lax.fori_loop(0, pairs, project, 0)
+    for qb in range(blocks):
+        rows = block_rows(qb)
+        keys = (qb + 1) * BLOCK
+        same = segc_ref[rows, :] == segr_ref[:, :keys]
+        query = lax.broadcasted_iota(jnp.int32, (BLOCK, keys), 0) + qb * BLOCK
+        key = lax.broadcasted_iota(jnp.int32, (BLOCK, keys), 1)
+        bias[rows, :keys] = jnp.where(same & (key <= query), 0.0, MASKED)
+
+    def attend(p, carry):
+        for k in range(1, count):
+            there(p, k).wait_recv()
         for qb in range(blocks):
-            rows = slice(qb * BLOCK, (qb + 1) * BLOCK)
+            rows = block_rows(qb)
+            q = rotated(qkv_ref[p, rows, :LANES], tab_ref, 0, rows) * (HEAD**-0.5)
+            q0, q1 = head_masks(q)
+            qs[0, rows, :] = q0.astype(BF16)
+            qs[1, rows, :] = q1.astype(BF16)
+            k = rotated(qkv_ref[p, rows, LANES : 2 * LANES], tab_ref, 2, rows)
+            ks[rows, :] = k.astype(BF16)
+        for qb in range(blocks):
+            rows = block_rows(qb)
             keys = (qb + 1) * BLOCK
-            same = segc_ref[rows, :] == segr_ref[:, :keys]
-            row = lax.broadcasted_iota(jnp.int32, (BLOCK, keys), 0) + qb * BLOCK
-            col = lax.broadcasted_iota(jnp.int32, (BLOCK, keys), 1)
-            bias[rows, :keys] = jnp.where(same & (col <= row), 0.0, MASKED)
-
-    for qb in range(blocks):
-        rows = slice(qb * BLOCK, (qb + 1) * BLOCK)
-        q = q_ref[rows, :].astype(F32)
-        q = (q * tab_ref[0, rows, :] + swap_halves(q) * tab_ref[1, rows, :]) * (HEAD**-0.5)
-        q0, q1 = head_masks(q)
-        qs[0, rows, :] = q0.astype(BF16)
-        qs[1, rows, :] = q1.astype(BF16)
-        k = k_ref[rows, :].astype(F32)
-        k = k * tab_ref[2, rows, :] + swap_halves(k) * tab_ref[3, rows, :]
-        ks[rows, :] = k.astype(BF16)
-    for qb in range(blocks):
-        rows = slice(qb * BLOCK, (qb + 1) * BLOCK)
-        keys = (qb + 1) * BLOCK
-        outs = []
-        logs = []
-        for h in range(2):
-            scores = dot(qs[h, rows, :], ks[:keys, :], 1, 1) + bias[rows, :keys]
-            top = jnp.max(scores, axis=1, keepdims=True)
-            expo = jnp.exp(scores - top)
-            total = jnp.sum(expo, axis=1, keepdims=True)
-            outs.append(dot(expo.astype(BF16), v_ref[:keys, :], 1, 0) / total)
-            logs.append(jnp.broadcast_to(top + jnp.log(total), (BLOCK, LANES)))
-        lane = lax.broadcasted_iota(jnp.int32, (BLOCK, LANES), 1)
-        o_ref[rows, :] = jnp.where(lane < HEAD, outs[0], outs[1]).astype(BF16)
-        logs_t = jnp.transpose(jnp.where(lane < HEAD, logs[0], logs[1]))
-        lse_ref[0, 0:1, rows] = logs_t[0:1]
-        lse_ref[0, 1:2, rows] = logs_t[HEAD : HEAD + 1]
-
-
-def attend(q, k, v, tables, seg_col, seg_row):
-    length, width = q.shape
-    pairs = width // LANES
-    lane_block = pl.BlockSpec((length, LANES), lambda p: (0, p))
+            outs = []
+            logs = []
+            for h in range(2):
+                scores = dot(qs[h, rows, :], ks[:keys, :], 1, 1) + bias[rows, :keys]
+                top = jnp.max(scores, axis=1, keepdims=True)
+                expo = jnp.exp(scores - top)
+                total = jnp.sum(expo, axis=1, keepdims=True)
+                outs.append(dot(expo.astype(BF16), qkv_ref[p, :keys, 2 * LANES :], 1, 0) / total)
+                logs.append(jnp.broadcast_to(top + jnp.log(total), (BLOCK, LANES)))
+            lane = lax.broadcasted_iota(jnp.int32, (BLOCK, LANES), 1)
+            o_ref[p, rows, :] = jnp.where(lane < HEAD, outs[0], outs[1]).astype(BF16)
+            logs_t = jnp.transpose(jnp.where(lane < HEAD, logs[0], logs[1]))
+            lse_ref[p, 0:1, rows] = logs_t[0:1]
+            lse_ref[p, 1:2, rows] = logs_t[HEAD : HEAD + 1]
+        for k in range(1, count):
+            back(p, k).start()
+        mixed_ref[spans(row, span), spans(mine * pairs + p, LANES)] = o_ref[p, spans(me, span), :]
+        return carry
+
+    lax.fori_loop(0, pairs, attend, 0)
+
+    def drain(p, carry):
+        for k in range(1, count):
+            there(p, k).wait_send()
+            back(p, k).wait()
+        return carry
+
+    lax.fori_loop(0, pairs, drain, 0)
+
+
+def front(x, w_query, w_key, w_value, gain, bias, tables, seg_col, seg_row, count, groups, collective_id):
+    tokens, model_width = x.shape
+    head_width = w_query.shape[1]
+    length = seg_col.shape[0]
+    pairs = head_width // groups // LANES
+    whole = pl.BlockSpec(memory_space=pltpu.VMEM)
+    any_space = pl.BlockSpec(memory_space=pl.ANY)
     return pl.pallas_call(
-        functools.partial(attend_kernel, length),
-        grid=(pairs,),
+        functools.partial(front_kernel, count, groups),
         out_shape=[
-            jax.ShapeDtypeStruct((length, width), BF16),
+            jax.ShapeDtypeStruct((tokens, model_width), BF16),
+            jax.ShapeDtypeStruct((pairs, length, 3 * LANES), BF16),
+            jax.ShapeDtypeStruct((pairs, length, LANES), BF16),
             jax.ShapeDtypeStruct((pairs, 8, length), F32),
+            jax.ShapeDtypeStruct((tokens, head_width), BF16),
         ],
-        in_specs=[
-            lane_block,
-            lane_block,
-            lane_block,
-            pl.BlockSpec((4, length, LANES), lambda p: (0, 0, 0)),
-            pl.BlockSpec((length, 1), lambda p: (0, 0)),
-            pl.BlockSpec((1, length), lambda p: (0, 0)),
-        ],
-        out_specs=[lane_block, pl.BlockSpec((1, 8, length), lambda p: (p, 0, 0))],
+        in_specs=[whole] + [any_space] * 3 + [whole] * 5,
+        out_specs=[whole] * 5,
         scratch_shapes=[
+            pltpu.VMEM((pairs * groups, model_width, 3 * LANES), BF16),
+            pltpu.VMEM((pairs * groups, tokens, 3 * LANES), BF16),
             pltpu.VMEM((length, length), F32),
             pltpu.VMEM((2, length, LANES), BF16),
             pltpu.VMEM((length, LANES), BF16),
-        ],
-        compiler_params=pltpu.CompilerParams(vmem_limit_bytes=VMEM_LIMIT),
-        cost_estimate=cost(17),
-    )(q, k, v, tables, seg_col, seg_row)
-
-
-def attend_back_kernel(
-    length, q_ref, k_ref, v_ref, do_ref, o_ref, lse_ref, tab_ref, segc_ref, segr_ref,
-    dq_ref, dk_ref, dv_ref, bias, qs, ks, kms, dos, delta, dq, dk, dv,
+            pltpu.SemaphoreType.DMA((3 * pairs * groups,)),
+        ]
+        + [pltpu.SemaphoreType.DMA((pairs, count))] * 4,
+        compiler_params=pltpu.CompilerParams(
+            collective_id=collective_id, has_side_effects=True, vmem_limit_bytes=VMEM_LIMIT
+        ),
+        cost_estimate=cost(60),
+    )(x, w_query, w_key, w_value, gain, bias, tables, seg_col, seg_row)
+
+
+def back_kernel(
+    count, groups, do_ref, qkv_ref, o_ref, lse_ref, tab_ref, segc_ref, segr_ref, grads_ref,
+    do_row, made, bias, qs, ks, kms, dos, delta, dq, dk, dv,
+    send_sem, recv_sem, back_send_sem, back_recv_sem,
 ):
+    me = lax.axis_index("seq")
+    pairs, length = qkv_ref.shape[:2]
+    span = length // count
     blocks = length // BLOCK
-
-    @pl.when(pl.program_id(0) == 0)
-    def _():
-        for kb in range(blocks):
-            rows = slice(kb * BLOCK, (kb + 1) * BLOCK)
-            first = kb * BLOCK
-            shape = (BLOCK, length - first)
-            same = segc_ref[rows, :] == segr_ref[:, first:]
-            key = lax.broadcasted_iota(jnp.int32, shape, 0)
-            query = lax.broadcasted_iota(jnp.int32, shape, 1)
-            bias[rows, first:] = jnp.where(same & (key <= query), 0.0, MASKED)
-
-    for qb in range(blocks):
-        rows = slice(qb * BLOCK, (qb + 1) * BLOCK)
-        q = q_ref[rows, :].astype(F32)
-        q = (q * tab_ref[0, rows, :] + swap_halves(q) * tab_ref[1, rows, :]) * (HEAD**-0.5)
-        q0, q1 = head_masks(q)
-        qs[0, rows, :] = q0.astype(BF16)
-        qs[1, rows, :] = q1.astype(BF16)
-        k = k_ref[rows, :].astype(F32)
-        k = k * tab_ref[2, rows, :] + swap_halves(k) * tab_ref[3, rows, :]
-        ks[rows, :] = k.astype(BF16)
-        k0, k1 = head_masks(k)
-        kms[0, rows, :] = k0.astype(BF16)
-        kms[1, rows, :] = k1.astype(BF16)
-        grad = do_ref[rows, :].astype(F32)
-        d0, d1 = head_masks(grad)
-        dos[0, rows, :] = d0.astype(BF16)
-        dos[1, rows, :] = d1.astype(BF16)
-        prod = jnp.transpose(grad * o_ref[rows, :].astype(F32))
-        delta[0:1, rows] = jnp.sum(prod[:HEAD], axis=0, keepdims=True)
-        delta[1:2, rows] = jnp.sum(prod[HEAD:], axis=0, keepdims=True)
-    dq[...] = jnp.zeros_like(dq)
-    dk[...] = jnp.zeros_like(dk)
-    dv[...] = jnp.zeros_like(dv)
-    for qb in range(blocks):
-        cols = slice(qb * BLOCK, (qb + 1) * BLOCK)
-        for kb in range(qb + 1):
-            rows = slice(kb * BLOCK, (kb + 1) * BLOCK)
-            for h in range(2):
-                scores = dot(ks[rows, :], qs[h, cols, :], 1, 1) + bias[rows, cols]
-                probs = jnp.exp(scores - lse_ref[0, h : h + 1, cols])
-                grads = dot(v_ref[rows, :], dos[h, cols, :], 1, 1)
-                dscores = (probs * (grads - delta[h : h + 1, cols])).astype(BF16)
-                dv[rows, :] += dot(probs.astype(BF16), dos[h, cols, :], 1, 0)
-                dk[rows, :] += dot(dscores, qs[h, cols, :], 1, 0)
-                dq[cols, :] += dot(dscores, kms[h, rows, :], 0, 0)
-    for qb in range(blocks):
-        rows = slice(qb * BLOCK, (qb + 1) * BLOCK)
-        grad = dq[rows, :] * (HEAD**-0.5)
-        dq_ref[rows, :] = (
-            grad * tab_ref[0, rows, :] - swap_halves(grad) * tab_ref[1, rows, :]
-        ).astype(BF16)
-        grad = dk[rows, :]
-        dk_ref[rows, :] = (
-            grad * tab_ref[2, rows, :] - swap_halves(grad) * tab_ref[3, rows, :]
-        ).astype(BF16)
-        dv_ref[rows, :] = dv[rows, :].astype(BF16)
-
-
-def attend_back(q, k, v, do, o, lse, tables, seg_col, seg_row):
-    length, width = q.shape
-    pairs = width // LANES
-    lane_block = pl.BlockSpec((length, LANES), lambda p: (0, p))
+    mine, row = lax.rem(me, groups), me // groups
+    seq_signal(count)
+
+    def there(p, k):
+        device = lax.rem(me + k, count)
+        return send(
+            do_ref.at[spans(device // groups, span), spans(lax.rem(device, groups) * pairs + p, LANES)],
+            do_row.at[p, spans(me, span), :],
+            send_sem.at[p, k],
+            recv_sem.at[p, k],
+            device,
+        )
+
+    def back(p, k):
+        device = lax.rem(me + k, count)
+        return send(
+            made.at[p, :, spans(device, span), :],
+            grads_ref.at[:, spans(row, span), spans(mine * pairs + p, LANES)],
+            back_send_sem.at[p, k],
+            back_recv_sem.at[p, k],
+            device,
+        )
+
+    seq_wait(count)
+
+    def share_out(p, carry):
+        for k in range(1, count):
+            there(p, k).start()
+        do_row[p, spans(me, span), :] = do_ref[spans(row, span), spans(mine * pairs + p, LANES)]
+        return carry
+
+    lax.fori_loop(0, pairs, share_out, 0)
+    for kb in range(blocks):
+        rows = block_rows(kb)
+        start = kb * BLOCK
+        shape = (BLOCK, length - start)
+        same = segc_ref[rows, :] == segr_ref[:, start:]
+        key = lax.broadcasted_iota(jnp.int32, shape, 0)
+        query = lax.broadcasted_iota(jnp.int32, shape, 1)
+        bias[rows, start:] = jnp.where(same & (key <= query), 0.0, MASKED)
+
+    def attend(p, carry):
+        for qb in range(blocks):
+            rows = block_rows(qb)
+            q = rotated(qkv_ref[p, rows, :LANES], tab_ref, 0, rows) * (HEAD**-0.5)
+            q0, q1 = head_masks(q)
+            qs[0, rows, :] = q0.astype(BF16)
+            qs[1, rows, :] = q1.astype(BF16)
+            k = rotated(qkv_ref[p, rows, LANES : 2 * LANES], tab_ref, 2, rows)
+            ks[rows, :] = k.astype(BF16)
+            k0, k1 = head_masks(k)
+            kms[0, rows, :] = k0.astype(BF16)
+            kms[1, rows, :] = k1.astype(BF16)
+        dq[...] = jnp.zeros_like(dq)
+        dk[...] = jnp.zeros_like(dk)
+        dv[...] = jnp.zeros_like(dv)
+        for k in range(1, count):
+            there(p, k).wait_recv()
+        for qb in range(blocks):
+            rows = block_rows(qb)
+            grad = do_row[p, rows, :].astype(F32)
+            d0, d1 = head_masks(grad)
+            dos[0, rows, :] = d0.astype(BF16)
+            dos[1, rows, :] = d1.astype(BF16)
+            prod = jnp.transpose(grad * o_ref[p, rows, :].astype(F32))
+            delta[0:1, rows] = jnp.sum(prod[:HEAD], axis=0, keepdims=True)
+            delta[1:2, rows] = jnp.sum(prod[HEAD:], axis=0, keepdims=True)
+        for qb in range(blocks):
+            cols = block_rows(qb)
+            for kb in range(qb + 1):
+                rows = block_rows(kb)
+                value = qkv_ref[p, rows, 2 * LANES :]
+                for h in range(2):
+                    scores = dot(ks[rows, :], qs[h, cols, :], 1, 1) + bias[rows, cols]
+                    probs = jnp.exp(scores - lse_ref[p, h : h + 1, cols])
+                    grads = dot(value, dos[h, cols, :], 1, 1)
+                    dscores = (probs * (grads - delta[h : h + 1, cols])).astype(BF16)
+                    dv[rows, :] += dot(probs.astype(BF16), dos[h, cols, :], 1, 0)
+                    dk[rows, :] += dot(dscores, qs[h, cols, :], 1, 0)
+                    dq[cols, :] += dot(dscores, kms[h, rows, :], 0, 0)
+        for qb in range(blocks):
+            rows = block_rows(qb)
+            grad = dq[rows, :] * (HEAD**-0.5)
+            made[p, 0, rows, :] = rotated_back(grad, tab_ref, 0, rows).astype(BF16)
+            made[p, 1, rows, :] = rotated_back(dk[rows, :], tab_ref, 2, rows).astype(BF16)
+            made[p, 2, rows, :] = dv[rows, :].astype(BF16)
+        for k in range(1, count):
+            back(p, k).start()
+        for i in range(3):
+            grads_ref[i, spans(row, span), spans(mine * pairs + p, LANES)] = made[
+                p, i, spans(me, span), :
+            ]
+        return carry
+
+    lax.fori_loop(0, pairs, attend, 0)
+
+    def drain(p, carry):
+        for k in range(1, count):
+            there(p, k).wait_send()
+            back(p, k).wait()
+        return carry
+
+    lax.fori_loop(0, pairs, drain, 0)
+
+
+def attend_back(do, qkv, o, lse, tables, seg_col, seg_row, count, groups, collective_id):
+    tokens, head_width = do.shape
+    pairs, length = qkv.shape[:2]
+    whole = pl.BlockSpec(memory_space=pltpu.VMEM)
     return pl.pallas_call(
-        functools.partial(attend_back_kernel, length),
-        grid=(pairs,),
-        out_shape=[jax.ShapeDtypeStruct((length, width), BF16)] * 3,
-        in_specs=[lane_block] * 5
-        + [
-            pl.BlockSpec((1, 8, length), lambda p: (p, 0, 0)),
-            pl.BlockSpec((4, length, LANES), lambda p: (0, 0, 0)),
-            pl.BlockSpec((length, 1), lambda p: (0, 0)),
-            pl.BlockSpec((1, length), lambda p: (0, 0)),
-        ],
-        out_specs=[lane_block] * 3,
+        functools.partial(back_kernel, count, groups),
+        out_shape=jax.ShapeDtypeStruct((3, tokens, head_width), BF16),
+        in_specs=[whole] * 7,
+        out_specs=whole,
         scratch_shapes=[
+            pltpu.VMEM((pairs, length, LANES), BF16),
+            pltpu.VMEM((pairs, 3, length, LANES), BF16),
             pltpu.VMEM((length, length), F32),
             pltpu.VMEM((2, length, LANES), BF16),
             pltpu.VMEM((length, LANES), BF16),
@@ -314,17 +392,13 @@
             pltpu.VMEM((length, LANES), F32),
             pltpu.VMEM((length, LANES), F32),
             pltpu.VMEM((length, LANES), F32),
-        ],
-        compiler_params=pltpu.CompilerParams(vmem_limit_bytes=VMEM_LIMIT),
-        cost_estimate=cost(30),
-    )(q, k, v, do, o, lse, tables, seg_col, seg_row)
-
-
-def norm_parts(values):
-    center = jnp.mean(values, axis=-1, keepdims=True)
-    shifted = values - center
-    inverse = lax.rsqrt(jnp.mean(shifted * shifted, axis=-1, keepdims=True) + EPSILON)
-    return shifted * inverse, inverse
+        ]
+        + [pltpu.SemaphoreType.DMA((pairs, count))] * 4,
+        compiler_params=pltpu.CompilerParams(
+            collective_id=collective_id, has_side_effects=True, vmem_limit_bytes=VMEM_LIMIT
+        ),
+        cost_estimate=cost(60),
+    )(do, qkv, o, lse, tables, seg_col, seg_row)
 
 
 def fold(values):
@@ -817,7 +891,6 @@
     head_width = w_query.shape[1]
     hidden_width = w_up.shape[1] * tp_count
     groups = seq_count // row_count
-    width = head_width // groups
 
     first_gain_f = first_gain.astype(F32)[None]
     first_bias_f = first_bias.astype(F32)[None]
@@ -836,18 +909,21 @@
     block = block_in.reshape(tokens, model_width)
     cotangent = out_cotangent.reshape(tokens, model_width)
 
-    normed_one, _ = norm_parts(block.astype(F32))
-    first_act = (normed_one * first_gain_f + first_bias_f).astype(BF16)
-    shape3 = (row_count, span, head_width)
-    query = matmul(first_act, w_query, 1, 0, BF16).reshape(shape3)
-    key = matmul(first_act, w_key, 1, 0, BF16).reshape(shape3)
-    value = matmul(first_act, w_value, 1, 0, BF16).reshape(shape3)
-    q_row, k_row, v_row = exchange(
-        rows_out_kernel, seq_count, groups, (query, key, value), (length, width), 1
-    )
-    o_row, lse = attend(q_row, k_row, v_row, tables, seg_col, seg_row)
-    (mixed,) = exchange(rows_back_kernel, seq_count, groups, (o_row,), shape3, 2)
-    mixed = mixed.reshape(tokens, head_width).astype(F32)
+    first_act, qkv_row, o_row, lse, mixed = front(
+        block,
+        w_query,
+        w_key,
+        w_value,
+        first_gain_f,
+        first_bias_f,
+        tables,
+        seg_col,
+        seg_row,
+        seq_count,
+        groups,
+        1,
+    )
+    mixed = mixed.astype(F32)
     head_sums = tp_sum(
         jnp.stack([jnp.sum(mixed, axis=-1), jnp.sum(mixed * mixed, axis=-1)]), tp_count, 9
     )
@@ -946,17 +1022,10 @@
     )
     head_back = head_back[:, :, None] / model_width
     grad_mixed = head_inverse * (head_scaled - head_back[0] - head_normed * head_back[1])
-    (do_row,) = exchange(
-        rows_out_kernel,
-        seq_count,
-        groups,
-        (grad_mixed.astype(BF16).reshape(shape3),),
-        (length, width),
-        6,
-    )
-    grads_row = attend_back(q_row, k_row, v_row, do_row, o_row, lse, tables, seg_col, seg_row)
-    grads = exchange(rows_back_kernel, seq_count, groups, grads_row, shape3, 7)
-    grad_query, grad_key, grad_value = (g.reshape(tokens, head_width) for g in grads)
+    grads = attend_back(
+        grad_mixed.astype(BF16), qkv_row, o_row, lse, tables, seg_col, seg_row, seq_count, groups, 6
+    )
+    grad_query, grad_key, grad_value = grads[0], grads[1], grads[2]
     head_terms = (
         jnp.concatenate(
             [
@@ -968,8 +1037,8 @@
             axis=1,
         )
     )
-    grad_query, head_terms, w_down_grad, block_out = lax.optimization_barrier(
-        (grad_query, head_terms, w_down_grad, block_out)
+    grad_query, head_terms, w_down_grad = lax.optimization_barrier(
+        (grad_query, head_terms, w_down_grad)
     )
     head_grads = scatter(head_terms)
     w_query_grad, w_key_grad, w_value_grad, w_out_grad = jnp.split(

time: 755 us -> 733 us (0.971)
  Pallas kernels: 575 us -> 540 us
  waiting for transfers between devices: 15.2 us -> 39.9 us
  matrix products: 69.4 us -> 53.5 us
    pallas_call x6 -> x2, Pallas kernels: 174 us -> 140 us  [the longest x1 77.4 us: attend_back(): pl.pallas_call(functools.partial(back_kernel, count, groups), out_shape=j...]
    psum x1, waiting for transfers between devices: 14.2 us -> 38.9 us  [body(): block_out = lax.psum(down_part, 'tp')]
    dot_general x9 -> x6, matrix products: 69.4 us -> 53.5 us  [dot(): lax.dot_general(left, right, (((left_dim,), (right_dim,)), ((), ())), pre...]
  transfers between devices with their start and end apart: 4 -> 4, of which waited for: 1 -> 1; matrix products, arithmetic and copies ran while one was open for 5% -> 6% of each run, Pallas kernels for 32% -> 30%
where the time goes in v4:
time: 733 us; the launch traced here: 724 us
  Pallas kernels  540 us (74%)
  matrix products  53.5 us (7%)
  other arithmetic  51 us (7%)
  waiting for transfers between devices  39.9 us (5%)
  local copies, waits for them, and re-layouts  22.4 us (3%)
  between operations  16.5 us (2%)
    pallas_call x3, Pallas kernels, line_sum(): pl.pallas_call(functools.partial(line_kernel, plan, count, CHUNKS, SLACK)...  367 us
    pallas_call x1, Pallas kernels, attend_back(): pl.pallas_call(functools.partial(back_kernel, count, groups), out_shape=j...  77.4 us
    pallas_call x1, Pallas kernels, front(): pl.pallas_call(functools.partial(front_kernel, count, groups), out_shape=...  62.4 us
    dot_general x6, matrix products, dot(): lax.dot_general(left, right, (((left_dim,), (right_dim,)), ((), ())), pre...  53.5 us
    psum x1, waiting for transfers between devices, body(): block_out = lax.psum(down_part, 'tp')  38.9 us
    pallas_call x3, Pallas kernels, tp_sum(): pl.pallas_call(functools.partial(tp_sum_kernel, count), out_shape=jax.Sha...  21.8 us
    reduce_sum x1, other arithmetic, body(): hidden_gain_grad = jnp.sum(grad_hidden_act * hidden_normed, axis=0)  15.9 us
  transfers between devices with their start and end apart: 4, of which 1 were waited for; matrix products, arithmetic and copies ran while one was open for 6% of the time, Pallas kernels for 30%

profile of v4, /device:TPU:0, one launch (start us, length us, event | category | flops | bytes accessed | tf_op | source)
XLA Modules:
  0.0 723.6 jit_solution(12165580094715131472)
XLA Ops:
  19.5 2.0 exponential_bitcast_fusion.1
  25.6 62.4 %shard_map.288 = (bf16[1024,2048]{1,0:T(8,128)(2,1)}, bf16[4,1024,384]{2,1,0:T(8,128)(2,1)}, bf16[4,1024,128]{2,1,0:T(8,128)(2,1)}, f32[4,8,1024]{2,1,0:T(8,128)}, bf16[1024,512]{1,0:T(8,128)(2,1)}) custom-call(bf16[1024,2048]{1,0:T(8,128)(2,1)} %bitcast.109, bf16[2048,512]{1,0:T(8,128)(2,1)} %refs_1_.5, bf16[2048,512]{1,0:T(8,128)(2,1)} %refs_3_.1, ...), custom_call_target="tpu_custom_call" | custom-call | flops 65999998976 | tf_op jit(solution)/shard_map/pallas_call | solution.py:233
  90.2 7.4 %shard_map.289 = f32[2,1024]{1,0:T(2,128)} custom-call(f32[2,1024]{1,0:T(2,128)} %pad_maximum_fusion.8.x_ref), custom_call_target="tpu_custom_call" | custom-call | flops 5500000256 | tf_op jit(solution)/shard_map/pallas_call | solution.py:782
  99.8 117.8 %shard_map.290 = (bf16[1024,2048]{1,0:T(8,128)(2,1)}, f32[512,2048]{1,0:T(8,128)}, bf16[1024,2048]{1,0:T(8,128)(2,1)}) custom-call(bf16[1024,512]{1,0:T(8,128)(2,1)} %fusion.28.refs_0_, bf16[2048,512]{1,0:T(8,128)(2,1)} %refs_1_.3, bf16[1024,2048]{1,0:T(8,128)(2,1)} %bitcast.110, bf16[1024,2048]{1,0:T(8,128)(2,1)} %bitcast.107, bf16[2048,2048]{1,0:T(8,128)(2,1)} %refs_5_.2, ...), custom_call_target="tpu_custom_call" | custom-call | flops 121000001536 | tf_op jit(solution)/shard_map/pallas_call | solution.py:711
  217.6 35.1 %fusion.42 = (f32[1024]{0:T(1024)S(1)}, f32[1024]{0:T(1024)S(1)}, f32[1024]{0:T(1024)S(1)}, f32[1024]{0:T(1024)S(1)}, f32[2048]{0:T(1024)}, /*index=5*/f32[1024,...) fusion(f32[2048]{0:T(1024)S(1)} %copy-done.15, bf16[1024,2048]{1,0:T(8,128)(2,1)} %get-tuple-element.39, ...), kind=kOutput, calls=%fused_computation.104 | convolution fusion | flops 8740923392 | bytes 41975808 | tf_op jit(solution)/shard_map/dot_general | solution.py:32
  253.4 7.0 shard_map.291
  261.1 15.9 %fusion.10 = (f32[2048]{0:T(1024)S(1)}, bf16[1024,2048]{1,0:T(8,128)(2,1)}, bf16[1024,2048]{1,0:T(8,128)(2,1)}) fusion(bf16[1024,2048]{1,0:T(8,128)(2,1)} %get-tuple-element.39, f32[1024,2048]{1,0:T(8,128)} %get-tuple-element.117, f32[1024]{0:T(1024)S(1)} %bitcast.86, f32[1024]{0:T(1024)S(1)} %get-tuple-element.143, f32[1024,2048]{1,0:T(8,128)} %get-tuple-element.118, ...), kind=kLoop, calls=%fused_computation.15 | loop fusion | flops 41940992 | bytes 37789696 | tf_op jit(solution)/shard_map/reduce_sum | solution.py:974
  277.0 128.1 %shard_map.292 = (bf16[1024,2048]{1,0:T(8,128)(2,1)}, f32[2,8,2048]{2,1,0:T(8,128)}, f32[512,2048]{1,0:T(8,128)}, bf16[1024,2048]{1,0:T(8,128)(2,1)}, bf16[2048,...) custom-call(bf16[1024,2048]{1,0:T(8,128)(2,1)} %get-tuple-element.120.refs_0_, bf16[2048,2048]{1,0:T(8,128)(2,1)} %refs_1_.4, ...), custom_call_target="tpu_custom_call" | custom-call | flops 121000001536 | tf_op jit(solution)/shard_map/pallas_call | solution.py:711
  407.0 5.6 fusion.33
  413.9 7.5 %shard_map.293 = f32[2,1024]{1,0:T(2,128)} custom-call(f32[2,1024]{1,0:T(2,128)} %pad_maximum_fusion.9.x_ref), custom_call_target="tpu_custom_call" | custom-call | flops 5500000256 | tf_op jit(solution)/shard_map/pallas_call | solution.py:782
  422.1 1.7 fusion.32.do_ref
  423.8 77.4 %shard_map.294 = bf16[3,1024,512]{2,1,0:T(8,128)(2,1)} custom-call(bf16[1024,512]{1,0:T(8,128)(2,1)} %fusion.32.do_ref, bf16[4,1024,384]{2,1,0:T(8,128)(2,1)} %get-tuple-element.43.qkv_ref, bf16[4,1024,128]{2,1,0:T(8,128)(2,1)} %get-tuple-element.44.o_ref, f32[4,8,1024]{2,1,0:T(8,128)} %get-tuple-element.45.lse_ref, ...), custom_call_target="tpu_custom_call" | custom-call | flops 65999998976 | tf_op jit(solution)/shard_map/pallas_call | solution.py:378
  501.2 3.6 slice_bitcast_fusion
  504.8 5.4 convolution_convert_fusion
  510.3 2.4 convolution_convert_fusion.3
  512.7 2.4 convolution_convert_fusion.1
  515.2 2.4 convolution_convert_fusion.2
  517.6 4.1 pad_maximum_fusion
  521.7 38.9 %all-reduce.2.cloned.1.call-done = bf16[8,128,2048]{2,1,0:T(8,128)(2,1)} async-done(((bf16[8,128,2048]{2,1,0:T(8,128)(2,1)}), bf16[8,128,2048]{2,1,0:T(8,128)(2,1)}) %all-reduce.2.cloned.1.call-update) | async-done | bytes 4194320 | tf_op jit(solution)/shard_map/psum | solution.py:1006
  560.6 121.1 %shard_map.295 = (bf16[1024,2048]{1,0:T(8,128)(2,1)}, f32[2,8,2048]{2,1,0:T(8,128)}) custom-call(bf16[1024,512]{1,0:T(8,128)(2,1)} %get-tuple-element.48.refs_0_, bf16[2048,512]{1,0:T(8,128)(2,1)} %refs_1_.5, bf16[1024,512]{1,0:T(8,128)(2,1)} %get-tuple-element.123.refs_2_, bf16[2048,512]{1,0:T(8,128)(2,1)} %refs_3_.1, ...), custom_call_target="tpu_custom_call" | custom-call | flops 121000001536 | tf_op jit(solution)/shard_map/pallas_call | solution.py:711
  684.9 2.8 convert_element_type.82
  687.7 11.4 %shard_map.296 = (f32[8,128]{1,0:T(8,128)}, f32[40,128]{1,0:T(8,128)}) custom-call(f32[8,8,128]{2,1,0:T(8,128)} %reshape.1114.full_ref, f32[40,128]{1,0:T(8,128)} %maximum_bitcast_fusion.split_ref), custom_call_target="tpu_custom_call" | custom-call | flops 11000000512 | tf_op jit(solution)/shard_map/pallas_call | solution.py:823
  708.6 4.9 copy.52
  713.6 2.0 copy.53
  (96 shorter events, 37.6 us)
Async XLA Ops:
  8.0 552.5 %all-reduce.2.cloned.1.call-start = ((), (), s32[]{:S(2)}) async-start(), calls=%async_computation.3 | async-start | bytes 8388608 | tf_op jit(solution)/shard_map/psum | solution.py:1006
  8.8 16.8 %copy-start.12 = (s32[1,1024]{1,0:T(1,128)}, s32[1,1024]{1,0:T(1,128)S(1)}, u32[]{:S(2)}) copy-start(s32[1,1024]{1,0:T(1,128)S(1)} %constant_dynamic-slice_fusion.segr_ref) | copy-start | bytes 12292
  9.5 88.8 %copy-start.17 = (f32[512]{0:T(512)}, f32[512]{0:T(512)S(1)}, u32[]{:S(2)}) copy-start(f32[512]{0:T(512)S(1)} %convert_element_type.68) | copy-start | bytes 6148
  90.2 8.2 %copy-start.2 = (bf16[1024,512]{1,0:T(8,128)(2,1)S(1)}, bf16[1024,512]{1,0:T(8,128)(2,1)}, u32[]{:S(2)}) copy-start(bf16[1024,512]{1,0:T(8,128)(2,1)} %get-tuple-element.37) | copy-start | bytes 3145732
  98.3 119.3 %copy-start.10 = (f32[1,1024]{1,0:T(1,128)}, f32[1,1024]{1,0:T(1,128)S(1)}, u32[]{:S(2)}) copy-start(f32[1,1024]{1,0:T(1,128)S(1)} %get-tuple-element.145) | copy-start | bytes 12292
  98.4 119.3 %copy-start.13 = (f32[1024]{0:T(1024)}, f32[1024]{0:T(1024)S(1)}, u32[]{:S(2)}) copy-start(f32[1024]{0:T(1024)S(1)} %add_rsqrt_fusion.1) | copy-start | bytes 12292
  99.8 117.8 %copy-start.15 = (f32[2048]{0:T(1024)S(1)}, f32[2048]{0:T(1024)}, u32[]{:S(2)}) copy-start(f32[2048]{0:T(1024)} %convert_element_type.72) | copy-start | bytes 24580
  253.4 7.7 %copy-start.16 = (f32[2048]{0:T(1024)S(1)}, f32[2048]{0:T(1024)}, u32[]{:S(2)}) copy-start(f32[2048]{0:T(1024)} %convert_element_type.74) | copy-start | bytes 24580
  405.1 155.4 %reduce-scatter.4.cloned.1.call-start = ((), (), s32[]{:S(2)}) async-start(), calls=%async_computation.4 | async-start | bytes 9437184 | tf_op jit(solution)/shard_map/reduce_scatter | solution.py:1009
  405.2 1.2 copy-start.8
  405.2 1.8 copy-start.3
  405.2 1.8 copy-start.11
  405.2 1.8 copy-start.14
  405.2 1.8 copy-start.18
  405.7 279.2 %reduce-scatter.8.cloned.1.call-start = ((), (), s32[]{:S(2)}) async-start(), calls=%async_computation.6 | async-start | bytes 9437184 | tf_op jit(solution)/shard_map/reduce_scatter | solution.py:1009
  406.3 297.0 %reduce-scatter.6.cloned.1.call-start = ((), (), s32[]{:S(2)}) async-start(), calls=%async_computation.5 | async-start | bytes 9437184 | tf_op jit(solution)/shard_map/reduce_scatter | solution.py:1009
  407.0 6.3 copy-start.19
  423.8 81.0 %copy-start.7 = (bf16[1024,512]{1,0:T(8,128)(2,1)S(1)}, bf16[1024,512]{1,0:T(8,128)(2,1)}, u32[]{:S(2)}) copy-start(bf16[1024,512]{1,0:T(8,128)(2,1)} %fusion.28.refs_0_) | copy-start | bytes 3145732
  504.8 5.5 copy-start.5
  504.8 5.5 copy-start.20
  560.6 122.1 %copy-start.9 = (f32[2,2048]{1,0:T(2,128)S(1)}, f32[2,2048]{1,0:T(2,128)}, u32[]{:S(2)}) copy-start(f32[2,2048]{1,0:T(2,128)} %reduce_sum.144) | copy-start | bytes 49156
  560.6 122.8 %copy-start.6 = (bf16[256,2048]{1,0:T(8,128)(2,1)S(1)}, bf16[256,2048]{1,0:T(8,128)(2,1)}, u32[]{:S(2)}) copy-start(bf16[256,2048]{1,0:T(8,128)(2,1)} %reduce-scatter.4.cloned.1.call-done) | copy-start | bytes 3145732
  708.6 4.9 copy-start.4
  708.6 7.0 copy-start.1
  (1 other events, 0.8 us)
Sparse Core Ops, SparseCore 0:
  405.3 155.2 all-reduce.1
Sparse Core Ops, SparseCore 1:
  409.5 111.5 reduce-scatter.3
  524.3 71.1 reduce-scatter.7
  599.2 71.1 reduce-scatter.5

commit v5 on v4

--- a/solution.py
+++ b/solution.py
@@ -98,7 +98,7 @@
 
 
 def front_kernel(
-    count, groups, x_ref, wq_ref, wk_ref, wv_ref, gain_ref, bias_ref, tab_ref, segc_ref, segr_ref,
+    count, groups, x_ref, wq_ref, wk_ref, wv_ref, gains_ref, tab_ref, segc_ref, segr_ref,
     act_ref, qkv_ref, o_ref, lse_ref, mixed_ref,
     weights, staged, bias, qs, ks, load_sem, send_sem, recv_sem, back_send_sem, back_recv_sem,
 ):
@@ -123,7 +123,7 @@
     def norm_step(r, carry):
         rows = pl.ds(pl.multiple_of(r * LANES, LANES), LANES)
         normed, _ = norm_parts(x_ref[rows, :].astype(F32))
-        act_ref[rows, :] = (normed * gain_ref[...] + bias_ref[...]).astype(BF16)
+        act_ref[rows, :] = (normed * gains_ref[0:1] + gains_ref[1:2]).astype(BF16)
         return carry
 
     lax.fori_loop(0, tokens // LANES, norm_step, 0)
@@ -223,7 +223,7 @@
     lax.fori_loop(0, pairs, drain, 0)
 
 
-def front(x, w_query, w_key, w_value, gain, bias, tables, seg_col, seg_row, count, groups, collective_id):
+def front(x, w_query, w_key, w_value, gains, tables, seg_col, seg_row, count, groups, collective_id):
     tokens, model_width = x.shape
     head_width = w_query.shape[1]
     length = seg_col.shape[0]
@@ -239,7 +239,7 @@
             jax.ShapeDtypeStruct((pairs, 8, length), F32),
             jax.ShapeDtypeStruct((tokens, head_width), BF16),
         ],
-        in_specs=[whole] + [any_space] * 3 + [whole] * 5,
+        in_specs=[whole] + [any_space] * 3 + [whole] * 4,
         out_specs=[whole] * 5,
         scratch_shapes=[
             pltpu.VMEM((pairs * groups, model_width, 3 * LANES), BF16),
@@ -254,7 +254,7 @@
             collective_id=collective_id, has_side_effects=True, vmem_limit_bytes=VMEM_LIMIT
         ),
         cost_estimate=cost(60),
-    )(x, w_query, w_key, w_value, gain, bias, tables, seg_col, seg_row)
+    )(x, w_query, w_key, w_value, gains, tables, seg_col, seg_row)
 
 
 def back_kernel(
@@ -406,16 +406,16 @@
     return jnp.sum(values.reshape(rows // 8, 8, width), axis=0)
 
 
-def finish_middle(total, here, own, held, vecs, outs):
-    middle = held["block"][here, :].astype(F32) + total
-    outs[0][own, :] = middle
+def finish_middle(total, here, own, env):
+    middle = env["block"][here, :].astype(F32) + total
+    env["middle"][own, :] = middle
     normed, _ = norm_parts(middle)
-    return normed * vecs[0][...] + vecs[1][...]
-
-
-def norm_back(base, values, total, vecs, sums):
+    return normed * env["gains"][2:3] + env["gains"][3:4]
+
+
+def norm_back(base, values, total, gain, sums):
     normed, inverse = norm_parts(values)
-    scaled = total * vecs[0][...]
+    scaled = total * gain
     grad = base + inverse * (
         scaled
         - jnp.mean(scaled, axis=-1, keepdims=True)
@@ -426,38 +426,133 @@
     return grad
 
 
-def finish_second(total, here, own, held, vecs, outs):
-    base = held["cotangent"][here, :].astype(F32)
-    grad = norm_back(base, held["middle"][own, :], total, vecs, outs[0])
-    outs[1][own, :] = grad
+def finish_second(total, here, own, env):
+    base = env["cotangent"][here, :].astype(F32)
+    grad = norm_back(base, env["middle"][own, :], total, env["gains"][2:3], env["sums"])
+    env["middle_grad"][own, :] = grad
     return grad
 
 
-def finish_first(total, here, own, held, vecs, outs):
-    values = held["block"][here, :].astype(F32)
-    return norm_back(held["middle_grad"][own, :], values, total, vecs, outs[0])
+def finish_first(total, here, own, env):
+    values = env["block"][here, :].astype(F32)
+    return norm_back(env["middle_grad"][own, :], values, total, env["gains"][0:1], env["sums"])
+
+
+def to_row(columns):
+    lane = lax.broadcasted_iota(jnp.int32, (LANES, LANES), 1)
+    packed = jnp.zeros((LANES, LANES), F32)
+    for i, column in enumerate(columns):
+        packed = jnp.where(lane == i, column, packed)
+    return jnp.transpose(packed)[:8]
+
+
+def to_columns(rows, number):
+    packed = jnp.transpose(jnp.concatenate([rows] * (LANES // 8), axis=0))
+    return [packed[:, i : i + 1] for i in range(number)]
+
+
+def row_block(r):
+    return pl.ds(pl.multiple_of(r * LANES, LANES), LANES)
+
+
+def tp_total(part, landed, send_sem, recv_sem, count):
+    copies = share("tp", count, lambda d: part, landed, send_sem, recv_sem)
+    landed[lax.axis_index("tp")] = part[...]
+    for copy in copies:
+        copy.wait()
+    part[...] = total_of(landed, count)
+
+
+def norm_heads(env, count, features):
+    mixed, act, part = env["mixed"], env["head_act"], env["head_sums"]
+    blocks = mixed.shape[0] // LANES
+
+    def sums(r, carry):
+        values = mixed[row_block(r), :].astype(F32)
+        part[:, row_block(r)] = to_row(
+            [
+                jnp.sum(values, axis=-1, keepdims=True),
+                jnp.sum(values * values, axis=-1, keepdims=True),
+            ]
+        )
+        return carry
+
+    lax.fori_loop(0, blocks, sums, 0)
+    tp_total(part, env["head_landed"], env["head_send"], env["head_recv"], count)
+
+    def apply(r, carry):
+        first, second = to_columns(part[:, row_block(r)], 2)
+        center = first / features
+        inverse = lax.rsqrt(second / features - center * center + EPSILON)
+        values = (mixed[row_block(r), :].astype(F32) - center) * inverse
+        act[row_block(r), :] = (values * env["head_vecs"][0:1] + env["head_vecs"][1:2]).astype(BF16)
+        return carry
+
+    lax.fori_loop(0, blocks, apply, 0)
+
+
+def normal_parts(values):
+    size = jnp.abs(values) * (0.5**0.5)
+    bell = jnp.exp(-0.5 * values * values)
+    t = 1.0 / (1.0 + 0.3275911 * size)
+    poly = 1.061405429
+    for factor in (-1.453152027, 1.421413741, -0.284496736, 0.254829592):
+        poly = poly * t + factor
+    tail = 0.5 * poly * t * bell
+    return jnp.where(values < 0.0, tail, 1.0 - tail), bell * (1.0 / math.sqrt(2.0 * math.pi))
+
+
+def hidden_rows(env, rows, row):
+    width = env["w_up"].shape[1]
+    sums = [jnp.zeros((LANES, 1), F32)] * 4
+    for n in range(width // TILE):
+        cols = slice(n * TILE, (n + 1) * TILE)
+        values = dot(env["out"][rows, :], env["w_up"][:, cols], 1, 0)
+        below, density = normal_parts(values)
+        active = values * below
+        env["hidden_act"][rows, cols] = active.astype(BF16)
+        env["grad_up"][rows, cols] = (below + values * density).astype(BF16)
+        scaled = env["hidden_grad"][rows, cols].astype(F32) * env["hidden_vecs"][0:1, cols]
+        for i, term in enumerate((active, active * active, scaled, scaled * active)):
+            sums[i] = sums[i] + jnp.sum(term, axis=-1, keepdims=True)
+    env["hidden_sums"][:, row] = to_row(sums)
+
+
+def norm_hidden(env, count, features):
+    act, slope, part = env["hidden_act"], env["grad_up"], env["hidden_sums"]
+    tokens, width = act.shape
+    tp_total(part, env["hidden_landed"], env["hidden_send"], env["hidden_recv"], count)
+    env["hidden_vec_grads"][...] = jnp.zeros_like(env["hidden_vec_grads"])
+
+    def apply(r, carry):
+        rows = row_block(r)
+        sums = [column / features for column in to_columns(part[:, rows], 4)]
+        center = sums[0]
+        inverse = lax.rsqrt(sums[1] - center * center + EPSILON)
+        cross = inverse * (sums[3] - center * sums[2])
+        for n in range(width // TILE):
+            cols = slice(n * TILE, (n + 1) * TILE)
+            gain = env["hidden_vecs"][0:1, cols]
+            normed = (act[rows, cols].astype(F32) - center) * inverse
+            grad = env["hidden_grad"][rows, cols].astype(F32)
+            back = inverse * (grad * gain - sums[2] - normed * cross)
+            slope[rows, cols] = (back * slope[rows, cols].astype(F32)).astype(BF16)
+            act[rows, cols] = (normed * gain + env["hidden_vecs"][1:2, cols]).astype(BF16)
+            env["hidden_vec_grads"][0, :, cols] += fold(grad * normed)
+            env["hidden_vec_grads"][1, :, cols] += fold(grad)
+        return carry
+
+    lax.fori_loop(0, tokens // LANES, apply, 0)
 
 
 def line_kernel(plan, count, chunks, slack, *refs):
-    finish, clear = plan["finish"], plan["clear"]
-    names, parts, tasks = plan["names"], plan["parts"], plan["tasks"]
-    num_vec, num_own, num_task = plan["vecs"], plan["owns"], len(tasks)
-    refs = list(refs)
-
-    def take(number):
-        taken = refs[:number]
-        del refs[:number]
-        return taken
-
-    sources = take(len(names))
-    vecs = take(num_vec)
-    (out_ref,) = take(1)
-    outs = take(num_own)
-    task_outs = take(num_task)
-    held = dict(zip(names, take(len(names))))
-    in_a, in_b, part, turned, stage = take(5)
-    load_sem, stage_sem = take(2)
-    (rsa_s, rsa_r, rsb_s, rsb_r, aga_s, aga_r, agb_s, agb_r) = refs
+    env = dict(zip(plan["order"], refs, strict=True))
+    finish, parts, tasks = plan["finish"], plan["parts"], plan["tasks"]
+    num_task = len(tasks)
+    out_ref, part = env["out"], env["part"]
+    in_a, in_b = env["in_a"], env["in_b"]
+    rsa_s, rsa_r, rsb_s, rsb_r = (env[name] for name in ("rsa_s", "rsa_r", "rsb_s", "rsb_r"))
+    aga_s, aga_r, agb_s, agb_r = (env[name] for name in ("aga_s", "aga_r", "agb_s", "agb_r"))
     z = lax.axis_index("tp")
     tokens, width = out_ref.shape
     half = tokens // 2
@@ -470,32 +565,14 @@
     down = jnp.maximum(z - 1, 0)
 
     loads = {
-        name: pltpu.make_async_copy(source, held[name], load_sem.at[i])
-        for i, (name, source) in enumerate(zip(names, sources))
+        name: pltpu.make_async_copy(env["source " + name], env[name], env["load_sem"].at[i])
+        for i, name in enumerate(plan["held"])
     }
-    for name in names:
+    for name in plan["held"]:
         loads[name].start()
-
-    barrier = pltpu.get_barrier_semaphore()
-
-    @pl.when(jnp.logical_not(last))
-    def _():
-        pl.semaphore_signal(barrier, inc=1, device_id={"tp": up}, device_id_type=MESH)
-
-    @pl.when(jnp.logical_not(first))
-    def _():
-        pl.semaphore_signal(barrier, inc=1, device_id={"tp": down}, device_id_type=MESH)
-
-    @pl.when(first | last)
-    def _():
-        pl.semaphore_wait(barrier, 1)
-
-    @pl.when(jnp.logical_not(first | last))
-    def _():
-        pl.semaphore_wait(barrier, 2)
-
-    if clear:
-        outs[0][...] = jnp.zeros_like(outs[0])
+    axis_barrier([("tp", count)])
+    if "sums" in env:
+        env["sums"][...] = jnp.zeros_like(env["sums"])
 
     def own_rows(c):
         return pl.ds(pl.multiple_of(c * size, size), size)
@@ -558,7 +635,7 @@
         @pl.when(ends)
         def _():
             total = landed[own, :].astype(F32) + part[term_rows, :]
-            out_ref[here, :] = finish(total, here, own, held, vecs, outs).astype(BF16)
+            out_ref[here, :] = finish(total, here, own, env).astype(BF16)
             gather(c).start()
 
     def gather_step(c, gather, starts, ends):
@@ -581,53 +658,56 @@
             cols = pl.ds(pl.multiple_of(n * TILE, TILE), TILE)
             total = 0.0
             for left, right in parts:
-                rows = jnp.concatenate([held[left][top, :], held[left][low, :]], axis=0)
-                total = total + dot(rows, held[right][cols, :], 1, 1)
+                rows = jnp.concatenate([env[left][top, :], env[left][low, :]], axis=0)
+                total = total + dot(rows, env[right][cols, :], 1, 1)
             part[:, cols] = total
             return carry
 
         lax.fori_loop(0, width // TILE, columns, 0)
 
     def run_task(index, tile, slot):
-        kind, left, right = tasks[index]
-        target = task_outs[index]
-        wide = target.shape[1]
+        kind, left, right, name = tasks[index]
+        target = env[name]
         rows = pl.ds(pl.multiple_of(tile * ROWS, ROWS), ROWS)
         if kind == "weight":
-            depth = tokens
-            turned[:, :depth] = jnp.transpose(held[left][:, rows])
+            env["turned"][...] = jnp.transpose(env[left][:, rows])
 
         def columns(n, carry):
             cols = pl.ds(pl.multiple_of(n * TILE, TILE), TILE)
             if kind == "weight":
-                value = dot(turned[:, :depth], held[right][:, cols], 1, 0)
-            elif kind == "rows":
-                value = dot(held[left][rows, :], held[right][:, cols], 1, 0)
+                value = dot(env["turned"][...], env[right][:, cols], 1, 0)
+            elif kind == "keep":
+                value = dot(env[left][rows, :], env[right][:, cols], 1, 0)
             else:
-                value = dot(held[left][rows, :], held[right][cols, :], 1, 1)
+                value = dot(env[left][rows, :], env[right][cols, :], 1, 1)
                 top = tile * ROWS < half
                 mine = (first & top) | (last & jnp.logical_not(top))
                 own = pl.multiple_of(lax.rem(tile * ROWS, half), ROWS)
-                base = held["middle"][pl.ds(own, ROWS), cols]
+                base = env["middle"][pl.ds(own, ROWS), cols]
                 value = value + jnp.where(mine, base, 0.0)
-            stage[slot, :, cols] = value.astype(BF16)
+            if kind == "keep":
+                target[rows, cols] = value.astype(BF16)
+            else:
+                env["stage"][slot, :, cols] = value.astype(BF16)
             return carry
 
-        lax.fori_loop(0, wide // TILE, columns, 0)
-        stage_copy(index, tile, slot).start()
+        lax.fori_loop(0, target.shape[1] // TILE, columns, 0)
+        if kind != "keep":
+            stage_copy(index, tile, slot).start()
 
     def stage_copy(index, tile, slot):
-        target = task_outs[index]
+        target = env[tasks[index][3]]
         rows = pl.ds(pl.multiple_of(tile * ROWS, ROWS), ROWS)
         return pltpu.make_async_copy(
-            stage.at[slot, :, : target.shape[1]], target.at[rows, :], stage_sem.at[slot]
+            env["stage"].at[slot, :, : target.shape[1]], target.at[rows, :], env["stage_sem"].at[slot]
         )
 
     starts_at = [0]
-    for index in range(num_task):
-        starts_at.append(starts_at[-1] + task_outs[index].shape[0] // ROWS)
+    for task in tasks:
+        starts_at.append(starts_at[-1] + env[task[3]].shape[0] // ROWS)
     task_total = starts_at[-1]
     per_group = GROUP - 1
+    staged = any(task[0] != "keep" for task in tasks)
 
     def step(t, carry):
         pl.when(lax.rem(t, GROUP) == 0)(lambda: make_parts(t))
@@ -651,7 +731,7 @@
                 for name in plan["late"]:
                     loads[name].wait()
 
-            for index in range(num_task):
+            for index in range(num_task if staged else 0):
                 low, high = starts_at[index] + 2, min(starts_at[index + 1] + 2, task_total)
                 pl.when(free & (turn >= low) & (turn < high))(
                     lambda index=index, low=low: stage_copy(index, turn - low, slot).wait()
@@ -661,17 +741,35 @@
                 pl.when(free & (turn >= low) & (turn < high))(
                     lambda index=index, low=low: run_task(index, turn - low, slot)
                 )
+        if plan["rows_done"]:
+            done_a = t - ahead - from_first - (GROUP - 1)
+            done_b = t - ahead - from_last - (GROUP - 1)
+            has_a = (done_a >= 0) & (done_a < chunks) & (lax.rem(done_a + 64, GROUP) == 0)
+            has_b = (done_b >= 0) & (done_b < chunks) & (lax.rem(done_b + 64, GROUP) == 0)
+
+            @pl.when(has_a | has_b)
+            def _():
+                start = jnp.where(has_a, done_a * size, half + done_b * size)
+                rows = pl.ds(pl.multiple_of(start, LANES), LANES)
+                plan["rows_done"](env, rows, rows)
+
         return carry
 
-    for name in names:
+    for name in plan["held"]:
         if name not in plan["late"]:
             loads[name].wait()
+    if plan["before"]:
+        plan["before"](env)
     lax.fori_loop(0, steps, step, 0)
     if num_task:
-        assert task_total >= 2 and (steps // GROUP) * per_group >= task_total
+        assert (steps // GROUP) * per_group >= task_total
+    if staged:
+        assert task_total >= 2
         for turn in (task_total - 2, task_total - 1):
             index = max(i for i in range(num_task) if starts_at[i] <= turn)
             stage_copy(index, turn - starts_at[index], turn % 2).wait()
+    if plan["after"]:
+        plan["after"](env)
 
     def drain(c, carry):
         @pl.when(jnp.logical_not(first))
@@ -689,47 +787,63 @@
     lax.fori_loop(0, chunks, drain, 0)
 
 
-def line_sum(finish, count, held, vecs, parts, late, tasks, own_shapes, clear, collective_id):
-    names = list(held)
-    tokens = held[parts[0][0]].shape[0]
+def line_sum(
+    finish, count, held, vecs, parts, collective_id, *, tokens, late=(), tasks=(), owns=(), sent=(),
+    scratch=(), before=None, rows_done=None, after=None, micros=110,
+):
     width = held[parts[0][1]].shape[0]
     half = tokens // 2
+    depth = tokens if any(task[0] == "weight" for task in tasks) else LANES
+    stage_width = max([shape.shape[1] for _, shape in sent] + [LANES])
+    fixed = [
+        ("in_a", pltpu.VMEM((half, width), BF16)),
+        ("in_b", pltpu.VMEM((half, width), BF16)),
+        ("part", pltpu.VMEM((2 * GROUP * half // CHUNKS, width), F32)),
+        ("turned", pltpu.VMEM((ROWS, depth), BF16)),
+        ("stage", pltpu.VMEM((2, ROWS if sent else 16, stage_width), BF16)),
+        ("load_sem", pltpu.SemaphoreType.DMA((len(held),))),
+        ("stage_sem", pltpu.SemaphoreType.DMA((2,))),
+    ] + [
+        (name, pltpu.SemaphoreType.DMA((CHUNKS,)))
+        for name in ("rsa_s", "rsa_r", "rsb_s", "rsb_r", "aga_s", "aga_r", "agb_s", "agb_r")
+    ]
+    scratch = list(scratch) + fixed
+    order = (
+        ["source " + name for name in held]
+        + list(vecs)
+        + ["out"]
+        + [name for name, _ in owns]
+        + [name for name, _ in sent]
+        + list(held)
+        + [name for name, _ in scratch]
+    )
     plan = dict(
         finish=finish,
-        clear=clear,
-        names=names,
+        order=order,
+        held=list(held),
         parts=parts,
         late=late,
-        tasks=[task[:3] for task in tasks],
-        vecs=len(vecs),
-        owns=len(own_shapes),
+        tasks=tasks,
+        before=before,
+        rows_done=rows_done,
+        after=after,
     )
     whole = pl.BlockSpec(memory_space=pltpu.VMEM)
     any_space = pl.BlockSpec(memory_space=pl.ANY)
-    depth = tokens if any(task[0] == "weight" for task in tasks) else LANES
-    stage_width = max([task[3][1] for task in tasks] + [LANES])
     return pl.pallas_call(
         functools.partial(line_kernel, plan, count, CHUNKS, SLACK),
         out_shape=[jax.ShapeDtypeStruct((tokens, width), BF16)]
-        + own_shapes
-        + [jax.ShapeDtypeStruct(task[3], BF16) for task in tasks],
-        in_specs=[any_space] * len(names) + [whole] * len(vecs),
-        out_specs=[whole] * (1 + len(own_shapes)) + [any_space] * len(tasks),
+        + [shape for _, shape in owns]
+        + [shape for _, shape in sent],
+        in_specs=[any_space] * len(held) + [whole] * len(vecs),
+        out_specs=[whole] * (1 + len(owns)) + [any_space] * len(sent),
         scratch_shapes=[pltpu.VMEM(array.shape, array.dtype) for array in held.values()]
-        + [pltpu.VMEM((half, width), BF16)] * 2
-        + [
-            pltpu.VMEM((2 * GROUP * half // CHUNKS, width), F32),
-            pltpu.VMEM((ROWS, depth), BF16),
-            pltpu.VMEM((2, ROWS if tasks else 16, stage_width), BF16),
-            pltpu.SemaphoreType.DMA((len(names),)),
-            pltpu.SemaphoreType.DMA((2,)),
-        ]
-        + [pltpu.SemaphoreType.DMA((CHUNKS,))] * 8,
+        + [shape for _, shape in scratch],
         compiler_params=pltpu.CompilerParams(
             collective_id=collective_id, has_side_effects=True, vmem_limit_bytes=VMEM_LIMIT
         ),
-        cost_estimate=cost(110),
-    )(*held.values(), *vecs)
+        cost_estimate=cost(micros),
+    )(*held.values(), *vecs.values())
 
 
 def axis_barrier(counts):
@@ -892,14 +1006,9 @@
     hidden_width = w_up.shape[1] * tp_count
     groups = seq_count // row_count
 
-    first_gain_f = first_gain.astype(F32)[None]
-    first_bias_f = first_bias.astype(F32)[None]
-    second_gain_f = second_gain.astype(F32)[None]
-    second_bias_f = second_bias.astype(F32)[None]
-    head_gain_f = head_gain.astype(F32)[None]
-    head_bias_f = head_bias.astype(F32)[None]
-    hidden_gain_f = hidden_gain.astype(F32)[None]
-    hidden_bias_f = hidden_bias.astype(F32)[None]
+    gains = jnp.stack([first_gain, first_bias, second_gain, second_bias]).astype(F32)
+    head_vecs = jnp.stack([head_gain, head_bias]).astype(F32)
+    hidden_vecs = jnp.stack([hidden_gain, hidden_bias]).astype(F32)
 
     seg_row = lax.dynamic_slice_in_dim(segment_ids, seq_index // groups, 1, 0)
     seg_col = seg_row.reshape(length, 1)
@@ -914,8 +1023,7 @@
         w_query,
         w_key,
         w_value,
-        first_gain_f,
-        first_bias_f,
+        gains,
         tables,
         seg_col,
         seg_row,
@@ -923,62 +1031,51 @@
         groups,
         1,
     )
-    mixed = mixed.astype(F32)
-    head_sums = tp_sum(
-        jnp.stack([jnp.sum(mixed, axis=-1), jnp.sum(mixed * mixed, axis=-1)]), tp_count, 9
-    )
-    head_center = head_sums[0][:, None] / model_width
-    head_inverse = lax.rsqrt(
-        head_sums[1][:, None] / model_width - head_center * head_center + EPSILON
-    )
-    head_normed = (mixed - head_center) * head_inverse
-    head_act = (head_normed * head_gain_f + head_bias_f).astype(BF16)
-    own_shape = jax.ShapeDtypeStruct((tokens // 2, model_width), F32)
-    sums_shape = jax.ShapeDtypeStruct((2, 8, model_width), F32)
+    def shape_of(dims, kind=F32):
+        return jax.ShapeDtypeStruct(dims, kind)
+
     hidden_size = hidden_gain.shape[0]
-    second_act, middle_own, grad_hidden_act = line_sum(
+    own_shape = shape_of((tokens // 2, model_width))
+    sums_shape = shape_of((2, 8, model_width))
+    landed = pltpu.VMEM((tp_count, 8, tokens), F32)
+    pair_sem = pltpu.SemaphoreType.DMA((tp_count,))
+    (
+        second_act, middle_own, head_act, head_sums, hidden_act, grad_up, hidden_vec_grads
+    ) = line_sum(
         finish_middle,
         tp_count,
-        dict(head_act=head_act, w_out=w_out, block=block, cotangent=cotangent, w_down=w_down),
-        (second_gain_f, second_bias_f),
-        [("head_act", "w_out")],
-        ("cotangent", "w_down"),
-        [("rows", "cotangent", "w_down", (tokens, hidden_size))],
-        [own_shape],
-        False,
+        dict(mixed=mixed, w_out=w_out, block=block, cotangent=cotangent, w_down=w_down, w_up=w_up),
+        dict(gains=gains, head_vecs=head_vecs, hidden_vecs=hidden_vecs),
+        (("head_act", "w_out"),),
         3,
-    )
-    grad_hidden_act = grad_hidden_act.astype(F32)
-
-    up_pre = matmul(second_act, w_up, 1, 0)
-    cdf = 0.5 * lax.erfc(up_pre * (-(0.5**0.5)))
-    gelu_out = up_pre * cdf
-    hidden_scaled = grad_hidden_act * hidden_gain_f
-    stats = tp_sum(
-        jnp.stack(
-            [
-                jnp.sum(gelu_out, axis=-1),
-                jnp.sum(gelu_out * gelu_out, axis=-1),
-                jnp.sum(hidden_scaled, axis=-1),
-                jnp.sum(hidden_scaled * gelu_out, axis=-1),
-            ]
+        tokens=tokens,
+        late=("cotangent", "w_down", "w_up"),
+        tasks=(("keep", "cotangent", "w_down", "hidden_grad"),),
+        owns=(
+            ("middle", own_shape),
+            ("head_act", shape_of((tokens, head_width), BF16)),
+            ("head_sums", shape_of((8, tokens))),
+            ("hidden_act", shape_of((tokens, hidden_size), BF16)),
+            ("grad_up", shape_of((tokens, hidden_size), BF16)),
+            ("hidden_vec_grads", shape_of((2, 8, hidden_size))),
         ),
-        tp_count,
-        10,
-    )
-    stats = stats[:, :, None] / hidden_width
-    hidden_center = stats[0]
-    hidden_inverse = lax.rsqrt(stats[1] - hidden_center * hidden_center + EPSILON)
-    hidden_normed = (gelu_out - hidden_center) * hidden_inverse
-    hidden_act = (hidden_normed * hidden_gain_f + hidden_bias_f).astype(BF16)
-    hidden_gain_grad = jnp.sum(grad_hidden_act * hidden_normed, axis=0)
-    hidden_bias_grad = jnp.sum(grad_hidden_act, axis=0)
-    hidden_cross = hidden_inverse * (stats[3] - hidden_center * stats[2])
-    grad_gelu = hidden_inverse * (hidden_scaled - stats[2] - hidden_normed * hidden_cross)
-    pdf = jnp.exp(-0.5 * up_pre * up_pre) * (1.0 / math.sqrt(2.0 * math.pi))
-    grad_up = (grad_gelu * (cdf + up_pre * pdf)).astype(BF16)
-
-    weight_shape = (model_width, hidden_size)
+        scratch=(
+            ("hidden_grad", pltpu.VMEM((tokens, hidden_size), BF16)),
+            ("hidden_sums", pltpu.VMEM((8, tokens), F32)),
+            ("head_landed", landed),
+            ("hidden_landed", landed),
+            ("head_send", pair_sem),
+            ("head_recv", pair_sem),
+            ("hidden_send", pair_sem),
+            ("hidden_recv", pair_sem),
+        ),
+        before=lambda env: norm_heads(env, tp_count, model_width),
+        rows_done=hidden_rows,
+        after=lambda env: norm_hidden(env, tp_count, hidden_width),
+        micros=140,
+    )
+
+    weight_shape = shape_of((model_width, hidden_size), BF16)
     grad_middle_low, second_sums, grad_middle_own, down_part, w_down_terms, w_up_terms = line_sum(
         finish_second,
         tp_count,
@@ -991,19 +1088,30 @@
             w_down=w_down,
             second_act=second_act,
         ),
-        (second_gain_f,),
-        [("grad_up", "w_up")],
-        ("hidden_act", "w_down", "second_act"),
-        [
-            ("down", "hidden_act", "w_down", (tokens, model_width)),
-            ("weight", "cotangent", "hidden_act", weight_shape),
-            ("weight", "second_act", "grad_up", weight_shape),
-        ],
-        [sums_shape, own_shape],
-        True,
+        dict(gains=gains),
+        (("grad_up", "w_up"),),
         4,
+        tokens=tokens,
+        late=("hidden_act", "w_down", "second_act"),
+        tasks=(
+            ("down", "hidden_act", "w_down", "down_part"),
+            ("weight", "cotangent", "hidden_act", "w_down_terms"),
+            ("weight", "second_act", "grad_up", "w_up_terms"),
+        ),
+        owns=(("sums", sums_shape), ("middle_grad", own_shape)),
+        sent=(
+            ("down_part", shape_of((tokens, model_width), BF16)),
+            ("w_down_terms", weight_shape),
+            ("w_up_terms", weight_shape),
+        ),
     )
     block_out = lax.psum(down_part, "tp")
+
+    head_center = head_sums[0][:, None] / model_width
+    head_inverse = lax.rsqrt(
+        head_sums[1][:, None] / model_width - head_center * head_center + EPSILON
+    )
+    head_normed = (mixed.astype(F32) - head_center) * head_inverse
 
     def scatter(grad):
         return lax.psum_scatter(grad, "seq", scatter_dimension=0, tiled=True)
@@ -1014,7 +1122,7 @@
     grad_head_act = matmul(grad_middle_low, w_out, 1, 0)
     head_gain_grad = jnp.sum(grad_head_act * head_normed, axis=0)
     head_bias_grad = jnp.sum(grad_head_act, axis=0)
-    head_scaled = grad_head_act * head_gain_f
+    head_scaled = grad_head_act * head_vecs[0:1]
     head_back = tp_sum(
         jnp.stack([jnp.sum(head_scaled, axis=-1), jnp.sum(head_scaled * head_normed, axis=-1)]),
         tp_count,
@@ -1057,20 +1165,19 @@
             block=block,
             middle_grad=grad_middle_own,
         ),
-        (first_gain_f,),
-        [("grad_query", "w_query"), ("grad_key", "w_key"), ("grad_value", "w_value")],
-        (),
-        [],
-        [sums_shape],
-        True,
+        dict(gains=gains),
+        (("grad_query", "w_query"), ("grad_key", "w_key"), ("grad_value", "w_value")),
         8,
+        tokens=tokens,
+        owns=(("sums", sums_shape),),
     )
 
     own_width = model_width // seq_count
     full = jnp.concatenate([jnp.sum(second_sums, axis=1), jnp.sum(first_sums, axis=1)])
     full = full.reshape(4, seq_count, own_width).transpose(1, 0, 2)
     full = full.reshape(seq_count, 4 * own_width // LANES, LANES)
-    split = jnp.concatenate([hidden_gain_grad, hidden_bias_grad, head_gain_grad, head_bias_grad])
+    hidden_vec_grads = jnp.sum(hidden_vec_grads, axis=1).reshape(-1)
+    split = jnp.concatenate([hidden_vec_grads, head_gain_grad, head_bias_grad])
     norm_own, split = norm_sum(
         full, split.reshape(split.shape[0] // LANES, LANES), seq_count, tp_count, 12
     )

time: 733 us -> 682 us (0.930)
  matrix products: 53.5 us -> 18.9 us
  other arithmetic: 51 us -> 23.1 us
  Pallas kernels: 540 us -> 551 us
    dot_general x6 -> x5, matrix products: 53.5 us -> 18.9 us  [dot(): lax.dot_general(left, right, (((left_dim,), (right_dim,)), ((), ())), pre...]
    pallas_call x3, Pallas kernels: 367 us -> 394 us  [line_sum(): pl.pallas_call(functools.partial(line_kernel, plan, count, CHUNKS, SLACK)...]
    reduce_sum x2 -> x1, other arithmetic: 17.5 us -> 0.05 us  [body(): hidden_vec_grads = jnp.sum(hidden_vec_grads, axis=1).reshape(-1)]
    pallas_call x3 -> x1, Pallas kernels: 21.8 us -> 7.3 us  [tp_sum(): pl.pallas_call(functools.partial(tp_sum_kernel, count), out_shape=jax.Sha...]
  transfers between devices with their start and end apart: 4 -> 4, of which waited for: 1 -> 1; matrix products, arithmetic and copies ran while one was open for 6% -> 6% of each run, Pallas kernels for 30% -> 32%
where the time goes in v5:
time: 682 us; the launch traced here: 676 us
  Pallas kernels  551 us (81%)
  waiting for transfers between devices  38 us (6%)
  local copies, waits for them, and re-layouts  28.4 us (4%)
  other arithmetic  23.1 us (3%)
  matrix products  18.9 us (3%)
  between operations  16.2 us (2%)
    pallas_call x3, Pallas kernels, line_sum(): pl.pallas_call(functools.partial(line_kernel, plan, count, CHUNKS, SLACK)...  394 us
    pallas_call x1, Pallas kernels, attend_back(): pl.pallas_call(functools.partial(back_kernel, count, groups), out_shape=j...  76.3 us
    pallas_call x1, Pallas kernels, front(): pl.pallas_call(functools.partial(front_kernel, count, groups), out_shape=...  62.8 us
    psum x1, waiting for transfers between devices, body(): block_out = lax.psum(down_part, 'tp')  37 us
    dot_general x5, matrix products, dot(): lax.dot_general(left, right, (((left_dim,), (right_dim,)), ((), ())), pre...  18.9 us
  transfers between devices with their start and end apart: 4, of which 1 were waited for; matrix products, arithmetic and copies ran while one was open for 6% of the time, Pallas kernels for 32%

profile of v5, /device:TPU:0, one launch (start us, length us, event | category | flops | bytes accessed | tf_op | source)
XLA Modules:
  0.0 676.2 jit_solution(14231853115313911309)
XLA Ops:
  17.2 2.0 exponential_bitcast_fusion.1
  22.4 1.5 pad_maximum_fusion.1.tab_ref
  23.9 62.8 %shard_map.288 = (bf16[1024,2048]{1,0:T(8,128)(2,1)}, bf16[4,1024,384]{2,1,0:T(8,128)(2,1)}, bf16[4,1024,128]{2,1,0:T(8,128)(2,1)}, f32[4,8,1024]{2,1,0:T(8,128)}, bf16[1024,512]{1,0:T(8,128)(2,1)}) custom-call(bf16[1024,2048]{1,0:T(8,128)(2,1)} %bitcast.81, bf16[2048,512]{1,0:T(8,128)(2,1)} %refs_1_.5, bf16[2048,512]{1,0:T(8,128)(2,1)} %refs_3_.1, ...), custom_call_target="tpu_custom_call" | custom-call | flops 65999998976 | tf_op jit(solution)/shard_map/pallas_call | solution.py:233
  86.6 144.8 %shard_map.289 = (bf16[1024,2048]{1,0:T(8,128)(2,1)}, f32[512,2048]{1,0:T(8,128)}, bf16[1024,512]{1,0:T(8,128)(2,1)}, f32[8,1024]{1,0:T(8,128)}, bf16[1024,2048]...) custom-call(bf16[1024,512]{1,0:T(8,128)(2,1)} %get-tuple-element.41.refs_0_, ...), custom_call_target="tpu_custom_call" | custom-call | flops 153999998976 | tf_op jit(solution)/shard_map/pallas_call | solution.py:833
  231.5 127.8 %shard_map.290 = (bf16[1024,2048]{1,0:T(8,128)(2,1)}, f32[2,8,2048]{2,1,0:T(8,128)}, f32[512,2048]{1,0:T(8,128)}, bf16[1024,2048]{1,0:T(8,128)(2,1)}, bf16[2048,...) custom-call(bf16[1024,2048]{1,0:T(8,128)(2,1)} %get-tuple-element.42.refs_0_, bf16[2048,2048]{1,0:T(8,128)(2,1)} %refs_1_.4, ...), custom_call_target="tpu_custom_call" | custom-call | flops 121000001536 | tf_op jit(solution)/shard_map/pallas_call | solution.py:833
  362.4 6.4 multiply_reduce_fusion
  370.1 7.3 %shard_map.291 = f32[2,1024]{1,0:T(2,128)} custom-call(f32[2,1024]{1,0:T(2,128)} %pad_maximum_fusion.7.x_ref), custom_call_target="tpu_custom_call" | custom-call | flops 5500000256 | tf_op jit(solution)/shard_map/pallas_call | solution.py:896
  378.1 1.7 multiply_convert_fusion.do_ref
  379.8 76.3 %shard_map.292 = bf16[3,1024,512]{2,1,0:T(8,128)(2,1)} custom-call(bf16[1024,512]{1,0:T(8,128)(2,1)} %multiply_convert_fusion.do_ref, bf16[4,1024,384]{2,1,0:T(8,128)(2,1)} %get-tuple-element.49.qkv_ref, bf16[4,1024,128]{2,1,0:T(8,128)(2,1)} %get-tuple-element.50.o_ref, f32[4,8,1024]{2,1,0:T(8,128)} %get-tuple-element.51.lse_ref, ...), custom_call_target="tpu_custom_call" | custom-call | flops 65999998976 | tf_op jit(solution)/shard_map/pallas_call | solution.py:378
  456.1 3.7 slice_bitcast_fusion
  459.8 5.2 convolution_convert_fusion.3
  465.0 2.4 convolution_convert_fusion.1
  467.5 2.4 convolution_convert_fusion.2
  470.0 2.4 convolution_convert_fusion
  472.4 4.1 pad_maximum_fusion
  476.5 37.0 %all-reduce.2.cloned.1.call-done = bf16[8,128,2048]{2,1,0:T(8,128)(2,1)} async-done(((bf16[8,128,2048]{2,1,0:T(8,128)(2,1)}), bf16[8,128,2048]{2,1,0:T(8,128)(2,1)}) %all-reduce.2.cloned.1.call-update) | async-done | bytes 4194320 | tf_op jit(solution)/shard_map/psum | solution.py:1108
  513.6 121.0 %shard_map.293 = (bf16[1024,2048]{1,0:T(8,128)(2,1)}, f32[2,8,2048]{2,1,0:T(8,128)}) custom-call(bf16[1024,512]{1,0:T(8,128)(2,1)} %get-tuple-element.55.refs_0_, bf16[2048,512]{1,0:T(8,128)(2,1)} %refs_1_.5, bf16[1024,512]{1,0:T(8,128)(2,1)} %get-tuple-element.119.refs_2_, bf16[2048,512]{1,0:T(8,128)(2,1)} %refs_3_.1, ...), custom_call_target="tpu_custom_call" | custom-call | flops 121000001536 | tf_op jit(solution)/shard_map/pallas_call | solution.py:833
  636.2 1.6 convert_element_type.59
  637.8 2.8 convert_element_type.58
  640.6 11.4 %shard_map.294 = (f32[8,128]{1,0:T(8,128)}, f32[40,128]{1,0:T(8,128)}) custom-call(f32[8,8,128]{2,1,0:T(8,128)} %reshape.1052.full_ref, f32[40,128]{1,0:T(8,128)} %maximum_bitcast_fusion.split_ref), custom_call_target="tpu_custom_call" | custom-call | flops 11000000512 | tf_op jit(solution)/shard_map/pallas_call | solution.py:937
  652.0 1.4 slice_bitcast_fusion.7
  656.1 1.4 fusion.8
  661.4 4.9 copy.53
  666.4 2.0 copy.54
  (77 shorter events, 25.7 us)
Async XLA Ops:
  8.0 0.8 copy-start
  8.0 505.5 %all-reduce.2.cloned.1.call-start = ((), (), s32[]{:S(2)}) async-start(), calls=%async_computation.3 | async-start | bytes 8388608 | tf_op jit(solution)/shard_map/psum | solution.py:1108
  8.8 13.0 %copy-start.9 = (s32[1,1024]{1,0:T(1,128)}, s32[1,1024]{1,0:T(1,128)S(1)}, u32[]{:S(2)}) copy-start(s32[1,1024]{1,0:T(1,128)S(1)} %constant_dynamic-slice_fusion.segr_ref) | copy-start | bytes 12292
  359.3 154.2 %reduce-scatter.4.cloned.1.call-start = ((), (), s32[]{:S(2)}) async-start(), calls=%async_computation.4 | async-start | bytes 9437184 | tf_op jit(solution)/shard_map/reduce_scatter | solution.py:1117
  359.9 277.9 %reduce-scatter.8.cloned.1.call-start = ((), (), s32[]{:S(2)}) async-start(), calls=%async_computation.6 | async-start | bytes 9437184 | tf_op jit(solution)/shard_map/reduce_scatter | solution.py:1117
  359.9 0.7 copy-start.10
  359.9 0.9 copy-start.6
  360.0 1.0 copy-start.7
  360.0 2.5 copy-start.5
  360.5 295.6 %reduce-scatter.6.cloned.1.call-start = ((), (), s32[]{:S(2)}) async-start(), calls=%async_computation.5 | async-start | bytes 9437184 | tf_op jit(solution)/shard_map/reduce_scatter | solution.py:1117
  456.1 3.7 copy-start.3
  459.8 5.2 copy-start.11
  467.5 2.5 copy-start.12
  467.5 2.5 copy-start.13
  513.6 122.0 %copy-start.8 = (f32[2,2048]{1,0:T(2,128)S(1)}, f32[2,2048]{1,0:T(2,128)}, u32[]{:S(2)}) copy-start(f32[2,2048]{1,0:T(2,128)} %reduce_sum.75) | copy-start | bytes 49156
  513.6 122.7 %copy-start.4 = (bf16[256,2048]{1,0:T(8,128)(2,1)S(1)}, bf16[256,2048]{1,0:T(8,128)(2,1)}, u32[]{:S(2)}) copy-start(bf16[256,2048]{1,0:T(8,128)(2,1)} %reduce-scatter.4.cloned.1.call-done) | copy-start | bytes 3145732
  661.4 4.9 copy-start.2
  661.4 7.0 %copy-start.1 = (s32[8,1024]{1,0:T(8,128)S(1)}, s32[8,1024]{1,0:T(8,128)}, u32[]{:S(2)}) copy-start(s32[8,1024]{1,0:T(8,128)} %param.18) | copy-start | bytes 98308
Sparse Core Ops, SparseCore 0:
  359.4 154.0 all-reduce.1
Sparse Core Ops, SparseCore 1:
  363.6 111.4 reduce-scatter.3
  478.4 71.1 reduce-scatter.7
  553.3 71.1 reduce-scatter.5

commit v6 on v5

--- a/solution.py
+++ b/solution.py
@@ -97,14 +97,39 @@
     return shifted * inverse, inverse
 
 
+def expand_tables(packed, tables):
+    quarter = HEAD // 2
+    for block in range(packed.shape[0] // BLOCK):
+        rows = block_rows(block)
+        lane = lax.broadcasted_iota(jnp.int32, (BLOCK, LANES), 1)
+        group = lane // quarter
+        turns = [packed[rows, :]]
+        for k in range(1, 4):
+            turns.append(pltpu.roll(turns[0], k * quarter, 1))
+
+        def spread(index):
+            values = turns[(0 - index) % 4]
+            for g in range(1, 4):
+                values = jnp.where(group == g, turns[(g - index) % 4], values)
+            return values
+
+        cos_part = spread(0)
+        sin_part = spread(1)
+        sin_part = jnp.where(lane % HEAD < quarter, -sin_part, sin_part)
+        for k in range(2):
+            factor = spread(2 + k)
+            tables[2 * k, rows, :] = cos_part * factor
+            tables[2 * k + 1, rows, :] = sin_part * factor
+
+
 def front_kernel(
-    count, groups, x_ref, wq_ref, wk_ref, wv_ref, gains_ref, tab_ref, segc_ref, segr_ref,
+    count, groups, x_ref, wq_ref, wk_ref, wv_ref, vecs_ref, packed_ref, segc_ref, segr_ref,
     act_ref, qkv_ref, o_ref, lse_ref, mixed_ref,
-    weights, staged, bias, qs, ks, load_sem, send_sem, recv_sem, back_send_sem, back_recv_sem,
+    weights, staged, tab_ref, bias, qs, ks, load_sem, send_sem, recv_sem, back_send_sem, back_recv_sem,
 ):
     me = lax.axis_index("seq")
     pairs, length = qkv_ref.shape[:2]
-    tokens = x_ref.shape[0]
+    tokens, width = x_ref.shape
     span = length // count
     blocks = length // BLOCK
     mine, row = lax.rem(me, groups), me // groups
@@ -123,7 +148,7 @@
     def norm_step(r, carry):
         rows = pl.ds(pl.multiple_of(r * LANES, LANES), LANES)
         normed, _ = norm_parts(x_ref[rows, :].astype(F32))
-        act_ref[rows, :] = (normed * gains_ref[0:1] + gains_ref[1:2]).astype(BF16)
+        act_ref[rows, :] = (normed * vecs_ref[:, :width] + vecs_ref[:, width : 2 * width]).astype(BF16)
         return carry
 
     lax.fori_loop(0, tokens // LANES, norm_step, 0)
@@ -171,6 +196,7 @@
         return carry
 
     lax.fori_loop(0, pairs, project, 0)
+    expand_tables(packed_ref, tab_ref)
     for qb in range(blocks):
         rows = block_rows(qb)
         keys = (qb + 1) * BLOCK
@@ -223,7 +249,7 @@
     lax.fori_loop(0, pairs, drain, 0)
 
 
-def front(x, w_query, w_key, w_value, gains, tables, seg_col, seg_row, count, groups, collective_id):
+def front(x, w_query, w_key, w_value, vecs, tables, seg_col, seg_row, count, groups, collective_id):
     tokens, model_width = x.shape
     head_width = w_query.shape[1]
     length = seg_col.shape[0]
@@ -244,6 +270,7 @@
         scratch_shapes=[
             pltpu.VMEM((pairs * groups, model_width, 3 * LANES), BF16),
             pltpu.VMEM((pairs * groups, tokens, 3 * LANES), BF16),
+            pltpu.VMEM((4, length, LANES), F32),
             pltpu.VMEM((length, length), F32),
             pltpu.VMEM((2, length, LANES), BF16),
             pltpu.VMEM((length, LANES), BF16),
@@ -254,20 +281,64 @@
             collective_id=collective_id, has_side_effects=True, vmem_limit_bytes=VMEM_LIMIT
         ),
         cost_estimate=cost(60),
-    )(x, w_query, w_key, w_value, gains, tables, seg_col, seg_row)
+    )(x, w_query, w_key, w_value, vecs, tables, seg_col, seg_row)
 
 
 def back_kernel(
-    count, groups, do_ref, qkv_ref, o_ref, lse_ref, tab_ref, segc_ref, segr_ref, grads_ref,
+    count, tp_count, groups, low_ref, wout_ref, mixed_ref, sums_ref, vecs_ref,
+    qkv_ref, o_ref, lse_ref, packed_ref, segc_ref, segr_ref, grads_ref, vec_grads_ref,
+    do_ref, scaled, part, landed, tab_ref,
     do_row, made, bias, qs, ks, kms, dos, delta, dq, dk, dv,
-    send_sem, recv_sem, back_send_sem, back_recv_sem,
+    tp_send, tp_recv, send_sem, recv_sem, back_send_sem, back_recv_sem,
 ):
     me = lax.axis_index("seq")
     pairs, length = qkv_ref.shape[:2]
+    tokens, features = low_ref.shape
+    head_width = mixed_ref.shape[1]
     span = length // count
     blocks = length // BLOCK
     mine, row = lax.rem(me, groups), me // groups
-    seq_signal(count)
+    axis_barrier([("seq", count), ("tp", tp_count)])
+    gain = head_vec(vecs_ref, head_width, 0)
+    vec_grads_ref[...] = jnp.zeros_like(vec_grads_ref)
+
+    def normed_rows(rows):
+        first, second = to_columns(sums_ref[:, rows], 2)
+        center = first / features
+        inverse = lax.rsqrt(second / features - center * center + EPSILON)
+        return (mixed_ref[rows, :].astype(F32) - center) * inverse, inverse
+
+    def head_terms(r, carry):
+        wide = pl.ds(pl.multiple_of(r * BLOCK, BLOCK), BLOCK)
+        scaled[wide, :] = dot(low_ref[wide, :], wout_ref[...], 1, 0)
+        for k in range(BLOCK // LANES):
+            rows = row_block(r * (BLOCK // LANES) + k)
+            normed, _ = normed_rows(rows)
+            grad = scaled[rows, :]
+            vec_grads_ref[0] += fold(grad * normed)
+            vec_grads_ref[1] += fold(grad)
+            grad = grad * gain
+            scaled[rows, :] = grad
+            part[:, rows] = to_row(
+                [
+                    jnp.sum(grad, axis=-1, keepdims=True),
+                    jnp.sum(grad * normed, axis=-1, keepdims=True),
+                ]
+            )
+        return carry
+
+    lax.fori_loop(0, tokens // BLOCK, head_terms, 0)
+    tp_total(part, landed, tp_send, tp_recv, tp_count)
+
+    def head_apply(r, carry):
+        rows = row_block(r)
+        normed, inverse = normed_rows(rows)
+        first, second = to_columns(part[:, rows], 2)
+        grad = scaled[rows, :] - first / features - normed * (second / features)
+        do_ref[rows, :] = (inverse * grad).astype(BF16)
+        return carry
+
+    lax.fori_loop(0, tokens // LANES, head_apply, 0)
 
     def there(p, k):
         device = lax.rem(me + k, count)
@@ -282,14 +353,12 @@
     def back(p, k):
         device = lax.rem(me + k, count)
         return send(
-            made.at[p, :, spans(device, span), :],
-            grads_ref.at[:, spans(row, span), spans(mine * pairs + p, LANES)],
+            made.at[p, spans(device, span), :],
+            grads_ref.at[spans(row, span), spans(mine * pairs + p, 3 * LANES)],
             back_send_sem.at[p, k],
             back_recv_sem.at[p, k],
             device,
         )
-
-    seq_wait(count)
 
     def share_out(p, carry):
         for k in range(1, count):
@@ -298,6 +367,7 @@
         return carry
 
     lax.fori_loop(0, pairs, share_out, 0)
+    expand_tables(packed_ref, tab_ref)
     for kb in range(blocks):
         rows = block_rows(kb)
         start = kb * BLOCK
@@ -349,15 +419,12 @@
         for qb in range(blocks):
             rows = block_rows(qb)
             grad = dq[rows, :] * (HEAD**-0.5)
-            made[p, 0, rows, :] = rotated_back(grad, tab_ref, 0, rows).astype(BF16)
-            made[p, 1, rows, :] = rotated_back(dk[rows, :], tab_ref, 2, rows).astype(BF16)
-            made[p, 2, rows, :] = dv[rows, :].astype(BF16)
+            made[p, rows, :LANES] = rotated_back(grad, tab_ref, 0, rows).astype(BF16)
+            made[p, rows, LANES : 2 * LANES] = rotated_back(dk[rows, :], tab_ref, 2, rows).astype(BF16)
+            made[p, rows, 2 * LANES :] = dv[rows, :].astype(BF16)
         for k in range(1, count):
             back(p, k).start()
-        for i in range(3):
-            grads_ref[i, spans(row, span), spans(mine * pairs + p, LANES)] = made[
-                p, i, spans(me, span), :
-            ]
+        grads_ref[spans(row, span), spans(mine * pairs + p, 3 * LANES)] = made[p, spans(me, span), :]
         return carry
 
     lax.fori_loop(0, pairs, attend, 0)
@@ -371,18 +438,29 @@
     lax.fori_loop(0, pairs, drain, 0)
 
 
-def attend_back(do, qkv, o, lse, tables, seg_col, seg_row, count, groups, collective_id):
-    tokens, head_width = do.shape
+def attend_back(
+    low, w_out, mixed, head_sums, vecs, qkv, o, lse, tables, seg_col, seg_row, count, tp_count,
+    groups, collective_id,
+):
+    tokens, head_width = mixed.shape
     pairs, length = qkv.shape[:2]
     whole = pl.BlockSpec(memory_space=pltpu.VMEM)
     return pl.pallas_call(
-        functools.partial(back_kernel, count, groups),
-        out_shape=jax.ShapeDtypeStruct((3, tokens, head_width), BF16),
-        in_specs=[whole] * 7,
-        out_specs=whole,
+        functools.partial(back_kernel, count, tp_count, groups),
+        out_shape=[
+            jax.ShapeDtypeStruct((tokens, 3 * head_width), BF16),
+            jax.ShapeDtypeStruct((2, 8, head_width), F32),
+        ],
+        in_specs=[whole] * 11,
+        out_specs=[whole] * 2,
         scratch_shapes=[
+            pltpu.VMEM((tokens, head_width), BF16),
+            pltpu.VMEM((tokens, head_width), F32),
+            pltpu.VMEM((8, tokens), F32),
+            pltpu.VMEM((tp_count, 8, tokens), F32),
+            pltpu.VMEM((4, length, LANES), F32),
             pltpu.VMEM((pairs, length, LANES), BF16),
-            pltpu.VMEM((pairs, 3, length, LANES), BF16),
+            pltpu.VMEM((pairs, length, 3 * LANES), BF16),
             pltpu.VMEM((length, length), F32),
             pltpu.VMEM((2, length, LANES), BF16),
             pltpu.VMEM((length, LANES), BF16),
@@ -393,24 +471,68 @@
             pltpu.VMEM((length, LANES), F32),
             pltpu.VMEM((length, LANES), F32),
         ]
+        + [pltpu.SemaphoreType.DMA((tp_count,))] * 2
         + [pltpu.SemaphoreType.DMA((pairs, count))] * 4,
         compiler_params=pltpu.CompilerParams(
             collective_id=collective_id, has_side_effects=True, vmem_limit_bytes=VMEM_LIMIT
         ),
-        cost_estimate=cost(60),
-    )(do, qkv, o, lse, tables, seg_col, seg_row)
+        cost_estimate=cost(70),
+    )(low, w_out, mixed, head_sums, vecs, qkv, o, lse, tables, seg_col, seg_row)
+
+
+def weight_kernel(act_ref, grads_ref, low_ref, head_ref, out_ref):
+    wide = grads_ref.shape[1]
+    out_ref[:, :wide] = dot(jnp.transpose(act_ref[...]), grads_ref[...], 1, 0).astype(BF16)
+    out_ref[:, wide:] = dot(jnp.transpose(low_ref[...]), head_ref[...], 1, 0).astype(BF16)
+
+
+def head_weights(act, grads, low, head_act):
+    tokens, model_width = act.shape
+    wide, narrow = grads.shape[1], head_act.shape[1]
+    tile = pl.BlockSpec((tokens, ROWS), lambda i: (0, i))
+    return pl.pallas_call(
+        weight_kernel,
+        grid=(model_width // ROWS,),
+        out_shape=jax.ShapeDtypeStruct((model_width, wide + narrow), BF16),
+        in_specs=[
+            tile,
+            pl.BlockSpec((tokens, wide), lambda i: (0, 0)),
+            tile,
+            pl.BlockSpec((tokens, narrow), lambda i: (0, 0)),
+        ],
+        out_specs=pl.BlockSpec((ROWS, wide + narrow), lambda i: (i, 0)),
+        compiler_params=pltpu.CompilerParams(vmem_limit_bytes=VMEM_LIMIT),
+        cost_estimate=cost(10),
+    )(act, grads, low, head_act)
 
 
 def fold(values):
     rows, width = values.shape
     return jnp.sum(values.reshape(rows // 8, 8, width), axis=0)
+
+
+def model_vec(env, index):
+    width = env["out"].shape[1]
+    return env["vecs"][:, index * width : (index + 1) * width]
+
+
+def hidden_vec(env, index, cols=slice(None)):
+    width = env["hidden_act"].shape[1]
+    first = 4 * env["out"].shape[1] + index * width
+    return env["vecs"][:, first : first + width][:, cols]
+
+
+def head_vec(vecs_ref, width, index):
+    total = vecs_ref.shape[1]
+    first = total - (2 - index) * width
+    return vecs_ref[:, first : first + width]
 
 
 def finish_middle(total, here, own, env):
     middle = env["block"][here, :].astype(F32) + total
     env["middle"][own, :] = middle
     normed, _ = norm_parts(middle)
-    return normed * env["gains"][2:3] + env["gains"][3:4]
+    return normed * model_vec(env, 2) + model_vec(env, 3)
 
 
 def norm_back(base, values, total, gain, sums):
@@ -428,14 +550,14 @@
 
 def finish_second(total, here, own, env):
     base = env["cotangent"][here, :].astype(F32)
-    grad = norm_back(base, env["middle"][own, :], total, env["gains"][2:3], env["sums"])
+    grad = norm_back(base, env["middle"][own, :], total, model_vec(env, 2), env["sums"])
     env["middle_grad"][own, :] = grad
     return grad
 
 
 def finish_first(total, here, own, env):
     values = env["block"][here, :].astype(F32)
-    return norm_back(env["middle_grad"][own, :], values, total, env["gains"][0:1], env["sums"])
+    return norm_back(env["middle_grad"][own, :], values, total, model_vec(env, 0), env["sums"])
 
 
 def to_row(columns):
@@ -485,7 +607,9 @@
         center = first / features
         inverse = lax.rsqrt(second / features - center * center + EPSILON)
         values = (mixed[row_block(r), :].astype(F32) - center) * inverse
-        act[row_block(r), :] = (values * env["head_vecs"][0:1] + env["head_vecs"][1:2]).astype(BF16)
+        act[row_block(r), :] = (
+            values * head_vec(env["vecs"], act.shape[1], 0) + head_vec(env["vecs"], act.shape[1], 1)
+        ).astype(BF16)
         return carry
 
     lax.fori_loop(0, blocks, apply, 0)
@@ -512,7 +636,7 @@
         active = values * below
         env["hidden_act"][rows, cols] = active.astype(BF16)
         env["grad_up"][rows, cols] = (below + values * density).astype(BF16)
-        scaled = env["hidden_grad"][rows, cols].astype(F32) * env["hidden_vecs"][0:1, cols]
+        scaled = env["hidden_grad"][rows, cols].astype(F32) * hidden_vec(env, 0, cols)
         for i, term in enumerate((active, active * active, scaled, scaled * active)):
             sums[i] = sums[i] + jnp.sum(term, axis=-1, keepdims=True)
     env["hidden_sums"][:, row] = to_row(sums)
@@ -532,17 +656,90 @@
         cross = inverse * (sums[3] - center * sums[2])
         for n in range(width // TILE):
             cols = slice(n * TILE, (n + 1) * TILE)
-            gain = env["hidden_vecs"][0:1, cols]
+            gain = hidden_vec(env, 0, cols)
             normed = (act[rows, cols].astype(F32) - center) * inverse
             grad = env["hidden_grad"][rows, cols].astype(F32)
             back = inverse * (grad * gain - sums[2] - normed * cross)
             slope[rows, cols] = (back * slope[rows, cols].astype(F32)).astype(BF16)
-            act[rows, cols] = (normed * gain + env["hidden_vecs"][1:2, cols]).astype(BF16)
+            act[rows, cols] = (normed * gain + hidden_vec(env, 1, cols)).astype(BF16)
             env["hidden_vec_grads"][0, :, cols] += fold(grad * normed)
             env["hidden_vec_grads"][1, :, cols] += fold(grad)
         return carry
 
     lax.fori_loop(0, tokens // LANES, apply, 0)
+
+
+def split_copies(env, seq_count):
+    split = env["split"]
+    return share("seq", seq_count, lambda d: split, env["split_landed"], *env_pair(env, "split"), False)
+
+
+def env_pair(env, name):
+    return env[name + "_send"], env[name + "_recv"]
+
+
+def split_start(env, seq_count):
+    hidden = env["hidden_vec_grads"].shape[2]
+    split = env["split"]
+    split[...] = jnp.zeros_like(split)
+    for i in range(2):
+        split[i : i + 1, :hidden] = jnp.sum(env["hidden_vec_grads"][i], axis=0, keepdims=True)
+        split[i : i + 1, hidden:] = jnp.sum(env["head_vec_grads"][i], axis=0, keepdims=True)
+    for copy in split_copies(env, seq_count):
+        copy.start()
+    env["split_landed"][lax.axis_index("seq")] = split[...]
+
+
+def full_copies(env, count):
+    full = env["full"]
+    return share("tp", count, lambda d: full, env["full_landed"], *env_pair(env, "full"), False)
+
+
+def full_start(env, count):
+    full = env["full"]
+    full[...] = jnp.zeros_like(full)
+    for i in range(2):
+        full[i : i + 1, :] = jnp.sum(env["second_sums"][i], axis=0, keepdims=True)
+        full[2 + i : 3 + i, :] = jnp.sum(env["sums"][i], axis=0, keepdims=True)
+    for copy in full_copies(env, count):
+        copy.start()
+    env["full_landed"][lax.axis_index("tp")] = full[...]
+
+
+def norm_finish(env, seq_count, count):
+    full, own = env["full"], env["norm_own"].shape[1]
+    me = lax.axis_index("seq")
+    for copy in full_copies(env, count):
+        copy.wait()
+    full[...] = total_of(env["full_landed"], count)
+
+    def piece(device):
+        return pl.ds(pl.multiple_of(device * own, LANES), own)
+
+    copies = share(
+        "seq", seq_count, lambda d: full.at[:, piece(d)], env["own_landed"], *env_pair(env, "own")
+    )
+    env["own_landed"][me] = full[:, piece(me)]
+    for copy in split_copies(env, seq_count):
+        copy.wait()
+    env["norm_split"][...] = total_of(env["split_landed"], seq_count)
+    for copy in copies:
+        copy.wait()
+    env["norm_own"][...] = total_of(env["own_landed"], seq_count)
+
+
+def load_pairs(env):
+    copies = []
+    for i, name in enumerate(("w_query", "w_key", "w_value")):
+        for j in range(env[name].shape[1] // LANES):
+            copy = pltpu.make_async_copy(
+                env[name].at[:, j * LANES : (j + 1) * LANES],
+                env["w_pairs"].at[:, (3 * j + i) * LANES : (3 * j + i + 1) * LANES],
+                env["pair_sem"].at[3 * j + i],
+            )
+            copy.start()
+            copies.append(copy)
+    return copies
 
 
 def line_kernel(plan, count, chunks, slack, *refs):
@@ -570,9 +767,13 @@
     }
     for name in plan["held"]:
         loads[name].start()
-    axis_barrier([("tp", count)])
+    started = plan["start"](env) if plan["start"] else []
+    seq_count = plan["seq_count"]
+    axis_barrier([("tp", count)] + ([("seq", seq_count)] if seq_count else []))
     if "sums" in env:
         env["sums"][...] = jnp.zeros_like(env["sums"])
+    if seq_count:
+        split_start(env, seq_count)
 
     def own_rows(c):
         return pl.ds(pl.multiple_of(c * size, size), size)
@@ -741,6 +942,8 @@
                 pl.when(free & (turn >= low) & (turn < high))(
                     lambda index=index, low=low: run_task(index, turn - low, slot)
                 )
+        if seq_count:
+            pl.when(t == chunks + ahead)(lambda: full_start(env, count))
         if plan["rows_done"]:
             done_a = t - ahead - from_first - (GROUP - 1)
             done_b = t - ahead - from_last - (GROUP - 1)
@@ -758,6 +961,8 @@
     for name in plan["held"]:
         if name not in plan["late"]:
             loads[name].wait()
+    for copy in started:
+        copy.wait()
     if plan["before"]:
         plan["before"](env)
     lax.fori_loop(0, steps, step, 0)
@@ -770,6 +975,8 @@
             stage_copy(index, turn - starts_at[index], turn % 2).wait()
     if plan["after"]:
         plan["after"](env)
+    if seq_count:
+        norm_finish(env, seq_count, count)
 
     def drain(c, carry):
         @pl.when(jnp.logical_not(first))
@@ -789,9 +996,10 @@
 
 def line_sum(
     finish, count, held, vecs, parts, collective_id, *, tokens, late=(), tasks=(), owns=(), sent=(),
-    scratch=(), before=None, rows_done=None, after=None, micros=110,
+    scratch=(), loose=(), start=None, before=None, rows_done=None, after=None, seq_count=0, micros=110,
 ):
-    width = held[parts[0][1]].shape[0]
+    names = dict(scratch)
+    width = (held.get(parts[0][1]) if parts[0][1] in held else names[parts[0][1]]).shape[0]
     half = tokens // 2
     depth = tokens if any(task[0] == "weight" for task in tasks) else LANES
     stage_width = max([shape.shape[1] for _, shape in sent] + [LANES])
@@ -808,8 +1016,10 @@
         for name in ("rsa_s", "rsa_r", "rsb_s", "rsb_r", "aga_s", "aga_r", "agb_s", "agb_r")
     ]
     scratch = list(scratch) + fixed
+    loose = dict(loose)
     order = (
         ["source " + name for name in held]
+        + list(loose)
         + list(vecs)
         + ["out"]
         + [name for name, _ in owns]
@@ -824,6 +1034,8 @@
         parts=parts,
         late=late,
         tasks=tasks,
+        start=start,
+        seq_count=seq_count,
         before=before,
         rows_done=rows_done,
         after=after,
@@ -835,7 +1047,7 @@
         out_shape=[jax.ShapeDtypeStruct((tokens, width), BF16)]
         + [shape for _, shape in owns]
         + [shape for _, shape in sent],
-        in_specs=[any_space] * len(held) + [whole] * len(vecs),
+        in_specs=[any_space] * (len(held) + len(loose)) + [whole] * len(vecs),
         out_specs=[whole] * (1 + len(owns)) + [any_space] * len(sent),
         scratch_shapes=[pltpu.VMEM(array.shape, array.dtype) for array in held.values()]
         + [shape for _, shape in scratch],
@@ -843,7 +1055,7 @@
             collective_id=collective_id, has_side_effects=True, vmem_limit_bytes=VMEM_LIMIT
         ),
         cost_estimate=cost(micros),
-    )(*held.values(), *vecs.values())
+    )(*held.values(), *loose.values(), *vecs.values())
 
 
 def axis_barrier(counts):
@@ -857,7 +1069,7 @@
     pl.semaphore_wait(barrier, sum(count - 1 for _, count in counts))
 
 
-def share(axis, count, pick, landed, send_sem, recv_sem):
+def share(axis, count, pick, landed, send_sem, recv_sem, start=True):
     me = lax.axis_index(axis)
     copies = []
     for k in range(1, count):
@@ -870,7 +1082,8 @@
             device_id={axis: device},
             device_id_type=MESH,
         )
-        copy.start()
+        if start:
+            copy.start()
         copies.append(copy)
     return copies
 
@@ -880,80 +1093,6 @@
     for k in range(1, count):
         total = total + landed[k]
     return total
-
-
-def tp_sum_kernel(count, x_ref, out_ref, landed, send_sem, recv_sem):
-    axis_barrier([("tp", count)])
-    copies = share("tp", count, lambda d: x_ref, landed, send_sem, recv_sem)
-    landed[lax.axis_index("tp")] = x_ref[...]
-    for copy in copies:
-        copy.wait()
-    out_ref[...] = total_of(landed, count)
-
-
-def tp_sum(values, count, collective_id):
-    whole = pl.BlockSpec(memory_space=pltpu.VMEM)
-    return pl.pallas_call(
-        functools.partial(tp_sum_kernel, count),
-        out_shape=jax.ShapeDtypeStruct(values.shape, F32),
-        in_specs=[whole],
-        out_specs=whole,
-        scratch_shapes=[
-            pltpu.VMEM((count,) + values.shape, F32),
-            pltpu.SemaphoreType.DMA((count,)),
-            pltpu.SemaphoreType.DMA((count,)),
-        ],
-        compiler_params=pltpu.CompilerParams(collective_id=collective_id, has_side_effects=True),
-        cost_estimate=cost(5),
-    )(values)
-
-
-def norm_sum_kernel(
-    seq_count, tp_count, full_ref, split_ref, own_ref, sum_ref,
-    tp_landed, summed, own_landed, split_landed, sem_a, sem_b, sem_c, sem_d, sem_e, sem_f,
-):
-    me = lax.axis_index("seq")
-    axis_barrier([("seq", seq_count), ("tp", tp_count)])
-    tp_copies = share("tp", tp_count, lambda d: full_ref, tp_landed, sem_a, sem_b)
-    split_copies = share("seq", seq_count, lambda d: split_ref, split_landed, sem_c, sem_d)
-    tp_landed[lax.axis_index("tp")] = full_ref[...]
-    split_landed[me] = split_ref[...]
-    for copy in tp_copies:
-        copy.wait()
-    summed[...] = total_of(tp_landed, tp_count)
-    own_copies = share("seq", seq_count, lambda d: summed.at[d], own_landed, sem_e, sem_f)
-    own_landed[me] = summed[me]
-    for copy in split_copies:
-        copy.wait()
-    sum_ref[...] = total_of(split_landed, seq_count)
-    for copy in own_copies:
-        copy.wait()
-    own_ref[...] = total_of(own_landed, seq_count)
-
-
-def norm_sum(full, split, seq_count, tp_count, collective_id):
-    whole = pl.BlockSpec(memory_space=pltpu.VMEM)
-    piece = full.shape[1:]
-    return pl.pallas_call(
-        functools.partial(norm_sum_kernel, seq_count, tp_count),
-        out_shape=[
-            jax.ShapeDtypeStruct(piece, F32),
-            jax.ShapeDtypeStruct(split.shape, F32),
-        ],
-        in_specs=[whole] * 2,
-        out_specs=[whole] * 2,
-        scratch_shapes=[
-            pltpu.VMEM((tp_count,) + full.shape, F32),
-            pltpu.VMEM(full.shape, F32),
-            pltpu.VMEM((seq_count,) + piece, F32),
-            pltpu.VMEM((seq_count,) + split.shape, F32),
-            pltpu.SemaphoreType.DMA((tp_count,)),
-            pltpu.SemaphoreType.DMA((tp_count,)),
-        ]
-        + [pltpu.SemaphoreType.DMA((seq_count,))] * 4,
-        compiler_params=pltpu.CompilerParams(collective_id=collective_id, has_side_effects=True),
-        cost_estimate=cost(10),
-    )(full, split)
 
 
 def matmul(left, right, left_dim, right_dim, kind=F32):
@@ -968,13 +1107,9 @@
     place_float = positions.astype(F32)[..., None]
     angles = place_float * theta_rate
     power = jnp.log(zeta_base) * place_float / 512.0
-    cos_part, sin_part = jnp.cos(angles), jnp.sin(angles)
-    grow, shrink = jnp.exp(power), jnp.exp(-power)
-    cos_full = jnp.concatenate([cos_part] * 4, axis=-1)
-    sin_full = jnp.concatenate([-sin_part, sin_part] * 2, axis=-1)
-    grow = jnp.concatenate([grow] * 4, axis=-1)
-    shrink = jnp.concatenate([shrink] * 4, axis=-1)
-    return jnp.stack([cos_full * grow, sin_full * grow, cos_full * shrink, sin_full * shrink])
+    return jnp.concatenate(
+        [jnp.cos(angles), jnp.sin(angles), jnp.exp(power), jnp.exp(-power)], axis=-1
+    )
 
 
 def body(
@@ -1006,9 +1141,12 @@
     hidden_width = w_up.shape[1] * tp_count
     groups = seq_count // row_count
 
-    gains = jnp.stack([first_gain, first_bias, second_gain, second_bias]).astype(F32)
-    head_vecs = jnp.stack([head_gain, head_bias]).astype(F32)
-    hidden_vecs = jnp.stack([hidden_gain, hidden_bias]).astype(F32)
+    vecs = jnp.concatenate(
+        [
+            first_gain, first_bias, second_gain, second_bias,
+            hidden_gain, hidden_bias, head_gain, head_bias,
+        ]
+    ).astype(F32)[None]
 
     seg_row = lax.dynamic_slice_in_dim(segment_ids, seq_index // groups, 1, 0)
     seg_col = seg_row.reshape(length, 1)
@@ -1023,7 +1161,7 @@
         w_query,
         w_key,
         w_value,
-        gains,
+        vecs,
         tables,
         seg_col,
         seg_row,
@@ -1045,7 +1183,7 @@
         finish_middle,
         tp_count,
         dict(mixed=mixed, w_out=w_out, block=block, cotangent=cotangent, w_down=w_down, w_up=w_up),
-        dict(gains=gains, head_vecs=head_vecs, hidden_vecs=hidden_vecs),
+        dict(vecs=vecs),
         (("head_act", "w_out"),),
         3,
         tokens=tokens,
@@ -1088,7 +1226,7 @@
             w_down=w_down,
             second_act=second_act,
         ),
-        dict(gains=gains),
+        dict(vecs=vecs),
         (("grad_up", "w_up"),),
         4,
         tokens=tokens,
@@ -1107,104 +1245,97 @@
     )
     block_out = lax.psum(down_part, "tp")
 
-    head_center = head_sums[0][:, None] / model_width
-    head_inverse = lax.rsqrt(
-        head_sums[1][:, None] / model_width - head_center * head_center + EPSILON
-    )
-    head_normed = (mixed.astype(F32) - head_center) * head_inverse
-
     def scatter(grad):
         return lax.psum_scatter(grad, "seq", scatter_dimension=0, tiled=True)
 
     w_down_grad = scatter(w_down_terms)
     w_up_grad = scatter(w_up_terms)
 
-    grad_head_act = matmul(grad_middle_low, w_out, 1, 0)
-    head_gain_grad = jnp.sum(grad_head_act * head_normed, axis=0)
-    head_bias_grad = jnp.sum(grad_head_act, axis=0)
-    head_scaled = grad_head_act * head_vecs[0:1]
-    head_back = tp_sum(
-        jnp.stack([jnp.sum(head_scaled, axis=-1), jnp.sum(head_scaled * head_normed, axis=-1)]),
+    grads, head_vec_grads = attend_back(
+        grad_middle_low,
+        w_out,
+        mixed,
+        head_sums,
+        vecs,
+        qkv_row,
+        o_row,
+        lse,
+        tables,
+        seg_col,
+        seg_row,
+        seq_count,
         tp_count,
-        11,
-    )
-    head_back = head_back[:, :, None] / model_width
-    grad_mixed = head_inverse * (head_scaled - head_back[0] - head_normed * head_back[1])
-    grads = attend_back(
-        grad_mixed.astype(BF16), qkv_row, o_row, lse, tables, seg_col, seg_row, seq_count, groups, 6
-    )
-    grad_query, grad_key, grad_value = grads[0], grads[1], grads[2]
-    head_terms = (
-        jnp.concatenate(
-            [
-                matmul(first_act, grad_query, 0, 0, BF16),
-                matmul(first_act, grad_key, 0, 0, BF16),
-                matmul(first_act, grad_value, 0, 0, BF16),
-                matmul(grad_middle_low, head_act, 0, 0, BF16),
-            ],
-            axis=1,
-        )
-    )
-    grad_query, head_terms, w_down_grad = lax.optimization_barrier(
-        (grad_query, head_terms, w_down_grad)
-    )
+        groups,
+        6,
+    )
+    head_terms = head_weights(first_act, grads, grad_middle_low, head_act)
+    grads, head_terms, w_down_grad = lax.optimization_barrier((grads, head_terms, w_down_grad))
     head_grads = scatter(head_terms)
-    w_query_grad, w_key_grad, w_value_grad, w_out_grad = jnp.split(
-        head_grads.astype(F32), 4, axis=1
-    )
-    input_grad, first_sums = line_sum(
+    own_width = model_width // seq_count
+    split_width = hidden_size + head_width
+    seq_sem = pltpu.SemaphoreType.DMA((seq_count,))
+    input_grad, _, norm_own, norm_split = line_sum(
         finish_first,
         tp_count,
+        dict(grads=grads, block=block, middle_grad=grad_middle_own),
         dict(
-            grad_query=grad_query,
-            w_query=w_query,
-            grad_key=grad_key,
-            w_key=w_key,
-            grad_value=grad_value,
-            w_value=w_value,
-            block=block,
-            middle_grad=grad_middle_own,
+            vecs=vecs,
+            second_sums=second_sums,
+            hidden_vec_grads=hidden_vec_grads,
+            head_vec_grads=head_vec_grads,
         ),
-        dict(gains=gains),
-        (("grad_query", "w_query"), ("grad_key", "w_key"), ("grad_value", "w_value")),
+        (("grads", "w_pairs"),),
         8,
         tokens=tokens,
-        owns=(("sums", sums_shape),),
-    )
-
-    own_width = model_width // seq_count
-    full = jnp.concatenate([jnp.sum(second_sums, axis=1), jnp.sum(first_sums, axis=1)])
-    full = full.reshape(4, seq_count, own_width).transpose(1, 0, 2)
-    full = full.reshape(seq_count, 4 * own_width // LANES, LANES)
-    hidden_vec_grads = jnp.sum(hidden_vec_grads, axis=1).reshape(-1)
-    split = jnp.concatenate([hidden_vec_grads, head_gain_grad, head_bias_grad])
-    norm_own, split = norm_sum(
-        full, split.reshape(split.shape[0] // LANES, LANES), seq_count, tp_count, 12
-    )
-    norm_own = norm_own.reshape(4, own_width)
-    split = split.reshape(-1)
-    split_sums = (
-        split[2 * hidden_size : 2 * hidden_size + head_width],
-        split[2 * hidden_size + head_width :],
-        split[:hidden_size],
-        split[hidden_size : 2 * hidden_size],
-    )
+        loose=dict(w_query=w_query, w_key=w_key, w_value=w_value),
+        owns=(
+            ("sums", sums_shape),
+            ("norm_own", shape_of((8, own_width))),
+            ("norm_split", shape_of((8, split_width))),
+        ),
+        scratch=(
+            ("w_pairs", pltpu.VMEM((model_width, 3 * head_width), BF16)),
+            ("pair_sem", pltpu.SemaphoreType.DMA((3 * head_width // LANES,))),
+            ("split", pltpu.VMEM((8, split_width), F32)),
+            ("split_landed", pltpu.VMEM((seq_count, 8, split_width), F32)),
+            ("full", pltpu.VMEM((8, model_width), F32)),
+            ("full_landed", pltpu.VMEM((tp_count, 8, model_width), F32)),
+            ("own_landed", pltpu.VMEM((seq_count, 8, own_width), F32)),
+            ("split_send", seq_sem),
+            ("split_recv", seq_sem),
+            ("full_send", pair_sem),
+            ("full_recv", pair_sem),
+            ("own_send", seq_sem),
+            ("own_recv", seq_sem),
+        ),
+        start=load_pairs,
+        seq_count=seq_count,
+    )
+    block_out, input_grad = lax.optimization_barrier((block_out, input_grad))
+
+    def head_grad(index):
+        columns = [
+            head_grads[:, (3 * j + index) * LANES : (3 * j + index + 1) * LANES]
+            for j in range(head_width // LANES)
+        ]
+        return jnp.concatenate(columns, axis=1).astype(F32)
+
     return (
         block_out.reshape(block_in.shape),
         input_grad.reshape(block_in.shape),
         norm_own[2],
         norm_own[3],
-        w_query_grad,
-        w_key_grad,
-        w_value_grad,
-        split_sums[0],
-        split_sums[1],
-        w_out_grad,
+        head_grad(0),
+        head_grad(1),
+        head_grad(2),
+        norm_split[0, hidden_size:],
+        norm_split[1, hidden_size:],
+        head_grads[:, 3 * head_width :].astype(F32),
         norm_own[0],
         norm_own[1],
         w_up_grad.astype(F32),
-        split_sums[2],
-        split_sums[3],
+        norm_split[0, :hidden_size],
+        norm_split[1, :hidden_size],
         w_down_grad.astype(F32),
     )
 

time: 682 us -> 657 us (0.963)
  Pallas kernels: 551 us -> 603 us
  waiting for transfers between devices: 38 us -> 5.98 us
  matrix products: 18.9 us -> 0 us
  local copies, waits for them, and re-layouts: 28.4 us -> 17.9 us
  other arithmetic: 23.1 us -> 13.2 us
    pallas_call x3, Pallas kernels: 394 us -> 437 us  [line_sum(): pl.pallas_call(functools.partial(line_kernel, plan, count, CHUNKS, SLACK)...]
    psum x1, waiting for transfers between devices: 37 us -> 0.03 us  [body(): block_out = lax.psum(down_part, 'tp')]
    dot_general x5 -> x0, matrix products: 18.9 us -> none  [dot(): lax.dot_general(left, right, (((left_dim,), (right_dim,)), ((), ())), pre...]
    pallas_call x3 -> x2, Pallas kernels: 95 us -> 104 us  [the longest x1 88.9 us: attend_back(): pl.pallas_call(functools.partial(back_kernel, count, tp_count, groups), o...]
  transfers between devices with their start and end apart: 4 -> 4, of which waited for: 1 -> 1; matrix products, arithmetic and copies ran while one was open for 6% -> 1% of each run, Pallas kernels for 32% -> 41%
where the time goes in v6:
time: 657 us; the launch traced here: 656 us
  Pallas kernels  603 us (92%)
  local copies, waits for them, and re-layouts  17.9 us (3%)
  between operations  15.3 us (2%)
  other arithmetic  13.2 us (2%)
    pallas_call x3, Pallas kernels, line_sum(): pl.pallas_call(functools.partial(line_kernel, plan, count, CHUNKS, SLACK)...  437 us
    pallas_call x1, Pallas kernels, attend_back(): pl.pallas_call(functools.partial(back_kernel, count, tp_count, groups), o...  88.9 us
    pallas_call x1, Pallas kernels, front(): pl.pallas_call(functools.partial(front_kernel, count, groups), out_shape=...  62.1 us
    pallas_call x1, Pallas kernels, head_weights(): pl.pallas_call(weight_kernel, grid=(model_width // ROWS,), out_shape=jax....  15.2 us
  transfers between devices with their start and end apart: 4, of which 1 were waited for; matrix products, arithmetic and copies ran while one was open for 1% of the time, Pallas kernels for 41%

profile of v6, /device:TPU:0, one launch (start us, length us, event | category | flops | bytes accessed | tf_op | source)
XLA Modules:
  0.0 656.0 jit_solution(5998646318388823350)
XLA Ops:
  10.1 0.7 constant_dynamic-update-slice_fusion.6
  10.8 0.7 constant_dynamic-update-slice_fusion.5
  15.6 1.0 copy.39.segc_ref
  16.7 2.0 multiply_cosine_fusion
  18.7 1.3 pad_maximum_fusion.packed_ref
  19.9 62.1 %shard_map.288 = (bf16[1024,2048]{1,0:T(8,128)(2,1)}, bf16[4,1024,384]{2,1,0:T(8,128)(2,1)}, bf16[4,1024,128]{2,1,0:T(8,128)(2,1)}, f32[4,8,1024]{2,1,0:T(8,128)}, bf16[1024,512]{1,0:T(8,128)(2,1)}) custom-call(bf16[1024,2048]{1,0:T(8,128)(2,1)} %bitcast.28, bf16[2048,512]{1,0:T(8,128)(2,1)} %refs_3_.1, bf16[2048,512]{1,0:T(8,128)(2,1)} %refs_4_.3, ...), custom_call_target="tpu_custom_call" | custom-call | flops 65999998976 | tf_op jit(solution)/shard_map/pallas_call | solution.py:259
  82.1 144.8 %shard_map.289 = (bf16[1024,2048]{1,0:T(8,128)(2,1)}, f32[512,2048]{1,0:T(8,128)}, bf16[1024,512]{1,0:T(8,128)(2,1)}, f32[8,1024]{1,0:T(8,128)}, bf16[1024,2048]...) custom-call(bf16[1024,512]{1,0:T(8,128)(2,1)} %get-tuple-element.44.refs_0_.mixed_ref, ...), custom_call_target="tpu_custom_call" | custom-call | flops 153999998976 | tf_op jit(solution)/shard_map/pallas_call | solution.py:1045
  226.9 128.2 %shard_map.290 = (bf16[1024,2048]{1,0:T(8,128)(2,1)}, f32[2,8,2048]{2,1,0:T(8,128)}, f32[512,2048]{1,0:T(8,128)}, bf16[1024,2048]{1,0:T(8,128)(2,1)}, bf16[2048,...) custom-call(bf16[1024,2048]{1,0:T(8,128)(2,1)} %get-tuple-element.45.refs_0_, bf16[2048,2048]{1,0:T(8,128)(2,1)} %refs_1_.3, ...), custom_call_target="tpu_custom_call" | custom-call | flops 121000001536 | tf_op jit(solution)/shard_map/pallas_call | solution.py:1045
  356.5 88.9 %shard_map.291 = (bf16[1024,1536]{1,0:T(8,128)(2,1)}, f32[2,8,512]{2,1,0:T(8,128)}) custom-call(bf16[1024,2048]{1,0:T(8,128)(2,1)} %get-tuple-element.50.low_ref, bf16[2048,512]{1,0:T(8,128)(2,1)} %wout_ref.1, bf16[1024,512]{1,0:T(8,128)(2,1)} %get-tuple-element.44.refs_0_.mixed_ref, f32[8,1024]{1,0:T(8,128)} %get-tuple-element.51.sums_ref, ...), custom_call_target="tpu_custom_call" | custom-call | flops 76999999488 | tf_op jit(solution)/shard_map/pallas_call | solution.py:448
  445.4 15.2 %shard_map.292 = bf16[2048,2048]{1,0:T(8,128)(2,1)} custom-call(bf16[1024,2048]{1,0:T(8,128)(2,1)} %get-tuple-element.56.act_ref, bf16[1024,1536]{1,0:T(8,128)(2,1)} %get-tuple-element.59.grads_ref.refs_0_, bf16[1024,2048]{1,0:T(8,128)(2,1)} %get-tuple-element.50.low_ref, bf16[1024,512]{1,0:T(8,128)(2,1)} %get-tuple-element.57.head_ref), custom_call_target="tpu_custom_call" | custom-call | flops 11000000512 | tf_op jit(solution)/shard_map/pallas_call | solution.py:493
  460.6 4.7 reduce-scatter.4.cloned.1.call-done
  465.3 164.3 %shard_map.293 = (bf16[1024,2048]{1,0:T(8,128)(2,1)}, f32[2,8,2048]{2,1,0:T(8,128)}, f32[8,256]{1,0:T(8,128)}, f32[8,2560]{1,0:T(8,128)}) custom-call(bf16[1024,1536]{1,0:T(8,128)(2,1)} %get-tuple-element.59.grads_ref.refs_0_, bf16[1024,2048]{1,0:T(8,128)(2,1)} %bitcast.30, f32[512,2048]{1,0:T(8,128)} %get-tuple-element.60.refs_2_, ...), custom_call_target="tpu_custom_call" | custom-call | flops 121000001536 | tf_op jit(solution)/shard_map/pallas_call | solution.py:1045
  629.6 1.6 convert_element_type.46
  631.2 2.8 convert_element_type.45
  634.6 1.4 fusion.3
  635.9 1.5 fusion.2
  637.5 1.4 fusion.1
  638.9 0.8 maximum_convert_fusion.2
  639.7 0.8 maximum_convert_fusion.1
  640.5 0.8 maximum_convert_fusion
  641.3 1.8 slice_convert_fusion
  643.2 2.1 copy.51
  645.3 1.6 copy-done.3
  646.9 2.0 copy.52
  (37 shorter events, 8.2 us)
Async XLA Ops:
  8.0 0.8 copy-start
  8.0 457.3 %reduce-scatter.4.cloned.1.call-start = ((), (), s32[]{:S(2)}) async-start(), calls=%async_computation.4 | async-start | bytes 9437184 | tf_op jit(solution)/shard_map/reduce_scatter | solution.py:1249
  8.8 11.1 %copy-start.5 = (s32[1,1024]{1,0:T(1,128)}, s32[1,1024]{1,0:T(1,128)S(1)}, u32[]{:S(2)}) copy-start(s32[1,1024]{1,0:T(1,128)S(1)} %constant_dynamic-slice_fusion.segr_ref) | copy-start | bytes 12292
  355.1 274.5 %all-reduce.2.cloned.1.call-start = ((), (), s32[]{:S(2)}) async-start(), calls=%async_computation.3 | async-start | bytes 8388608 | tf_op jit(solution)/shard_map/psum | solution.py:1246
  355.7 275.5 %reduce-scatter.8.cloned.1.call-start = ((), (), s32[]{:S(2)}) async-start(), calls=%async_computation.6 | async-start | bytes 9437184 | tf_op jit(solution)/shard_map/reduce_scatter | solution.py:1249
  356.5 281.0 %reduce-scatter.6.cloned.1.call-start = ((), (), s32[]{:S(2)}) async-start(), calls=%async_computation.5 | async-start | bytes 9437184 | tf_op jit(solution)/shard_map/reduce_scatter | solution.py:1249
  465.3 164.3 %copy-start.4 = (bf16[256,2048]{1,0:T(8,128)(2,1)S(1)}, bf16[256,2048]{1,0:T(8,128)(2,1)}, u32[]{:S(2)}) copy-start(bf16[256,2048]{1,0:T(8,128)(2,1)} %reduce-scatter.4.cloned.1.call-done) | copy-start | bytes 3145732
  629.6 4.4 copy-start.6
  637.5 5.7 copy-start.2
  643.1 3.7 copy-start.3
  643.2 5.7 copy-start.1
Sparse Core Ops, SparseCore 0:
  355.3 109.9 reduce-scatter.3
  468.7 71.2 reduce-scatter.7
  543.9 71.2 reduce-scatter.5
Sparse Core Ops, SparseCore 1:
  358.0 186.3 all-reduce.1

commit v7 on v6

--- a/solution.py
+++ b/solution.py
@@ -284,13 +284,14 @@
     )(x, w_query, w_key, w_value, vecs, tables, seg_col, seg_row)
 
 
-def back_kernel(
-    count, tp_count, groups, low_ref, wout_ref, mixed_ref, sums_ref, vecs_ref,
-    qkv_ref, o_ref, lse_ref, packed_ref, segc_ref, segr_ref, grads_ref, vec_grads_ref,
-    do_ref, scaled, part, landed, tab_ref,
-    do_row, made, bias, qs, ks, kms, dos, delta, dq, dk, dv,
-    tp_send, tp_recv, send_sem, recv_sem, back_send_sem, back_recv_sem,
-):
+def back_work(env, count, tp_count, groups):
+    low_ref, wout_ref, mixed_ref = env["low"], env["w_out"], env["mixed"]
+    sums_ref, qkv_ref, o_ref, lse_ref = env["head_sums"], env["qkv"], env["o"], env["lse"]
+    segc_ref, segr_ref, tab_ref, bias = env["seg_col"], env["seg_row"], env["tables"], env["bias"]
+    grads_ref, vec_grads_ref = env["grads"], env["head_vec_grads"]
+    do_ref, scaled, part = env["do"], env["scaled"], env["head_part"]
+    do_row, made, delta = env["do_row"], env["made"], env["delta"]
+    qs, ks, kms, dos, dq, dk, dv = (env[name] for name in ("qs", "ks", "kms", "dos", "dq", "dk", "dv"))
     me = lax.axis_index("seq")
     pairs, length = qkv_ref.shape[:2]
     tokens, features = low_ref.shape
@@ -298,9 +299,7 @@
     span = length // count
     blocks = length // BLOCK
     mine, row = lax.rem(me, groups), me // groups
-    axis_barrier([("seq", count), ("tp", tp_count)])
-    gain = head_vec(vecs_ref, head_width, 0)
-    vec_grads_ref[...] = jnp.zeros_like(vec_grads_ref)
+    gain = head_vec(env["vecs"], head_width, 0)
 
     def normed_rows(rows):
         first, second = to_columns(sums_ref[:, rows], 2)
@@ -308,7 +307,7 @@
         inverse = lax.rsqrt(second / features - center * center + EPSILON)
         return (mixed_ref[rows, :].astype(F32) - center) * inverse, inverse
 
-    def head_terms(r, carry):
+    def head_terms(r):
         wide = pl.ds(pl.multiple_of(r * BLOCK, BLOCK), BLOCK)
         scaled[wide, :] = dot(low_ref[wide, :], wout_ref[...], 1, 0)
         for k in range(BLOCK // LANES):
@@ -325,10 +324,9 @@
                     jnp.sum(grad * normed, axis=-1, keepdims=True),
                 ]
             )
-        return carry
-
-    lax.fori_loop(0, tokens // BLOCK, head_terms, 0)
-    tp_total(part, landed, tp_send, tp_recv, tp_count)
+
+    def part_copies(start):
+        return share("tp", tp_count, lambda d: part, env["head_landed"], *env_pair(env, "head"), start)
 
     def head_apply(r, carry):
         rows = row_block(r)
@@ -338,15 +336,13 @@
         do_ref[rows, :] = (inverse * grad).astype(BF16)
         return carry
 
-    lax.fori_loop(0, tokens // LANES, head_apply, 0)
-
     def there(p, k):
         device = lax.rem(me + k, count)
         return send(
             do_ref.at[spans(device // groups, span), spans(lax.rem(device, groups) * pairs + p, LANES)],
             do_row.at[p, spans(me, span), :],
-            send_sem.at[p, k],
-            recv_sem.at[p, k],
+            env["there_send"].at[p, k],
+            env["there_recv"].at[p, k],
             device,
         )
 
@@ -355,8 +351,8 @@
         return send(
             made.at[p, spans(device, span), :],
             grads_ref.at[spans(row, span), spans(mine * pairs + p, 3 * LANES)],
-            back_send_sem.at[p, k],
-            back_recv_sem.at[p, k],
+            env["back_send"].at[p, k],
+            env["back_recv"].at[p, k],
             device,
         )
 
@@ -366,18 +362,18 @@
         do_row[p, spans(me, span), :] = do_ref[spans(row, span), spans(mine * pairs + p, LANES)]
         return carry
 
-    lax.fori_loop(0, pairs, share_out, 0)
-    expand_tables(packed_ref, tab_ref)
-    for kb in range(blocks):
-        rows = block_rows(kb)
-        start = kb * BLOCK
-        shape = (BLOCK, length - start)
-        same = segc_ref[rows, :] == segr_ref[:, start:]
-        key = lax.broadcasted_iota(jnp.int32, shape, 0)
-        query = lax.broadcasted_iota(jnp.int32, shape, 1)
-        bias[rows, start:] = jnp.where(same & (key <= query), 0.0, MASKED)
-
-    def attend(p, carry):
+    def prepare():
+        expand_tables(env["packed"], tab_ref)
+        for kb in range(blocks):
+            rows = block_rows(kb)
+            start = kb * BLOCK
+            shape = (BLOCK, length - start)
+            same = segc_ref[rows, :] == segr_ref[:, start:]
+            key = lax.broadcasted_iota(jnp.int32, shape, 0)
+            query = lax.broadcasted_iota(jnp.int32, shape, 1)
+            bias[rows, start:] = jnp.where(same & (key <= query), 0.0, MASKED)
+
+    def pair_start(p):
         for qb in range(blocks):
             rows = block_rows(qb)
             q = rotated(qkv_ref[p, rows, :LANES], tab_ref, 0, rows) * (HEAD**-0.5)
@@ -403,19 +399,22 @@
             prod = jnp.transpose(grad * o_ref[p, rows, :].astype(F32))
             delta[0:1, rows] = jnp.sum(prod[:HEAD], axis=0, keepdims=True)
             delta[1:2, rows] = jnp.sum(prod[HEAD:], axis=0, keepdims=True)
-        for qb in range(blocks):
-            cols = block_rows(qb)
-            for kb in range(qb + 1):
-                rows = block_rows(kb)
-                value = qkv_ref[p, rows, 2 * LANES :]
-                for h in range(2):
-                    scores = dot(ks[rows, :], qs[h, cols, :], 1, 1) + bias[rows, cols]
-                    probs = jnp.exp(scores - lse_ref[p, h : h + 1, cols])
-                    grads = dot(value, dos[h, cols, :], 1, 1)
-                    dscores = (probs * (grads - delta[h : h + 1, cols])).astype(BF16)
-                    dv[rows, :] += dot(probs.astype(BF16), dos[h, cols, :], 1, 0)
-                    dk[rows, :] += dot(dscores, qs[h, cols, :], 1, 0)
-                    dq[cols, :] += dot(dscores, kms[h, rows, :], 0, 0)
+
+    def pair_block(p, qb):
+        cols = block_rows(qb)
+        for kb in range(qb + 1):
+            rows = block_rows(kb)
+            value = qkv_ref[p, rows, 2 * LANES :]
+            for h in range(2):
+                scores = dot(ks[rows, :], qs[h, cols, :], 1, 1) + bias[rows, cols]
+                probs = jnp.exp(scores - lse_ref[p, h : h + 1, cols])
+                grads = dot(value, dos[h, cols, :], 1, 1)
+                dscores = (probs * (grads - delta[h : h + 1, cols])).astype(BF16)
+                dv[rows, :] += dot(probs.astype(BF16), dos[h, cols, :], 1, 0)
+                dk[rows, :] += dot(dscores, qs[h, cols, :], 1, 0)
+                dq[cols, :] += dot(dscores, kms[h, rows, :], 0, 0)
+
+    def pair_end(p):
         for qb in range(blocks):
             rows = block_rows(qb)
             grad = dq[rows, :] * (HEAD**-0.5)
@@ -425,59 +424,50 @@
         for k in range(1, count):
             back(p, k).start()
         grads_ref[spans(row, span), spans(mine * pairs + p, 3 * LANES)] = made[p, spans(me, span), :]
-        return carry
-
-    lax.fori_loop(0, pairs, attend, 0)
-
-    def drain(p, carry):
-        for k in range(1, count):
-            there(p, k).wait_send()
-            back(p, k).wait()
-        return carry
-
-    lax.fori_loop(0, pairs, drain, 0)
-
-
-def attend_back(
-    low, w_out, mixed, head_sums, vecs, qkv, o, lse, tables, seg_col, seg_row, count, tp_count,
-    groups, collective_id,
-):
-    tokens, head_width = mixed.shape
-    pairs, length = qkv.shape[:2]
-    whole = pl.BlockSpec(memory_space=pltpu.VMEM)
-    return pl.pallas_call(
-        functools.partial(back_kernel, count, tp_count, groups),
-        out_shape=[
-            jax.ShapeDtypeStruct((tokens, 3 * head_width), BF16),
-            jax.ShapeDtypeStruct((2, 8, head_width), F32),
-        ],
-        in_specs=[whole] * 11,
-        out_specs=[whole] * 2,
-        scratch_shapes=[
-            pltpu.VMEM((tokens, head_width), BF16),
-            pltpu.VMEM((tokens, head_width), F32),
-            pltpu.VMEM((8, tokens), F32),
-            pltpu.VMEM((tp_count, 8, tokens), F32),
-            pltpu.VMEM((4, length, LANES), F32),
-            pltpu.VMEM((pairs, length, LANES), BF16),
-            pltpu.VMEM((pairs, length, 3 * LANES), BF16),
-            pltpu.VMEM((length, length), F32),
-            pltpu.VMEM((2, length, LANES), BF16),
-            pltpu.VMEM((length, LANES), BF16),
-            pltpu.VMEM((2, length, LANES), BF16),
-            pltpu.VMEM((2, length, LANES), BF16),
-            pltpu.VMEM((8, length), F32),
-            pltpu.VMEM((length, LANES), F32),
-            pltpu.VMEM((length, LANES), F32),
-            pltpu.VMEM((length, LANES), F32),
-        ]
-        + [pltpu.SemaphoreType.DMA((tp_count,))] * 2
-        + [pltpu.SemaphoreType.DMA((pairs, count))] * 4,
-        compiler_params=pltpu.CompilerParams(
-            collective_id=collective_id, has_side_effects=True, vmem_limit_bytes=VMEM_LIMIT
-        ),
-        cost_estimate=cost(70),
-    )(low, w_out, mixed, head_sums, vecs, qkv, o, lse, tables, seg_col, seg_row)
+
+    head_steps = tokens // BLOCK
+    vec_grads_ref[...] = jnp.zeros_like(vec_grads_ref)
+
+    def step(t):
+        pl.when(t < head_steps)(lambda: head_terms(t))
+
+        @pl.when(t == head_steps - 1)
+        def _():
+            part_copies(True)
+            env["head_landed"][lax.axis_index("tp")] = part[...]
+
+        pl.when(t == head_steps)(prepare)
+
+        @pl.when(t == head_steps + 1)
+        def _():
+            for copy in part_copies(False):
+                copy.wait()
+            part[...] = total_of(env["head_landed"], tp_count)
+            lax.fori_loop(0, tokens // LANES, head_apply, 0)
+            lax.fori_loop(0, pairs, share_out, 0)
+
+        turn = t - (head_steps + 3)
+        p = turn // blocks
+        for qb in range(blocks):
+
+            @pl.when((turn >= 0) & (turn < pairs * blocks) & (lax.rem(turn + 8 * blocks, blocks) == qb))
+            def _():
+                if qb == 0:
+                    pair_start(p)
+                pair_block(p, qb)
+                if qb == blocks - 1:
+                    pair_end(p)
+
+    def end():
+        def drain(p, carry):
+            for k in range(1, count):
+                there(p, k).wait_send()
+                back(p, k).wait()
+            return carry
+
+        lax.fori_loop(0, pairs, drain, 0)
+
+    return step, end, head_steps + 3 + pairs * blocks
 
 
 def weight_kernel(act_ref, grads_ref, low_ref, head_ref, out_ref):
@@ -746,7 +736,7 @@
     env = dict(zip(plan["order"], refs, strict=True))
     finish, parts, tasks = plan["finish"], plan["parts"], plan["tasks"]
     num_task = len(tasks)
-    out_ref, part = env["out"], env["part"]
+    out_ref = env["out"]
     in_a, in_b = env["in_a"], env["in_b"]
     rsa_s, rsa_r, rsb_s, rsb_r = (env[name] for name in ("rsa_s", "rsa_r", "rsb_s", "rsb_r"))
     aga_s, aga_r, agb_s, agb_r = (env[name] for name in ("aga_s", "aga_r", "agb_s", "agb_r"))
@@ -769,7 +759,7 @@
         loads[name].start()
     started = plan["start"](env) if plan["start"] else []
     seq_count = plan["seq_count"]
-    axis_barrier([("tp", count)] + ([("seq", seq_count)] if seq_count else []))
+    axis_barrier([("tp", count)] + ([("seq", plan["seq_barrier"])] if plan["seq_barrier"] else []))
     if "sums" in env:
         env["sums"][...] = jnp.zeros_like(env["sums"])
     if seq_count:
@@ -816,12 +806,16 @@
     def reduce_step(t, c, offset, place, rows, landed, move, gather, starts, ends):
         here = rows(c)
         own = own_rows(c)
-        row = place * GROUP * size + c * size - block_start(t, offset)
-        term_rows = pl.ds(pl.multiple_of(row, size), size)
+
+        def term():
+            if not parts:
+                return env["ready"][here, :].astype(F32)
+            row = place * GROUP * size + c * size - block_start(t, offset)
+            return env["part"][pl.ds(pl.multiple_of(row, size), size), :]
 
         @pl.when(starts)
         def _():
-            landed[own, :] = part[term_rows, :].astype(BF16)
+            landed[own, :] = term().astype(BF16)
             move(c).start()
 
         @pl.when(jnp.logical_not(starts))
@@ -830,12 +824,12 @@
 
         @pl.when(jnp.logical_not(starts | ends))
         def _():
-            landed[own, :] = (landed[own, :].astype(F32) + part[term_rows, :]).astype(BF16)
+            landed[own, :] = (landed[own, :].astype(F32) + term()).astype(BF16)
             move(c).start()
 
         @pl.when(ends)
         def _():
-            total = landed[own, :].astype(F32) + part[term_rows, :]
+            total = landed[own, :].astype(F32) + term()
             out_ref[here, :] = finish(total, here, own, env).astype(BF16)
             gather(c).start()
 
@@ -861,7 +855,7 @@
             for left, right in parts:
                 rows = jnp.concatenate([env[left][top, :], env[left][low, :]], axis=0)
                 total = total + dot(rows, env[right][cols, :], 1, 1)
-            part[:, cols] = total
+            env["part"][:, cols] = total
             return carry
 
         lax.fori_loop(0, width // TILE, columns, 0)
@@ -911,7 +905,8 @@
     staged = any(task[0] != "keep" for task in tasks)
 
     def step(t, carry):
-        pl.when(lax.rem(t, GROUP) == 0)(lambda: make_parts(t))
+        if parts:
+            pl.when(lax.rem(t, GROUP) == 0)(lambda: make_parts(t))
         when_chunk(
             t - from_last,
             lambda c: reduce_step(t, c, from_last, 0, a_rows, in_a, reduce_a, gather_a, last, first),
@@ -942,6 +937,8 @@
                 pl.when(free & (turn >= low) & (turn < high))(
                     lambda index=index, low=low: run_task(index, turn - low, slot)
                 )
+        if work_step:
+            work_step(t)
         if seq_count:
             pl.when(t == chunks + ahead)(lambda: full_start(env, count))
         if plan["rows_done"]:
@@ -965,6 +962,10 @@
         copy.wait()
     if plan["before"]:
         plan["before"](env)
+    work_step = None
+    if plan["work"]:
+        work_step, work_end, work_steps = plan["work"](env)
+        assert work_steps <= steps
     lax.fori_loop(0, steps, step, 0)
     if num_task:
         assert (steps // GROUP) * per_group >= task_total
@@ -975,6 +976,8 @@
             stage_copy(index, turn - starts_at[index], turn % 2).wait()
     if plan["after"]:
         plan["after"](env)
+    if work_step:
+        work_end()
     if seq_count:
         norm_finish(env, seq_count, count)
 
@@ -996,17 +999,21 @@
 
 def line_sum(
     finish, count, held, vecs, parts, collective_id, *, tokens, late=(), tasks=(), owns=(), sent=(),
-    scratch=(), loose=(), start=None, before=None, rows_done=None, after=None, seq_count=0, micros=110,
+    scratch=(), loose=(), start=None, before=None, rows_done=None, after=None, work=None,
+    seq_count=0, seq_barrier=0, micros=110,
 ):
     names = dict(scratch)
-    width = (held.get(parts[0][1]) if parts[0][1] in held else names[parts[0][1]]).shape[0]
+    if parts:
+        width = (held.get(parts[0][1]) if parts[0][1] in held else names[parts[0][1]]).shape[0]
+    else:
+        width = held["ready"].shape[1]
     half = tokens // 2
     depth = tokens if any(task[0] == "weight" for task in tasks) else LANES
     stage_width = max([shape.shape[1] for _, shape in sent] + [LANES])
     fixed = [
         ("in_a", pltpu.VMEM((half, width), BF16)),
         ("in_b", pltpu.VMEM((half, width), BF16)),
-        ("part", pltpu.VMEM((2 * GROUP * half // CHUNKS, width), F32)),
+        ("part", pltpu.VMEM((2 * GROUP * half // CHUNKS if parts else 8, width), F32)),
         ("turned", pltpu.VMEM((ROWS, depth), BF16)),
         ("stage", pltpu.VMEM((2, ROWS if sent else 16, stage_width), BF16)),
         ("load_sem", pltpu.SemaphoreType.DMA((len(held),))),
@@ -1035,7 +1042,9 @@
         late=late,
         tasks=tasks,
         start=start,
+        work=work,
         seq_count=seq_count,
+        seq_barrier=seq_barrier or seq_count,
         before=before,
         rows_done=rows_done,
         after=after,
@@ -1243,30 +1252,65 @@
             ("w_up_terms", weight_shape),
         ),
     )
-    block_out = lax.psum(down_part, "tp")
-
     def scatter(grad):
         return lax.psum_scatter(grad, "seq", scatter_dimension=0, tiled=True)
 
     w_down_grad = scatter(w_down_terms)
     w_up_grad = scatter(w_up_terms)
 
-    grads, head_vec_grads = attend_back(
-        grad_middle_low,
-        w_out,
-        mixed,
-        head_sums,
-        vecs,
-        qkv_row,
-        o_row,
-        lse,
-        tables,
-        seg_col,
-        seg_row,
-        seq_count,
+    pairs = head_width // groups // LANES
+    many = pltpu.SemaphoreType.DMA((pairs, seq_count))
+    pair_rows = pltpu.VMEM((length, LANES), BF16)
+    pair_sums = pltpu.VMEM((length, LANES), F32)
+    pair_heads = pltpu.VMEM((2, length, LANES), BF16)
+    block_out, grads, head_vec_grads = line_sum(
+        lambda total, here, own, env: total,
         tp_count,
-        groups,
-        6,
+        dict(
+            ready=down_part,
+            low=grad_middle_low,
+            w_out=w_out,
+            mixed=mixed,
+            head_sums=head_sums,
+            qkv=qkv_row,
+            o=o_row,
+            lse=lse,
+            packed=tables,
+        ),
+        dict(vecs=vecs, seg_col=seg_col, seg_row=seg_row),
+        (),
+        5,
+        tokens=tokens,
+        owns=(
+            ("grads", shape_of((tokens, 3 * head_width), BF16)),
+            ("head_vec_grads", shape_of((2, 8, head_width))),
+        ),
+        scratch=(
+            ("do", pltpu.VMEM((tokens, head_width), BF16)),
+            ("scaled", pltpu.VMEM((tokens, head_width), F32)),
+            ("head_part", pltpu.VMEM((8, tokens), F32)),
+            ("head_landed", landed),
+            ("tables", pltpu.VMEM((4, length, LANES), F32)),
+            ("do_row", pltpu.VMEM((pairs, length, LANES), BF16)),
+            ("made", pltpu.VMEM((pairs, length, 3 * LANES), BF16)),
+            ("bias", pltpu.VMEM((length, length), F32)),
+            ("qs", pair_heads),
+            ("ks", pair_rows),
+            ("kms", pair_heads),
+            ("dos", pair_heads),
+            ("delta", pltpu.VMEM((8, length), F32)),
+            ("dq", pair_sums),
+            ("dk", pair_sums),
+            ("dv", pair_sums),
+            ("head_send", pair_sem),
+            ("head_recv", pair_sem),
+            ("there_send", many),
+            ("there_recv", many),
+            ("back_send", many),
+            ("back_recv", many),
+        ),
+        work=lambda env: back_work(env, seq_count, tp_count, groups),
+        seq_barrier=seq_count,
     )
     head_terms = head_weights(first_act, grads, grad_middle_low, head_act)
     grads, head_terms, w_down_grad = lax.optimization_barrier((grads, head_terms, w_down_grad))
@@ -1311,7 +1355,6 @@
         start=load_pairs,
         seq_count=seq_count,
     )
-    block_out, input_grad = lax.optimization_barrier((block_out, input_grad))
 
     def head_grad(index):
         columns = [

time: 657 us -> 647 us (0.985)
    pallas_call x1 -> x0, Pallas kernels: 88.9 us -> none  [attend_back(): pl.pallas_call(functools.partial(back_kernel, count, tp_count, groups), o...]
    pallas_call x3 -> x4, Pallas kernels: 437 us -> 523 us  [line_sum(): pl.pallas_call(functools.partial(line_kernel, plan, count, CHUNKS, SLACK)...]
  transfers between devices with their start and end apart: 4 -> 3, of which waited for: 1 -> 0; matrix products, arithmetic and copies ran while one was open for 1% -> 1% of each run, Pallas kernels for 41% -> 41%
where the time goes in v7:
time: 647 us; the launch traced here: 646 us
  Pallas kernels  600 us (93%)
  local copies, waits for them, and re-layouts  17.9 us (3%)
  between operations  13.9 us (2%)
  other arithmetic  13.2 us (2%)
    pallas_call x4, Pallas kernels, line_sum(): pl.pallas_call(functools.partial(line_kernel, plan, count, CHUNKS, SLACK)...  523 us
    pallas_call x1, Pallas kernels, front(): pl.pallas_call(functools.partial(front_kernel, count, groups), out_shape=...  62.2 us
    pallas_call x1, Pallas kernels, head_weights(): pl.pallas_call(weight_kernel, grid=(model_width // ROWS,), out_shape=jax....  15.2 us
  transfers between devices with their start and end apart: 3, of which 0 were waited for; matrix products, arithmetic and copies ran while one was open for 1% of the time, Pallas kernels for 41%

profile of v7, /device:TPU:0, one launch (start us, length us, event | category | flops | bytes accessed | tf_op | source)
XLA Modules:
  0.0 646.2 jit_solution(11744900710106358765)
XLA Ops:
  9.2 0.7 constant_dynamic-update-slice_fusion.6
  9.9 0.7 constant_dynamic-update-slice_fusion.5
  10.6 0.7 constant_dynamic-update-slice_fusion.4
  14.8 1.0 copy.39.segc_ref.refs_10_
  15.8 2.0 multiply_cosine_fusion
  17.8 1.3 pad_maximum_fusion.packed_ref.refs_8_
  19.1 62.2 %shard_map.288 = (bf16[1024,2048]{1,0:T(8,128)(2,1)}, bf16[4,1024,384]{2,1,0:T(8,128)(2,1)}, bf16[4,1024,128]{2,1,0:T(8,128)(2,1)}, f32[4,8,1024]{2,1,0:T(8,128)}, bf16[1024,512]{1,0:T(8,128)(2,1)}) custom-call(bf16[1024,2048]{1,0:T(8,128)(2,1)} %bitcast.28, bf16[2048,512]{1,0:T(8,128)(2,1)} %refs_3_.1, bf16[2048,512]{1,0:T(8,128)(2,1)} %refs_4_.3, ...), custom_call_target="tpu_custom_call" | custom-call | flops 65999998976 | tf_op jit(solution)/shard_map/pallas_call | solution.py:259
  81.3 144.7 %shard_map.289 = (bf16[1024,2048]{1,0:T(8,128)(2,1)}, f32[512,2048]{1,0:T(8,128)}, bf16[1024,512]{1,0:T(8,128)(2,1)}, f32[8,1024]{1,0:T(8,128)}, bf16[1024,2048]...) custom-call(bf16[1024,512]{1,0:T(8,128)(2,1)} %get-tuple-element.43.refs_0_.refs_3_, ...), custom_call_target="tpu_custom_call" | custom-call | flops 153999998976 | tf_op jit(solution)/shard_map/pallas_call | solution.py:1054
  226.0 128.3 %shard_map.290 = (bf16[1024,2048]{1,0:T(8,128)(2,1)}, f32[2,8,2048]{2,1,0:T(8,128)}, f32[512,2048]{1,0:T(8,128)}, bf16[1024,2048]{1,0:T(8,128)(2,1)}, bf16[2048,...) custom-call(bf16[1024,2048]{1,0:T(8,128)(2,1)} %get-tuple-element.44.refs_0_, bf16[2048,2048]{1,0:T(8,128)(2,1)} %refs_1_.3, ...), custom_call_target="tpu_custom_call" | custom-call | flops 121000001536 | tf_op jit(solution)/shard_map/pallas_call | solution.py:1054
  355.1 119.0 %shard_map.291 = (bf16[1024,2048]{1,0:T(8,128)(2,1)}, bf16[1024,1536]{1,0:T(8,128)(2,1)}, f32[2,8,512]{2,1,0:T(8,128)}) custom-call(bf16[1024,2048]{1,0:T(8,128)(2,1)} %get-tuple-element.48.refs_0_, bf16[1024,2048]{1,0:T(8,128)(2,1)} %get-tuple-element.49.refs_1_.low_ref, bf16[2048,512]{1,0:T(8,128)(2,1)} %refs_2_.1, ...), custom_call_target="tpu_custom_call" | custom-call | flops 121000001536 | tf_op jit(solution)/shard_map/pallas_call | solution.py:1054
  474.2 15.2 %shard_map.292 = bf16[2048,2048]{1,0:T(8,128)(2,1)} custom-call(bf16[1024,2048]{1,0:T(8,128)(2,1)} %get-tuple-element.56.act_ref, bf16[1024,1536]{1,0:T(8,128)(2,1)} %get-tuple-element.59.grads_ref.refs_0_, bf16[1024,2048]{1,0:T(8,128)(2,1)} %get-tuple-element.49.refs_1_.low_ref, bf16[1024,512]{1,0:T(8,128)(2,1)} %get-tuple-element.57.head_ref), custom_call_target="tpu_custom_call" | custom-call | flops 11000000512 | tf_op jit(solution)/shard_map/pallas_call | solution.py:483
  489.4 131.0 %shard_map.293 = (bf16[1024,2048]{1,0:T(8,128)(2,1)}, f32[2,8,2048]{2,1,0:T(8,128)}, f32[8,256]{1,0:T(8,128)}, f32[8,2560]{1,0:T(8,128)}) custom-call(bf16[1024,1536]{1,0:T(8,128)(2,1)} %get-tuple-element.59.grads_ref.refs_0_, bf16[1024,2048]{1,0:T(8,128)(2,1)} %bitcast.30, f32[512,2048]{1,0:T(8,128)} %get-tuple-element.60.refs_2_, ...), custom_call_target="tpu_custom_call" | custom-call | flops 121000001536 | tf_op jit(solution)/shard_map/pallas_call | solution.py:1054
  620.4 1.6 convert_element_type.46
  622.0 2.8 convert_element_type.45
  625.3 1.4 fusion.3
  626.7 1.5 fusion.2
  628.2 1.4 fusion.1
  629.6 0.8 maximum_convert_fusion.2
  630.5 0.8 maximum_convert_fusion.1
  631.3 0.8 maximum_convert_fusion
  632.1 1.8 slice_convert_fusion
  633.9 2.1 copy.50
  636.1 1.6 copy-done.3
  637.6 2.0 copy.51
  (34 shorter events, 6.9 us)
Async XLA Ops:
  7.2 0.8 copy-start
  7.2 482.1 %reduce-scatter.4.cloned.1.call-start = ((), (), s32[]{:S(2)}) async-start(), calls=%async_computation.3 | async-start | bytes 9437184 | tf_op jit(solution)/shard_map/reduce_scatter | solution.py:1256
  8.0 11.1 %copy-start.5 = (s32[1,1024]{1,0:T(1,128)}, s32[1,1024]{1,0:T(1,128)S(1)}, u32[]{:S(2)}) copy-start(s32[1,1024]{1,0:T(1,128)S(1)} %constant_dynamic-slice_fusion.segr_ref.refs_11_) | copy-start | bytes 12292
  354.3 267.6 %reduce-scatter.8.cloned.1.call-start = ((), (), s32[]{:S(2)}) async-start(), calls=%async_computation.5 | async-start | bytes 9437184 | tf_op jit(solution)/shard_map/reduce_scatter | solution.py:1256
  355.1 273.1 %reduce-scatter.6.cloned.1.call-start = ((), (), s32[]{:S(2)}) async-start(), calls=%async_computation.4 | async-start | bytes 9437184 | tf_op jit(solution)/shard_map/reduce_scatter | solution.py:1256
  489.4 131.0 %copy-start.4 = (bf16[256,2048]{1,0:T(8,128)(2,1)S(1)}, bf16[256,2048]{1,0:T(8,128)(2,1)}, u32[]{:S(2)}) copy-start(bf16[256,2048]{1,0:T(8,128)(2,1)} %reduce-scatter.4.cloned.1.call-done) | copy-start | bytes 3145732
  620.4 4.4 copy-start.6
  628.2 5.7 copy-start.2
  633.9 3.7 copy-start.3
  633.9 5.7 copy-start.1
Sparse Core Ops, SparseCore 0:
  354.5 95.1 reduce-scatter.3
  453.5 78.8 reduce-scatter.7
  535.8 71.3 reduce-scatter.5

commit v8 on v7

--- a/solution.py
+++ b/solution.py
@@ -428,8 +428,9 @@
     head_steps = tokens // BLOCK
     vec_grads_ref[...] = jnp.zeros_like(vec_grads_ref)
 
-    def step(t):
-        pl.when(t < head_steps)(lambda: head_terms(t))
+    def step(now):
+        t = now - 1
+        pl.when((t >= 0) & (t < head_steps))(lambda: head_terms(t))
 
         @pl.when(t == head_steps - 1)
         def _():
@@ -467,7 +468,7 @@
 
         lax.fori_loop(0, pairs, drain, 0)
 
-    return step, end, head_steps + 3 + pairs * blocks
+    return step, end, 1 + head_steps + 3 + pairs * blocks
 
 
 def weight_kernel(act_ref, grads_ref, low_ref, head_ref, out_ref):
@@ -616,7 +617,24 @@
     return jnp.where(values < 0.0, tail, 1.0 - tail), bell * (1.0 / math.sqrt(2.0 * math.pi))
 
 
-def hidden_rows(env, rows, row):
+def hidden_copies(env, count, block):
+    me = lax.axis_index("tp")
+    send_sem, recv_sem = env_pair(env, "hidden")
+    return [
+        pltpu.make_async_remote_copy(
+            src_ref=env["hidden_sums"].at[:, row_block(block)],
+            dst_ref=env["hidden_landed"].at[me, :, row_block(block)],
+            send_sem=send_sem.at[block, k],
+            recv_sem=recv_sem.at[block, k],
+            device_id={"tp": lax.rem(me + k, count)},
+            device_id_type=MESH,
+        )
+        for k in range(1, count)
+    ]
+
+
+def hidden_rows(env, count, block):
+    rows = row_block(block)
     width = env["w_up"].shape[1]
     sums = [jnp.zeros((LANES, 1), F32)] * 4
     for n in range(width // TILE):
@@ -629,34 +647,48 @@
         scaled = env["hidden_grad"][rows, cols].astype(F32) * hidden_vec(env, 0, cols)
         for i, term in enumerate((active, active * active, scaled, scaled * active)):
             sums[i] = sums[i] + jnp.sum(term, axis=-1, keepdims=True)
-    env["hidden_sums"][:, row] = to_row(sums)
-
-
-def norm_hidden(env, count, features):
-    act, slope, part = env["hidden_act"], env["grad_up"], env["hidden_sums"]
-    tokens, width = act.shape
-    tp_total(part, env["hidden_landed"], env["hidden_send"], env["hidden_recv"], count)
-    env["hidden_vec_grads"][...] = jnp.zeros_like(env["hidden_vec_grads"])
-
-    def apply(r, carry):
-        rows = row_block(r)
-        sums = [column / features for column in to_columns(part[:, rows], 4)]
-        center = sums[0]
-        inverse = lax.rsqrt(sums[1] - center * center + EPSILON)
-        cross = inverse * (sums[3] - center * sums[2])
-        for n in range(width // TILE):
-            cols = slice(n * TILE, (n + 1) * TILE)
-            gain = hidden_vec(env, 0, cols)
-            normed = (act[rows, cols].astype(F32) - center) * inverse
-            grad = env["hidden_grad"][rows, cols].astype(F32)
-            back = inverse * (grad * gain - sums[2] - normed * cross)
-            slope[rows, cols] = (back * slope[rows, cols].astype(F32)).astype(BF16)
-            act[rows, cols] = (normed * gain + hidden_vec(env, 1, cols)).astype(BF16)
-            env["hidden_vec_grads"][0, :, cols] += fold(grad * normed)
-            env["hidden_vec_grads"][1, :, cols] += fold(grad)
-        return carry
-
-    lax.fori_loop(0, tokens // LANES, apply, 0)
+    packed = to_row(sums)
+    env["hidden_sums"][:, rows] = packed
+    env["hidden_landed"][lax.axis_index("tp"), :, rows] = packed
+    for copy in hidden_copies(env, count, block):
+        copy.start()
+
+
+def norm_hidden(env, count, features, block):
+    act, slope, landed = env["hidden_act"], env["grad_up"], env["hidden_landed"]
+    rows = row_block(block)
+    for copy in hidden_copies(env, count, block):
+        copy.wait()
+    total = landed[0, :, rows]
+    for k in range(1, count):
+        total = total + landed[k, :, rows]
+    sums = [column / features for column in to_columns(total, 4)]
+    center = sums[0]
+    inverse = lax.rsqrt(sums[1] - center * center + EPSILON)
+    cross = inverse * (sums[3] - center * sums[2])
+    for n in range(act.shape[1] // TILE):
+        cols = slice(n * TILE, (n + 1) * TILE)
+        gain = hidden_vec(env, 0, cols)
+        normed = (act[rows, cols].astype(F32) - center) * inverse
+        grad = env["hidden_grad"][rows, cols].astype(F32)
+        back = inverse * (grad * gain - sums[2] - normed * cross)
+        slope[rows, cols] = (back * slope[rows, cols].astype(F32)).astype(BF16)
+        act[rows, cols] = (normed * gain + hidden_vec(env, 1, cols)).astype(BF16)
+        env["hidden_vec_grads"][0, :, cols] += fold(grad * normed)
+        env["hidden_vec_grads"][1, :, cols] += fold(grad)
+    for name in ("hidden_act", "grad_up"):
+        row_store(env, name, block).start()
+
+
+def row_store(env, name, block):
+    rows = row_block(block)
+    return pltpu.make_async_copy(
+        env[name].at[rows, :], env["target " + name].at[rows, :], env["sem " + name].at[block]
+    )
+
+
+def whole_store(env, name):
+    return pltpu.make_async_copy(env[name], env["target " + name], env["sem " + name].at[0])
 
 
 def split_copies(env, seq_count):
@@ -755,8 +787,10 @@
         name: pltpu.make_async_copy(env["source " + name], env[name], env["load_sem"].at[i])
         for i, name in enumerate(plan["held"])
     }
+    behind = plan["late"] + plan["later"]
     for name in plan["held"]:
-        loads[name].start()
+        if name not in behind:
+            loads[name].start()
     started = plan["start"](env) if plan["start"] else []
     seq_count = plan["seq_count"]
     axis_barrier([("tp", count)] + ([("seq", plan["seq_barrier"])] if plan["seq_barrier"] else []))
@@ -917,15 +951,17 @@
         )
         when_chunk(t - ahead - from_first, lambda c: gather_step(c, gather_a, first, last))
         when_chunk(t - ahead - from_last, lambda c: gather_step(c, gather_b, last, first))
+        for moment, group in ((1, plan["late"]), (4, plan["later"])):
+
+            @pl.when(t == moment)
+            def _():
+                for name in group:
+                    loads[name].wait()
+
         if num_task:
             turn = (t // GROUP) * per_group + lax.rem(t, GROUP) - 1
             free = lax.rem(t, GROUP) != 0
             slot = lax.rem(turn + per_group + 1, 2)
-
-            @pl.when(t == 1)
-            def _():
-                for name in plan["late"]:
-                    loads[name].wait()
 
             for index in range(num_task if staged else 0):
                 low, high = starts_at[index] + 2, min(starts_at[index + 1] + 2, task_total)
@@ -941,27 +977,44 @@
             work_step(t)
         if seq_count:
             pl.when(t == chunks + ahead)(lambda: full_start(env, count))
-        if plan["rows_done"]:
-            done_a = t - ahead - from_first - (GROUP - 1)
-            done_b = t - ahead - from_last - (GROUP - 1)
-            has_a = (done_a >= 0) & (done_a < chunks) & (lax.rem(done_a + 64, GROUP) == 0)
-            has_b = (done_b >= 0) & (done_b < chunks) & (lax.rem(done_b + 64, GROUP) == 0)
-
-            @pl.when(has_a | has_b)
+        for name, moment in plan["stores"].items():
+            if moment == "reduced":
+                pl.when(t == chunks + ahead)(lambda name=name: whole_store(env, name).start())
+        done_a = t - ahead - from_first - (GROUP - 1)
+        done_b = t - ahead - from_last - (GROUP - 1)
+        has_a = (done_a >= 0) & (done_a < chunks) & (lax.rem(done_a + 64, GROUP) == 0)
+        has_b = (done_b >= 0) & (done_b < chunks) & (lax.rem(done_b + 64, GROUP) == 0)
+
+        @pl.when(has_a | has_b)
+        def _():
+            block = jnp.where(has_a, done_a // GROUP, chunks // GROUP + done_b // GROUP)
+            row_store(env, "out", block).start()
+            if plan["rows_done"]:
+                plan["rows_done"](env, block)
+
+        if plan["rows_late"]:
+            late_a = t - 2 * ahead - (GROUP - 1) - 2
+
+            place = lax.rem(late_a + 64, GROUP)
+
+            @pl.when((late_a >= 0) & (place < 2))
             def _():
-                start = jnp.where(has_a, done_a * size, half + done_b * size)
-                rows = pl.ds(pl.multiple_of(start, LANES), LANES)
-                plan["rows_done"](env, rows, rows)
+                plan["rows_late"](env, place * (chunks // GROUP) + late_a // GROUP)
 
         return carry
 
     for name in plan["held"]:
-        if name not in plan["late"]:
+        if name not in behind:
             loads[name].wait()
     for copy in started:
         copy.wait()
+    for name in behind:
+        loads[name].start()
     if plan["before"]:
         plan["before"](env)
+    for name, moment in plan["stores"].items():
+        if moment == "before":
+            whole_store(env, name).start()
     work_step = None
     if plan["work"]:
         work_step, work_end, work_steps = plan["work"](env)
@@ -974,8 +1027,14 @@
         for turn in (task_total - 2, task_total - 1):
             index = max(i for i in range(num_task) if starts_at[i] <= turn)
             stage_copy(index, turn - starts_at[index], turn % 2).wait()
-    if plan["after"]:
-        plan["after"](env)
+    if plan["rows_late"]:
+        assert chunks + 2 * ahead == steps and GROUP == 4
+
+        def rest(place, carry):
+            plan["rows_late"](env, (place + 1) * (chunks // GROUP) - 1)
+            return carry
+
+        lax.fori_loop(0, 2, rest, 0)
     if work_step:
         work_end()
     if seq_count:
@@ -995,11 +1054,17 @@
         return carry
 
     lax.fori_loop(0, chunks, drain, 0)
+    for name, moment in plan["stores"].items():
+        if moment == "rows":
+            for block in range(tokens // LANES):
+                row_store(env, name, block).wait()
+        else:
+            whole_store(env, name).wait()
 
 
 def line_sum(
-    finish, count, held, vecs, parts, collective_id, *, tokens, late=(), tasks=(), owns=(), sent=(),
-    scratch=(), loose=(), start=None, before=None, rows_done=None, after=None, work=None,
+    finish, count, held, vecs, parts, collective_id, *, tokens, late=(), later=(), tasks=(), owns=(),
+    sent=(), stores=(), scratch=(), loose=(), start=None, before=None, rows_done=None, rows_late=None, work=None,
     seq_count=0, seq_barrier=0, micros=110,
 ):
     names = dict(scratch)
@@ -1022,14 +1087,21 @@
         (name, pltpu.SemaphoreType.DMA((CHUNKS,)))
         for name in ("rsa_s", "rsa_r", "rsb_s", "rsb_r", "aga_s", "aga_r", "agb_s", "agb_r")
     ]
+    assert half // CHUNKS * GROUP == LANES
+    loose = dict(loose)
+    stores = dict(stores, out="rows")
+    shapes = [("out", jax.ShapeDtypeStruct((tokens, width), BF16))] + list(owns)
     scratch = list(scratch) + fixed
-    loose = dict(loose)
+    for name, shape in shapes:
+        if name in stores:
+            scratch.append((name, pltpu.VMEM(shape.shape, shape.dtype)))
+            number = tokens // LANES if stores[name] == "rows" else 1
+            scratch.append(("sem " + name, pltpu.SemaphoreType.DMA((number,))))
     order = (
         ["source " + name for name in held]
         + list(loose)
         + list(vecs)
-        + ["out"]
-        + [name for name, _ in owns]
+        + ["target " + name if name in stores else name for name, _ in shapes]
         + [name for name, _ in sent]
         + list(held)
         + [name for name, _ in scratch]
@@ -1039,7 +1111,9 @@
         order=order,
         held=list(held),
         parts=parts,
-        late=late,
+        late=tuple(late),
+        later=tuple(later),
+        stores=stores,
         tasks=tasks,
         start=start,
         work=work,
@@ -1047,17 +1121,16 @@
         seq_barrier=seq_barrier or seq_count,
         before=before,
         rows_done=rows_done,
-        after=after,
+        rows_late=rows_late,
     )
     whole = pl.BlockSpec(memory_space=pltpu.VMEM)
     any_space = pl.BlockSpec(memory_space=pl.ANY)
     return pl.pallas_call(
         functools.partial(line_kernel, plan, count, CHUNKS, SLACK),
-        out_shape=[jax.ShapeDtypeStruct((tokens, width), BF16)]
-        + [shape for _, shape in owns]
-        + [shape for _, shape in sent],
+        out_shape=[shape for _, shape in shapes] + [shape for _, shape in sent],
         in_specs=[any_space] * (len(held) + len(loose)) + [whole] * len(vecs),
-        out_specs=[whole] * (1 + len(owns)) + [any_space] * len(sent),
+        out_specs=[any_space if name in stores else whole for name, _ in shapes]
+        + [any_space] * len(sent),
         scratch_shapes=[pltpu.VMEM(array.shape, array.dtype) for array in held.values()]
         + [shape for _, shape in scratch],
         compiler_params=pltpu.CompilerParams(
@@ -1186,6 +1259,12 @@
     sums_shape = shape_of((2, 8, model_width))
     landed = pltpu.VMEM((tp_count, 8, tokens), F32)
     pair_sem = pltpu.SemaphoreType.DMA((tp_count,))
+    block_sem = pltpu.SemaphoreType.DMA((tokens // LANES, tp_count))
+
+    def before_middle(env):
+        env["hidden_vec_grads"][...] = jnp.zeros_like(env["hidden_vec_grads"])
+        norm_heads(env, tp_count, model_width)
+
     (
         second_act, middle_own, head_act, head_sums, hidden_act, grad_up, hidden_vec_grads
     ) = line_sum(
@@ -1196,7 +1275,9 @@
         (("head_act", "w_out"),),
         3,
         tokens=tokens,
-        late=("cotangent", "w_down", "w_up"),
+        late=("cotangent", "w_down"),
+        later=("block", "w_up"),
+        stores=dict(middle="reduced", head_act="before", hidden_act="rows", grad_up="rows"),
         tasks=(("keep", "cotangent", "w_down", "hidden_grad"),),
         owns=(
             ("middle", own_shape),
@@ -1213,12 +1294,12 @@
             ("hidden_landed", landed),
             ("head_send", pair_sem),
             ("head_recv", pair_sem),
-            ("hidden_send", pair_sem),
-            ("hidden_recv", pair_sem),
+            ("hidden_send", block_sem),
+            ("hidden_recv", block_sem),
         ),
-        before=lambda env: norm_heads(env, tp_count, model_width),
-        rows_done=hidden_rows,
-        after=lambda env: norm_hidden(env, tp_count, hidden_width),
+        before=before_middle,
+        rows_done=lambda env, block: hidden_rows(env, tp_count, block),
+        rows_late=lambda env, block: norm_hidden(env, tp_count, hidden_width, block),
         micros=140,
     )
 
@@ -1239,7 +1320,9 @@
         (("grad_up", "w_up"),),
         4,
         tokens=tokens,
-        late=("hidden_act", "w_down", "second_act"),
+        late=("hidden_act", "w_down", "middle"),
+        later=("cotangent", "second_act"),
+        stores=dict(middle_grad="reduced"),
         tasks=(
             ("down", "hidden_act", "w_down", "down_part"),
             ("weight", "cotangent", "hidden_act", "w_down_terms"),
@@ -1281,6 +1364,8 @@
         (),
         5,
         tokens=tokens,
+        late=("low", "w_out", "mixed", "head_sums"),
+        later=("qkv", "o", "lse", "packed"),
         owns=(
             ("grads", shape_of((tokens, 3 * head_width), BF16)),
             ("head_vec_grads", shape_of((2, 8, head_width))),
@@ -1331,6 +1416,7 @@
         (("grads", "w_pairs"),),
         8,
         tokens=tokens,
+        later=("block", "middle_grad"),
         loose=dict(w_query=w_query, w_key=w_key, w_value=w_value),
         owns=(
             ("sums", sums_shape),

time: 647 us -> 626 us (0.968)
  Pallas kernels: 600 us -> 579 us
    pallas_call x4, Pallas kernels: 523 us -> 502 us  [line_sum(): pl.pallas_call(functools.partial(line_kernel, plan, count, CHUNKS, SLACK)...]
where the time goes in v8:
time: 626 us; the launch traced here: 625 us
  Pallas kernels  579 us (92%)
  local copies, waits for them, and re-layouts  17.9 us (3%)
  between operations  13.9 us (2%)
  other arithmetic  13.2 us (2%)
    pallas_call x4, Pallas kernels, line_sum(): pl.pallas_call(functools.partial(line_kernel, plan, count, CHUNKS, SLACK)...  502 us
    pallas_call x1, Pallas kernels, front(): pl.pallas_call(functools.partial(front_kernel, count, groups), out_shape=...  62.2 us
    pallas_call x1, Pallas kernels, head_weights(): pl.pallas_call(weight_kernel, grid=(model_width // ROWS,), out_shape=jax....  15.1 us
  transfers between devices with their start and end apart: 3, of which 0 were waited for; matrix products, arithmetic and copies ran while one was open for 1% of the time, Pallas kernels for 41%

profile of v8, /device:TPU:0, one launch (start us, length us, event | category | flops | bytes accessed | tf_op | source)
XLA Modules:
  0.0 624.9 jit_solution(6326773654804250973)
XLA Ops:
  9.2 0.7 constant_dynamic-update-slice_fusion.6
  9.9 0.7 constant_dynamic-update-slice_fusion.5
  10.6 0.7 constant_dynamic-update-slice_fusion.4
  14.8 1.0 copy.39.segc_ref.refs_10_
  15.8 2.0 multiply_cosine_fusion
  17.8 1.3 pad_maximum_fusion.packed_ref.refs_8_
  19.1 62.2 %shard_map.288 = (bf16[1024,2048]{1,0:T(8,128)(2,1)}, bf16[4,1024,384]{2,1,0:T(8,128)(2,1)}, bf16[4,1024,128]{2,1,0:T(8,128)(2,1)}, f32[4,8,1024]{2,1,0:T(8,128)}, bf16[1024,512]{1,0:T(8,128)(2,1)}) custom-call(bf16[1024,2048]{1,0:T(8,128)(2,1)} %bitcast.28, bf16[2048,512]{1,0:T(8,128)(2,1)} %refs_3_.1, bf16[2048,512]{1,0:T(8,128)(2,1)} %refs_4_.3, ...), custom_call_target="tpu_custom_call" | custom-call | flops 65999998976 | tf_op jit(solution)/shard_map/pallas_call | solution.py:259
  81.3 134.6 %shard_map.289 = (bf16[1024,2048]{1,0:T(8,128)(2,1)}, f32[512,2048]{1,0:T(8,128)}, bf16[1024,512]{1,0:T(8,128)(2,1)}, f32[8,1024]{1,0:T(8,128)}, bf16[1024,2048]...) custom-call(bf16[1024,512]{1,0:T(8,128)(2,1)} %get-tuple-element.43.refs_0_.refs_3_, ...), custom_call_target="tpu_custom_call" | custom-call | flops 153999998976 | tf_op jit(solution)/shard_map/pallas_call | solution.py:1128
  215.8 124.1 %shard_map.290 = (bf16[1024,2048]{1,0:T(8,128)(2,1)}, f32[2,8,2048]{2,1,0:T(8,128)}, f32[512,2048]{1,0:T(8,128)}, bf16[1024,2048]{1,0:T(8,128)(2,1)}, bf16[2048,...) custom-call(bf16[1024,2048]{1,0:T(8,128)(2,1)} %get-tuple-element.44.refs_0_, bf16[2048,2048]{1,0:T(8,128)(2,1)} %refs_1_.3, ...), custom_call_target="tpu_custom_call" | custom-call | flops 121000001536 | tf_op jit(solution)/shard_map/pallas_call | solution.py:1128
  340.8 116.7 %shard_map.291 = (bf16[1024,2048]{1,0:T(8,128)(2,1)}, bf16[1024,1536]{1,0:T(8,128)(2,1)}, f32[2,8,512]{2,1,0:T(8,128)}) custom-call(bf16[1024,2048]{1,0:T(8,128)(2,1)} %get-tuple-element.48.refs_0_, bf16[1024,2048]{1,0:T(8,128)(2,1)} %get-tuple-element.49.refs_1_.low_ref, bf16[2048,512]{1,0:T(8,128)(2,1)} %refs_2_.1, ...), custom_call_target="tpu_custom_call" | custom-call | flops 121000001536 | tf_op jit(solution)/shard_map/pallas_call | solution.py:1128
  457.5 15.1 %shard_map.292 = bf16[2048,2048]{1,0:T(8,128)(2,1)} custom-call(bf16[1024,2048]{1,0:T(8,128)(2,1)} %get-tuple-element.56.act_ref, bf16[1024,1536]{1,0:T(8,128)(2,1)} %get-tuple-element.59.grads_ref.refs_0_, bf16[1024,2048]{1,0:T(8,128)(2,1)} %get-tuple-element.49.refs_1_.low_ref, bf16[1024,512]{1,0:T(8,128)(2,1)} %get-tuple-element.57.head_ref), custom_call_target="tpu_custom_call" | custom-call | flops 11000000512 | tf_op jit(solution)/shard_map/pallas_call | solution.py:484
  472.7 126.3 %shard_map.293 = (bf16[1024,2048]{1,0:T(8,128)(2,1)}, f32[2,8,2048]{2,1,0:T(8,128)}, f32[8,256]{1,0:T(8,128)}, f32[8,2560]{1,0:T(8,128)}) custom-call(bf16[1024,1536]{1,0:T(8,128)(2,1)} %get-tuple-element.59.grads_ref.refs_0_, bf16[1024,2048]{1,0:T(8,128)(2,1)} %bitcast.30, f32[512,2048]{1,0:T(8,128)} %get-tuple-element.60.refs_2_, ...), custom_call_target="tpu_custom_call" | custom-call | flops 121000001536 | tf_op jit(solution)/shard_map/pallas_call | solution.py:1128
  599.1 1.6 convert_element_type.46
  600.7 2.8 convert_element_type.45
  604.0 1.4 fusion.3
  605.4 1.5 fusion.2
  606.9 1.4 fusion.1
  608.3 0.8 maximum_convert_fusion.2
  609.1 0.8 maximum_convert_fusion.1
  610.0 0.8 maximum_convert_fusion
  610.8 1.8 slice_convert_fusion
  612.6 2.1 copy.50
  614.7 1.6 copy-done.3
  616.3 2.0 copy.51
  (34 shorter events, 6.9 us)
Async XLA Ops:
  7.2 0.8 copy-start
  7.2 465.5 %reduce-scatter.4.cloned.1.call-start = ((), (), s32[]{:S(2)}) async-start(), calls=%async_computation.3 | async-start | bytes 9437184 | tf_op jit(solution)/shard_map/reduce_scatter | solution.py:1339
  8.0 11.1 %copy-start.5 = (s32[1,1024]{1,0:T(1,128)}, s32[1,1024]{1,0:T(1,128)S(1)}, u32[]{:S(2)}) copy-start(s32[1,1024]{1,0:T(1,128)S(1)} %constant_dynamic-slice_fusion.segr_ref.refs_11_) | copy-start | bytes 12292
  340.0 260.6 %reduce-scatter.8.cloned.1.call-start = ((), (), s32[]{:S(2)}) async-start(), calls=%async_computation.5 | async-start | bytes 9437184 | tf_op jit(solution)/shard_map/reduce_scatter | solution.py:1339
  340.8 266.2 %reduce-scatter.6.cloned.1.call-start = ((), (), s32[]{:S(2)}) async-start(), calls=%async_computation.4 | async-start | bytes 9437184 | tf_op jit(solution)/shard_map/reduce_scatter | solution.py:1339
  472.7 126.4 %copy-start.4 = (bf16[256,2048]{1,0:T(8,128)(2,1)S(1)}, bf16[256,2048]{1,0:T(8,128)(2,1)}, u32[]{:S(2)}) copy-start(bf16[256,2048]{1,0:T(8,128)(2,1)} %reduce-scatter.4.cloned.1.call-done) | copy-start | bytes 3145732
  599.1 4.4 copy-start.6
  606.9 5.7 copy-start.2
  612.6 3.7 copy-start.3
  612.6 5.7 copy-start.1
Sparse Core Ops, SparseCore 0:
  340.1 89.9 reduce-scatter.3
  434.0 84.2 reduce-scatter.7
  521.7 71.2 reduce-scatter.5

commit v9 on v8

--- a/solution.py
+++ b/solution.py
@@ -123,10 +123,14 @@
 
 
 def front_kernel(
-    count, groups, x_ref, wq_ref, wk_ref, wv_ref, vecs_ref, packed_ref, segc_ref, segr_ref,
-    act_ref, qkv_ref, o_ref, lse_ref, mixed_ref,
-    weights, staged, tab_ref, bias, qs, ks, load_sem, send_sem, recv_sem, back_send_sem, back_recv_sem,
+    count, groups, num_vec, *refs
 ):
+    (x_ref, wq_ref, wk_ref, wv_ref, packed_ref, segc_ref, segr_ref), refs = refs[:7], refs[7:]
+    pieces, refs = refs[:num_vec], refs[num_vec:]
+    (
+        act_out, qkv_out, o_ref, lse_ref, mixed_ref, vecs_ref, act_ref, qkv_ref,
+        weights, staged, tab_ref, bias, qs, ks, load_sem, act_sem, qkv_sem, send_sem, recv_sem, back_send_sem, back_recv_sem,
+    ) = refs
     me = lax.axis_index("seq")
     pairs, length = qkv_ref.shape[:2]
     tokens, width = x_ref.shape
@@ -145,18 +149,14 @@
             copy.start()
             loads.append(copy)
 
-    def norm_step(r, carry):
-        rows = pl.ds(pl.multiple_of(r * LANES, LANES), LANES)
-        normed, _ = norm_parts(x_ref[rows, :].astype(F32))
-        act_ref[rows, :] = (normed * vecs_ref[:, :width] + vecs_ref[:, width : 2 * width]).astype(BF16)
-        return carry
-
-    lax.fori_loop(0, tokens // LANES, norm_step, 0)
-    for copy in loads:
-        copy.wait()
-
-    def there(p, k):
-        device = lax.rem(me + k, count)
+    place = 0
+    for piece in pieces:
+        for i in range(piece.shape[0]):
+            vecs_ref[:, place : place + LANES] = piece[i : i + 1, :].astype(F32)
+            place += LANES
+
+    def there_to(p, device):
+        k = lax.rem(device - me + count, count)
         return send(
             staged.at[lax.rem(device, groups) * pairs + p, spans(device // groups, span), :],
             qkv_ref.at[p, spans(me, span), :],
@@ -164,6 +164,45 @@
             recv_sem.at[p, k],
             device,
         )
+
+    def there(p, k):
+        return there_to(p, lax.rem(me + k, count))
+
+    def project_rows(p, rows):
+        for group in range(groups):
+            j = group * pairs + p
+            staged[j, rows, :] = dot(act_ref[rows, :], weights[j], 1, 0).astype(BF16)
+
+    for copy in loads:
+        copy.wait()
+    seq_wait(count)
+    steps = tokens // BLOCK
+    rows_each = BLOCK // span
+
+    def first_step(b, carry):
+        block = lax.rem(row // rows_each + b, steps)
+        for i in range(BLOCK // LANES):
+            rows = pl.ds(pl.multiple_of(block * BLOCK + i * LANES, LANES), LANES)
+            normed, _ = norm_parts(x_ref[rows, :].astype(F32))
+            act = normed * vecs_ref[:, :width] + vecs_ref[:, width : 2 * width]
+            act_ref[rows, :] = act.astype(BF16)
+        project_rows(0, pl.ds(pl.multiple_of(block * BLOCK, BLOCK), BLOCK))
+        for i in range(rows_each * groups):
+            device = block * rows_each * groups + i
+            pl.when(device != me)(lambda device=device: there_to(0, device).start())
+        return carry
+
+    lax.fori_loop(0, steps, first_step, 0)
+    act_copy = pltpu.make_async_copy(act_ref, act_out, act_sem)
+    act_copy.start()
+
+    def qkv_copy(p):
+        return pltpu.make_async_copy(qkv_ref.at[p], qkv_out.at[p], qkv_sem.at[p])
+
+    def keep_own(p):
+        qkv_ref[p, spans(me, span), :] = staged[mine * pairs + p, spans(row, span), :]
+
+    keep_own(0)
 
     def back(p, k):
         device = lax.rem(me + k, count)
@@ -176,26 +215,17 @@
         )
 
     def project(p, carry):
-        for group in range(groups):
-
-            def rows_step(r, inner):
-                rows = pl.ds(pl.multiple_of(r * BLOCK, BLOCK), BLOCK)
-                j = group * pairs + p
-                staged[j, rows, :] = dot(act_ref[rows, :], weights[j], 1, 0).astype(BF16)
-                return inner
-
-            lax.fori_loop(0, tokens // BLOCK, rows_step, 0)
-
-        @pl.when(p == 0)
-        def _():
-            seq_wait(count)
-
+        def rows_step(r, inner):
+            project_rows(p, pl.ds(pl.multiple_of(r * BLOCK, BLOCK), BLOCK))
+            return inner
+
+        lax.fori_loop(0, steps, rows_step, 0)
         for k in range(1, count):
             there(p, k).start()
-        qkv_ref[p, spans(me, span), :] = staged[mine * pairs + p, spans(row, span), :]
+        keep_own(p)
         return carry
 
-    lax.fori_loop(0, pairs, project, 0)
+    lax.fori_loop(1, pairs, project, 0)
     expand_tables(packed_ref, tab_ref)
     for qb in range(blocks):
         rows = block_rows(qb)
@@ -208,6 +238,7 @@
     def attend(p, carry):
         for k in range(1, count):
             there(p, k).wait_recv()
+        qkv_copy(p).start()
         for qb in range(blocks):
             rows = block_rows(qb)
             q = rotated(qkv_ref[p, rows, :LANES], tab_ref, 0, rows) * (HEAD**-0.5)
@@ -247,27 +278,37 @@
         return carry
 
     lax.fori_loop(0, pairs, drain, 0)
-
-
-def front(x, w_query, w_key, w_value, vecs, tables, seg_col, seg_row, count, groups, collective_id):
+    act_copy.wait()
+    for p in range(pairs):
+        qkv_copy(p).wait()
+
+
+def front(
+    x, w_query, w_key, w_value, tables, seg_col, seg_row, vectors, count, groups, collective_id
+):
     tokens, model_width = x.shape
+    pieces = [vector.reshape(vector.shape[0] // LANES, LANES) for vector in vectors]
+    total = sum(vector.shape[0] for vector in vectors)
     head_width = w_query.shape[1]
     length = seg_col.shape[0]
     pairs = head_width // groups // LANES
     whole = pl.BlockSpec(memory_space=pltpu.VMEM)
     any_space = pl.BlockSpec(memory_space=pl.ANY)
     return pl.pallas_call(
-        functools.partial(front_kernel, count, groups),
+        functools.partial(front_kernel, count, groups, len(pieces)),
         out_shape=[
             jax.ShapeDtypeStruct((tokens, model_width), BF16),
             jax.ShapeDtypeStruct((pairs, length, 3 * LANES), BF16),
             jax.ShapeDtypeStruct((pairs, length, LANES), BF16),
             jax.ShapeDtypeStruct((pairs, 8, length), F32),
             jax.ShapeDtypeStruct((tokens, head_width), BF16),
+            jax.ShapeDtypeStruct((1, total), F32),
         ],
-        in_specs=[whole] + [any_space] * 3 + [whole] * 4,
-        out_specs=[whole] * 5,
+        in_specs=[whole] + [any_space] * 3 + [whole] * (3 + len(pieces)),
+        out_specs=[any_space] * 2 + [whole] * 4,
         scratch_shapes=[
+            pltpu.VMEM((tokens, model_width), BF16),
+            pltpu.VMEM((pairs, length, 3 * LANES), BF16),
             pltpu.VMEM((pairs * groups, model_width, 3 * LANES), BF16),
             pltpu.VMEM((pairs * groups, tokens, 3 * LANES), BF16),
             pltpu.VMEM((4, length, LANES), F32),
@@ -275,13 +316,15 @@
             pltpu.VMEM((2, length, LANES), BF16),
             pltpu.VMEM((length, LANES), BF16),
             pltpu.SemaphoreType.DMA((3 * pairs * groups,)),
+            pltpu.SemaphoreType.DMA,
+            pltpu.SemaphoreType.DMA((pairs,)),
         ]
         + [pltpu.SemaphoreType.DMA((pairs, count))] * 4,
         compiler_params=pltpu.CompilerParams(
             collective_id=collective_id, has_side_effects=True, vmem_limit_bytes=VMEM_LIMIT
         ),
         cost_estimate=cost(60),
-    )(x, w_query, w_key, w_value, vecs, tables, seg_col, seg_row)
+    )(x, w_query, w_key, w_value, tables, seg_col, seg_row, *pieces)
 
 
 def back_work(env, count, tp_count, groups):
@@ -471,30 +514,80 @@
     return step, end, 1 + head_steps + 3 + pairs * blocks
 
 
-def weight_kernel(act_ref, grads_ref, low_ref, head_ref, out_ref):
+def weight_kernel(
+    act_ref, grads_ref, low_ref, head_ref, down_ref, block_ref, out_ref, down_out, block_out
+):
     wide = grads_ref.shape[1]
     out_ref[:, :wide] = dot(jnp.transpose(act_ref[...]), grads_ref[...], 1, 0).astype(BF16)
     out_ref[:, wide:] = dot(jnp.transpose(low_ref[...]), head_ref[...], 1, 0).astype(BF16)
-
-
-def head_weights(act, grads, low, head_act):
+    down_out[...] = down_ref[...].astype(F32)
+    block_out[...] = block_ref[...]
+
+
+def head_weights(act, grads, low, head_act, down_grad, block_out):
     tokens, model_width = act.shape
     wide, narrow = grads.shape[1], head_act.shape[1]
+    steps = model_width // ROWS
     tile = pl.BlockSpec((tokens, ROWS), lambda i: (0, i))
+    part = pl.BlockSpec((tokens // steps, model_width), lambda i: (i, 0))
+    own_rows, own_width = down_grad.shape
+    own = pl.BlockSpec((own_rows // steps, own_width), lambda i: (i, 0))
     return pl.pallas_call(
         weight_kernel,
-        grid=(model_width // ROWS,),
-        out_shape=jax.ShapeDtypeStruct((model_width, wide + narrow), BF16),
+        grid=(steps,),
+        out_shape=[
+            jax.ShapeDtypeStruct((model_width, wide + narrow), BF16),
+            jax.ShapeDtypeStruct(down_grad.shape, F32),
+            jax.ShapeDtypeStruct(block_out.shape, BF16),
+        ],
         in_specs=[
             tile,
             pl.BlockSpec((tokens, wide), lambda i: (0, 0)),
             tile,
             pl.BlockSpec((tokens, narrow), lambda i: (0, 0)),
+            own,
+            part,
         ],
-        out_specs=pl.BlockSpec((ROWS, wide + narrow), lambda i: (i, 0)),
+        out_specs=[pl.BlockSpec((ROWS, wide + narrow), lambda i: (i, 0)), own, part],
         compiler_params=pltpu.CompilerParams(vmem_limit_bytes=VMEM_LIMIT),
         cost_estimate=cost(10),
-    )(act, grads, low, head_act)
+    )(act, grads, low, head_act, down_grad, block_out)
+
+
+def last_kernel(head_ref, up_ref, grad_ref, *refs):
+    outs, up_out, grad_out = refs[:4], refs[4], refs[5]
+    grad_out[...] = grad_ref[...]
+    width = outs[0].shape[1]
+    for j in range(width // LANES):
+        for i in range(3):
+            start = (3 * j + i) * LANES
+            outs[i][:, j * LANES : (j + 1) * LANES] = head_ref[:, start : start + LANES].astype(F32)
+    outs[3][...] = head_ref[:, 3 * width :].astype(F32)
+    up_out[...] = up_ref[...].astype(F32)
+
+
+def last_results(head_grads, up_grad, input_grad, head_width):
+    rows = head_grads.shape[0]
+    steps = rows // 32
+
+    def block(width):
+        return pl.BlockSpec((rows // steps, width), lambda i: (i, 0))
+
+    tokens, width = input_grad.shape
+    part = pl.BlockSpec((tokens // steps, width), lambda i: (i, 0))
+    return pl.pallas_call(
+        last_kernel,
+        grid=(steps,),
+        out_shape=[jax.ShapeDtypeStruct((rows, head_width), F32)] * 4
+        + [
+            jax.ShapeDtypeStruct(up_grad.shape, F32),
+            jax.ShapeDtypeStruct(input_grad.shape, BF16),
+        ],
+        in_specs=[block(head_grads.shape[1]), block(up_grad.shape[1]), part],
+        out_specs=[block(head_width)] * 4 + [block(up_grad.shape[1]), part],
+        compiler_params=pltpu.CompilerParams(vmem_limit_bytes=VMEM_LIMIT),
+        cost_estimate=cost(6),
+    )(head_grads, up_grad, input_grad)
 
 
 def fold(values):
@@ -1223,13 +1316,6 @@
     hidden_width = w_up.shape[1] * tp_count
     groups = seq_count // row_count
 
-    vecs = jnp.concatenate(
-        [
-            first_gain, first_bias, second_gain, second_bias,
-            hidden_gain, hidden_bias, head_gain, head_bias,
-        ]
-    ).astype(F32)[None]
-
     seg_row = lax.dynamic_slice_in_dim(segment_ids, seq_index // groups, 1, 0)
     seg_col = seg_row.reshape(length, 1)
     earlier = jnp.sum((seg_row < seg_col).astype(jnp.int32), axis=-1)
@@ -1238,15 +1324,18 @@
     block = block_in.reshape(tokens, model_width)
     cotangent = out_cotangent.reshape(tokens, model_width)
 
-    first_act, qkv_row, o_row, lse, mixed = front(
+    first_act, qkv_row, o_row, lse, mixed, vecs = front(
         block,
         w_query,
         w_key,
         w_value,
-        vecs,
         tables,
         seg_col,
         seg_row,
+        (
+            first_gain, first_bias, second_gain, second_bias,
+            hidden_gain, hidden_bias, head_gain, head_bias,
+        ),
         seq_count,
         groups,
         1,
@@ -1397,8 +1486,10 @@
         work=lambda env: back_work(env, seq_count, tp_count, groups),
         seq_barrier=seq_count,
     )
-    head_terms = head_weights(first_act, grads, grad_middle_low, head_act)
-    grads, head_terms, w_down_grad = lax.optimization_barrier((grads, head_terms, w_down_grad))
+    head_terms, w_down_grad, block_out = head_weights(
+        first_act, grads, grad_middle_low, head_act, w_down_grad, block_out
+    )
+    grads, head_terms = lax.optimization_barrier((grads, head_terms))
     head_grads = scatter(head_terms)
     own_width = model_width // seq_count
     split_width = hidden_size + head_width
@@ -1442,30 +1533,26 @@
         seq_count=seq_count,
     )
 
-    def head_grad(index):
-        columns = [
-            head_grads[:, (3 * j + index) * LANES : (3 * j + index + 1) * LANES]
-            for j in range(head_width // LANES)
-        ]
-        return jnp.concatenate(columns, axis=1).astype(F32)
-
+    w_query_grad, w_key_grad, w_value_grad, w_out_grad, w_up_grad, input_grad = last_results(
+        head_grads, w_up_grad, input_grad, head_width
+    )
     return (
         block_out.reshape(block_in.shape),
         input_grad.reshape(block_in.shape),
         norm_own[2],
         norm_own[3],
-        head_grad(0),
-        head_grad(1),
-        head_grad(2),
+        w_query_grad,
+        w_key_grad,
+        w_value_grad,
         norm_split[0, hidden_size:],
         norm_split[1, hidden_size:],
-        head_grads[:, 3 * head_width :].astype(F32),
+        w_out_grad,
         norm_own[0],
         norm_own[1],
-        w_up_grad.astype(F32),
+        w_up_grad,
         norm_split[0, :hidden_size],
         norm_split[1, :hidden_size],
-        w_down_grad.astype(F32),
+        w_down_grad,
     )
 
 

time: 626 us -> 614 us (0.981)
  local copies, waits for them, and re-layouts: 17.9 us -> 6.07 us
  Pallas kernels: 579 us -> 589 us
  other arithmetic: 13.2 us -> 3.84 us
    unnamed x23 -> x6, local copies, waits for them, and re-layouts: 11.3 us -> 0.69 us
    convert_element_type x7 -> x0, other arithmetic: 9.32 us -> none  [the longest x1 2.79 us: body(): w_up_grad.astype(F32)]
    pallas_call x2 -> x3, Pallas kernels: 77.3 us -> 86.2 us  [the longest x1 59.9 us: front(): pl.pallas_call(functools.partial(front_kernel, count, groups, len(pieces)...]
  transfers between devices with their start and end apart: 3 -> 3, of which waited for: 0 -> 0; matrix products, arithmetic and copies ran while one was open for 1% -> 1% of each run, Pallas kernels for 41% -> 43%
where the time goes in v9:
time: 614 us; the launch traced here: 613 us
  Pallas kernels  589 us (96%)
  between operations  13.9 us (2%)
    pallas_call x4, Pallas kernels, line_sum(): pl.pallas_call(functools.partial(line_kernel, plan, count, CHUNKS, SLACK)...  502 us
    pallas_call x1, Pallas kernels, front(): pl.pallas_call(functools.partial(front_kernel, count, groups, len(pieces)...  59.9 us
    pallas_call x1, Pallas kernels, head_weights(): pl.pallas_call(weight_kernel, grid=(steps,), out_shape=[jax.ShapeDtypeStr...  18.2 us
  transfers between devices with their start and end apart: 3, of which 0 were waited for; matrix products, arithmetic and copies ran while one was open for 1% of the time, Pallas kernels for 43%

profile of v9, /device:TPU:0, one launch (start us, length us, event | category | flops | bytes accessed | tf_op | source)
XLA Modules:
  0.0 613.2 jit_solution(13054629876379237944)
XLA Ops:
  7.2 0.0 copy-start
  7.2 0.0 reduce-scatter.4.cloned.1.call-start
  7.3 0.7 copy-done
  8.0 0.6 convert_reduce_fusion
  8.6 1.0 copy.39.refs_5_.refs_10_
  9.6 2.0 multiply_cosine_fusion
  11.6 1.3 pad_maximum_fusion.refs_4_.refs_8_
  12.9 0.0 copy-done.2
  12.9 59.9 %shard_map.288 = (bf16[1024,2048]{1,0:T(8,128)(2,1)}, bf16[4,1024,384]{2,1,0:T(8,128)(2,1)}, bf16[4,1024,128]{2,1,0:T(8,128)(2,1)}, f32[4,8,1024]{2,1,0:T(8,128)...) custom-call(bf16[1024,2048]{1,0:T(8,128)(2,1)} %bitcast.34, bf16[2048,512]{1,0:T(8,128)(2,1)} %refs_3_.3, ...), custom_call_target="tpu_custom_call" | custom-call | flops 65999998976 | tf_op jit(solution)/shard_map/pallas_call | solution.py:297
  72.8 134.7 %shard_map.289 = (bf16[1024,2048]{1,0:T(8,128)(2,1)}, f32[512,2048]{1,0:T(8,128)}, bf16[1024,512]{1,0:T(8,128)(2,1)}, f32[8,1024]{1,0:T(8,128)}, bf16[1024,2048]...) custom-call(bf16[1024,512]{1,0:T(8,128)(2,1)} %get-tuple-element.53.refs_0_.refs_3_, ...), custom_call_target="tpu_custom_call" | custom-call | flops 153999998976 | tf_op jit(solution)/shard_map/pallas_call | solution.py:1221
  207.5 124.2 %shard_map.290 = (bf16[1024,2048]{1,0:T(8,128)(2,1)}, f32[2,8,2048]{2,1,0:T(8,128)}, f32[512,2048]{1,0:T(8,128)}, bf16[1024,2048]{1,0:T(8,128)(2,1)}, bf16[2048,...) custom-call(bf16[1024,2048]{1,0:T(8,128)(2,1)} %get-tuple-element.55.refs_0_, bf16[2048,2048]{1,0:T(8,128)(2,1)} %refs_1_.5, ...), custom_call_target="tpu_custom_call" | custom-call | flops 121000001536 | tf_op jit(solution)/shard_map/pallas_call | solution.py:1221
  331.6 0.0 reduce-scatter.4.cloned.1.call-update
  331.7 0.0 reduce-scatter.8.cloned.1.call-start
  331.7 0.7 reduce-scatter.8.cloned.1.call-update
  332.4 0.0 reduce-scatter.6.cloned.1.call-start
  332.5 117.7 %shard_map.291 = (bf16[1024,2048]{1,0:T(8,128)(2,1)}, bf16[1024,1536]{1,0:T(8,128)(2,1)}, f32[2,8,512]{2,1,0:T(8,128)}) custom-call(bf16[1024,2048]{1,0:T(8,128)(2,1)} %get-tuple-element.59.refs_0_, bf16[1024,2048]{1,0:T(8,128)(2,1)} %get-tuple-element.60.refs_1_.low_ref, bf16[2048,512]{1,0:T(8,128)(2,1)} %refs_2_.3, ...), custom_call_target="tpu_custom_call" | custom-call | flops 121000001536 | tf_op jit(solution)/shard_map/pallas_call | solution.py:1221
  450.2 0.0 reduce-scatter.4.cloned.1.call-done.down_ref
  450.2 18.2 %shard_map.292 = (bf16[2048,2048]{1,0:T(8,128)(2,1)}, f32[256,2048]{1,0:T(8,128)}, bf16[1024,2048]{1,0:T(8,128)(2,1)}) custom-call(bf16[1024,2048]{1,0:T(8,128)(2,1)} %get-tuple-element.52.act_ref, bf16[1024,1536]{1,0:T(8,128)(2,1)} %get-tuple-element.73.grads_ref.refs_0_, bf16[1024,2048]{1,0:T(8,128)(2,1)} %get-tuple-element.60.refs_1_.low_ref, ...), custom_call_target="tpu_custom_call" | custom-call | flops 11000000512 | tf_op jit(solution)/shard_map/pallas_call | solution.py:535
  468.4 0.0 reduce-scatter.6.cloned.1.call-update
  468.5 125.7 %shard_map.293 = (bf16[1024,2048]{1,0:T(8,128)(2,1)}, f32[2,8,2048]{2,1,0:T(8,128)}, f32[8,256]{1,0:T(8,128)}, f32[8,2560]{1,0:T(8,128)}) custom-call(bf16[1024,1536]{1,0:T(8,128)(2,1)} %get-tuple-element.73.grads_ref.refs_0_, bf16[1024,2048]{1,0:T(8,128)(2,1)} %bitcast.36, f32[512,2048]{1,0:T(8,128)} %get-tuple-element.74.refs_2_, ...), custom_call_target="tpu_custom_call" | custom-call | flops 121000001536 | tf_op jit(solution)/shard_map/pallas_call | solution.py:1221
  594.2 1.4 fusion.3
  595.6 1.4 fusion.2
  597.0 1.5 fusion.1
  598.6 8.1 %shard_map.294 = (f32[256,512]{1,0:T(8,128)}, f32[256,512]{1,0:T(8,128)}, f32[256,512]{1,0:T(8,128)}, f32[256,512]{1,0:T(8,128)}, f32[256,2048]{1,0:T(8,128)}, /*index=5*/bf16[1024,2048]{1,0:T(8,128)(2,1)}) custom-call(bf16[256,2048]{1,0:T(8,128)(2,1)} %reduce-scatter.6.cloned.1.call-done.head_ref, ...), custom_call_target="tpu_custom_call" | custom-call | flops 6600000000 | tf_op jit(solution)/shard_map/pallas_call | solution.py:578
  (9 shorter events, 0.0 us)
Async XLA Ops:
  7.2 0.8 copy-start
  7.2 443.0 %reduce-scatter.4.cloned.1.call-start = ((), (), s32[]{:S(2)}) async-start(), calls=%async_computation.3 | async-start | bytes 9437184 | tf_op jit(solution)/shard_map/reduce_scatter | solution.py:1428
  8.0 4.9 copy-start.2
  331.7 266.9 %reduce-scatter.8.cloned.1.call-start = ((), (), s32[]{:S(2)}) async-start(), calls=%async_computation.5 | async-start | bytes 9437184 | tf_op jit(solution)/shard_map/reduce_scatter | solution.py:1428
  332.4 266.1 %reduce-scatter.6.cloned.1.call-start = ((), (), s32[]{:S(2)}) async-start(), calls=%async_computation.4 | async-start | bytes 9437184 | tf_op jit(solution)/shard_map/reduce_scatter | solution.py:1428
  598.6 8.1 %copy-start.1 = (s32[8,1024]{1,0:T(8,128)S(1)}, s32[8,1024]{1,0:T(8,128)}, u32[]{:S(2)}) copy-start(s32[8,1024]{1,0:T(8,128)} %param.18) | copy-start | bytes 98308
Sparse Core Ops, SparseCore 0:
  331.8 102.4 reduce-scatter.3
  438.1 78.4 reduce-scatter.7
  520.1 71.5 reduce-scatter.5

commit v10 on v9

--- a/solution.py
+++ b/solution.py
@@ -16,9 +16,7 @@
 MESH = pl.DeviceIdType.MESH
 F32 = jnp.float32
 BF16 = jnp.bfloat16
-CHUNKS = 16
 SLACK = 2
-GROUP = 4
 ROWS = 256
 TILE = 512
 VMEM_LIMIT = 60 * 1024 * 1024
@@ -469,6 +467,32 @@
         grads_ref[spans(row, span), spans(mine * pairs + p, 3 * LANES)] = made[p, spans(me, span), :]
 
     head_steps = tokens // BLOCK
+    attend_at = head_steps + 3
+    weights_at = attend_at + pairs * (blocks // 2) + 3
+    tiles = features // ROWS
+
+    def weight_copy(tile):
+        rows = pl.ds(pl.multiple_of(tile * ROWS, ROWS), ROWS)
+        slot = lax.rem(tile, 2)
+        return pltpu.make_async_copy(
+            env["weight_stage"].at[slot], env["head_terms"].at[rows, :], env["weight_sem"].at[slot]
+        )
+
+    def head_weights(tile):
+        cols = pl.ds(pl.multiple_of(tile * ROWS, ROWS), ROWS)
+        slot = lax.rem(tile, 2)
+        wide = 3 * head_width
+        for left, right, first in (
+            (env["first_act"], grads_ref, 0), (low_ref, env["head_act"], wide)
+        ):
+            env["turned"][...] = jnp.transpose(left[:, cols])
+            for n in range(right.shape[1] // head_width):
+                part_cols = slice(n * head_width, (n + 1) * head_width)
+                target = slice(first + n * head_width, first + (n + 1) * head_width)
+                value = dot(env["turned"][...], right[:, part_cols], 1, 0)
+                env["weight_stage"][slot, :, target] = value.astype(BF16)
+        weight_copy(tile).start()
+
     vec_grads_ref[...] = jnp.zeros_like(vec_grads_ref)
 
     def step(now):
@@ -490,104 +514,112 @@
             lax.fori_loop(0, tokens // LANES, head_apply, 0)
             lax.fori_loop(0, pairs, share_out, 0)
 
-        turn = t - (head_steps + 3)
-        p = turn // blocks
-        for qb in range(blocks):
-
-            @pl.when((turn >= 0) & (turn < pairs * blocks) & (lax.rem(turn + 8 * blocks, blocks) == qb))
+        each = blocks // 2
+        turn = t - attend_at
+        p = turn // each
+        for i in range(each):
+
+            @pl.when((turn >= 0) & (turn < pairs * each) & (lax.rem(turn + 32 * each, each) == i))
             def _():
-                if qb == 0:
+                if i == 0:
                     pair_start(p)
-                pair_block(p, qb)
-                if qb == blocks - 1:
+                pair_block(p, 2 * i)
+                pair_block(p, 2 * i + 1)
+                if i == each - 1:
                     pair_end(p)
+
+        tile = t - weights_at
+
+        @pl.when(tile == 0)
+        def _():
+            def arrive(p, carry):
+                for k in range(1, count):
+                    back(p, k).wait_recv()
+                return carry
+
+            lax.fori_loop(0, pairs, arrive, 0)
+
+        pl.when((tile >= 2) & (tile < tiles))(lambda: weight_copy(tile - 2).wait())
+        pl.when((tile >= 0) & (tile < tiles))(lambda: head_weights(tile))
 
     def end():
         def drain(p, carry):
             for k in range(1, count):
                 there(p, k).wait_send()
-                back(p, k).wait()
+                back(p, k).wait_send()
             return carry
 
         lax.fori_loop(0, pairs, drain, 0)
-
-    return step, end, 1 + head_steps + 3 + pairs * blocks
-
-
-def weight_kernel(
-    act_ref, grads_ref, low_ref, head_ref, down_ref, block_ref, out_ref, down_out, block_out
+        for tile in (tiles - 2, tiles - 1):
+            weight_copy(tile).wait()
+
+    return step, end, 1 + weights_at + tiles
+
+
+def last_kernel(
+    head_ref, up_ref, down_ref, grad_ref, block_ref, own_ref, split_ref,
+    query_out, key_out, value_out, out_out, up_out, down_out, grad_out, block_out, *vectors
 ):
-    wide = grads_ref.shape[1]
-    out_ref[:, :wide] = dot(jnp.transpose(act_ref[...]), grads_ref[...], 1, 0).astype(BF16)
-    out_ref[:, wide:] = dot(jnp.transpose(low_ref[...]), head_ref[...], 1, 0).astype(BF16)
-    down_out[...] = down_ref[...].astype(F32)
+    grad_out[...] = grad_ref[...]
     block_out[...] = block_ref[...]
-
-
-def head_weights(act, grads, low, head_act, down_grad, block_out):
-    tokens, model_width = act.shape
-    wide, narrow = grads.shape[1], head_act.shape[1]
-    steps = model_width // ROWS
-    tile = pl.BlockSpec((tokens, ROWS), lambda i: (0, i))
-    part = pl.BlockSpec((tokens // steps, model_width), lambda i: (i, 0))
-    own_rows, own_width = down_grad.shape
-    own = pl.BlockSpec((own_rows // steps, own_width), lambda i: (i, 0))
-    return pl.pallas_call(
-        weight_kernel,
-        grid=(steps,),
-        out_shape=[
-            jax.ShapeDtypeStruct((model_width, wide + narrow), BF16),
-            jax.ShapeDtypeStruct(down_grad.shape, F32),
-            jax.ShapeDtypeStruct(block_out.shape, BF16),
-        ],
-        in_specs=[
-            tile,
-            pl.BlockSpec((tokens, wide), lambda i: (0, 0)),
-            tile,
-            pl.BlockSpec((tokens, narrow), lambda i: (0, 0)),
-            own,
-            part,
-        ],
-        out_specs=[pl.BlockSpec((ROWS, wide + narrow), lambda i: (i, 0)), own, part],
-        compiler_params=pltpu.CompilerParams(vmem_limit_bytes=VMEM_LIMIT),
-        cost_estimate=cost(10),
-    )(act, grads, low, head_act, down_grad, block_out)
-
-
-def last_kernel(head_ref, up_ref, grad_ref, *refs):
-    outs, up_out, grad_out = refs[:4], refs[4], refs[5]
-    grad_out[...] = grad_ref[...]
-    width = outs[0].shape[1]
+    up_out[...] = up_ref[...].astype(F32)
+    down = down_ref[0].astype(F32)
+    for k in range(1, down_ref.shape[0]):
+        down = down + down_ref[k].astype(F32)
+    down_out[...] = down
+    width = out_out.shape[1]
     for j in range(width // LANES):
-        for i in range(3):
+        for i, target in enumerate((query_out, key_out, value_out)):
             start = (3 * j + i) * LANES
-            outs[i][:, j * LANES : (j + 1) * LANES] = head_ref[:, start : start + LANES].astype(F32)
-    outs[3][...] = head_ref[:, 3 * width :].astype(F32)
-    up_out[...] = up_ref[...].astype(F32)
-
-
-def last_results(head_grads, up_grad, input_grad, head_width):
+            target[:, j * LANES : (j + 1) * LANES] = head_ref[:, start : start + LANES].astype(F32)
+    out_out[...] = head_ref[:, 3 * width :].astype(F32)
+
+    @pl.when(pl.program_id(0) == 0)
+    def _():
+        places = [(own_ref, i, 0) for i in range(4)]
+        hidden = vectors[4].shape[0] * LANES
+        places += [(split_ref, i, 0) for i in range(2)] + [(split_ref, i, hidden) for i in range(2)]
+        for target, (source, row, first) in zip(vectors, places):
+            for i in range(target.shape[0]):
+                start = first + i * LANES
+                target[i : i + 1, :] = source[row : row + 1, start : start + LANES]
+
+
+def last_results(
+    head_grads, up_grad, down_terms, input_grad, block_out, norm_own, norm_split, head_width
+):
     rows = head_grads.shape[0]
     steps = rows // 32
-
-    def block(width):
-        return pl.BlockSpec((rows // steps, width), lambda i: (i, 0))
-
     tokens, width = input_grad.shape
+
+    def block(columns):
+        return pl.BlockSpec((rows // steps, columns), lambda i: (i, 0))
+
+    def whole(shape):
+        return pl.BlockSpec(shape, lambda i: (0, 0))
+
     part = pl.BlockSpec((tokens // steps, width), lambda i: (i, 0))
+    own = norm_own.shape[1]
+    hidden = norm_split.shape[1] - head_width
+    vectors = [(size // LANES, LANES) for size in (own,) * 4 + (hidden,) * 2 + (head_width,) * 2]
+    sizes = [head_width] * 4 + [up_grad.shape[1]] * 2
     return pl.pallas_call(
         last_kernel,
         grid=(steps,),
-        out_shape=[jax.ShapeDtypeStruct((rows, head_width), F32)] * 4
-        + [
-            jax.ShapeDtypeStruct(up_grad.shape, F32),
-            jax.ShapeDtypeStruct(input_grad.shape, BF16),
-        ],
-        in_specs=[block(head_grads.shape[1]), block(up_grad.shape[1]), part],
-        out_specs=[block(head_width)] * 4 + [block(up_grad.shape[1]), part],
+        out_shape=[jax.ShapeDtypeStruct((rows, size), F32) for size in sizes]
+        + [jax.ShapeDtypeStruct((tokens, width), BF16)] * 2
+        + [jax.ShapeDtypeStruct(shape, F32) for shape in vectors],
+        in_specs=[
+            block(head_grads.shape[1]),
+            block(up_grad.shape[1]),
+            pl.BlockSpec((down_terms.shape[0], rows // steps, down_terms.shape[2]), lambda i: (0, i, 0)),
+        ]
+        + [part] * 2
+        + [whole(norm_own.shape), whole(norm_split.shape)],
+        out_specs=[block(size) for size in sizes] + [part] * 2 + [whole(shape) for shape in vectors],
         compiler_params=pltpu.CompilerParams(vmem_limit_bytes=VMEM_LIMIT),
-        cost_estimate=cost(6),
-    )(head_grads, up_grad, input_grad)
+        cost_estimate=cost(10),
+    )(head_grads, up_grad, down_terms, input_grad, block_out, norm_own, norm_split)
 
 
 def fold(values):
@@ -784,6 +816,47 @@
     return pltpu.make_async_copy(env[name], env["target " + name], env["sem " + name].at[0])
 
 
+def spread_copy(env, device):
+    landed, terms = env["spread"], env["w_down_terms"]
+    count, own = landed.shape[:2]
+    me = lax.axis_index("seq")
+    k = lax.rem(device - me + count, count)
+    rows = pl.ds(pl.multiple_of(device * own, own), own)
+    return pltpu.make_async_remote_copy(
+        src_ref=terms.at[rows, :],
+        dst_ref=landed.at[me],
+        send_sem=env["spread_send"].at[k],
+        recv_sem=env["spread_recv"].at[k],
+        device_id={"seq": device},
+        device_id_type=MESH,
+    )
+
+
+def spread_own(env):
+    landed, terms = env["spread"], env["w_down_terms"]
+    own = landed.shape[1]
+    me = lax.axis_index("seq")
+    rows = pl.ds(pl.multiple_of(me * own, own), own)
+    return pltpu.make_async_copy(terms.at[rows, :], landed.at[me], env["spread_own"].at[0])
+
+
+def spread_rows(env, rows):
+    own = env["spread"].shape[1]
+    me = lax.axis_index("seq")
+    for i in range(ROWS // own):
+        device = rows.start // own + i
+        pl.when(device != me)(lambda device=device: spread_copy(env, device).start())
+        pl.when(device == me)(lambda: spread_own(env).start())
+
+
+def spread_wait(env):
+    count = env["spread"].shape[0]
+    me = lax.axis_index("seq")
+    for k in range(1, count):
+        spread_copy(env, lax.rem(me + k, count)).wait()
+    spread_own(env).wait()
+
+
 def split_copies(env, seq_count):
     split = env["split"]
     return share("seq", seq_count, lambda d: split, env["split_landed"], *env_pair(env, "split"), False)
@@ -857,7 +930,7 @@
     return copies
 
 
-def line_kernel(plan, count, chunks, slack, *refs):
+def line_kernel(plan, count, chunks, group, slack, *refs):
     env = dict(zip(plan["order"], refs, strict=True))
     finish, parts, tasks = plan["finish"], plan["parts"], plan["tasks"]
     num_task = len(tasks)
@@ -928,7 +1001,7 @@
         return hop(rows, rows, rsb_s, rsb_r, c, up)
 
     def block_start(t, offset):
-        return jnp.clip((t - lax.rem(t, GROUP) - offset) * size, 0, half - GROUP * size)
+        return jnp.clip((t - lax.rem(t, group) - offset) * size, 0, half - group * size)
 
     def reduce_step(t, c, offset, place, rows, landed, move, gather, starts, ends):
         here = rows(c)
@@ -937,7 +1010,7 @@
         def term():
             if not parts:
                 return env["ready"][here, :].astype(F32)
-            row = place * GROUP * size + c * size - block_start(t, offset)
+            row = place * group * size + c * size - block_start(t, offset)
             return env["part"][pl.ds(pl.multiple_of(row, size), size), :]
 
         @pl.when(starts)
@@ -973,8 +1046,8 @@
         pl.when((c >= 0) & (c < chunks))(lambda: work(c))
 
     def make_parts(t):
-        top = pl.ds(pl.multiple_of(block_start(t, from_last), size), GROUP * size)
-        low = pl.ds(pl.multiple_of(half + block_start(t, from_first), size), GROUP * size)
+        top = pl.ds(pl.multiple_of(block_start(t, from_last), size), group * size)
+        low = pl.ds(pl.multiple_of(half + block_start(t, from_first), size), group * size)
 
         def columns(n, carry):
             cols = pl.ds(pl.multiple_of(n * TILE, TILE), TILE)
@@ -987,16 +1060,23 @@
 
         lax.fori_loop(0, width // TILE, columns, 0)
 
+    def task_rows(index, tile):
+        if tasks[index][0] == "spread":
+            tiles = env[tasks[index][3]].shape[0] // ROWS
+            own = ROWS // env["spread"].shape[1]
+            tile = lax.rem(lax.axis_index("seq") // own + 1 + tile, tiles)
+        return pl.ds(pl.multiple_of(tile * ROWS, ROWS), ROWS)
+
     def run_task(index, tile, slot):
         kind, left, right, name = tasks[index]
         target = env[name]
-        rows = pl.ds(pl.multiple_of(tile * ROWS, ROWS), ROWS)
-        if kind == "weight":
+        rows = task_rows(index, tile)
+        if kind in ("weight", "spread"):
             env["turned"][...] = jnp.transpose(env[left][:, rows])
 
         def columns(n, carry):
             cols = pl.ds(pl.multiple_of(n * TILE, TILE), TILE)
-            if kind == "weight":
+            if kind in ("weight", "spread"):
                 value = dot(env["turned"][...], env[right][:, cols], 1, 0)
             elif kind == "keep":
                 value = dot(env[left][rows, :], env[right][:, cols], 1, 0)
@@ -1019,7 +1099,7 @@
 
     def stage_copy(index, tile, slot):
         target = env[tasks[index][3]]
-        rows = pl.ds(pl.multiple_of(tile * ROWS, ROWS), ROWS)
+        rows = task_rows(index, tile)
         return pltpu.make_async_copy(
             env["stage"].at[slot, :, : target.shape[1]], target.at[rows, :], env["stage_sem"].at[slot]
         )
@@ -1028,12 +1108,12 @@
     for task in tasks:
         starts_at.append(starts_at[-1] + env[task[3]].shape[0] // ROWS)
     task_total = starts_at[-1]
-    per_group = GROUP - 1
+    per_group = group - 1
     staged = any(task[0] != "keep" for task in tasks)
 
     def step(t, carry):
         if parts:
-            pl.when(lax.rem(t, GROUP) == 0)(lambda: make_parts(t))
+            pl.when(lax.rem(t, group) == 0)(lambda: make_parts(t))
         when_chunk(
             t - from_last,
             lambda c: reduce_step(t, c, from_last, 0, a_rows, in_a, reduce_a, gather_a, last, first),
@@ -1044,23 +1124,27 @@
         )
         when_chunk(t - ahead - from_first, lambda c: gather_step(c, gather_a, first, last))
         when_chunk(t - ahead - from_last, lambda c: gather_step(c, gather_b, last, first))
-        for moment, group in ((1, plan["late"]), (4, plan["later"])):
+        for moment, waited in ((1, plan["late"]), (4, plan["later"])):
 
             @pl.when(t == moment)
             def _():
-                for name in group:
+                for name in waited:
                     loads[name].wait()
 
         if num_task:
-            turn = (t // GROUP) * per_group + lax.rem(t, GROUP) - 1
-            free = lax.rem(t, GROUP) != 0
+            turn = (t // group) * per_group + lax.rem(t, group) - 1
+            free = lax.rem(t, group) != 0
             slot = lax.rem(turn + per_group + 1, 2)
 
             for index in range(num_task if staged else 0):
                 low, high = starts_at[index] + 2, min(starts_at[index + 1] + 2, task_total)
-                pl.when(free & (turn >= low) & (turn < high))(
-                    lambda index=index, low=low: stage_copy(index, turn - low, slot).wait()
-                )
+
+                def staged_done(index=index, low=low):
+                    stage_copy(index, turn - low, slot).wait()
+                    if tasks[index][0] == "spread":
+                        spread_rows(env, task_rows(index, turn - low))
+
+                pl.when(free & (turn >= low) & (turn < high))(staged_done)
             for index in range(num_task):
                 low, high = starts_at[index], starts_at[index + 1]
                 pl.when(free & (turn >= low) & (turn < high))(
@@ -1073,26 +1157,26 @@
         for name, moment in plan["stores"].items():
             if moment == "reduced":
                 pl.when(t == chunks + ahead)(lambda name=name: whole_store(env, name).start())
-        done_a = t - ahead - from_first - (GROUP - 1)
-        done_b = t - ahead - from_last - (GROUP - 1)
-        has_a = (done_a >= 0) & (done_a < chunks) & (lax.rem(done_a + 64, GROUP) == 0)
-        has_b = (done_b >= 0) & (done_b < chunks) & (lax.rem(done_b + 64, GROUP) == 0)
+        done_a = t - ahead - from_first - (group - 1)
+        done_b = t - ahead - from_last - (group - 1)
+        has_a = (done_a >= 0) & (done_a < chunks) & (lax.rem(done_a + 64, group) == 0)
+        has_b = (done_b >= 0) & (done_b < chunks) & (lax.rem(done_b + 64, group) == 0)
 
         @pl.when(has_a | has_b)
         def _():
-            block = jnp.where(has_a, done_a // GROUP, chunks // GROUP + done_b // GROUP)
+            block = jnp.where(has_a, done_a // group, chunks // group + done_b // group)
             row_store(env, "out", block).start()
             if plan["rows_done"]:
                 plan["rows_done"](env, block)
 
         if plan["rows_late"]:
-            late_a = t - 2 * ahead - (GROUP - 1) - 2
-
-            place = lax.rem(late_a + 64, GROUP)
+            late_a = t - 2 * ahead - (group - 1) - 2
+
+            place = lax.rem(late_a + 64, group)
 
             @pl.when((late_a >= 0) & (place < 2))
             def _():
-                plan["rows_late"](env, place * (chunks // GROUP) + late_a // GROUP)
+                plan["rows_late"](env, place * (chunks // group) + late_a // group)
 
         return carry
 
@@ -1114,17 +1198,19 @@
         assert work_steps <= steps
     lax.fori_loop(0, steps, step, 0)
     if num_task:
-        assert (steps // GROUP) * per_group >= task_total
+        assert (steps // group) * per_group >= task_total
     if staged:
         assert task_total >= 2
         for turn in (task_total - 2, task_total - 1):
             index = max(i for i in range(num_task) if starts_at[i] <= turn)
             stage_copy(index, turn - starts_at[index], turn % 2).wait()
+    if "spread" in env:
+        spread_wait(env)
     if plan["rows_late"]:
-        assert chunks + 2 * ahead == steps and GROUP == 4
+        assert chunks + 2 * ahead == steps and group == 4
 
         def rest(place, carry):
-            plan["rows_late"](env, (place + 1) * (chunks // GROUP) - 1)
+            plan["rows_late"](env, (place + 1) * (chunks // group) - 1)
             return carry
 
         lax.fori_loop(0, 2, rest, 0)
@@ -1157,7 +1243,7 @@
 
 def line_sum(
     finish, count, held, vecs, parts, collective_id, *, tokens, late=(), later=(), tasks=(), owns=(),
-    sent=(), stores=(), scratch=(), loose=(), start=None, before=None, rows_done=None, rows_late=None, work=None,
+    sent=(), stores=(), scratch=(), loose=(), chunks=16, group=4, turned=False, start=None, before=None, rows_done=None, rows_late=None, work=None,
     seq_count=0, seq_barrier=0, micros=110,
 ):
     names = dict(scratch)
@@ -1166,21 +1252,22 @@
     else:
         width = held["ready"].shape[1]
     half = tokens // 2
-    depth = tokens if any(task[0] == "weight" for task in tasks) else LANES
-    stage_width = max([shape.shape[1] for _, shape in sent] + [LANES])
+    depth = tokens if turned or any(task[0] == "weight" for task in tasks) else LANES
+    staged = [shape.shape[-1] for _, shape in sent] if tasks else []
+    stage_width = max(staged + [LANES])
     fixed = [
         ("in_a", pltpu.VMEM((half, width), BF16)),
         ("in_b", pltpu.VMEM((half, width), BF16)),
-        ("part", pltpu.VMEM((2 * GROUP * half // CHUNKS if parts else 8, width), F32)),
+        ("part", pltpu.VMEM((2 * group * half // chunks if parts else 8, width), F32)),
         ("turned", pltpu.VMEM((ROWS, depth), BF16)),
-        ("stage", pltpu.VMEM((2, ROWS if sent else 16, stage_width), BF16)),
+        ("stage", pltpu.VMEM((2, ROWS if staged else 16, stage_width), BF16)),
         ("load_sem", pltpu.SemaphoreType.DMA((len(held),))),
         ("stage_sem", pltpu.SemaphoreType.DMA((2,))),
     ] + [
-        (name, pltpu.SemaphoreType.DMA((CHUNKS,)))
+        (name, pltpu.SemaphoreType.DMA((chunks,)))
         for name in ("rsa_s", "rsa_r", "rsb_s", "rsb_r", "aga_s", "aga_r", "agb_s", "agb_r")
     ]
-    assert half // CHUNKS * GROUP == LANES
+    assert half // chunks * group == LANES
     loose = dict(loose)
     stores = dict(stores, out="rows")
     shapes = [("out", jax.ShapeDtypeStruct((tokens, width), BF16))] + list(owns)
@@ -1219,7 +1306,7 @@
     whole = pl.BlockSpec(memory_space=pltpu.VMEM)
     any_space = pl.BlockSpec(memory_space=pl.ANY)
     return pl.pallas_call(
-        functools.partial(line_kernel, plan, count, CHUNKS, SLACK),
+        functools.partial(line_kernel, plan, count, chunks, group, SLACK),
         out_shape=[shape for _, shape in shapes] + [shape for _, shape in sent],
         in_specs=[any_space] * (len(held) + len(loose)) + [whole] * len(vecs),
         out_specs=[any_space if name in stores else whole for name, _ in shapes]
@@ -1393,7 +1480,7 @@
     )
 
     weight_shape = shape_of((model_width, hidden_size), BF16)
-    grad_middle_low, second_sums, grad_middle_own, down_part, w_down_terms, w_up_terms = line_sum(
+    grad_middle_low, second_sums, grad_middle_own, down_part, _, w_up_terms, down_terms = line_sum(
         finish_second,
         tp_count,
         dict(
@@ -1409,12 +1496,12 @@
         (("grad_up", "w_up"),),
         4,
         tokens=tokens,
-        late=("hidden_act", "w_down", "middle"),
-        later=("cotangent", "second_act"),
+        late=("hidden_act", "cotangent"),
+        later=("w_down", "middle", "second_act"),
         stores=dict(middle_grad="reduced"),
         tasks=(
+            ("spread", "cotangent", "hidden_act", "w_down_terms"),
             ("down", "hidden_act", "w_down", "down_part"),
-            ("weight", "cotangent", "hidden_act", "w_down_terms"),
             ("weight", "second_act", "grad_up", "w_up_terms"),
         ),
         owns=(("sums", sums_shape), ("middle_grad", own_shape)),
@@ -1422,12 +1509,18 @@
             ("down_part", shape_of((tokens, model_width), BF16)),
             ("w_down_terms", weight_shape),
             ("w_up_terms", weight_shape),
+            ("spread", shape_of((seq_count, model_width // seq_count, hidden_size), BF16)),
         ),
+        scratch=(
+            ("spread_send", pltpu.SemaphoreType.DMA((seq_count,))),
+            ("spread_recv", pltpu.SemaphoreType.DMA((seq_count,))),
+            ("spread_own", pltpu.SemaphoreType.DMA((1,))),
+        ),
+        seq_barrier=seq_count,
     )
     def scatter(grad):
         return lax.psum_scatter(grad, "seq", scatter_dimension=0, tiled=True)
 
-    w_down_grad = scatter(w_down_terms)
     w_up_grad = scatter(w_up_terms)
 
     pairs = head_width // groups // LANES
@@ -1435,7 +1528,7 @@
     pair_rows = pltpu.VMEM((length, LANES), BF16)
     pair_sums = pltpu.VMEM((length, LANES), F32)
     pair_heads = pltpu.VMEM((2, length, LANES), BF16)
-    block_out, grads, head_vec_grads = line_sum(
+    block_out, grads, head_vec_grads, head_terms = line_sum(
         lambda total, here, own, env: total,
         tp_count,
         dict(
@@ -1448,18 +1541,24 @@
             o=o_row,
             lse=lse,
             packed=tables,
+            first_act=first_act,
+            head_act=head_act,
         ),
         dict(vecs=vecs, seg_col=seg_col, seg_row=seg_row),
         (),
         5,
         tokens=tokens,
         late=("low", "w_out", "mixed", "head_sums"),
-        later=("qkv", "o", "lse", "packed"),
+        later=("qkv", "o", "lse", "packed", "first_act", "head_act"),
         owns=(
             ("grads", shape_of((tokens, 3 * head_width), BF16)),
             ("head_vec_grads", shape_of((2, 8, head_width))),
         ),
+        sent=(("head_terms", shape_of((model_width, 4 * head_width), BF16)),),
+        turned=True,
         scratch=(
+            ("weight_stage", pltpu.VMEM((2, ROWS, 4 * head_width), BF16)),
+            ("weight_sem", pltpu.SemaphoreType.DMA((2,))),
             ("do", pltpu.VMEM((tokens, head_width), BF16)),
             ("scaled", pltpu.VMEM((tokens, head_width), F32)),
             ("head_part", pltpu.VMEM((8, tokens), F32)),
@@ -1486,10 +1585,7 @@
         work=lambda env: back_work(env, seq_count, tp_count, groups),
         seq_barrier=seq_count,
     )
-    head_terms, w_down_grad, block_out = head_weights(
-        first_act, grads, grad_middle_low, head_act, w_down_grad, block_out
-    )
-    grads, head_terms = lax.optimization_barrier((grads, head_terms))
+    grads, head_terms, w_up_grad = lax.optimization_barrier((grads, head_terms, w_up_grad))
     head_grads = scatter(head_terms)
     own_width = model_width // seq_count
     split_width = hidden_size + head_width
@@ -1507,6 +1603,8 @@
         (("grads", "w_pairs"),),
         8,
         tokens=tokens,
+        chunks=32,
+        group=8,
         later=("block", "middle_grad"),
         loose=dict(w_query=w_query, w_key=w_key, w_value=w_value),
         owns=(
@@ -1533,25 +1631,29 @@
         seq_count=seq_count,
     )
 
-    w_query_grad, w_key_grad, w_value_grad, w_out_grad, w_up_grad, input_grad = last_results(
-        head_grads, w_up_grad, input_grad, head_width
+    (
+        w_query_grad, w_key_grad, w_value_grad, w_out_grad, w_up_grad, w_down_grad, input_grad,
+        block_out, *vectors,
+    ) = last_results(
+        head_grads, w_up_grad, down_terms, input_grad, block_out, norm_own, norm_split, head_width
     )
+    vectors = [vector.reshape(-1) for vector in vectors]
     return (
         block_out.reshape(block_in.shape),
         input_grad.reshape(block_in.shape),
-        norm_own[2],
-        norm_own[3],
+        vectors[2],
+        vectors[3],
         w_query_grad,
         w_key_grad,
         w_value_grad,
-        norm_split[0, hidden_size:],
-        norm_split[1, hidden_size:],
+        vectors[6],
+        vectors[7],
         w_out_grad,
-        norm_own[0],
-        norm_own[1],
+        vectors[0],
+        vectors[1],
         w_up_grad,
-        norm_split[0, :hidden_size],
-        norm_split[1, :hidden_size],
+        vectors[4],
+        vectors[5],
         w_down_grad,
     )
 

time: 614 us -> 592 us (0.964)
  Pallas kernels: 589 us -> 572 us
    pallas_call x5 -> x4, Pallas kernels: 521 us -> 498 us  [line_sum(): pl.pallas_call(functools.partial(line_kernel, plan, count, chunks, group,...]
  transfers between devices with their start and end apart: 3 -> 2, of which waited for: 0 -> 0; matrix products, arithmetic and copies ran while one was open for 1% -> 0% of each run, Pallas kernels for 43% -> 41%
where the time goes in v10:
time: 592 us
  Pallas kernels  572 us (97%)
  between operations  14.2 us (2%)
    pallas_call x4, Pallas kernels, line_sum(): pl.pallas_call(functools.partial(line_kernel, plan, count, chunks, group,...  498 us
    pallas_call x1, Pallas kernels, front(): pl.pallas_call(functools.partial(front_kernel, count, groups, len(pieces)...  59.9 us
    pallas_call x1, Pallas kernels, last_results(): pl.pallas_call(last_kernel, grid=(steps,), out_shape=[jax.ShapeDtypeStruc...  13.6 us
  transfers between devices with their start and end apart: 2, of which 0 were waited for; matrix products, arithmetic and copies ran while one was open for 0% of the time, Pallas kernels for 41%

profile of v10, /device:TPU:0, one launch (start us, length us, event | category | flops | bytes accessed | tf_op | source)
XLA Modules:
  0.0 591.5 jit_solution(14166225476509848253)
XLA Ops:
  7.2 0.0 copy-start
  7.2 0.0 reduce-scatter.3.cloned.1.call-start
  7.3 0.7 copy-done
  8.0 0.0 copy-start.2
  8.0 0.6 convert_reduce_fusion
  8.6 1.0 copy.39.refs_5_.refs_12_
  9.6 2.0 multiply_cosine_fusion
  11.6 1.3 pad_maximum_fusion.refs_4_.refs_8_
  12.9 0.0 copy-done.2
  12.9 59.9 %shard_map.288 = (bf16[1024,2048]{1,0:T(8,128)(2,1)}, bf16[4,1024,384]{2,1,0:T(8,128)(2,1)}, bf16[4,1024,128]{2,1,0:T(8,128)(2,1)}, f32[4,8,1024]{2,1,0:T(8,128)...) custom-call(bf16[1024,2048]{1,0:T(8,128)(2,1)} %bitcast.26, bf16[2048,512]{1,0:T(8,128)(2,1)} %refs_3_.3, ...), custom_call_target="tpu_custom_call" | custom-call | flops 65999998976 | tf_op jit(solution)/shard_map/pallas_call | solution.py:295
  72.7 134.7 %shard_map.289 = (bf16[1024,2048]{1,0:T(8,128)(2,1)}, f32[512,2048]{1,0:T(8,128)}, bf16[1024,512]{1,0:T(8,128)(2,1)}, f32[8,1024]{1,0:T(8,128)}, bf16[1024,2048]...) custom-call(bf16[1024,512]{1,0:T(8,128)(2,1)} %get-tuple-element.61.refs_0_.refs_3_, ...), custom_call_target="tpu_custom_call" | custom-call | flops 153999998976 | tf_op jit(solution)/shard_map/pallas_call | solution.py:1308
  207.5 123.0 %shard_map.290 = (bf16[1024,2048]{1,0:T(8,128)(2,1)}, f32[2,8,2048]{2,1,0:T(8,128)}, f32[512,2048]{1,0:T(8,128)}, bf16[1024,2048]{1,0:T(8,128)(2,1)}, bf16[2048,...) custom-call(bf16[1024,2048]{1,0:T(8,128)(2,1)} %get-tuple-element.63.refs_0_, ...), custom_call_target="tpu_custom_call" | custom-call | flops 121000001536 | tf_op jit(solution)/shard_map/pallas_call | solution.py:1308
  330.5 0.0 reduce-scatter.3.cloned.1.call-update
  330.5 0.0 reduce-scatter.5.cloned.1.call-start
  330.5 119.0 %shard_map.291 = (bf16[1024,2048]{1,0:T(8,128)(2,1)}, bf16[1024,1536]{1,0:T(8,128)(2,1)}, f32[2,8,512]{2,1,0:T(8,128)}, bf16[2048,2048]{1,0:T(8,128)(2,1)}) custom-call(bf16[1024,2048]{1,0:T(8,128)(2,1)} %get-tuple-element.67.refs_0_, bf16[1024,2048]{1,0:T(8,128)(2,1)} %get-tuple-element.68.refs_1_, bf16[2048,512]{1,0:T(8,128)(2,1)} %refs_2_.3, ...), custom_call_target="tpu_custom_call" | custom-call | flops 121000001536 | tf_op jit(solution)/shard_map/pallas_call | solution.py:1308
  449.5 0.0 reduce-scatter.3.cloned.1.call-done.up_ref
  449.5 0.0 reduce-scatter.5.cloned.1.call-update
  449.6 121.4 %shard_map.292 = (bf16[1024,2048]{1,0:T(8,128)(2,1)}, f32[2,8,2048]{2,1,0:T(8,128)}, f32[8,256]{1,0:T(8,128)}, f32[8,2560]{1,0:T(8,128)}) custom-call(bf16[1024,1536]{1,0:T(8,128)(2,1)} %get-tuple-element.81.refs_0_, bf16[1024,2048]{1,0:T(8,128)(2,1)} %bitcast.28, f32[512,2048]{1,0:T(8,128)} %get-tuple-element.82.refs_2_, bf16[2048,512]{1,0:T(8,128)(2,1)} %refs_3_.3, ...), custom_call_target="tpu_custom_call" | custom-call | flops 121000001536 | tf_op jit(solution)/shard_map/pallas_call | solution.py:1308
  571.0 0.0 reduce-scatter.5.cloned.1.call-done.head_ref
  571.0 0.0 copy-start.1
  571.0 13.6 %shard_map.293 = (f32[256,512]{1,0:T(8,128)}, f32[256,512]{1,0:T(8,128)}, f32[256,512]{1,0:T(8,128)}, f32[256,512]{1,0:T(8,128)}, f32[256,2048]{1,0:T(8,128)}, /...) custom-call(bf16[256,2048]{1,0:T(8,128)(2,1)} %reduce-scatter.5.clon, ...), custom_call_target="tpu_custom_call" | custom-call | flops 11000000512 | tf_op jit(solution)/shard_map/pallas_call | solution.py:606
  584.7 0.0 copy-done.1
  (4 shorter events, 0.0 us)
Async XLA Ops:
  7.2 0.8 copy-start
  7.2 442.3 %reduce-scatter.3.cloned.1.call-start = ((), (), s32[]{:S(2)}) async-start(), calls=%async_computation.2 | async-start | bytes 9437184 | tf_op jit(solution)/shard_map/reduce_scatter | solution.py:1522
  8.0 4.9 copy-start.2
  330.5 240.5 %reduce-scatter.5.cloned.1.call-start = ((), (), s32[]{:S(2)}) async-start(), calls=%async_computation.3 | async-start | bytes 9437184 | tf_op jit(solution)/shard_map/reduce_scatter | solution.py:1522
  571.0 13.6 %copy-start.1 = (s32[8,1024]{1,0:T(8,128)S(1)}, s32[8,1024]{1,0:T(8,128)}, u32[]{:S(2)}) copy-start(s32[8,1024]{1,0:T(8,128)} %param.18) | copy-start | bytes 98308
Sparse Core Ops, SparseCore 0:
  330.6 111.4 reduce-scatter.2
  449.7 69.9 reduce-scatter.4

commit v11 on v10

--- a/solution.py
+++ b/solution.py
@@ -17,6 +17,7 @@
 F32 = jnp.float32
 BF16 = jnp.bfloat16
 SLACK = 2
+SLACK_OUT = 2
 ROWS = 256
 TILE = 512
 VMEM_LIMIT = 60 * 1024 * 1024
@@ -95,27 +96,30 @@
     return shifted * inverse, inverse
 
 
-def expand_tables(packed, tables):
-    quarter = HEAD // 2
-    for block in range(packed.shape[0] // BLOCK):
-        rows = block_rows(block)
-        lane = lax.broadcasted_iota(jnp.int32, (BLOCK, LANES), 1)
-        group = lane // quarter
-        turns = [packed[rows, :]]
-        for k in range(1, 4):
-            turns.append(pltpu.roll(turns[0], k * quarter, 1))
-
-        def spread(index):
-            values = turns[(0 - index) % 4]
-            for g in range(1, 4):
-                values = jnp.where(group == g, turns[(g - index) % 4], values)
-            return values
-
-        cos_part = spread(0)
-        sin_part = spread(1)
-        sin_part = jnp.where(lane % HEAD < quarter, -sin_part, sin_part)
-        for k in range(2):
-            factor = spread(2 + k)
+def seg_column(seg_row, index, size):
+    columns = []
+    for i in range(size // LANES):
+        start = index * size + i * LANES
+        square = jnp.broadcast_to(seg_row[:, start : start + LANES], (LANES, LANES))
+        columns.append(jnp.transpose(square)[:, :1])
+    return jnp.concatenate(columns, axis=0)
+
+
+def make_tables(seg_row, tables):
+    lane = lax.broadcasted_iota(jnp.int32, (1, LANES), 1)
+    index = (lane % (HEAD // 2)).astype(F32)
+    theta_rate = jnp.exp(-2.0 * index / HEAD * math.log(10000.0))
+    zeta_base = (2.0 * index + 0.4 * HEAD) / (1.4 * HEAD)
+    rate = jnp.log(zeta_base) / 512.0
+    for block in range(seg_row.shape[1] // LANES):
+        rows = slice(block * LANES, (block + 1) * LANES)
+        before = (seg_row[...] < seg_column(seg_row, block, LANES)).astype(F32)
+        place = lax.broadcasted_iota(jnp.int32, (LANES, 1), 0) + block * LANES
+        place = place.astype(F32) - jnp.sum(before, axis=1, keepdims=True)
+        cos_part = jnp.cos(place * theta_rate)
+        sin_part = jnp.sin(place * theta_rate)
+        sin_part = jnp.where(lane % HEAD < HEAD // 2, -sin_part, sin_part)
+        for k, factor in enumerate((jnp.exp(place * rate), jnp.exp(-place * rate))):
             tables[2 * k, rows, :] = cos_part * factor
             tables[2 * k + 1, rows, :] = sin_part * factor
 
@@ -123,11 +127,11 @@
 def front_kernel(
     count, groups, num_vec, *refs
 ):
-    (x_ref, wq_ref, wk_ref, wv_ref, packed_ref, segc_ref, segr_ref), refs = refs[:7], refs[7:]
+    (x_ref, wq_ref, wk_ref, wv_ref, segr_ref), refs = refs[:5], refs[5:]
     pieces, refs = refs[:num_vec], refs[num_vec:]
     (
-        act_out, qkv_out, o_ref, lse_ref, mixed_ref, vecs_ref, act_ref, qkv_ref,
-        weights, staged, tab_ref, bias, qs, ks, load_sem, act_sem, qkv_sem, send_sem, recv_sem, back_send_sem, back_recv_sem,
+        act_out, qkv_out, tab_out, o_ref, lse_ref, mixed_ref, vecs_ref, act_ref, qkv_ref,
+        weights, staged, tab_ref, bias, qs, ks, load_sem, act_sem, tab_sem, qkv_sem, send_sem, recv_sem, back_send_sem, back_recv_sem,
     ) = refs
     me = lax.axis_index("seq")
     pairs, length = qkv_ref.shape[:2]
@@ -224,11 +228,13 @@
         return carry
 
     lax.fori_loop(1, pairs, project, 0)
-    expand_tables(packed_ref, tab_ref)
+    make_tables(segr_ref, tab_ref)
+    tab_copy = pltpu.make_async_copy(tab_ref, tab_out, tab_sem)
+    tab_copy.start()
     for qb in range(blocks):
         rows = block_rows(qb)
         keys = (qb + 1) * BLOCK
-        same = segc_ref[rows, :] == segr_ref[:, :keys]
+        same = seg_column(segr_ref, qb, BLOCK) == segr_ref[:, :keys]
         query = lax.broadcasted_iota(jnp.int32, (BLOCK, keys), 0) + qb * BLOCK
         key = lax.broadcasted_iota(jnp.int32, (BLOCK, keys), 1)
         bias[rows, :keys] = jnp.where(same & (key <= query), 0.0, MASKED)
@@ -277,18 +283,19 @@
 
     lax.fori_loop(0, pairs, drain, 0)
     act_copy.wait()
+    tab_copy.wait()
     for p in range(pairs):
         qkv_copy(p).wait()
 
 
 def front(
-    x, w_query, w_key, w_value, tables, seg_col, seg_row, vectors, count, groups, collective_id
+    x, w_query, w_key, w_value, seg_row, vectors, count, groups, collective_id
 ):
     tokens, model_width = x.shape
     pieces = [vector.reshape(vector.shape[0] // LANES, LANES) for vector in vectors]
     total = sum(vector.shape[0] for vector in vectors)
     head_width = w_query.shape[1]
-    length = seg_col.shape[0]
+    length = seg_row.shape[1]
     pairs = head_width // groups // LANES
     whole = pl.BlockSpec(memory_space=pltpu.VMEM)
     any_space = pl.BlockSpec(memory_space=pl.ANY)
@@ -297,13 +304,14 @@
         out_shape=[
             jax.ShapeDtypeStruct((tokens, model_width), BF16),
             jax.ShapeDtypeStruct((pairs, length, 3 * LANES), BF16),
+            jax.ShapeDtypeStruct((4, length, LANES), F32),
             jax.ShapeDtypeStruct((pairs, length, LANES), BF16),
             jax.ShapeDtypeStruct((pairs, 8, length), F32),
             jax.ShapeDtypeStruct((tokens, head_width), BF16),
             jax.ShapeDtypeStruct((1, total), F32),
         ],
-        in_specs=[whole] + [any_space] * 3 + [whole] * (3 + len(pieces)),
-        out_specs=[any_space] * 2 + [whole] * 4,
+        in_specs=[whole] + [any_space] * 3 + [whole] * (1 + len(pieces)),
+        out_specs=[any_space] * 3 + [whole] * 4,
         scratch_shapes=[
             pltpu.VMEM((tokens, model_width), BF16),
             pltpu.VMEM((pairs, length, 3 * LANES), BF16),
@@ -315,6 +323,7 @@
             pltpu.VMEM((length, LANES), BF16),
             pltpu.SemaphoreType.DMA((3 * pairs * groups,)),
             pltpu.SemaphoreType.DMA,
+            pltpu.SemaphoreType.DMA,
             pltpu.SemaphoreType.DMA((pairs,)),
         ]
         + [pltpu.SemaphoreType.DMA((pairs, count))] * 4,
@@ -322,13 +331,13 @@
             collective_id=collective_id, has_side_effects=True, vmem_limit_bytes=VMEM_LIMIT
         ),
         cost_estimate=cost(60),
-    )(x, w_query, w_key, w_value, tables, seg_col, seg_row, *pieces)
+    )(x, w_query, w_key, w_value, seg_row, *pieces)
 
 
 def back_work(env, count, tp_count, groups):
     low_ref, wout_ref, mixed_ref = env["low"], env["w_out"], env["mixed"]
     sums_ref, qkv_ref, o_ref, lse_ref = env["head_sums"], env["qkv"], env["o"], env["lse"]
-    segc_ref, segr_ref, tab_ref, bias = env["seg_col"], env["seg_row"], env["tables"], env["bias"]
+    segr_ref, tab_ref, bias = env["seg_row"], env["tables"], env["bias"]
     grads_ref, vec_grads_ref = env["grads"], env["head_vec_grads"]
     do_ref, scaled, part = env["do"], env["scaled"], env["head_part"]
     do_row, made, delta = env["do_row"], env["made"], env["delta"]
@@ -404,12 +413,11 @@
         return carry
 
     def prepare():
-        expand_tables(env["packed"], tab_ref)
         for kb in range(blocks):
             rows = block_rows(kb)
             start = kb * BLOCK
             shape = (BLOCK, length - start)
-            same = segc_ref[rows, :] == segr_ref[:, start:]
+            same = seg_column(segr_ref, kb, BLOCK) == segr_ref[:, start:]
             key = lax.broadcasted_iota(jnp.int32, shape, 0)
             query = lax.broadcasted_iota(jnp.int32, shape, 1)
             bias[rows, start:] = jnp.where(same & (key <= query), 0.0, MASKED)
@@ -943,8 +951,10 @@
     half = tokens // 2
     size = half // chunks
     ahead = slack * (count - 1)
-    steps = chunks + 2 * ahead
+    spread_out = SLACK_OUT * (count - 1)
+    steps = chunks + ahead + spread_out
     from_first, from_last = slack * z, slack * (count - 1 - z)
+    out_first, out_last = SLACK_OUT * z, SLACK_OUT * (count - 1 - z)
     first, last = z == 0, z == count - 1
     up = jnp.minimum(z + 1, count - 1)
     down = jnp.maximum(z - 1, 0)
@@ -1108,7 +1118,6 @@
     for task in tasks:
         starts_at.append(starts_at[-1] + env[task[3]].shape[0] // ROWS)
     task_total = starts_at[-1]
-    per_group = group - 1
     staged = any(task[0] != "keep" for task in tasks)
 
     def step(t, carry):
@@ -1122,8 +1131,8 @@
             t - from_first,
             lambda c: reduce_step(t, c, from_first, 1, b_rows, in_b, reduce_b, gather_b, first, last),
         )
-        when_chunk(t - ahead - from_first, lambda c: gather_step(c, gather_a, first, last))
-        when_chunk(t - ahead - from_last, lambda c: gather_step(c, gather_b, last, first))
+        when_chunk(t - ahead - out_first, lambda c: gather_step(c, gather_a, first, last))
+        when_chunk(t - ahead - out_last, lambda c: gather_step(c, gather_b, last, first))
         for moment, waited in ((1, plan["late"]), (4, plan["later"])):
 
             @pl.when(t == moment)
@@ -1132,9 +1141,8 @@
                     loads[name].wait()
 
         if num_task:
-            turn = (t // group) * per_group + lax.rem(t, group) - 1
-            free = lax.rem(t, group) != 0
-            slot = lax.rem(turn + per_group + 1, 2)
+            turn = t - 1
+            slot = lax.rem(turn + 2, 2)
 
             for index in range(num_task if staged else 0):
                 low, high = starts_at[index] + 2, min(starts_at[index + 1] + 2, task_total)
@@ -1144,10 +1152,10 @@
                     if tasks[index][0] == "spread":
                         spread_rows(env, task_rows(index, turn - low))
 
-                pl.when(free & (turn >= low) & (turn < high))(staged_done)
+                pl.when((turn >= low) & (turn < high))(staged_done)
             for index in range(num_task):
                 low, high = starts_at[index], starts_at[index + 1]
-                pl.when(free & (turn >= low) & (turn < high))(
+                pl.when((turn >= low) & (turn < high))(
                     lambda index=index, low=low: run_task(index, turn - low, slot)
                 )
         if work_step:
@@ -1157,8 +1165,8 @@
         for name, moment in plan["stores"].items():
             if moment == "reduced":
                 pl.when(t == chunks + ahead)(lambda name=name: whole_store(env, name).start())
-        done_a = t - ahead - from_first - (group - 1)
-        done_b = t - ahead - from_last - (group - 1)
+        done_a = t - ahead - out_first - (group - 1)
+        done_b = t - ahead - out_last - (group - 1)
         has_a = (done_a >= 0) & (done_a < chunks) & (lax.rem(done_a + 64, group) == 0)
         has_b = (done_b >= 0) & (done_b < chunks) & (lax.rem(done_b + 64, group) == 0)
 
@@ -1170,7 +1178,7 @@
                 plan["rows_done"](env, block)
 
         if plan["rows_late"]:
-            late_a = t - 2 * ahead - (group - 1) - 2
+            late_a = t - ahead - spread_out - (group - 1) - 2
 
             place = lax.rem(late_a + 64, group)
 
@@ -1198,7 +1206,7 @@
         assert work_steps <= steps
     lax.fori_loop(0, steps, step, 0)
     if num_task:
-        assert (steps // group) * per_group >= task_total
+        assert steps - 1 >= task_total
     if staged:
         assert task_total >= 2
         for turn in (task_total - 2, task_total - 1):
@@ -1207,7 +1215,7 @@
     if "spread" in env:
         spread_wait(env)
     if plan["rows_late"]:
-        assert chunks + 2 * ahead == steps and group == 4
+        assert group > 2
 
         def rest(place, carry):
             plan["rows_late"](env, (place + 1) * (chunks // group) - 1)
@@ -1361,19 +1369,6 @@
     return dot(left, right, left_dim, right_dim).astype(kind)
 
 
-def rotation_tables(positions):
-    half_size = HEAD // 2
-    index_pairs = jnp.arange(half_size, dtype=F32)
-    theta_rate = jnp.exp(-2.0 * index_pairs / HEAD * jnp.log(10000.0))
-    zeta_base = (2.0 * index_pairs + 0.4 * HEAD) / (1.4 * HEAD)
-    place_float = positions.astype(F32)[..., None]
-    angles = place_float * theta_rate
-    power = jnp.log(zeta_base) * place_float / 512.0
-    return jnp.concatenate(
-        [jnp.cos(angles), jnp.sin(angles), jnp.exp(power), jnp.exp(-power)], axis=-1
-    )
-
-
 def body(
     seq_count,
     tp_count,
@@ -1404,20 +1399,14 @@
     groups = seq_count // row_count
 
     seg_row = lax.dynamic_slice_in_dim(segment_ids, seq_index // groups, 1, 0)
-    seg_col = seg_row.reshape(length, 1)
-    earlier = jnp.sum((seg_row < seg_col).astype(jnp.int32), axis=-1)
-    tables = rotation_tables(jnp.arange(length, dtype=jnp.int32) - earlier)
-
     block = block_in.reshape(tokens, model_width)
     cotangent = out_cotangent.reshape(tokens, model_width)
 
-    first_act, qkv_row, o_row, lse, mixed, vecs = front(
+    first_act, qkv_row, tables, o_row, lse, mixed, vecs = front(
         block,
         w_query,
         w_key,
         w_value,
-        tables,
-        seg_col,
         seg_row,
         (
             first_gain, first_bias, second_gain, second_bias,
@@ -1540,16 +1529,16 @@
             qkv=qkv_row,
             o=o_row,
             lse=lse,
-            packed=tables,
+            tables=tables,
             first_act=first_act,
             head_act=head_act,
         ),
-        dict(vecs=vecs, seg_col=seg_col, seg_row=seg_row),
+        dict(vecs=vecs, seg_row=seg_row),
         (),
         5,
         tokens=tokens,
         late=("low", "w_out", "mixed", "head_sums"),
-        later=("qkv", "o", "lse", "packed", "first_act", "head_act"),
+        later=("qkv", "o", "lse", "tables", "first_act", "head_act"),
         owns=(
             ("grads", shape_of((tokens, 3 * head_width), BF16)),
             ("head_vec_grads", shape_of((2, 8, head_width))),
@@ -1563,7 +1552,6 @@
             ("scaled", pltpu.VMEM((tokens, head_width), F32)),
             ("head_part", pltpu.VMEM((8, tokens), F32)),
             ("head_landed", landed),
-            ("tables", pltpu.VMEM((4, length, LANES), F32)),
             ("do_row", pltpu.VMEM((pairs, length, LANES), BF16)),
             ("made", pltpu.VMEM((pairs, length, 3 * LANES), BF16)),
             ("bias", pltpu.VMEM((length, length), F32)),

time: 592 us -> 584 us (0.986)
  no operation moved by 1% of the time
where the time goes in v11:
time: 584 us; the launch traced here: 583 us
  Pallas kernels  568 us (97%)
  between operations  14.2 us (2%)
    pallas_call x4, Pallas kernels, line_sum(): pl.pallas_call(functools.partial(line_kernel, plan, count, chunks, group,...  495 us
    pallas_call x1, Pallas kernels, front(): pl.pallas_call(functools.partial(front_kernel, count, groups, len(pieces)...  59.6 us
    pallas_call x1, Pallas kernels, last_results(): pl.pallas_call(last_kernel, grid=(steps,), out_shape=[jax.ShapeDtypeStruc...  13.6 us
  transfers between devices with their start and end apart: 2, of which 0 were waited for; matrix products, arithmetic and copies ran while one was open for 0% of the time, Pallas kernels for 41%

profile of v11, /device:TPU:0, one launch (start us, length us, event | category | flops | bytes accessed | tf_op | source)
XLA Modules:
  0.0 583.4 jit_solution(13416369547180429827)
XLA Ops:
  7.2 0.0 copy-start
  7.2 0.0 reduce-scatter.3.cloned.1.call-start
  7.2 0.7 copy-done
  7.9 0.6 constant_dynamic-slice_fusion.refs_4_.refs_12_
  8.5 59.6 %shard_map.288 = (bf16[1024,2048]{1,0:T(8,128)(2,1)}, bf16[4,1024,384]{2,1,0:T(8,128)(2,1)}, f32[4,1024,128]{2,1,0:T(8,128)}, bf16[4,1024,128]{2,1,0:T(8,128)(2,...) custom-call(bf16[1024,2048]{1,0:T(8,128)(2,1)} %bitcast.22, bf16[2048,512]{1,0:T(8,128)(2,1)} %refs_3_.3, ...), custom_call_target="tpu_custom_call" | custom-call | flops 65999998976 | tf_op jit(solution)/shard_map/pallas_call | solution.py:302
  68.1 134.9 %shard_map.289 = (bf16[1024,2048]{1,0:T(8,128)(2,1)}, f32[512,2048]{1,0:T(8,128)}, bf16[1024,512]{1,0:T(8,128)(2,1)}, f32[8,1024]{1,0:T(8,128)}, bf16[1024,2048]...) custom-call(bf16[1024,512]{1,0:T(8,128)(2,1)} %get-tuple-element.62.refs_0_.refs_3_, ...), custom_call_target="tpu_custom_call" | custom-call | flops 153999998976 | tf_op jit(solution)/shard_map/pallas_call | solution.py:1316
  203.0 118.9 %shard_map.290 = (bf16[1024,2048]{1,0:T(8,128)(2,1)}, f32[2,8,2048]{2,1,0:T(8,128)}, f32[512,2048]{1,0:T(8,128)}, bf16[1024,2048]{1,0:T(8,128)(2,1)}, bf16[2048,...) custom-call(bf16[1024,2048]{1,0:T(8,128)(2,1)} %get-tuple-element.64.refs_0_, ...), custom_call_target="tpu_custom_call" | custom-call | flops 121000001536 | tf_op jit(solution)/shard_map/pallas_call | solution.py:1316
  321.9 0.0 reduce-scatter.3.cloned.1.call-update
  322.0 0.0 reduce-scatter.5.cloned.1.call-start
  322.0 118.3 %shard_map.291 = (bf16[1024,2048]{1,0:T(8,128)(2,1)}, bf16[1024,1536]{1,0:T(8,128)(2,1)}, f32[2,8,512]{2,1,0:T(8,128)}, bf16[2048,2048]{1,0:T(8,128)(2,1)}) custom-call(bf16[1024,2048]{1,0:T(8,128)(2,1)} %get-tuple-element.68.refs_0_, bf16[1024,2048]{1,0:T(8,128)(2,1)} %get-tuple-element.69.refs_1_, bf16[2048,512]{1,0:T(8,128)(2,1)} %refs_2_.3, ...), custom_call_target="tpu_custom_call" | custom-call | flops 121000001536 | tf_op jit(solution)/shard_map/pallas_call | solution.py:1316
  440.4 0.0 reduce-scatter.3.cloned.1.call-done.up_ref
  440.4 0.0 reduce-scatter.5.cloned.1.call-update
  440.4 122.4 %shard_map.292 = (bf16[1024,2048]{1,0:T(8,128)(2,1)}, f32[2,8,2048]{2,1,0:T(8,128)}, f32[8,256]{1,0:T(8,128)}, f32[8,2560]{1,0:T(8,128)}) custom-call(bf16[1024,1536]{1,0:T(8,128)(2,1)} %get-tuple-element.83.refs_0_, bf16[1024,2048]{1,0:T(8,128)(2,1)} %bitcast.24, f32[512,2048]{1,0:T(8,128)} %get-tuple-element.84.refs_2_, bf16[2048,512]{1,0:T(8,128)(2,1)} %refs_3_.3, ...), custom_call_target="tpu_custom_call" | custom-call | flops 121000001536 | tf_op jit(solution)/shard_map/pallas_call | solution.py:1316
  562.9 0.0 reduce-scatter.5.cloned.1.call-done.head_ref
  562.9 0.0 copy-start.1
  562.9 13.6 %shard_map.293 = (f32[256,512]{1,0:T(8,128)}, f32[256,512]{1,0:T(8,128)}, f32[256,512]{1,0:T(8,128)}, f32[256,512]{1,0:T(8,128)}, f32[256,2048]{1,0:T(8,128)}, /...) custom-call(bf16[256,2048]{1,0:T(8,128)(2,1)} %reduce-scatter.5.clon, ...), custom_call_target="tpu_custom_call" | custom-call | flops 11000000512 | tf_op jit(solution)/shard_map/pallas_call | solution.py:614
  576.5 0.0 copy-done.1
Async XLA Ops:
  7.2 0.8 copy-start
  7.2 433.2 %reduce-scatter.3.cloned.1.call-start = ((), (), s32[]{:S(2)}) async-start(), calls=%async_computation.2 | async-start | bytes 9437184 | tf_op jit(solution)/shard_map/reduce_scatter | solution.py:1511
  322.0 240.9 %reduce-scatter.5.cloned.1.call-start = ((), (), s32[]{:S(2)}) async-start(), calls=%async_computation.3 | async-start | bytes 9437184 | tf_op jit(solution)/shard_map/reduce_scatter | solution.py:1511
  562.9 13.6 %copy-start.1 = (s32[8,1024]{1,0:T(8,128)S(1)}, s32[8,1024]{1,0:T(8,128)}, u32[]{:S(2)}) copy-start(s32[8,1024]{1,0:T(8,128)} %param.18) | copy-start | bytes 98308
Sparse Core Ops, SparseCore 0:
  322.1 110.8 reduce-scatter.2
  440.5 70.8 reduce-scatter.4

commit v12 on v11

--- a/solution.py
+++ b/solution.py
@@ -19,7 +19,7 @@
 SLACK = 2
 SLACK_OUT = 2
 ROWS = 256
-TILE = 512
+TILE = 1024
 VMEM_LIMIT = 60 * 1024 * 1024
 
 

time: 584 us -> 581 us (level)
  no operation moved by 1% of the time
where the time goes in v12:
time: 581 us
  Pallas kernels  565 us (97%)
  between operations  14.2 us (2%)
    pallas_call x4, Pallas kernels, line_sum(): pl.pallas_call(functools.partial(line_kernel, plan, count, chunks, group,...  492 us
    pallas_call x1, Pallas kernels, front(): pl.pallas_call(functools.partial(front_kernel, count, groups, len(pieces)...  59.6 us
    pallas_call x1, Pallas kernels, last_results(): pl.pallas_call(last_kernel, grid=(steps,), out_shape=[jax.ShapeDtypeStruc...  13.6 us
  transfers between devices with their start and end apart: 2, of which 0 were waited for; matrix products, arithmetic and copies ran while one was open for 0% of the time, Pallas kernels for 41%

profile of v12, /device:TPU:0, one launch (start us, length us, event | category | flops | bytes accessed | tf_op | source)
XLA Modules:
  0.0 580.9 jit_solution(7290538300477173029)
XLA Ops:
  7.2 0.0 copy-start
  7.2 0.0 reduce-scatter.3.cloned.1.call-start
  7.2 0.7 copy-done
  7.9 0.6 constant_dynamic-slice_fusion.refs_4_.refs_12_
  8.5 59.6 %shard_map.288 = (bf16[1024,2048]{1,0:T(8,128)(2,1)}, bf16[4,1024,384]{2,1,0:T(8,128)(2,1)}, f32[4,1024,128]{2,1,0:T(8,128)}, bf16[4,1024,128]{2,1,0:T(8,128)(2,...) custom-call(bf16[1024,2048]{1,0:T(8,128)(2,1)} %bitcast.22, bf16[2048,512]{1,0:T(8,128)(2,1)} %refs_3_.3, ...), custom_call_target="tpu_custom_call" | custom-call | flops 65999998976 | tf_op jit(solution)/shard_map/pallas_call | solution.py:302
  68.1 134.2 %shard_map.289 = (bf16[1024,2048]{1,0:T(8,128)(2,1)}, f32[512,2048]{1,0:T(8,128)}, bf16[1024,512]{1,0:T(8,128)(2,1)}, f32[8,1024]{1,0:T(8,128)}, bf16[1024,2048]...) custom-call(bf16[1024,512]{1,0:T(8,128)(2,1)} %get-tuple-element.62.refs_0_.refs_3_, ...), custom_call_target="tpu_custom_call" | custom-call | flops 153999998976 | tf_op jit(solution)/shard_map/pallas_call | solution.py:1316
  202.3 117.6 %shard_map.290 = (bf16[1024,2048]{1,0:T(8,128)(2,1)}, f32[2,8,2048]{2,1,0:T(8,128)}, f32[512,2048]{1,0:T(8,128)}, bf16[1024,2048]{1,0:T(8,128)(2,1)}, bf16[2048,...) custom-call(bf16[1024,2048]{1,0:T(8,128)(2,1)} %get-tuple-element.64.refs_0_, ...), custom_call_target="tpu_custom_call" | custom-call | flops 121000001536 | tf_op jit(solution)/shard_map/pallas_call | solution.py:1316
  319.9 0.0 reduce-scatter.3.cloned.1.call-update
  320.0 0.0 reduce-scatter.5.cloned.1.call-start
  320.0 118.8 %shard_map.291 = (bf16[1024,2048]{1,0:T(8,128)(2,1)}, bf16[1024,1536]{1,0:T(8,128)(2,1)}, f32[2,8,512]{2,1,0:T(8,128)}, bf16[2048,2048]{1,0:T(8,128)(2,1)}) custom-call(bf16[1024,2048]{1,0:T(8,128)(2,1)} %get-tuple-element.68.refs_0_, bf16[1024,2048]{1,0:T(8,128)(2,1)} %get-tuple-element.69.refs_1_, bf16[2048,512]{1,0:T(8,128)(2,1)} %refs_2_.3, ...), custom_call_target="tpu_custom_call" | custom-call | flops 121000001536 | tf_op jit(solution)/shard_map/pallas_call | solution.py:1316
  438.8 0.0 reduce-scatter.3.cloned.1.call-done.up_ref
  438.9 0.0 reduce-scatter.5.cloned.1.call-update
  438.9 121.5 %shard_map.292 = (bf16[1024,2048]{1,0:T(8,128)(2,1)}, f32[2,8,2048]{2,1,0:T(8,128)}, f32[8,256]{1,0:T(8,128)}, f32[8,2560]{1,0:T(8,128)}) custom-call(bf16[1024,1536]{1,0:T(8,128)(2,1)} %get-tuple-element.83.refs_0_, bf16[1024,2048]{1,0:T(8,128)(2,1)} %bitcast.24, f32[512,2048]{1,0:T(8,128)} %get-tuple-element.84.refs_2_, bf16[2048,512]{1,0:T(8,128)(2,1)} %refs_3_.3, ...), custom_call_target="tpu_custom_call" | custom-call | flops 121000001536 | tf_op jit(solution)/shard_map/pallas_call | solution.py:1316
  560.4 0.0 reduce-scatter.5.cloned.1.call-done.head_ref
  560.4 0.0 copy-start.1
  560.4 13.6 %shard_map.293 = (f32[256,512]{1,0:T(8,128)}, f32[256,512]{1,0:T(8,128)}, f32[256,512]{1,0:T(8,128)}, f32[256,512]{1,0:T(8,128)}, f32[256,2048]{1,0:T(8,128)}, /...) custom-call(bf16[256,2048]{1,0:T(8,128)(2,1)} %reduce-scatter.5.clon, ...), custom_call_target="tpu_custom_call" | custom-call | flops 11000000512 | tf_op jit(solution)/shard_map/pallas_call | solution.py:614
  574.0 0.0 copy-done.1
Async XLA Ops:
  7.2 0.8 copy-start
  7.2 431.7 %reduce-scatter.3.cloned.1.call-start = ((), (), s32[]{:S(2)}) async-start(), calls=%async_computation.2 | async-start | bytes 9437184 | tf_op jit(solution)/shard_map/reduce_scatter | solution.py:1511
  320.0 240.4 %reduce-scatter.5.cloned.1.call-start = ((), (), s32[]{:S(2)}) async-start(), calls=%async_computation.3 | async-start | bytes 9437184 | tf_op jit(solution)/shard_map/reduce_scatter | solution.py:1511
  560.4 13.6 %copy-start.1 = (s32[8,1024]{1,0:T(8,128)S(1)}, s32[8,1024]{1,0:T(8,128)}, u32[]{:S(2)}) copy-start(s32[8,1024]{1,0:T(8,128)} %param.18) | copy-start | bytes 98308
Sparse Core Ops, SparseCore 0:
  320.1 111.0 reduce-scatter.2
  439.0 69.3 reduce-scatter.4
